TPU v7x, 128 devices: a whole 4x4x4 slice. The times are simulated.
128 devices in a mesh: row: 8 (over y, z_lo), col: 8 (over x, core), feat: 2 (over z_hi).
Axes of the slice: x: 4, y: 4, z: 4 (z_hi: 2, z_lo: 2; z = z_hi * 2 + z_lo), core: 2. Of those that a mesh axis runs over, the one named last changes fastest.
Arguments:
- features: bfloat16 [32768, 128], P(('col', 'row')), may hold values from -6 to 6
- weight: bfloat16 [128, 256], P(None, 'feat'), may hold values from -0.5 to 0.5
- hidden_bias: float32 [256], P('feat'), may hold values from -4 to 4
- adjacency_tiles: bfloat16 [8, 8, 640, 128, 128], P('row', 'col'), may hold values from -0.078125 to 0.078125
- tile_rows: int32 [8, 8, 640], P('row', 'col'), may hold values from 0 to 31
- tile_columns: int32 [8, 8, 640], P('row', 'col'), may hold values from 0 to 31
- tile_count: int32 [8, 8], P('row', 'col'), may hold values from 1 to 640, as said below
- cotangent: bfloat16 [32768, 256], P(('row', 'col'), 'feat'), may hold values from -6 to 6
Outputs:
- activations: bfloat16 [32768, 256], P(('row', 'col'), 'feat')
- grad_features: float32 [32768, 128], P(('col', 'row'))
- grad_weight: float32 [128, 256], P(None, 'feat')
- grad_bias: float32 [256], P('feat')
Inputs may be any that keep to these rules, and one draw needn't show every extreme that they name: `tile_count`: tiles at or past this count on a device are ignored; some device uses all 640.
All inputs are finite; a program needn't handle non-finite values.
Results may differ from a plain program's by a relative error of at most 0.024.
Values may be sent and summed in bfloat16 or wider, within the bound.
No kernel may reach another device: no remote copies, remote signals or barrier semaphores. Data moves between devices by JAX's collectives and lax.ppermute only.
A program may use at most 128 MiB of HBM per device.

v0:
```python
import functools

import jax
import jax.numpy as jnp
from jax import lax
from jax.experimental import pallas as pl
from jax.experimental.pallas import tpu as pltpu
from jax.sharding import PartitionSpec as P

F32 = jnp.float32
BF16 = jnp.bfloat16
TILE = 128
PER = 32
FORWARD = 2
BACKWARD = 4
VMEM = pl.BlockSpec(memory_space=pltpu.VMEM)
SMEM = pl.BlockSpec(memory_space=pltpu.SMEM)
ANY = pl.BlockSpec(memory_space=pl.ANY)
PARAMS = pltpu.CompilerParams(vmem_limit_bytes=8 * 1024 * 1024)
PICK_PARAMS = pltpu.CompilerParams(vmem_limit_bytes=16 * 1024 * 1024)


def swap(values, axis, mask):
    size = lax.axis_size(axis)
    return lax.ppermute(values, axis, [(i, i ^ mask) for i in range(size)])


def near(values):
    return pltpu.with_memory_space_constraint(values, pltpu.VMEM)


def iota(shape, dim):
    return lax.broadcasted_iota(jnp.int32, shape, dim)


def order(key, used, source, item, n_keys, length, width):
    n = key.shape[1]
    hit = ((iota((n_keys, n), 0) == key) & used).astype(F32)
    upto = (iota((n, n), 0) <= iota((n, n), 1)).astype(BF16)
    rank = jnp.dot(hit.astype(BF16), upto, preferred_element_type=F32)
    groups = jnp.floor((rank[:, n - 1 :] + (width - 1)) * (1.0 / width))
    below = (iota((n_keys, n_keys), 0) >= iota((n_keys, n_keys), 1)).astype(BF16)
    high = jnp.floor(groups * (1.0 / 128))
    lane = iota((n_keys, TILE), 1)
    parts = jnp.where(lane == 0, groups - high * 128, jnp.where(lane == 1, high, 0.0))
    ends = jnp.dot(below, parts.astype(BF16), preferred_element_type=F32)
    end = ends[:, 0:1] + ends[:, 1:2] * 128
    first = (end - groups) * width
    slot = jnp.sum(hit * (first + rank - 1.0), axis=0, keepdims=True)
    slot = jnp.where(used, slot.astype(jnp.int32), -1)
    at = (iota((length, n), 0) == slot).astype(F32).astype(BF16)
    line = iota((8, n), 0)
    values = jnp.where(line == 2, source, 1)
    values = jnp.where(line == 0, item & 255, jnp.where(line == 1, item >> 8, values))
    found = lax.dot_general(
        values.astype(F32).astype(BF16), at, (((1,), (1,)), ((), ())), preferred_element_type=F32
    ).astype(jnp.int32)
    passed = (end * width).astype(jnp.int32) <= iota((n_keys, length), 1)
    target = jnp.sum(passed.astype(F32), axis=0, keepdims=True).astype(jnp.int32)
    items = jnp.where(found[3:4] > 0, found[0:1] + found[1:2] * 256, -1)
    steps = (jnp.max(end).astype(jnp.int32) * width + PER - 1) // PER
    return items, found[2:3], target, steps, slot


def pick_kernel(n_out, n_back, count, ids, rows, columns, fetched, forward, backward, steps):
    row, column = rows[0], columns[0]
    index = iota(row.shape, 1)
    length = forward.shape[1]
    used = (index < count[0, 0]) & (((column >> 1) & 1) == ids[0])
    place = (column >> 2) * 2 + (column & 1)
    near_place = jnp.bitwise_xor(column >> 2, ids[2]) * 2 + (column & 1)
    near_row = jnp.bitwise_xor(row >> 2, ids[1]) * 4 + (row & 3)
    items, source, target, steps[0], slot = order(
        row, used, near_place, index, n_out, length, FORWARD
    )
    fetched[...] = jnp.maximum(items, 0)
    here = jnp.where(items >= 0, iota(items.shape, 1), length)
    forward[...] = here + source * 1024 + target * 65536
    items, source, target, steps[1], slot = order(
        place, used, near_row, slot, n_back, length, BACKWARD
    )
    here = jnp.where(items >= 0, items, length)
    backward[...] = here + source * 1024 + target * 65536


def pick(count, ids, rows, columns, n_out, n_back):
    length = rows.shape[-1] + max(n_out * (FORWARD - 1), n_back * (BACKWARD - 1)) + PER
    length = -(-length // TILE) * TILE
    slots = jax.ShapeDtypeStruct((1, length), jnp.int32)
    return pl.pallas_call(
        functools.partial(pick_kernel, n_out, n_back),
        out_shape=[slots, slots, slots, jax.ShapeDtypeStruct((2,), jnp.int32)],
        in_specs=[SMEM, SMEM, VMEM, VMEM],
        out_specs=[VMEM, VMEM, VMEM, SMEM],
        compiler_params=PICK_PARAMS,
        name="pick_tiles",
    )(count, ids, rows, columns)


def add_products(flipped, g, picked, held, source, total):
    width = BACKWARD if flipped else FORWARD
    places = []
    products = []
    for at in range(0, PER, width):
        codes = [picked[0, g * PER + at + j] for j in range(width)]
        places.append(codes[0] >> 16)
        mine = [held[code & 1023] for code in codes]
        other = [source[(code >> 10) & 63] for code in codes]
        left, right = (other, mine) if flipped else (mine, other)
        products.append(
            jnp.dot(
                jnp.concatenate(left, 1), jnp.concatenate(right, 0), preferred_element_type=F32
            )
        )
    for place, product in zip(places, products):
        total[place] += product


def forward_kernel(steps, ids, fetched, picked, tiles, *refs):
    sources, (held, kept, sent, gathered, total, arrived) = refs[:-6], refs[-6:]
    count = steps[0]

    def start(g, carry):
        for j in range(PER):
            source = tiles.at[fetched[0, g * PER + j]]
            pltpu.make_async_copy(source, held.at[g * PER + j], arrived.at[g]).start()
        return carry

    lax.fori_loop(0, count, start, 0)
    held[held.shape[0] - 1] = jnp.zeros((TILE, TILE), BF16)
    total[...] = jnp.zeros_like(total)
    for m, source in enumerate(sources):
        gathered[2 * m : 2 * m + 2] = source[...].reshape(2, TILE, TILE)

    def step(g, carry):
        block = held.at[pl.ds(g * PER, PER)]
        pltpu.make_async_copy(tiles.at[pl.ds(0, PER)], block, arrived.at[g]).wait()
        add_products(False, g, picked, held, gathered, total)
        return carry

    lax.fori_loop(0, count, step, 0)
    for k in range(kept.shape[0]):
        own = jnp.bitwise_xor(ids[1], 2 * k)
        kept[k] = total[pl.ds(own * 4, 4)]
        sent[k] = total[pl.ds(jnp.bitwise_xor(own, 1) * 4, 4)].astype(BF16)


def tiles_forward(steps, ids, fetched, picked, tiles, sources, n_out):
    shape = (n_out // 8, 4, TILE, TILE)
    length = fetched.shape[1]
    return pl.pallas_call(
        forward_kernel,
        out_shape=[
            pltpu.VMEM((length + 1, TILE, TILE), BF16),
            pltpu.VMEM(shape, F32),
            pltpu.VMEM(shape, BF16),
        ],
        in_specs=[SMEM, SMEM, SMEM, SMEM, ANY] + [VMEM] * len(sources),
        out_specs=[VMEM] * 3,
        scratch_shapes=[
            pltpu.VMEM((2 * len(sources), TILE, TILE), BF16),
            pltpu.VMEM((n_out + 1, TILE, TILE), F32),
            pltpu.SemaphoreType.DMA((length // PER,)),
        ],
        compiler_params=PARAMS,
        name="tiles_forward",
    )(
        steps,
        ids,
        fetched,
        picked,
        pltpu.with_memory_space_constraint(tiles, pltpu.HBM),
        *[near(values) for values in sources],
    )


def backward_kernel(steps, ids, picked, held, *refs):
    sources, (kept, first, second, third, gathered, total) = refs[:-6], refs[-6:]
    total[...] = jnp.zeros_like(total)
    for m, source in enumerate(sources):
        gathered[4 * m : 4 * m + 4] = source[0 : 4 * TILE].reshape(4, TILE, TILE)

    def step(g, carry):
        add_products(True, g, picked, held, gathered, total)
        return carry

    lax.fori_loop(0, steps[1], step, 0)
    across = ids[2] >> 1
    kept[...] = total[pl.ds(across * 4, 4)]
    for k, out in enumerate((first, second, third)):
        out[...] = total[pl.ds(jnp.bitwise_xor(across, k + 1) * 4, 4)].astype(BF16)


def tiles_backward(steps, ids, picked, held, sources, n_back):
    shape = (n_back // 4, TILE, TILE)
    return pl.pallas_call(
        backward_kernel,
        out_shape=[pltpu.VMEM(shape, F32)] + [pltpu.VMEM(shape, BF16)] * 3,
        in_specs=[SMEM, SMEM, SMEM] + [VMEM] * (1 + len(sources)),
        out_specs=[VMEM] * 4,
        scratch_shapes=[
            pltpu.VMEM((4 * len(sources), TILE, TILE), BF16),
            pltpu.VMEM((n_back + 1, TILE, TILE), F32),
        ],
        compiler_params=PARAMS,
        name="tiles_backward",
    )(steps, ids, picked, near(held), *[near(values) for values in sources])


def pair_kernel(kept, got, first, *others):
    first[...] = kept[0] + got[0].astype(F32)
    for k, other in enumerate(others):
        other[...] = (kept[k + 1] + got[k + 1].astype(F32)).astype(BF16)


def pair_sum(kept, got):
    shape = kept.shape[1:]
    n = kept.shape[0] - 1
    return pl.pallas_call(
        pair_kernel,
        out_shape=[pltpu.VMEM(shape, F32)] + [pltpu.VMEM(shape, BF16)] * n,
        in_specs=[VMEM] * 2,
        out_specs=[VMEM] * (n + 1),
        compiler_params=PARAMS,
        name="pair_sum",
    )(near(kept), near(got))


def own_kernel(first, a, b, c, total, sent):
    value = first[...] + a[...].astype(F32) + b[...].astype(F32) + c[...].astype(F32)
    total[...] = value
    sent[...] = value.astype(BF16)


def own_sum(first, others):
    return pl.pallas_call(
        own_kernel,
        out_shape=[pltpu.VMEM(first.shape, F32), pltpu.VMEM(first.shape, BF16)],
        in_specs=[VMEM] * 4,
        out_specs=[VMEM] * 2,
        compiler_params=PARAMS,
        name="own_sum",
    )(near(first), *[near(values) for values in others])


def middle_kernel(own, other, weight, bias, cotangent, activations, back, back_sent, grads):
    blocks = own.shape[0]
    rows = blocks * TILE
    sums = (own[...] + other[...].astype(F32)).astype(BF16).reshape(rows, TILE)
    preact = jnp.dot(sums, weight[...], preferred_element_type=F32) + bias[...]
    sigma = jax.nn.sigmoid(preact)
    activations[...] = (preact * sigma).astype(BF16)
    grad = cotangent[...].astype(F32) * (sigma * (1.0 + preact * (1.0 - sigma)))
    grad_pre = grad.astype(BF16)
    grads[0:TILE] = lax.dot_general(
        sums, grad_pre, (((0,), (0,)), ((), ())), preferred_element_type=F32
    )
    total = jnp.sum(grad_pre.astype(F32), axis=0, keepdims=True)
    grads[TILE : TILE + 8] = jnp.broadcast_to(total, (8, TILE))
    for b in range(blocks):
        value = lax.dot_general(
            weight[...],
            grad_pre[b * TILE : (b + 1) * TILE],
            (((1,), (1,)), ((), ())),
            preferred_element_type=F32,
        )
        back[b] = value
        back_sent[b] = value.astype(BF16)


def middle(own, other, weight, bias, cotangent):
    return pl.pallas_call(
        middle_kernel,
        out_shape=[
            jax.ShapeDtypeStruct(cotangent.shape, BF16),
            pltpu.VMEM(own.shape, F32),
            pltpu.VMEM(own.shape, BF16),
            pltpu.VMEM((TILE + 8, TILE), F32),
        ],
        in_specs=[VMEM] * 5,
        out_specs=[VMEM] * 4,
        compiler_params=PARAMS,
        name="middle",
    )(near(own), near(other), weight, bias, cotangent)


def message_kernel(back, other, grads, message):
    blocks = back.shape[0]
    value = back[...] + other[...].astype(F32)
    message[0 : blocks * TILE] = value.astype(BF16).reshape(blocks * TILE, TILE)
    message[blocks * TILE : (blocks + 1) * TILE] = grads[0:TILE].astype(BF16)
    rest = jnp.concatenate([grads[TILE : TILE + 8]] * 2, 0)
    line = iota(rest.shape, 0)
    terms = jnp.zeros(rest.shape, F32)
    for k in range(3):
        term = rest.astype(BF16).astype(F32)
        terms = jnp.where(line == k, term, terms)
        rest = rest - term
    message[(blocks + 1) * TILE : (blocks + 1) * TILE + 16] = terms.astype(BF16)


def message(back, other, grads):
    rows = (back.shape[0] + 1) * TILE + 16
    return pl.pallas_call(
        message_kernel,
        out_shape=pltpu.VMEM((rows, TILE), BF16),
        in_specs=[VMEM] * 3,
        out_specs=VMEM,
        compiler_params=PARAMS,
        name="message",
    )(near(back), near(other), near(grads))


def grad_kernel(*refs):
    messages, grads = refs[:-1], refs[-1]
    last = messages[0].shape[0] - 16
    weight = jnp.zeros((TILE, TILE), F32)
    bias = jnp.zeros((16, TILE), F32)
    for one in messages:
        weight = weight + one[last - TILE : last].astype(F32)
        bias = bias + one[last : last + 16].astype(F32)
    grads[0:TILE] = weight
    grads[TILE : TILE + 8] = jnp.broadcast_to(jnp.sum(bias, axis=0, keepdims=True), (8, TILE))


def grad_sum(messages):
    return pl.pallas_call(
        grad_kernel,
        out_shape=pltpu.VMEM((TILE + 8, TILE), F32),
        in_specs=[VMEM] * len(messages),
        out_specs=VMEM,
        compiler_params=PARAMS,
        name="grad_sum",
    )(*[near(one) for one in messages])


def line_kernel(ids, kept, a, b, c, own, own_sent, other_sent):
    value = kept[...] + a[...].astype(F32) + b[...].astype(F32) + c[...].astype(F32)
    blocks = own.shape[0]
    side = ids[2] & 1
    for z in range(2):
        half = value[z * blocks : (z + 1) * blocks]

        @pl.when(side == z)
        def _():
            own[...] = half
            own_sent[...] = half.astype(BF16)

        @pl.when(side != z)
        def _():
            other_sent[...] = half.astype(BF16)


def line_sum(ids, kept, others):
    shape = (kept.shape[0] // 2, TILE, TILE)
    return pl.pallas_call(
        line_kernel,
        out_shape=[pltpu.VMEM(shape, F32), pltpu.VMEM(shape, BF16), pltpu.VMEM(shape, BF16)],
        in_specs=[SMEM] + [VMEM] * 4,
        out_specs=[VMEM] * 3,
        compiler_params=PARAMS,
        name="line_sum",
    )(ids, near(kept), *[near(values) for values in others])


def finish_kernel(ids, own, beside, far, corner, grads, more, features, weight, bias):
    blocks = own.shape[0]
    for b in range(blocks):
        mine = own[b] + beside[b].astype(F32)
        other = far[b].astype(F32) + corner[b].astype(F32)
        features[pl.ds((ids[0] * blocks + b) * TILE, TILE)] = mine.T
        features[pl.ds(((1 - ids[0]) * blocks + b) * TILE, TILE)] = other.T
    weight[...] = grads[0:TILE] + more[0:TILE]
    bias[...] = grads[TILE : TILE + 1] + more[TILE : TILE + 1]


def finish(ids, own, beside, far, corner, grads, more):
    return pl.pallas_call(
        finish_kernel,
        out_shape=[
            jax.ShapeDtypeStruct((2 * own.shape[0] * TILE, TILE), F32),
            jax.ShapeDtypeStruct((TILE, TILE), F32),
            jax.ShapeDtypeStruct((1, TILE), F32),
        ],
        in_specs=[SMEM] + [VMEM] * 6,
        out_specs=[VMEM] * 3,
        compiler_params=PARAMS,
        name="finish",
    )(ids, near(own), near(beside), near(far), near(corner), near(grads), near(more))


def local(
    features, weight, hidden_bias, adjacency_tiles, tile_rows, tile_columns, tile_count, cotangent
):
    tiles = adjacency_tiles[0, 0]
    n_row, n_col = lax.axis_size("row"), lax.axis_size("col")
    own_rows, fin = features.shape
    blocks = own_rows // TILE
    n_out, n_back = blocks * n_col, blocks // 2 * n_row
    half = lax.axis_index("feat")
    ids = jnp.stack([half, lax.axis_index("col"), lax.axis_index("row")]).astype(jnp.int32)

    mine = lax.dynamic_slice_in_dim(features, half * (own_rows // 2), own_rows // 2, 0)
    sources = [swap(mine, "row", mask) for mask in range(1, n_row)]
    lists = pick(tile_count, ids, tile_rows, tile_columns, n_out, n_back)
    lists, sources = lax.optimization_barrier((lists, sources))
    fetched, forward, backward, steps = lists

    held, kept, sent = tiles_forward(steps, ids, fetched, forward, tiles, [mine, *sources], n_out)
    first, *others = pair_sum(kept, swap(sent, "col", 1))
    others = [swap(other, "col", 2 * k + 2) for k, other in enumerate(others)]
    own, sent = own_sum(first, others)
    other = swap(sent, "feat", 1)
    activations, back, back_sent, grads = middle(own, other, weight, hidden_bias[None], cotangent)

    mine = message(back, swap(back_sent, "feat", 1), grads)
    far = [swap(mine, "col", mask) for mask in (2, 6, 4)]
    beside = swap(mine, "col", 1)
    far = lax.optimization_barrier(far)
    across = [swap(values, "col", 1) for values in far]
    sources = [mine, beside, far[0], across[0], far[2], across[2], far[1], across[1]]
    grads = grad_sum(sources)
    more = swap(grads, "row", 1)
    kept, *others = tiles_backward(steps, ids, backward, held, sources, n_back)
    others, more = lax.optimization_barrier((others, more))
    grads = grads + more

    others = [swap(other, "row", 2 * k + 2) for k, other in enumerate(others)]
    others, more = lax.optimization_barrier((others, swap(grads, "row", 2)))
    grads = grads + more
    own, own_sent, other_sent = line_sum(ids, kept, others)
    far = swap(own_sent, "feat", 1)
    corner = swap(other_sent, ("row", "feat"), 3)
    beside = swap(other_sent, "row", 1)
    far, corner, beside, more = lax.optimization_barrier(
        (far, corner, beside, swap(grads, "row", 4))
    )
    grad_features, grad_weight, grad_bias = finish(ids, own, beside, far, corner, grads, more)
    return (activations, grad_features, grad_weight, grad_bias[0])


def solution(mesh):
    placed = (
        P(("col", "row"), None),
        P(None, "feat"),
        P("feat"),
        P("row", "col", None, None, None),
        P("row", "col", None),
        P("row", "col", None),
        P("row", "col"),
        P(("row", "col"), "feat"),
    )
    return jax.shard_map(
        local,
        mesh=mesh,
        in_specs=placed,
        out_specs=(P(("row", "col"), "feat"), P(("col", "row"), None), P(None, "feat"), P("feat")),
        check_vma=False,
    )
```

profile of v0, /device:TPU:0, one launch (start us, length us, event | category | flops | bytes accessed | tf_op | source)
XLA Modules:
  0.0 97.8 jit_solution(10515643374151291247)
XLA Ops:
  0.6 0.0 copy-start
  0.7 0.9 copy-done
  1.5 4.5 %collective-permute-start.6 = (bf16[256,128]{1,0:T(8,128)(2,1)S(1)}, bf16[256,128]{1,0:T(8,128)(2,1)S(1)}, u32[]{:S(2)}, u32[]{:S(2)}) collective-permute-start(bf16[256,128]{1,0:T(8,128)(2,1)S(1)} %constant_dynamic-slice_fusion.refs_0_), channel_id=1, source_target_pairs={{0,112},{16,96},{32,80},{48,64},{64,48},{80,32},{96,16},{112,0},{1... | collective-permute-start | bytes 196616 | tf_op jit(solution)/shard_map/ppermute | solution.py:25
  6.0 0.2 collective-permute-start.5
  6.2 1.5 %collective-permute-start.4 = (bf16[256,128]{1,0:T(8,128)(2,1)S(1)}, bf16[256,128]{1,0:T(8,128)(2,1)S(1)}, u32[]{:S(2)}, u32[]{:S(2)}) collective-permute-start(bf16[256,128]{1,0:T(8,128)(2,1)S(1)} %constant_dynamic-slice_fusion.refs_0_), channel_id=1, source_target_pairs={{0,80},{16,64},{32,112},{48,96},{64,16},{80,0},{96,48},{112,32},{1... | collective-permute-start | bytes 196616 | tf_op jit(solution)/shard_map/ppermute | solution.py:25
  7.7 1.9 %collective-permute-start.3 = (bf16[256,128]{1,0:T(8,128)(2,1)S(1)}, bf16[256,128]{1,0:T(8,128)(2,1)S(1)}, u32[]{:S(2)}, u32[]{:S(2)}) collective-permute-start(bf16[256,128]{1,0:T(8,128)(2,1)S(1)} %constant_dynamic-slice_fusion.refs_0_), channel_id=1, source_target_pairs={{0,64},{16,80},{32,96},{48,112},{64,0},{80,16},{96,32},{112,48},{1... | collective-permute-start | bytes 196616 | tf_op jit(solution)/shard_map/ppermute | solution.py:25
  9.6 1.4 %collective-permute-start.2 = (bf16[256,128]{1,0:T(8,128)(2,1)S(1)}, bf16[256,128]{1,0:T(8,128)(2,1)S(1)}, u32[]{:S(2)}, u32[]{:S(2)}) collective-permute-start(bf16[256,128]{1,0:T(8,128)(2,1)S(1)} %constant_dynamic-slice_fusion.refs_0_), channel_id=1, source_target_pairs={{0,48},{16,32},{32,16},{48,0},{64,112},{80,96},{96,80},{112,64},{1... | collective-permute-start | bytes 196616 | tf_op jit(solution)/shard_map/ppermute | solution.py:25
  11.7 0.0 collective-permute-done.6.refs_7_
  11.7 1.7 %collective-permute-start.1 = (bf16[256,128]{1,0:T(8,128)(2,1)S(1)}, bf16[256,128]{1,0:T(8,128)(2,1)S(1)}, u32[]{:S(2)}, u32[]{:S(2)}) collective-permute-start(bf16[256,128]{1,0:T(8,128)(2,1)S(1)} %constant_dynamic-slice_fusion.refs_0_), channel_id=1, source_target_pairs={{0,32},{16,48},{32,0},{48,16},{64,96},{80,112},{96,64},{112,80},{1... | collective-permute-start | bytes 196616 | tf_op jit(solution)/shard_map/ppermute | solution.py:25
  13.4 0.2 collective-permute-done.5.refs_6_
  13.6 0.3 collective-permute-start
  13.8 0.1 pad_add_fusion.ids
  13.9 0.7 copy-done.3
  14.6 0.7 copy-done.4
  15.3 2.7 %pick_tiles.1 = (s32[1,768]{1,0:T(1,128)S(1)}, s32[1,768]{1,0:T(1,128)S(1)}, s32[1,768]{1,0:T(1,128)S(1)}, s32[2]{0:T(128)S(1)}) custom-call(s32[1,1]{1,0:T(1,128)S(6)} %copy.12.count, s32[3]{0:T(128)S(1)} %pad_add_fusion.ids, s32[1,1,640]{2,1,0:T(1,128)S(1)} %copy-done.3, s32[1,1,640]{2,1,0:T(1,128)S(1)} %copy-done.4), custom_call_target="tpu_custom_call" | custom-call | tf_op jit(solution)/shard_map/pick_tiles/pallas_call | solution.py:90
  18.0 0.0 collective-permute-done.3.refs_4_
  18.0 0.0 collective-permute-done.2.refs_3_
  18.1 4.6 %tiles_forward.1 = (bf16[769,128,128]{2,1,0:T(8,128)(2,1)S(1)}, f32[4,4,128,128]{3,2,1,0:T(8,128)S(1)}, bf16[4,4,128,128]{3,2,1,0:T(8,128)(2,1)S(1)}) custom-call(s32[2]{0:T(128)S(1)} %get-tuple-element.61.steps, s32[3]{0:T(128)S(1)} %pad_add_fusion.ids, s32[1,768]{1,0:T(1,128)S(1)} %get-tuple-element.62.fetched, s32[1,768]{1,0:T(1,128)S(1)} %get-tuple-element.63.picked, ...), custom_call_target="tpu_custom_call" | custom-call | tf_op jit(solution)/shard_map/tiles_forward/pallas_call | solution.py:151
  22.7 0.1 collective-permute-start.7
  22.8 1.9 %collective-permute-done.7.got = bf16[4,4,128,128]{3,2,1,0:T(8,128)(2,1)S(1)} collective-permute-done((bf16[4,4,128,128]{3,2,1,0:T(8,128)(2,1)S(1)}, bf16[4,4,128,128]{3,2,1,0:T(8,128)(2,1)S(1)}, u32[]{:S(2)}, u32[]{:S(2)}) %collective-permute-start.7) | collective-permute-done | bytes 524320 | tf_op jit(solution)/shard_map/ppermute | solution.py:25
  24.7 0.1 pair_sum.1
  24.8 2.1 %collective-permute-start.8 = (bf16[4,128,128]{2,1,0:T(8,128)(2,1)S(1)}, bf16[4,128,128]{2,1,0:T(8,128)(2,1)S(1)}, u32[]{:S(2)}, u32[]{:S(2)}) collective-permute-start(bf16[4,128,128]{2,1,0:T(8,128)(2,1)S(1)} %get-tuple-element.74), channel_id=1, source_target_pairs={{0,4},{2,6},{4,0},{6,2},{8,12},{10,14},{12,8},{14,10},{1,5},{3,7},... | collective-permute-start | bytes 393224 | tf_op jit(solution)/shard_map/ppermute | solution.py:25
  26.9 1.2 %collective-permute-start.9 = (bf16[4,128,128]{2,1,0:T(8,128)(2,1)S(1)}, bf16[4,128,128]{2,1,0:T(8,128)(2,1)S(1)}, u32[]{:S(2)}, u32[]{:S(2)}) collective-permute-start(bf16[4,128,128]{2,1,0:T(8,128)(2,1)S(1)} %get-tuple-element.75), channel_id=1, source_target_pairs={{0,8},{2,10},{4,12},{6,14},{8,0},{10,2},{12,4},{14,6},{1,9},{3,11}... | collective-permute-start | bytes 393224 | tf_op jit(solution)/shard_map/ppermute | solution.py:25
  28.1 1.6 %collective-permute-start.10 = (bf16[4,128,128]{2,1,0:T(8,128)(2,1)S(1)}, bf16[4,128,128]{2,1,0:T(8,128)(2,1)S(1)}, u32[]{:S(2)}, u32[]{:S(2)}) collective-permute-start(bf16[4,128,128]{2,1,0:T(8,128)(2,1)S(1)} %get-tuple-element.76), channel_id=1, source_target_pairs={{0,12},{2,14},{4,8},{6,10},{8,4},{10,6},{12,0},{14,2},{1,13},{3,15... | collective-permute-start | bytes 393224 | tf_op jit(solution)/shard_map/ppermute | solution.py:25
  29.7 1.5 %collective-permute-done.8.a = bf16[4,128,128]{2,1,0:T(8,128)(2,1)S(1)} collective-permute-done((bf16[4,128,128]{2,1,0:T(8,128)(2,1)S(1)}, bf16[4,128,128]{2,1,0:T(8,128)(2,1)S(1)}, u32[]{:S(2)}, u32[]{:S(2)}) %collective-permute-start.8) | collective-permute-done | bytes 131104 | tf_op jit(solution)/shard_map/ppermute | solution.py:25
  31.2 3.3 %collective-permute-done.9.b = bf16[4,128,128]{2,1,0:T(8,128)(2,1)S(1)} collective-permute-done((bf16[4,128,128]{2,1,0:T(8,128)(2,1)S(1)}, bf16[4,128,128]{2,1,0:T(8,128)(2,1)S(1)}, u32[]{:S(2)}, u32[]{:S(2)}) %collective-permute-start.9) | collective-permute-done | bytes 131104 | tf_op jit(solution)/shard_map/ppermute | solution.py:25
  34.5 2.3 %collective-permute-done.10.c = bf16[4,128,128]{2,1,0:T(8,128)(2,1)S(1)} collective-permute-done((bf16[4,128,128]{2,1,0:T(8,128)(2,1)S(1)}, bf16[4,128,128]{2,1,0:T(8,128)(2,1)S(1)}, u32[]{:S(2)}, u32[]{:S(2)}) %collective-permute-start.10) | collective-permute-done | bytes 131104 | tf_op jit(solution)/shard_map/ppermute | solution.py:25
  36.8 0.1 own_sum.1
  36.9 4.0 %collective-permute-start.11 = (bf16[4,128,128]{2,1,0:T(8,128)(2,1)S(1)}, bf16[4,128,128]{2,1,0:T(8,128)(2,1)S(1)}, u32[]{:S(2)}, u32[]{:S(2)}) collective-permute-start(bf16[4,128,128]{2,1,0:T(8,128)(2,1)S(1)} %get-tuple-element.78), channel_id=1, source_target_pairs={{0,1},{1,0},{2,3},{3,2},{4,5},{5,4},{6,7},{7,6},{8,9},{9,8},{10,11... | collective-permute-start | bytes 393224 | tf_op jit(solution)/shard_map/ppermute | solution.py:25
  40.8 3.2 %collective-permute-done.11.other = bf16[4,128,128]{2,1,0:T(8,128)(2,1)S(1)} collective-permute-done((bf16[4,128,128]{2,1,0:T(8,128)(2,1)S(1)}, bf16[4,128,128]{2,1,0:T(8,128)(2,1)S(1)}, u32[]{:S(2)}, u32[]{:S(2)}) %collective-permute-start.11) | collective-permute-done | bytes 131104 | tf_op jit(solution)/shard_map/ppermute | solution.py:25
  44.0 0.9 copy-done.1
  44.9 0.8 copy-done.2
  45.7 0.7 copy-done.5
  46.3 0.9 middle.1
  47.2 3.3 %collective-permute-start.12 = (bf16[4,128,128]{2,1,0:T(8,128)(2,1)S(1)}, bf16[4,128,128]{2,1,0:T(8,128)(2,1)S(1)}, u32[]{:S(2)}, u32[]{:S(2)}) collective-permute-start(bf16[4,128,128]{2,1,0:T(8,128)(2,1)S(1)} %get-tuple-element.83), channel_id=1, source_target_pairs={{0,1},{1,0},{2,3},{3,2},{4,5},{5,4},{6,7},{7,6},{8,9},{9,8},{10,11... | collective-permute-start | bytes 393224 | tf_op jit(solution)/shard_map/ppermute | solution.py:25
  50.5 3.2 %collective-permute-done.12.other = bf16[4,128,128]{2,1,0:T(8,128)(2,1)S(1)} collective-permute-done((bf16[4,128,128]{2,1,0:T(8,128)(2,1)S(1)}, bf16[4,128,128]{2,1,0:T(8,128)(2,1)S(1)}, u32[]{:S(2)}, u32[]{:S(2)}) %collective-permute-start.12) | collective-permute-done | bytes 131104 | tf_op jit(solution)/shard_map/ppermute | solution.py:25
  53.7 0.9 collective-permute-start.16
  54.7 1.5 %collective-permute-start.15 = (bf16[656,128]{1,0:T(8,128)(2,1)S(1)}, bf16[656,128]{1,0:T(8,128)(2,1)S(1)}, u32[]{:S(2)}, u32[]{:S(2)}) collective-permute-start(bf16[656,128]{1,0:T(8,128)(2,1)S(1)} %message.1.refs_0_), channel_id=1, source_target_pairs={{0,12},{2,14},{4,8},{6,10},{8,4},{10,6},{12,0},{14,2},{1,13},{3,15... | collective-permute-start | bytes 503816 | tf_op jit(solution)/shard_map/ppermute | solution.py:25
  56.2 1.1 %collective-permute-start.14 = (bf16[656,128]{1,0:T(8,128)(2,1)S(1)}, bf16[656,128]{1,0:T(8,128)(2,1)S(1)}, u32[]{:S(2)}, u32[]{:S(2)}) collective-permute-start(bf16[656,128]{1,0:T(8,128)(2,1)S(1)} %message.1.refs_0_), channel_id=1, source_target_pairs={{0,4},{2,6},{4,0},{6,2},{8,12},{10,14},{12,8},{14,10},{1,5},{3,7},... | collective-permute-start | bytes 503816 | tf_op jit(solution)/shard_map/ppermute | solution.py:25
  57.3 3.9 %collective-permute-done.16.refs_4_ = bf16[656,128]{1,0:T(8,128)(2,1)S(1)} collective-permute-done((bf16[656,128]{1,0:T(8,128)(2,1)S(1)}, bf16[656,128]{1,0:T(8,128)(2,1)S(1)}, u32[]{:S(2)}, u32[]{:S(2)}) %collective-permute-start.16) | collective-permute-done | bytes 167968 | tf_op jit(solution)/shard_map/ppermute | solution.py:25
  61.2 1.6 %collective-permute-done.15.refs_6_ = bf16[656,128]{1,0:T(8,128)(2,1)S(1)} collective-permute-done((bf16[656,128]{1,0:T(8,128)(2,1)S(1)}, bf16[656,128]{1,0:T(8,128)(2,1)S(1)}, u32[]{:S(2)}, u32[]{:S(2)}) %collective-permute-start.15) | collective-permute-done | bytes 167968 | tf_op jit(solution)/shard_map/ppermute | solution.py:25
  62.8 0.5 collective-permute-start.18
  63.3 0.0 collective-permute-start.19
  63.3 0.9 collective-permute-done.17.refs_3_
  64.2 0.2 collective-permute-done.18.refs_5_
  64.4 0.3 collective-permute-done.19.refs_7_
  64.7 0.1 grad_sum.1
  64.8 2.7 %collective-permute-start.20 = (f32[136,128]{1,0:T(8,128)S(1)}, f32[136,128]{1,0:T(8,128)S(1)}, u32[]{:S(2)}, u32[]{:S(2)}) collective-permute-start(f32[136,128]{1,0:T(8,128)S(1)} %grad_sum.1), channel_id=1, source_target_pairs={{0,16},{16,0},{32,48},{48,32},{64,80},{80,64},{96,112},{112,96},{1... | collective-permute-start | bytes 208904 | tf_op jit(solution)/shard_map/ppermute | solution.py:25
  67.4 2.1 %tiles_backward.1 = (f32[4,128,128]{2,1,0:T(8,128)S(1)}, bf16[4,128,128]{2,1,0:T(8,128)(2,1)S(1)}, bf16[4,128,128]{2,1,0:T(8,128)(2,1)S(1)}, bf16[4,128,128]{2,1,0:T(8,128)(2,1)S(1)}) custom-call(s32[2]{0:T(128)S(1)} %get-tuple-element.61.steps, s32[3]{0:T(128)S(1)} %pad_add_fusion.ids, s32[1,768]{1,0:T(1,128)S(1)} %get-tuple-element.80.picked, ...), custom_call_target="tpu_custom_call" | custom-call | tf_op jit(solution)/shard_map/tiles_backward/pallas_call | solution.py:196
  69.5 0.5 collective-permute-done.20
  70.0 2.6 %collective-permute-start.21 = (bf16[4,128,128]{2,1,0:T(8,128)(2,1)S(1)}, bf16[4,128,128]{2,1,0:T(8,128)(2,1)S(1)}, u32[]{:S(2)}, u32[]{:S(2)}) collective-permute-start(bf16[4,128,128]{2,1,0:T(8,128)(2,1)S(1)} %get-tuple-element.92), channel_id=1, source_target_pairs={{0,32},{16,48},{32,0},{48,16},{64,96},{80,112},{96,64},{112,80},{1... | collective-permute-start | bytes 393224 | tf_op jit(solution)/shard_map/ppermute | solution.py:25
  72.6 6.4 %collective-permute-start.22 = (bf16[4,128,128]{2,1,0:T(8,128)(2,1)S(1)}, bf16[4,128,128]{2,1,0:T(8,128)(2,1)S(1)}, u32[]{:S(2)}, u32[]{:S(2)}) collective-permute-start(bf16[4,128,128]{2,1,0:T(8,128)(2,1)S(1)} %get-tuple-element.93), channel_id=1, source_target_pairs={{0,64},{16,80},{32,96},{48,112},{64,0},{80,16},{96,32},{112,48},{1... | collective-permute-start | bytes 393224 | tf_op jit(solution)/shard_map/ppermute | solution.py:25
  79.1 0.1 collective-permute-start.24
  79.2 4.3 %collective-permute-done.24 = f32[136,128]{1,0:T(8,128)S(1)} collective-permute-done((f32[136,128]{1,0:T(8,128)S(1)}, f32[136,128]{1,0:T(8,128)S(1)}, u32[]{:S(2)}, u32[]{:S(2)}) %collective-permute-start.24) | collective-permute-done | bytes 69664 | tf_op jit(solution)/shard_map/ppermute | solution.py:25
  83.5 0.7 collective-permute-done.22.b
  84.2 2.1 %collective-permute-done.23.c = bf16[4,128,128]{2,1,0:T(8,128)(2,1)S(1)} collective-permute-done((bf16[4,128,128]{2,1,0:T(8,128)(2,1)S(1)}, bf16[4,128,128]{2,1,0:T(8,128)(2,1)S(1)}, u32[]{:S(2)}, u32[]{:S(2)}) %collective-permute-start.23) | collective-permute-done | bytes 131104 | tf_op jit(solution)/shard_map/ppermute | solution.py:25
  86.3 0.4 collective-permute-start.28
  86.7 0.6 line_sum.1
  87.3 3.7 %collective-permute-start.25 = (bf16[2,128,128]{2,1,0:T(8,128)(2,1)S(1)}, bf16[2,128,128]{2,1,0:T(8,128)(2,1)S(1)}, u32[]{:S(2)}, u32[]{:S(2)}) collective-permute-start(bf16[2,128,128]{2,1,0:T(8,128)(2,1)S(1)} %get-tuple-element.100), channel_id=1, source_target_pairs={{0,1},{1,0},{2,3},{3,2},{4,5},{5,4},{6,7},{7,6},{8,9},{9,8},{10,11... | collective-permute-start | bytes 196616 | tf_op jit(solution)/shard_map/ppermute | solution.py:25
  91.0 0.9 collective-permute-start.26
  91.8 1.6 %collective-permute-done.25.far = bf16[2,128,128]{2,1,0:T(8,128)(2,1)S(1)} collective-permute-done((bf16[2,128,128]{2,1,0:T(8,128)(2,1)S(1)}, bf16[2,128,128]{2,1,0:T(8,128)(2,1)S(1)}, u32[]{:S(2)}, u32[]{:S(2)}) %collective-permute-start.25) | collective-permute-done | bytes 65568 | tf_op jit(solution)/shard_map/ppermute | solution.py:25
  93.4 1.8 %collective-permute-done.27.beside = bf16[2,128,128]{2,1,0:T(8,128)(2,1)S(1)} collective-permute-done((bf16[2,128,128]{2,1,0:T(8,128)(2,1)S(1)}, bf16[2,128,128]{2,1,0:T(8,128)(2,1)S(1)}, u32[]{:S(2)}, u32[]{:S(2)}) %collective-permute-start.27) | collective-permute-done | bytes 65568 | tf_op jit(solution)/shard_map/ppermute | solution.py:25
  95.2 1.2 %collective-permute-done.26.corner = bf16[2,128,128]{2,1,0:T(8,128)(2,1)S(1)} collective-permute-done((bf16[2,128,128]{2,1,0:T(8,128)(2,1)S(1)}, bf16[2,128,128]{2,1,0:T(8,128)(2,1)S(1)}, u32[]{:S(2)}, u32[]{:S(2)}) %collective-permute-start.26) | collective-permute-done | bytes 65568 | tf_op jit(solution)/shard_map/ppermute | solution.py:25
  96.5 1.4 %finish.1 = (f32[512,128]{1,0:T(8,128)}, f32[128,128]{1,0:T(8,128)}, f32[1,128]{1,0:T(1,128)}) custom-call(s32[3]{0:T(128)S(1)} %pad_add_fusion.ids, f32[2,128,128]{2,1,0:T(8,128)S(1)} %get-tuple-element.99.own, bf16[2,128,128]{2,1,0:T(8,128)(2,1)S(1)} %collective-permute-done.27.beside, bf16[2,128,128]{2,1,0:T(8,128)(2,1)S(1)} %collective-permute-done.25.far, ...), custom_call_target="tpu_custom_call" | custom-call | tf_op jit(solution)/shard_map/finish/pallas_call | solution.py:378
  (20 shorter events, 0.1 us)
Async XLA Ops:
  0.6 0.9 copy-start
  1.5 10.1 %collective-permute-start.6 = (bf16[256,128]{1,0:T(8,128)(2,1)S(1)}, bf16[256,128]{1,0:T(8,128)(2,1)S(1)}, u32[]{:S(2)}, u32[]{:S(2)}) collective-permute-start(bf16[256,128]{1,0:T(8,128)(2,1)S(1)} %constant_dynamic-slice_fusion.refs_0_), channel_id=1, source_target_pairs={{0,112},{16,96},{32,80},{48,64},{64,48},{80,32},{96,16},{112,0},{1... | collective-permute-start | bytes 196616 | tf_op jit(solution)/shard_map/ppermute | solution.py:25
  6.0 7.6 %collective-permute-start.5 = (bf16[256,128]{1,0:T(8,128)(2,1)S(1)}, bf16[256,128]{1,0:T(8,128)(2,1)S(1)}, u32[]{:S(2)}, u32[]{:S(2)}) collective-permute-start(bf16[256,128]{1,0:T(8,128)(2,1)S(1)} %constant_dynamic-slice_fusion.refs_0_), channel_id=1, source_target_pairs={{0,96},{16,112},{32,64},{48,80},{64,32},{80,48},{96,0},{112,16},{1... | collective-permute-start | bytes 196616 | tf_op jit(solution)/shard_map/ppermute | solution.py:25
  6.2 11.8 %collective-permute-start.4 = (bf16[256,128]{1,0:T(8,128)(2,1)S(1)}, bf16[256,128]{1,0:T(8,128)(2,1)S(1)}, u32[]{:S(2)}, u32[]{:S(2)}) collective-permute-start(bf16[256,128]{1,0:T(8,128)(2,1)S(1)} %constant_dynamic-slice_fusion.refs_0_), channel_id=1, source_target_pairs={{0,80},{16,64},{32,112},{48,96},{64,16},{80,0},{96,48},{112,32},{1... | collective-permute-start | bytes 196616 | tf_op jit(solution)/shard_map/ppermute | solution.py:25
  7.7 10.3 %collective-permute-start.3 = (bf16[256,128]{1,0:T(8,128)(2,1)S(1)}, bf16[256,128]{1,0:T(8,128)(2,1)S(1)}, u32[]{:S(2)}, u32[]{:S(2)}) collective-permute-start(bf16[256,128]{1,0:T(8,128)(2,1)S(1)} %constant_dynamic-slice_fusion.refs_0_), channel_id=1, source_target_pairs={{0,64},{16,80},{32,96},{48,112},{64,0},{80,16},{96,32},{112,48},{1... | collective-permute-start | bytes 196616 | tf_op jit(solution)/shard_map/ppermute | solution.py:25
  9.6 8.4 %collective-permute-start.2 = (bf16[256,128]{1,0:T(8,128)(2,1)S(1)}, bf16[256,128]{1,0:T(8,128)(2,1)S(1)}, u32[]{:S(2)}, u32[]{:S(2)}) collective-permute-start(bf16[256,128]{1,0:T(8,128)(2,1)S(1)} %constant_dynamic-slice_fusion.refs_0_), channel_id=1, source_target_pairs={{0,48},{16,32},{32,16},{48,0},{64,112},{80,96},{96,80},{112,64},{1... | collective-permute-start | bytes 196616 | tf_op jit(solution)/shard_map/ppermute | solution.py:25
  11.7 6.4 %collective-permute-start.1 = (bf16[256,128]{1,0:T(8,128)(2,1)S(1)}, bf16[256,128]{1,0:T(8,128)(2,1)S(1)}, u32[]{:S(2)}, u32[]{:S(2)}) collective-permute-start(bf16[256,128]{1,0:T(8,128)(2,1)S(1)} %constant_dynamic-slice_fusion.refs_0_), channel_id=1, source_target_pairs={{0,32},{16,48},{32,0},{48,16},{64,96},{80,112},{96,64},{112,80},{1... | collective-permute-start | bytes 196616 | tf_op jit(solution)/shard_map/ppermute | solution.py:25
  13.6 4.5 %collective-permute-start = (bf16[256,128]{1,0:T(8,128)(2,1)S(1)}, bf16[256,128]{1,0:T(8,128)(2,1)S(1)}, u32[]{:S(2)}, u32[]{:S(2)}) collective-permute-start(bf16[256,128]{1,0:T(8,128)(2,1)S(1)} %constant_dynamic-slice_fusion.refs_0_), channel_id=1, source_target_pairs={{0,16},{16,0},{32,48},{48,32},{64,80},{80,64},{96,112},{112,96},{1... | collective-permute-start | bytes 196616 | tf_op jit(solution)/shard_map/ppermute | solution.py:25
  13.9 0.7 copy-start.3
  14.6 0.7 copy-start.4
  22.7 2.0 %collective-permute-start.7 = (bf16[4,4,128,128]{3,2,1,0:T(8,128)(2,1)S(1)}, bf16[4,4,128,128]{3,2,1,0:T(8,128)(2,1)S(1)}, u32[]{:S(2)}, u32[]{:S(2)}) collective-permute-start(bf16[4,4,128,128]{3,2,1,0:T(8,128)(2,1)S(1)} %get-tuple-element.72), channel_id=1, source_target_pairs={{0,2},{2,0},{4,6},{6,4},{8,10},{10,8},{12,14},{14,12},{1,3},{3,1},... | collective-permute-start | bytes 1572872 | tf_op jit(solution)/shard_map/ppermute | solution.py:25
  24.8 6.4 %collective-permute-start.8 = (bf16[4,128,128]{2,1,0:T(8,128)(2,1)S(1)}, bf16[4,128,128]{2,1,0:T(8,128)(2,1)S(1)}, u32[]{:S(2)}, u32[]{:S(2)}) collective-permute-start(bf16[4,128,128]{2,1,0:T(8,128)(2,1)S(1)} %get-tuple-element.74), channel_id=1, source_target_pairs={{0,4},{2,6},{4,0},{6,2},{8,12},{10,14},{12,8},{14,10},{1,5},{3,7},... | collective-permute-start | bytes 393224 | tf_op jit(solution)/shard_map/ppermute | solution.py:25
  26.9 7.6 %collective-permute-start.9 = (bf16[4,128,128]{2,1,0:T(8,128)(2,1)S(1)}, bf16[4,128,128]{2,1,0:T(8,128)(2,1)S(1)}, u32[]{:S(2)}, u32[]{:S(2)}) collective-permute-start(bf16[4,128,128]{2,1,0:T(8,128)(2,1)S(1)} %get-tuple-element.75), channel_id=1, source_target_pairs={{0,8},{2,10},{4,12},{6,14},{8,0},{10,2},{12,4},{14,6},{1,9},{3,11}... | collective-permute-start | bytes 393224 | tf_op jit(solution)/shard_map/ppermute | solution.py:25
  28.1 8.7 %collective-permute-start.10 = (bf16[4,128,128]{2,1,0:T(8,128)(2,1)S(1)}, bf16[4,128,128]{2,1,0:T(8,128)(2,1)S(1)}, u32[]{:S(2)}, u32[]{:S(2)}) collective-permute-start(bf16[4,128,128]{2,1,0:T(8,128)(2,1)S(1)} %get-tuple-element.76), channel_id=1, source_target_pairs={{0,12},{2,14},{4,8},{6,10},{8,4},{10,6},{12,0},{14,2},{1,13},{3,15... | collective-permute-start | bytes 393224 | tf_op jit(solution)/shard_map/ppermute | solution.py:25
  36.9 7.1 %collective-permute-start.11 = (bf16[4,128,128]{2,1,0:T(8,128)(2,1)S(1)}, bf16[4,128,128]{2,1,0:T(8,128)(2,1)S(1)}, u32[]{:S(2)}, u32[]{:S(2)}) collective-permute-start(bf16[4,128,128]{2,1,0:T(8,128)(2,1)S(1)} %get-tuple-element.78), channel_id=1, source_target_pairs={{0,1},{1,0},{2,3},{3,2},{4,5},{5,4},{6,7},{7,6},{8,9},{9,8},{10,11... | collective-permute-start | bytes 393224 | tf_op jit(solution)/shard_map/ppermute | solution.py:25
  44.0 0.9 copy-start.1
  44.9 0.8 copy-start.2
  45.7 0.7 copy-start.5
  47.2 6.5 %collective-permute-start.12 = (bf16[4,128,128]{2,1,0:T(8,128)(2,1)S(1)}, bf16[4,128,128]{2,1,0:T(8,128)(2,1)S(1)}, u32[]{:S(2)}, u32[]{:S(2)}) collective-permute-start(bf16[4,128,128]{2,1,0:T(8,128)(2,1)S(1)} %get-tuple-element.83), channel_id=1, source_target_pairs={{0,1},{1,0},{2,3},{3,2},{4,5},{5,4},{6,7},{7,6},{8,9},{9,8},{10,11... | collective-permute-start | bytes 393224 | tf_op jit(solution)/shard_map/ppermute | solution.py:25
  53.7 7.5 %collective-permute-start.16 = (bf16[656,128]{1,0:T(8,128)(2,1)S(1)}, bf16[656,128]{1,0:T(8,128)(2,1)S(1)}, u32[]{:S(2)}, u32[]{:S(2)}) collective-permute-start(bf16[656,128]{1,0:T(8,128)(2,1)S(1)} %message.1.refs_0_), channel_id=1, source_target_pairs={{0,8},{2,10},{4,12},{6,14},{8,0},{10,2},{12,4},{14,6},{1,9},{3,11}... | collective-permute-start | bytes 503816 | tf_op jit(solution)/shard_map/ppermute | solution.py:25
  54.7 8.1 %collective-permute-start.15 = (bf16[656,128]{1,0:T(8,128)(2,1)S(1)}, bf16[656,128]{1,0:T(8,128)(2,1)S(1)}, u32[]{:S(2)}, u32[]{:S(2)}) collective-permute-start(bf16[656,128]{1,0:T(8,128)(2,1)S(1)} %message.1.refs_0_), channel_id=1, source_target_pairs={{0,12},{2,14},{4,8},{6,10},{8,4},{10,6},{12,0},{14,2},{1,13},{3,15... | collective-permute-start | bytes 503816 | tf_op jit(solution)/shard_map/ppermute | solution.py:25
  56.2 6.6 %collective-permute-start.14 = (bf16[656,128]{1,0:T(8,128)(2,1)S(1)}, bf16[656,128]{1,0:T(8,128)(2,1)S(1)}, u32[]{:S(2)}, u32[]{:S(2)}) collective-permute-start(bf16[656,128]{1,0:T(8,128)(2,1)S(1)} %message.1.refs_0_), channel_id=1, source_target_pairs={{0,4},{2,6},{4,0},{6,2},{8,12},{10,14},{12,8},{14,10},{1,5},{3,7},... | collective-permute-start | bytes 503816 | tf_op jit(solution)/shard_map/ppermute | solution.py:25
  57.3 6.0 %collective-permute-start.13 = (bf16[656,128]{1,0:T(8,128)(2,1)S(1)}, bf16[656,128]{1,0:T(8,128)(2,1)S(1)}, u32[]{:S(2)}, u32[]{:S(2)}) collective-permute-start(bf16[656,128]{1,0:T(8,128)(2,1)S(1)} %message.1.refs_0_), channel_id=1, source_target_pairs={{0,2},{2,0},{4,6},{6,4},{8,10},{10,8},{12,14},{14,12},{1,3},{3,1},... | collective-permute-start | bytes 503816 | tf_op jit(solution)/shard_map/ppermute | solution.py:25
  62.8 1.4 %collective-permute-start.17 = (bf16[656,128]{1,0:T(8,128)(2,1)S(1)}, bf16[656,128]{1,0:T(8,128)(2,1)S(1)}, u32[]{:S(2)}, u32[]{:S(2)}) collective-permute-start(bf16[656,128]{1,0:T(8,128)(2,1)S(1)} %collective-permute-done.14.refs_2_), channel_id=1, source_target_pairs={{0,2},{2,0},{4,6},{6,4},{8,10},{10,8},{12,14},{14,12},{1,3},{3,1},... | collective-permute-start | bytes 503816 | tf_op jit(solution)/shard_map/ppermute | solution.py:25
  62.8 1.6 %collective-permute-start.18 = (bf16[656,128]{1,0:T(8,128)(2,1)S(1)}, bf16[656,128]{1,0:T(8,128)(2,1)S(1)}, u32[]{:S(2)}, u32[]{:S(2)}) collective-permute-start(bf16[656,128]{1,0:T(8,128)(2,1)S(1)} %collective-permute-done.16.refs_4_), channel_id=1, source_target_pairs={{0,2},{2,0},{4,6},{6,4},{8,10},{10,8},{12,14},{14,12},{1,3},{3,1},... | collective-permute-start | bytes 503816 | tf_op jit(solution)/shard_map/ppermute | solution.py:25
  63.3 1.4 %collective-permute-start.19 = (bf16[656,128]{1,0:T(8,128)(2,1)S(1)}, bf16[656,128]{1,0:T(8,128)(2,1)S(1)}, u32[]{:S(2)}, u32[]{:S(2)}) collective-permute-start(bf16[656,128]{1,0:T(8,128)(2,1)S(1)} %collective-permute-done.15.refs_6_), channel_id=1, source_target_pairs={{0,2},{2,0},{4,6},{6,4},{8,10},{10,8},{12,14},{14,12},{1,3},{3,1},... | collective-permute-start | bytes 503816 | tf_op jit(solution)/shard_map/ppermute | solution.py:25
  64.8 5.3 %collective-permute-start.20 = (f32[136,128]{1,0:T(8,128)S(1)}, f32[136,128]{1,0:T(8,128)S(1)}, u32[]{:S(2)}, u32[]{:S(2)}) collective-permute-start(f32[136,128]{1,0:T(8,128)S(1)} %grad_sum.1), channel_id=1, source_target_pairs={{0,16},{16,0},{32,48},{48,32},{64,80},{80,64},{96,112},{112,96},{1... | collective-permute-start | bytes 208904 | tf_op jit(solution)/shard_map/ppermute | solution.py:25
  70.0 13.4 %collective-permute-start.21 = (bf16[4,128,128]{2,1,0:T(8,128)(2,1)S(1)}, bf16[4,128,128]{2,1,0:T(8,128)(2,1)S(1)}, u32[]{:S(2)}, u32[]{:S(2)}) collective-permute-start(bf16[4,128,128]{2,1,0:T(8,128)(2,1)S(1)} %get-tuple-element.92), channel_id=1, source_target_pairs={{0,32},{16,48},{32,0},{48,16},{64,96},{80,112},{96,64},{112,80},{1... | collective-permute-start | bytes 393224 | tf_op jit(solution)/shard_map/ppermute | solution.py:25
  72.6 11.6 %collective-permute-start.22 = (bf16[4,128,128]{2,1,0:T(8,128)(2,1)S(1)}, bf16[4,128,128]{2,1,0:T(8,128)(2,1)S(1)}, u32[]{:S(2)}, u32[]{:S(2)}) collective-permute-start(bf16[4,128,128]{2,1,0:T(8,128)(2,1)S(1)} %get-tuple-element.93), channel_id=1, source_target_pairs={{0,64},{16,80},{32,96},{48,112},{64,0},{80,16},{96,32},{112,48},{1... | collective-permute-start | bytes 393224 | tf_op jit(solution)/shard_map/ppermute | solution.py:25
  79.0 7.2 %collective-permute-start.23 = (bf16[4,128,128]{2,1,0:T(8,128)(2,1)S(1)}, bf16[4,128,128]{2,1,0:T(8,128)(2,1)S(1)}, u32[]{:S(2)}, u32[]{:S(2)}) collective-permute-start(bf16[4,128,128]{2,1,0:T(8,128)(2,1)S(1)} %get-tuple-element.94), channel_id=1, source_target_pairs={{0,96},{16,112},{32,64},{48,80},{64,32},{80,48},{96,0},{112,16},{1... | collective-permute-start | bytes 393224 | tf_op jit(solution)/shard_map/ppermute | solution.py:25
  79.1 4.4 %collective-permute-start.24 = (f32[136,128]{1,0:T(8,128)S(1)}, f32[136,128]{1,0:T(8,128)S(1)}, u32[]{:S(2)}, u32[]{:S(2)}) collective-permute-start(f32[136,128]{1,0:T(8,128)S(1)} %add.10), channel_id=1, source_target_pairs={{0,32},{16,48},{32,0},{48,16},{64,96},{80,112},{96,64},{112,80},{1... | collective-permute-start | bytes 208904 | tf_op jit(solution)/shard_map/ppermute | solution.py:25
  86.3 10.2 %collective-permute-start.28 = (f32[136,128]{1,0:T(8,128)S(1)}, f32[136,128]{1,0:T(8,128)S(1)}, u32[]{:S(2)}, u32[]{:S(2)}) collective-permute-start(f32[136,128]{1,0:T(8,128)S(1)} %add.11.grads), channel_id=1, source_target_pairs={{0,64},{16,80},{32,96},{48,112},{64,0},{80,16},{96,32},{112,48},{1... | collective-permute-start | bytes 208904 | tf_op jit(solution)/shard_map/ppermute | solution.py:25
  87.3 6.1 %collective-permute-start.25 = (bf16[2,128,128]{2,1,0:T(8,128)(2,1)S(1)}, bf16[2,128,128]{2,1,0:T(8,128)(2,1)S(1)}, u32[]{:S(2)}, u32[]{:S(2)}) collective-permute-start(bf16[2,128,128]{2,1,0:T(8,128)(2,1)S(1)} %get-tuple-element.100), channel_id=1, source_target_pairs={{0,1},{1,0},{2,3},{3,2},{4,5},{5,4},{6,7},{7,6},{8,9},{9,8},{10,11... | collective-permute-start | bytes 196616 | tf_op jit(solution)/shard_map/ppermute | solution.py:25
  91.0 4.3 %collective-permute-start.27 = (bf16[2,128,128]{2,1,0:T(8,128)(2,1)S(1)}, bf16[2,128,128]{2,1,0:T(8,128)(2,1)S(1)}, u32[]{:S(2)}, u32[]{:S(2)}) collective-permute-start(bf16[2,128,128]{2,1,0:T(8,128)(2,1)S(1)} %get-tuple-element.101), channel_id=1, source_target_pairs={{0,16},{16,0},{32,48},{48,32},{64,80},{80,64},{96,112},{112,96},{1... | collective-permute-start | bytes 196616 | tf_op jit(solution)/shard_map/ppermute | solution.py:25
  91.0 5.5 %collective-permute-start.26 = (bf16[2,128,128]{2,1,0:T(8,128)(2,1)S(1)}, bf16[2,128,128]{2,1,0:T(8,128)(2,1)S(1)}, u32[]{:S(2)}, u32[]{:S(2)}) collective-permute-start(bf16[2,128,128]{2,1,0:T(8,128)(2,1)S(1)} %get-tuple-element.101), channel_id=1, source_target_pairs={{0,17},{1,16},{16,1},{17,0},{32,49},{33,48},{48,33},{49,32},{64,81... | collective-permute-start | bytes 196616 | tf_op jit(solution)/shard_map/ppermute | solution.py:25
where the time goes:
time: 98.3 us; the launch traced here: 97.8 us
  starting transfers between devices  44.5 us (45%)
  waiting for transfers between devices  34.6 us (35%)
  Pallas kernels  12.6 us (13%)
  local copies, waits for them, and re-layouts  4.59 us (5%)
  between operations  1.44 us (1%)
    ppermute x29, starting transfers between devices, swap(): return lax.ppermute(values, axis, [(i, i ^ mask) for i in range(size)])  44.5 us
    ppermute x29, waiting for transfers between devices, swap(): return lax.ppermute(values, axis, [(i, i ^ mask) for i in range(size)])  34.6 us
    pallas_call x1, Pallas kernels, tiles_forward(): pl.pallas_call(forward_kernel, out_shape=[pltpu.VMEM((length + 1, TILE, T...  4.65 us
    unnamed x12, local copies, waits for them, and re-layouts  4.58 us
    pallas_call x1, Pallas kernels, pick(): pl.pallas_call(functools.partial(pick_kernel, n_out, n_back), out_shape=[...  2.7 us
    pallas_call x1, Pallas kernels, tiles_backward(): pl.pallas_call(backward_kernel, out_shape=[pltpu.VMEM(shape, F32)] + [plt...  2.07 us
  transfers between devices with their start and end apart: 29, of which 19 were waited for; matrix products, arithmetic and copies ran while one was open for 0% of the time, Pallas kernels for 6%

commit v1 on v0

--- a/solution.py
+++ b/solution.py
@@ -27,6 +27,10 @@
 
 def near(values):
     return pltpu.with_memory_space_constraint(values, pltpu.VMEM)
+
+
+def far(values):
+    return pltpu.with_memory_space_constraint(values, pltpu.HBM)
 
 
 def iota(shape, dim):
@@ -62,39 +66,119 @@
     return items, found[2:3], target, steps, slot
 
 
-def pick_kernel(n_out, n_back, count, ids, rows, columns, fetched, forward, backward, steps):
-    row, column = rows[0], columns[0]
+def pick_kernel(n_out, count, ids, rows, columns, fetched, forward, slots, steps, row_copy, column_copy, arrived):
+    copies = [
+        pltpu.make_async_copy(rows.at[0], row_copy, arrived.at[0]),
+        pltpu.make_async_copy(columns.at[0], column_copy, arrived.at[1]),
+    ]
+    for copy in copies:
+        copy.start()
+    for copy in copies:
+        copy.wait()
+    row, column = row_copy[...], column_copy[...]
     index = iota(row.shape, 1)
     length = forward.shape[1]
     used = (index < count[0, 0]) & (((column >> 1) & 1) == ids[0])
-    place = (column >> 2) * 2 + (column & 1)
-    near_place = jnp.bitwise_xor(column >> 2, ids[2]) * 2 + (column & 1)
-    near_row = jnp.bitwise_xor(row >> 2, ids[1]) * 4 + (row & 3)
-    items, source, target, steps[0], slot = order(
-        row, used, near_place, index, n_out, length, FORWARD
-    )
+    source = jnp.bitwise_xor(column >> 2, ids[2]) * 2 + (column & 1)
+    items, source, target, steps[0], slot = order(row, used, source, index, n_out, length, FORWARD)
     fetched[...] = jnp.maximum(items, 0)
     here = jnp.where(items >= 0, iota(items.shape, 1), length)
     forward[...] = here + source * 1024 + target * 65536
-    items, source, target, steps[1], slot = order(
-        place, used, near_row, slot, n_back, length, BACKWARD
-    )
-    here = jnp.where(items >= 0, items, length)
-    backward[...] = here + source * 1024 + target * 65536
+    slots[...] = slot
 
 
 def pick(count, ids, rows, columns, n_out, n_back):
     length = rows.shape[-1] + max(n_out * (FORWARD - 1), n_back * (BACKWARD - 1)) + PER
     length = -(-length // TILE) * TILE
-    slots = jax.ShapeDtypeStruct((1, length), jnp.int32)
-    return pl.pallas_call(
-        functools.partial(pick_kernel, n_out, n_back),
-        out_shape=[slots, slots, slots, jax.ShapeDtypeStruct((2,), jnp.int32)],
-        in_specs=[SMEM, SMEM, VMEM, VMEM],
+    listed = jax.ShapeDtypeStruct((1, length), jnp.int32)
+    return pl.pallas_call(
+        functools.partial(pick_kernel, n_out),
+        out_shape=[
+            listed,
+            listed,
+            pltpu.VMEM(rows.shape[1:], jnp.int32),
+            jax.ShapeDtypeStruct((1,), jnp.int32),
+        ],
+        in_specs=[SMEM, SMEM, ANY, ANY],
         out_specs=[VMEM, VMEM, VMEM, SMEM],
+        scratch_shapes=[
+            pltpu.VMEM(rows.shape[1:], jnp.int32),
+            pltpu.VMEM(rows.shape[1:], jnp.int32),
+            pltpu.SemaphoreType.DMA((2,)),
+        ],
         compiler_params=PICK_PARAMS,
         name="pick_tiles",
-    )(count, ids, rows, columns)
+    )(count, ids, far(rows), far(columns))
+
+
+def prepare_kernel(
+    n_back, ids, rows, columns, slots, weight, bias, cotangent, *refs
+):
+    backward, steps, weight_copy, bias_copy, cotangent_copy, row_copy, column_copy, arrived = refs
+    pairs = [
+        (rows.at[0], row_copy),
+        (columns.at[0], column_copy),
+        (weight, weight_copy),
+        (bias, bias_copy),
+        (cotangent, cotangent_copy),
+    ]
+    copies = [
+        pltpu.make_async_copy(source, target, arrived.at[k])
+        for k, (source, target) in enumerate(pairs)
+    ]
+    for copy in copies:
+        copy.start()
+    for copy in copies:
+        copy.wait()
+    row, column, slot = row_copy[...], column_copy[...], slots[...]
+    length = backward.shape[1]
+    place = (column >> 2) * 2 + (column & 1)
+    source = jnp.bitwise_xor(row >> 2, ids[1]) * 4 + (row & 3)
+    used = slot >= 0
+    items, source, target, steps[0], slot = order(
+        place, used, source, slot, n_back, length, BACKWARD
+    )
+    here = jnp.where(items >= 0, items, length)
+    backward[...] = here + source * 1024 + target * 65536
+
+
+def prepare(ids, rows, columns, slots, length, n_back, weight, bias, cotangent):
+    return pl.pallas_call(
+        functools.partial(prepare_kernel, n_back),
+        out_shape=[
+            jax.ShapeDtypeStruct((1, length), jnp.int32),
+            jax.ShapeDtypeStruct((1,), jnp.int32),
+            pltpu.VMEM(weight.shape, weight.dtype),
+            pltpu.VMEM(bias.shape, bias.dtype),
+            pltpu.VMEM(cotangent.shape, cotangent.dtype),
+        ],
+        in_specs=[SMEM, ANY, ANY, VMEM, ANY, ANY, ANY],
+        out_specs=[VMEM, SMEM, VMEM, VMEM, VMEM],
+        scratch_shapes=[
+            pltpu.VMEM(rows.shape[1:], jnp.int32),
+            pltpu.VMEM(rows.shape[1:], jnp.int32),
+            pltpu.SemaphoreType.DMA((5,)),
+        ],
+        compiler_params=PICK_PARAMS,
+        name="prepare",
+    )(ids, far(rows), far(columns), near(slots), far(weight), far(bias), far(cotangent))
+
+
+def join_kernel(a, b, out):
+    rows = a.shape[0]
+    out[0:rows] = a[...]
+    out[rows : 2 * rows] = b[...]
+
+
+def join(a, b):
+    return pl.pallas_call(
+        join_kernel,
+        out_shape=pltpu.VMEM((2 * a.shape[0], a.shape[1]), a.dtype),
+        in_specs=[VMEM] * 2,
+        out_specs=VMEM,
+        compiler_params=PARAMS,
+        name="join",
+    )(near(a), near(b))
 
 
 def add_products(flipped, g, picked, held, source, total):
@@ -130,7 +214,7 @@
     held[held.shape[0] - 1] = jnp.zeros((TILE, TILE), BF16)
     total[...] = jnp.zeros_like(total)
     for m, source in enumerate(sources):
-        gathered[2 * m : 2 * m + 2] = source[...].reshape(2, TILE, TILE)
+        gathered[4 * m : 4 * m + 4] = source[...].reshape(4, TILE, TILE)
 
     def step(g, carry):
         block = held.at[pl.ds(g * PER, PER)]
@@ -158,7 +242,7 @@
         in_specs=[SMEM, SMEM, SMEM, SMEM, ANY] + [VMEM] * len(sources),
         out_specs=[VMEM] * 3,
         scratch_shapes=[
-            pltpu.VMEM((2 * len(sources), TILE, TILE), BF16),
+            pltpu.VMEM((4 * len(sources), TILE, TILE), BF16),
             pltpu.VMEM((n_out + 1, TILE, TILE), F32),
             pltpu.SemaphoreType.DMA((length // PER,)),
         ],
@@ -169,7 +253,7 @@
         ids,
         fetched,
         picked,
-        pltpu.with_memory_space_constraint(tiles, pltpu.HBM),
+        far(tiles),
         *[near(values) for values in sources],
     )
 
@@ -184,7 +268,7 @@
         add_products(True, g, picked, held, gathered, total)
         return carry
 
-    lax.fori_loop(0, steps[1], step, 0)
+    lax.fori_loop(0, steps[0], step, 0)
     across = ids[2] >> 1
     kept[...] = total[pl.ds(across * 4, 4)]
     for k, out in enumerate((first, second, third)):
@@ -281,7 +365,7 @@
         out_specs=[VMEM] * 4,
         compiler_params=PARAMS,
         name="middle",
-    )(near(own), near(other), weight, bias, cotangent)
+    )(near(own), near(other), near(weight), near(bias), near(cotangent))
 
 
 def message_kernel(back, other, grads, message):
@@ -335,20 +419,18 @@
 
 
 def line_kernel(ids, kept, a, b, c, own, own_sent, other_sent):
-    value = kept[...] + a[...].astype(F32) + b[...].astype(F32) + c[...].astype(F32)
     blocks = own.shape[0]
     side = ids[2] & 1
-    for z in range(2):
-        half = value[z * blocks : (z + 1) * blocks]
-
-        @pl.when(side == z)
-        def _():
-            own[...] = half
-            own_sent[...] = half.astype(BF16)
-
-        @pl.when(side != z)
-        def _():
-            other_sent[...] = half.astype(BF16)
+
+    def half(z):
+        block = pl.ds(z * blocks, blocks)
+        terms = [values[block].astype(F32) for values in (a, b, c)]
+        return kept[block] + terms[0] + terms[1] + terms[2]
+
+    mine = half(side)
+    own[...] = mine
+    own_sent[...] = mine.astype(BF16)
+    other_sent[...] = half(1 - side).astype(BF16)
 
 
 def line_sum(ids, kept, others):
@@ -363,18 +445,18 @@
     )(ids, near(kept), *[near(values) for values in others])
 
 
-def finish_kernel(ids, own, beside, far, corner, grads, more, features, weight, bias):
+def finish_kernel(ids, own, beside, opposite, corner, grads, more, features, weight, bias):
     blocks = own.shape[0]
     for b in range(blocks):
         mine = own[b] + beside[b].astype(F32)
-        other = far[b].astype(F32) + corner[b].astype(F32)
+        other = opposite[b].astype(F32) + corner[b].astype(F32)
         features[pl.ds((ids[0] * blocks + b) * TILE, TILE)] = mine.T
         features[pl.ds(((1 - ids[0]) * blocks + b) * TILE, TILE)] = other.T
     weight[...] = grads[0:TILE] + more[0:TILE]
     bias[...] = grads[TILE : TILE + 1] + more[TILE : TILE + 1]
 
 
-def finish(ids, own, beside, far, corner, grads, more):
+def finish(ids, own, beside, opposite, corner, grads, more):
     return pl.pallas_call(
         finish_kernel,
         out_shape=[
@@ -386,7 +468,7 @@
         out_specs=[VMEM] * 3,
         compiler_params=PARAMS,
         name="finish",
-    )(ids, near(own), near(beside), near(far), near(corner), near(grads), near(more))
+    )(ids, near(own), near(beside), near(opposite), near(corner), near(grads), near(more))
 
 
 def local(
@@ -401,24 +483,31 @@
     ids = jnp.stack([half, lax.axis_index("col"), lax.axis_index("row")]).astype(jnp.int32)
 
     mine = lax.dynamic_slice_in_dim(features, half * (own_rows // 2), own_rows // 2, 0)
-    sources = [swap(mine, "row", mask) for mask in range(1, n_row)]
+    beside, ids = lax.optimization_barrier((swap(mine, "row", 1), ids))
+    pair = join(mine, beside)
+    sources = [swap(pair, "row", mask) for mask in range(2, n_row, 2)]
     lists = pick(tile_count, ids, tile_rows, tile_columns, n_out, n_back)
     lists, sources = lax.optimization_barrier((lists, sources))
-    fetched, forward, backward, steps = lists
-
-    held, kept, sent = tiles_forward(steps, ids, fetched, forward, tiles, [mine, *sources], n_out)
+    fetched, forward, slots, steps = lists
+
+    held, kept, sent = tiles_forward(steps, ids, fetched, forward, tiles, [pair, *sources], n_out)
     first, *others = pair_sum(kept, swap(sent, "col", 1))
     others = [swap(other, "col", 2 * k + 2) for k, other in enumerate(others)]
     own, sent = own_sum(first, others)
-    other = swap(sent, "feat", 1)
-    activations, back, back_sent, grads = middle(own, other, weight, hidden_bias[None], cotangent)
+    sent, slots = lax.optimization_barrier((sent, slots))
+    ready = prepare(
+        ids, tile_rows, tile_columns, slots, forward.shape[1], n_back, weight, hidden_bias[None], cotangent
+    )
+    other, ready = lax.optimization_barrier((swap(sent, "feat", 1), ready))
+    backward, steps, weight, bias, cotangent = ready
+    activations, back, back_sent, grads = middle(own, other, weight, bias, cotangent)
 
     mine = message(back, swap(back_sent, "feat", 1), grads)
-    far = [swap(mine, "col", mask) for mask in (2, 6, 4)]
+    across = [swap(mine, "col", mask) for mask in (2, 6, 4)]
     beside = swap(mine, "col", 1)
-    far = lax.optimization_barrier(far)
-    across = [swap(values, "col", 1) for values in far]
-    sources = [mine, beside, far[0], across[0], far[2], across[2], far[1], across[1]]
+    across = lax.optimization_barrier(across)
+    corners = [swap(values, "col", 1) for values in across]
+    sources = [mine, beside, across[0], corners[0], across[2], corners[2], across[1], corners[1]]
     grads = grad_sum(sources)
     more = swap(grads, "row", 1)
     kept, *others = tiles_backward(steps, ids, backward, held, sources, n_back)
@@ -429,13 +518,13 @@
     others, more = lax.optimization_barrier((others, swap(grads, "row", 2)))
     grads = grads + more
     own, own_sent, other_sent = line_sum(ids, kept, others)
-    far = swap(own_sent, "feat", 1)
+    opposite = swap(own_sent, "feat", 1)
     corner = swap(other_sent, ("row", "feat"), 3)
     beside = swap(other_sent, "row", 1)
-    far, corner, beside, more = lax.optimization_barrier(
-        (far, corner, beside, swap(grads, "row", 4))
-    )
-    grad_features, grad_weight, grad_bias = finish(ids, own, beside, far, corner, grads, more)
+    opposite, corner, beside, more = lax.optimization_barrier(
+        (opposite, corner, beside, swap(grads, "row", 4))
+    )
+    grad_features, grad_weight, grad_bias = finish(ids, own, beside, opposite, corner, grads, more)
     return (activations, grad_features, grad_weight, grad_bias[0])
 
 

time: 98.3 us -> 94.1 us (0.957)
  starting transfers between devices: 44.5 us -> 37.3 us
  Pallas kernels: 12.6 us -> 16.4 us
  waiting for transfers between devices: 34.6 us -> 38.3 us
  local copies, waits for them, and re-layouts: 4.59 us -> 0.9 us
    ppermute x29 -> x26, starting transfers between devices: 44.5 us -> 37.3 us  [swap(): return lax.ppermute(values, axis, [(i, i ^ mask) for i in range(size)])]
    unnamed x12 -> x2, local copies, waits for them, and re-layouts: 4.58 us -> 0.9 us
    ppermute x29 -> x26, waiting for transfers between devices: 34.6 us -> 38.3 us  [swap(): return lax.ppermute(values, axis, [(i, i ^ mask) for i in range(size)])]
    pallas_call x1 -> x3, Pallas kernels: 2.7 us -> 5.13 us  [the longest x1 2.7 us: prepare(): pl.pallas_call(functools.partial(prepare_kernel, n_back), out_shape=[jax....]
  transfers between devices with their start and end apart: 29 -> 26, of which waited for: 19 -> 20; matrix products, arithmetic and copies ran while one was open for 0% -> 0% of each run, Pallas kernels for 6% -> 9%
where the time goes in v1:
time: 94.1 us; the launch traced here: 94.4 us
  waiting for transfers between devices  38.3 us (41%)
  starting transfers between devices  37.3 us (40%)
  Pallas kernels  16.4 us (17%)
  between operations  1.4 us (1%)
    ppermute x26, waiting for transfers between devices, swap(): return lax.ppermute(values, axis, [(i, i ^ mask) for i in range(size)])  38.3 us
    ppermute x26, starting transfers between devices, swap(): return lax.ppermute(values, axis, [(i, i ^ mask) for i in range(size)])  37.3 us
    pallas_call x1, Pallas kernels, tiles_forward(): pl.pallas_call(forward_kernel, out_shape=[pltpu.VMEM((length + 1, TILE, T...  5.39 us
    pallas_call x1, Pallas kernels, tiles_backward(): pl.pallas_call(backward_kernel, out_shape=[pltpu.VMEM(shape, F32)] + [plt...  2.71 us
    pallas_call x1, Pallas kernels, prepare(): pl.pallas_call(functools.partial(prepare_kernel, n_back), out_shape=[jax....  2.7 us
    pallas_call x1, Pallas kernels, pick(): pl.pallas_call(functools.partial(pick_kernel, n_out), out_shape=[listed,...  2.41 us
  transfers between devices with their start and end apart: 26, of which 20 were waited for; matrix products, arithmetic and copies ran while one was open for 0% of the time, Pallas kernels for 9%

profile of v1, /device:TPU:0, one launch (start us, length us, event | category | flops | bytes accessed | tf_op | source)
XLA Modules:
  0.0 94.4 jit_solution(2144736024849292628)
XLA Ops:
  0.6 0.0 copy-start
  0.7 0.9 copy-done
  1.5 2.0 %collective-permute-start = (bf16[256,128]{1,0:T(8,128)(2,1)S(1)}, bf16[256,128]{1,0:T(8,128)(2,1)S(1)}, u32[]{:S(2)}, u32[]{:S(2)}) collective-permute-start(bf16[256,128]{1,0:T(8,128)(2,1)S(1)} %constant_dynamic-slice_fusion.a), channel_id=1, source_target_pairs={{0,16},{16,0},{32,48},{48,32},{64,80},{80,64},{96,112},{112,96},{1... | collective-permute-start | bytes 196616 | tf_op jit(solution)/shard_map/ppermute | solution.py:25
  3.5 0.1 pad_add_fusion.ids
  3.6 2.2 %collective-permute-done.b = bf16[256,128]{1,0:T(8,128)(2,1)S(1)} collective-permute-done((bf16[256,128]{1,0:T(8,128)(2,1)S(1)}, bf16[256,128]{1,0:T(8,128)(2,1)S(1)}, u32[]{:S(2)}, u32[]{:S(2)}) %collective-permute-start) | collective-permute-done | bytes 65568 | tf_op jit(solution)/shard_map/ppermute | solution.py:25
  5.8 3.2 %collective-permute-start.3 = (bf16[512,128]{1,0:T(8,128)(2,1)S(1)}, bf16[512,128]{1,0:T(8,128)(2,1)S(1)}, u32[]{:S(2)}, u32[]{:S(2)}) collective-permute-start(bf16[512,128]{1,0:T(8,128)(2,1)S(1)} %join.1.refs_0_), channel_id=1, source_target_pairs={{0,96},{16,112},{32,64},{48,80},{64,32},{80,48},{96,0},{112,16},{1... | collective-permute-start | bytes 393224 | tf_op jit(solution)/shard_map/ppermute | solution.py:25
  9.0 0.6 collective-permute-start.2
  9.6 0.4 collective-permute-start.1
  10.7 2.4 %pick_tiles.1 = (s32[1,768]{1,0:T(1,128)S(1)}, s32[1,768]{1,0:T(1,128)S(1)}, s32[1,640]{1,0:T(1,128)S(1)}, s32[1]{0:T(128)}) custom-call(s32[1,1]{1,0:T(1,128)S(6)} %copy.12.count, s32[3]{0:T(128)S(1)} %pad_add_fusion.ids, s32[1,1,640]{2,1,0:T(1,128)} %rows.3, s32[1,1,640]{2,1,0:T(1,128)} %columns.3), custom_call_target="tpu_custom_call" | custom-call | tf_op jit(solution)/shard_map/pick_tiles/pallas_call | solution.py:94
  13.1 0.6 collective-permute-done.3.refs_3_
  13.6 2.3 %collective-permute-done.2.refs_2_ = bf16[512,128]{1,0:T(8,128)(2,1)S(1)} collective-permute-done((bf16[512,128]{1,0:T(8,128)(2,1)S(1)}, bf16[512,128]{1,0:T(8,128)(2,1)S(1)}, u32[]{:S(2)}, u32[]{:S(2)}) %collective-permute-start.2) | collective-permute-done | bytes 131104 | tf_op jit(solution)/shard_map/ppermute | solution.py:25
  15.9 0.0 collective-permute-done.1.refs_1_
  15.9 5.4 %tiles_forward.1 = (bf16[769,128,128]{2,1,0:T(8,128)(2,1)S(1)}, f32[4,4,128,128]{3,2,1,0:T(8,128)S(1)}, bf16[4,4,128,128]{3,2,1,0:T(8,128)(2,1)S(1)}) custom-call(s32[1]{0:T(128)} %get-tuple-element.74.steps, s32[3]{0:T(128)S(1)} %pad_add_fusion.ids, s32[1,768]{1,0:T(1,128)S(1)} %get-tuple-element.75.fetched, s32[1,768]{1,0:T(1,128)S(1)} %get-tuple-element.76.picked, ...), custom_call_target="tpu_custom_call" | custom-call | tf_op jit(solution)/shard_map/tiles_forward/pallas_call | solution.py:235
  21.3 0.3 collective-permute-start.4
  21.6 1.7 %collective-permute-done.4.got = bf16[4,4,128,128]{3,2,1,0:T(8,128)(2,1)S(1)} collective-permute-done((bf16[4,4,128,128]{3,2,1,0:T(8,128)(2,1)S(1)}, bf16[4,4,128,128]{3,2,1,0:T(8,128)(2,1)S(1)}, u32[]{:S(2)}, u32[]{:S(2)}) %collective-permute-start.4) | collective-permute-done | bytes 524320 | tf_op jit(solution)/shard_map/ppermute | solution.py:25
  23.3 0.1 pair_sum.1
  23.4 0.9 collective-permute-start.5
  24.3 3.7 %collective-permute-start.6 = (bf16[4,128,128]{2,1,0:T(8,128)(2,1)S(1)}, bf16[4,128,128]{2,1,0:T(8,128)(2,1)S(1)}, u32[]{:S(2)}, u32[]{:S(2)}) collective-permute-start(bf16[4,128,128]{2,1,0:T(8,128)(2,1)S(1)} %get-tuple-element.84), channel_id=1, source_target_pairs={{0,8},{2,10},{4,12},{6,14},{8,0},{10,2},{12,4},{14,6},{1,9},{3,11}... | collective-permute-start | bytes 393224 | tf_op jit(solution)/shard_map/ppermute | solution.py:25
  28.0 0.2 collective-permute-start.7
  28.2 1.6 %collective-permute-done.5.a = bf16[4,128,128]{2,1,0:T(8,128)(2,1)S(1)} collective-permute-done((bf16[4,128,128]{2,1,0:T(8,128)(2,1)S(1)}, bf16[4,128,128]{2,1,0:T(8,128)(2,1)S(1)}, u32[]{:S(2)}, u32[]{:S(2)}) %collective-permute-start.5) | collective-permute-done | bytes 131104 | tf_op jit(solution)/shard_map/ppermute | solution.py:25
  29.8 4.6 %collective-permute-done.6.b = bf16[4,128,128]{2,1,0:T(8,128)(2,1)S(1)} collective-permute-done((bf16[4,128,128]{2,1,0:T(8,128)(2,1)S(1)}, bf16[4,128,128]{2,1,0:T(8,128)(2,1)S(1)}, u32[]{:S(2)}, u32[]{:S(2)}) %collective-permute-start.6) | collective-permute-done | bytes 131104 | tf_op jit(solution)/shard_map/ppermute | solution.py:25
  34.4 2.2 %collective-permute-done.7.c = bf16[4,128,128]{2,1,0:T(8,128)(2,1)S(1)} collective-permute-done((bf16[4,128,128]{2,1,0:T(8,128)(2,1)S(1)}, bf16[4,128,128]{2,1,0:T(8,128)(2,1)S(1)}, u32[]{:S(2)}, u32[]{:S(2)}) %collective-permute-start.7) | collective-permute-done | bytes 131104 | tf_op jit(solution)/shard_map/ppermute | solution.py:25
  36.7 0.1 own_sum.1
  36.7 2.6 %collective-permute-start.8 = (bf16[4,128,128]{2,1,0:T(8,128)(2,1)S(1)}, bf16[4,128,128]{2,1,0:T(8,128)(2,1)S(1)}, u32[]{:S(2)}, u32[]{:S(2)}) collective-permute-start(bf16[4,128,128]{2,1,0:T(8,128)(2,1)S(1)} %get-tuple-element.89), channel_id=1, source_target_pairs={{0,1},{1,0},{2,3},{3,2},{4,5},{5,4},{6,7},{7,6},{8,9},{9,8},{10,11... | collective-permute-start | bytes 393224 | tf_op jit(solution)/shard_map/ppermute | solution.py:25
  39.3 2.7 %prepare.1 = (s32[1,768]{1,0:T(1,128)S(1)}, s32[1]{0:T(128)}, bf16[128,128]{1,0:T(8,128)(2,1)S(1)}, f32[1,128]{1,0:T(1,128)S(1)}, bf16[512,128]{1,0:T(8,128)(2,1)S(1)}) custom-call(s32[3]{0:T(128)S(1)} %pad_add_fusion.ids, s32[1,1,640]{2,1,0:T(1,128)} %rows.3, s32[1,1,640]{2,1,0:T(1,128)} %columns.3, s32[1,640]{1,0:T(1,128)S(1)} %get-tuple-element.90.slots, ...), custom_call_target="tpu_custom_call" | custom-call | tf_op jit(solution)/shard_map/prepare/pallas_call | solution.py:146
  42.1 1.2 %collective-permute-done.8.other = bf16[4,128,128]{2,1,0:T(8,128)(2,1)S(1)} collective-permute-done((bf16[4,128,128]{2,1,0:T(8,128)(2,1)S(1)}, bf16[4,128,128]{2,1,0:T(8,128)(2,1)S(1)}, u32[]{:S(2)}, u32[]{:S(2)}) %collective-permute-start.8) | collective-permute-done | bytes 131104 | tf_op jit(solution)/shard_map/ppermute | solution.py:25
  43.3 0.9 middle.1
  44.2 2.5 %collective-permute-start.9 = (bf16[4,128,128]{2,1,0:T(8,128)(2,1)S(1)}, bf16[4,128,128]{2,1,0:T(8,128)(2,1)S(1)}, u32[]{:S(2)}, u32[]{:S(2)}) collective-permute-start(bf16[4,128,128]{2,1,0:T(8,128)(2,1)S(1)} %get-tuple-element.105), channel_id=1, source_target_pairs={{0,1},{1,0},{2,3},{3,2},{4,5},{5,4},{6,7},{7,6},{8,9},{9,8},{10,11... | collective-permute-start | bytes 393224 | tf_op jit(solution)/shard_map/ppermute | solution.py:25
  46.7 3.9 %collective-permute-done.9.other = bf16[4,128,128]{2,1,0:T(8,128)(2,1)S(1)} collective-permute-done((bf16[4,128,128]{2,1,0:T(8,128)(2,1)S(1)}, bf16[4,128,128]{2,1,0:T(8,128)(2,1)S(1)}, u32[]{:S(2)}, u32[]{:S(2)}) %collective-permute-start.9) | collective-permute-done | bytes 131104 | tf_op jit(solution)/shard_map/ppermute | solution.py:25
  50.7 0.1 collective-permute-start.13
  50.8 1.7 %collective-permute-start.12 = (bf16[656,128]{1,0:T(8,128)(2,1)S(1)}, bf16[656,128]{1,0:T(8,128)(2,1)S(1)}, u32[]{:S(2)}, u32[]{:S(2)}) collective-permute-start(bf16[656,128]{1,0:T(8,128)(2,1)S(1)} %message.1.refs_0_), channel_id=1, source_target_pairs={{0,12},{2,14},{4,8},{6,10},{8,4},{10,6},{12,0},{14,2},{1,13},{3,15... | collective-permute-start | bytes 503816 | tf_op jit(solution)/shard_map/ppermute | solution.py:25
  52.5 1.8 %collective-permute-start.11 = (bf16[656,128]{1,0:T(8,128)(2,1)S(1)}, bf16[656,128]{1,0:T(8,128)(2,1)S(1)}, u32[]{:S(2)}, u32[]{:S(2)}) collective-permute-start(bf16[656,128]{1,0:T(8,128)(2,1)S(1)} %message.1.refs_0_), channel_id=1, source_target_pairs={{0,4},{2,6},{4,0},{6,2},{8,12},{10,14},{12,8},{14,10},{1,5},{3,7},... | collective-permute-start | bytes 503816 | tf_op jit(solution)/shard_map/ppermute | solution.py:25
  54.3 0.0 collective-permute-start.10
  54.3 3.5 %collective-permute-done.13.refs_4_ = bf16[656,128]{1,0:T(8,128)(2,1)S(1)} collective-permute-done((bf16[656,128]{1,0:T(8,128)(2,1)S(1)}, bf16[656,128]{1,0:T(8,128)(2,1)S(1)}, u32[]{:S(2)}, u32[]{:S(2)}) %collective-permute-start.13) | collective-permute-done | bytes 167968 | tf_op jit(solution)/shard_map/ppermute | solution.py:25
  57.8 1.5 %collective-permute-done.12.refs_6_ = bf16[656,128]{1,0:T(8,128)(2,1)S(1)} collective-permute-done((bf16[656,128]{1,0:T(8,128)(2,1)S(1)}, bf16[656,128]{1,0:T(8,128)(2,1)S(1)}, u32[]{:S(2)}, u32[]{:S(2)}) %collective-permute-start.12) | collective-permute-done | bytes 167968 | tf_op jit(solution)/shard_map/ppermute | solution.py:25
  59.3 0.0 collective-permute-done.11.refs_2_
  59.3 0.0 collective-permute-start.14
  59.3 0.5 collective-permute-start.15
  59.8 0.0 collective-permute-start.16
  59.8 0.0 collective-permute-done.10.refs_1_
  59.8 0.9 collective-permute-done.14.refs_3_
  60.7 0.2 collective-permute-done.15.refs_5_
  60.9 0.3 collective-permute-done.16.refs_7_
  61.2 0.1 grad_sum.1
  61.2 2.4 %collective-permute-start.17 = (f32[136,128]{1,0:T(8,128)S(1)}, f32[136,128]{1,0:T(8,128)S(1)}, u32[]{:S(2)}, u32[]{:S(2)}) collective-permute-start(f32[136,128]{1,0:T(8,128)S(1)} %grad_sum.1), channel_id=1, source_target_pairs={{0,16},{16,0},{32,48},{48,32},{64,80},{80,64},{96,112},{112,96},{1... | collective-permute-start | bytes 208904 | tf_op jit(solution)/shard_map/ppermute | solution.py:25
  63.7 2.7 %tiles_backward.1 = (f32[4,128,128]{2,1,0:T(8,128)S(1)}, bf16[4,128,128]{2,1,0:T(8,128)(2,1)S(1)}, bf16[4,128,128]{2,1,0:T(8,128)(2,1)S(1)}, bf16[4,128,128]{2,1,0:T(8,128)(2,1)S(1)}) custom-call(s32[1]{0:T(128)} %get-tuple-element.101.steps, s32[3]{0:T(128)S(1)} %pad_add_fusion.ids, s32[1,768]{1,0:T(1,128)S(1)} %get-tuple-element.102.picked, ...), custom_call_target="tpu_custom_call" | custom-call | tf_op jit(solution)/shard_map/tiles_backward/pallas_call | solution.py:280
  66.4 0.0 collective-permute-done.17
  66.4 2.5 %collective-permute-start.18 = (bf16[4,128,128]{2,1,0:T(8,128)(2,1)S(1)}, bf16[4,128,128]{2,1,0:T(8,128)(2,1)S(1)}, u32[]{:S(2)}, u32[]{:S(2)}) collective-permute-start(bf16[4,128,128]{2,1,0:T(8,128)(2,1)S(1)} %get-tuple-element.114), channel_id=1, source_target_pairs={{0,32},{16,48},{32,0},{48,16},{64,96},{80,112},{96,64},{112,80},{1... | collective-permute-start | bytes 393224 | tf_op jit(solution)/shard_map/ppermute | solution.py:25
  68.8 6.8 %collective-permute-start.19 = (bf16[4,128,128]{2,1,0:T(8,128)(2,1)S(1)}, bf16[4,128,128]{2,1,0:T(8,128)(2,1)S(1)}, u32[]{:S(2)}, u32[]{:S(2)}) collective-permute-start(bf16[4,128,128]{2,1,0:T(8,128)(2,1)S(1)} %get-tuple-element.115), channel_id=1, source_target_pairs={{0,64},{16,80},{32,96},{48,112},{64,0},{80,16},{96,32},{112,48},{1... | collective-permute-start | bytes 393224 | tf_op jit(solution)/shard_map/ppermute | solution.py:25
  75.6 0.0 collective-permute-start.20
  75.6 0.1 collective-permute-start.21
  75.7 4.3 %collective-permute-done.21 = f32[136,128]{1,0:T(8,128)S(1)} collective-permute-done((f32[136,128]{1,0:T(8,128)S(1)}, f32[136,128]{1,0:T(8,128)S(1)}, u32[]{:S(2)}, u32[]{:S(2)}) %collective-permute-start.21) | collective-permute-done | bytes 69664 | tf_op jit(solution)/shard_map/ppermute | solution.py:25
  80.0 0.0 collective-permute-done.18.a
  80.0 0.1 collective-permute-done.19.b
  80.1 1.7 %collective-permute-done.20.c = bf16[4,128,128]{2,1,0:T(8,128)(2,1)S(1)} collective-permute-done((bf16[4,128,128]{2,1,0:T(8,128)(2,1)S(1)}, bf16[4,128,128]{2,1,0:T(8,128)(2,1)S(1)}, u32[]{:S(2)}, u32[]{:S(2)}) %collective-permute-start.20) | collective-permute-done | bytes 131104 | tf_op jit(solution)/shard_map/ppermute | solution.py:25
  81.8 1.0 %collective-permute-start.25 = (f32[136,128]{1,0:T(8,128)S(1)}, f32[136,128]{1,0:T(8,128)S(1)}, u32[]{:S(2)}, u32[]{:S(2)}) collective-permute-start(f32[136,128]{1,0:T(8,128)S(1)} %add.11.grads), channel_id=1, source_target_pairs={{0,64},{16,80},{32,96},{48,112},{64,0},{80,16},{96,32},{112,48},{1... | collective-permute-start | bytes 208904 | tf_op jit(solution)/shard_map/ppermute | solution.py:25
  82.8 0.6 line_sum.1
  83.4 3.3 %collective-permute-start.22 = (bf16[2,128,128]{2,1,0:T(8,128)(2,1)S(1)}, bf16[2,128,128]{2,1,0:T(8,128)(2,1)S(1)}, u32[]{:S(2)}, u32[]{:S(2)}) collective-permute-start(bf16[2,128,128]{2,1,0:T(8,128)(2,1)S(1)} %get-tuple-element.122), channel_id=1, source_target_pairs={{0,1},{1,0},{2,3},{3,2},{4,5},{5,4},{6,7},{7,6},{8,9},{9,8},{10,11... | collective-permute-start | bytes 196616 | tf_op jit(solution)/shard_map/ppermute | solution.py:25
  86.7 0.8 collective-permute-start.24
  87.5 0.1 collective-permute-start.23
  87.6 1.7 %collective-permute-done.22.opposite = bf16[2,128,128]{2,1,0:T(8,128)(2,1)S(1)} collective-permute-done((bf16[2,128,128]{2,1,0:T(8,128)(2,1)S(1)}, bf16[2,128,128]{2,1,0:T(8,128)(2,1)S(1)}, u32[]{:S(2)}, u32[]{:S(2)}) %collective-permute-start.22) | collective-permute-done | bytes 65568 | tf_op jit(solution)/shard_map/ppermute | solution.py:25
  89.3 1.7 %collective-permute-done.24.beside = bf16[2,128,128]{2,1,0:T(8,128)(2,1)S(1)} collective-permute-done((bf16[2,128,128]{2,1,0:T(8,128)(2,1)S(1)}, bf16[2,128,128]{2,1,0:T(8,128)(2,1)S(1)}, u32[]{:S(2)}, u32[]{:S(2)}) %collective-permute-start.24) | collective-permute-done | bytes 65568 | tf_op jit(solution)/shard_map/ppermute | solution.py:25
  91.0 2.0 %collective-permute-done.23.corner = bf16[2,128,128]{2,1,0:T(8,128)(2,1)S(1)} collective-permute-done((bf16[2,128,128]{2,1,0:T(8,128)(2,1)S(1)}, bf16[2,128,128]{2,1,0:T(8,128)(2,1)S(1)}, u32[]{:S(2)}, u32[]{:S(2)}) %collective-permute-start.23) | collective-permute-done | bytes 65568 | tf_op jit(solution)/shard_map/ppermute | solution.py:25
  93.0 1.4 %finish.1 = (f32[512,128]{1,0:T(8,128)}, f32[128,128]{1,0:T(8,128)}, f32[1,128]{1,0:T(1,128)}) custom-call(s32[3]{0:T(128)S(1)} %pad_add_fusion.ids, f32[2,128,128]{2,1,0:T(8,128)S(1)} %get-tuple-element.121.own, bf16[2,128,128]{2,1,0:T(8,128)(2,1)S(1)} %collective-permute-done.24.beside, bf16[2,128,128]{2,1,0:T(8,128)(2,1)S(1)} %collective-permute-done.22.opposite, ...), custom_call_target="tpu_custom_call" | custom-call | tf_op jit(solution)/shard_map/finish/pallas_call | solution.py:460
  (6 shorter events, 0.1 us)
Async XLA Ops:
  0.6 0.9 copy-start
  1.5 4.3 %collective-permute-start = (bf16[256,128]{1,0:T(8,128)(2,1)S(1)}, bf16[256,128]{1,0:T(8,128)(2,1)S(1)}, u32[]{:S(2)}, u32[]{:S(2)}) collective-permute-start(bf16[256,128]{1,0:T(8,128)(2,1)S(1)} %constant_dynamic-slice_fusion.a), channel_id=1, source_target_pairs={{0,16},{16,0},{32,48},{48,32},{64,80},{80,64},{96,112},{112,96},{1... | collective-permute-start | bytes 196616 | tf_op jit(solution)/shard_map/ppermute | solution.py:25
  5.8 7.8 %collective-permute-start.3 = (bf16[512,128]{1,0:T(8,128)(2,1)S(1)}, bf16[512,128]{1,0:T(8,128)(2,1)S(1)}, u32[]{:S(2)}, u32[]{:S(2)}) collective-permute-start(bf16[512,128]{1,0:T(8,128)(2,1)S(1)} %join.1.refs_0_), channel_id=1, source_target_pairs={{0,96},{16,112},{32,64},{48,80},{64,32},{80,48},{96,0},{112,16},{1... | collective-permute-start | bytes 393224 | tf_op jit(solution)/shard_map/ppermute | solution.py:25
  9.0 6.9 %collective-permute-start.2 = (bf16[512,128]{1,0:T(8,128)(2,1)S(1)}, bf16[512,128]{1,0:T(8,128)(2,1)S(1)}, u32[]{:S(2)}, u32[]{:S(2)}) collective-permute-start(bf16[512,128]{1,0:T(8,128)(2,1)S(1)} %join.1.refs_0_), channel_id=1, source_target_pairs={{0,64},{16,80},{32,96},{48,112},{64,0},{80,16},{96,32},{112,48},{1... | collective-permute-start | bytes 393224 | tf_op jit(solution)/shard_map/ppermute | solution.py:25
  9.6 6.3 %collective-permute-start.1 = (bf16[512,128]{1,0:T(8,128)(2,1)S(1)}, bf16[512,128]{1,0:T(8,128)(2,1)S(1)}, u32[]{:S(2)}, u32[]{:S(2)}) collective-permute-start(bf16[512,128]{1,0:T(8,128)(2,1)S(1)} %join.1.refs_0_), channel_id=1, source_target_pairs={{0,32},{16,48},{32,0},{48,16},{64,96},{80,112},{96,64},{112,80},{1... | collective-permute-start | bytes 393224 | tf_op jit(solution)/shard_map/ppermute | solution.py:25
  21.3 2.0 %collective-permute-start.4 = (bf16[4,4,128,128]{3,2,1,0:T(8,128)(2,1)S(1)}, bf16[4,4,128,128]{3,2,1,0:T(8,128)(2,1)S(1)}, u32[]{:S(2)}, u32[]{:S(2)}) collective-permute-start(bf16[4,4,128,128]{3,2,1,0:T(8,128)(2,1)S(1)} %get-tuple-element.81), channel_id=1, source_target_pairs={{0,2},{2,0},{4,6},{6,4},{8,10},{10,8},{12,14},{14,12},{1,3},{3,1},... | collective-permute-start | bytes 1572872 | tf_op jit(solution)/shard_map/ppermute | solution.py:25
  23.4 6.4 %collective-permute-start.5 = (bf16[4,128,128]{2,1,0:T(8,128)(2,1)S(1)}, bf16[4,128,128]{2,1,0:T(8,128)(2,1)S(1)}, u32[]{:S(2)}, u32[]{:S(2)}) collective-permute-start(bf16[4,128,128]{2,1,0:T(8,128)(2,1)S(1)} %get-tuple-element.83), channel_id=1, source_target_pairs={{0,4},{2,6},{4,0},{6,2},{8,12},{10,14},{12,8},{14,10},{1,5},{3,7},... | collective-permute-start | bytes 393224 | tf_op jit(solution)/shard_map/ppermute | solution.py:25
  24.3 10.2 %collective-permute-start.6 = (bf16[4,128,128]{2,1,0:T(8,128)(2,1)S(1)}, bf16[4,128,128]{2,1,0:T(8,128)(2,1)S(1)}, u32[]{:S(2)}, u32[]{:S(2)}) collective-permute-start(bf16[4,128,128]{2,1,0:T(8,128)(2,1)S(1)} %get-tuple-element.84), channel_id=1, source_target_pairs={{0,8},{2,10},{4,12},{6,14},{8,0},{10,2},{12,4},{14,6},{1,9},{3,11}... | collective-permute-start | bytes 393224 | tf_op jit(solution)/shard_map/ppermute | solution.py:25
  28.0 8.7 %collective-permute-start.7 = (bf16[4,128,128]{2,1,0:T(8,128)(2,1)S(1)}, bf16[4,128,128]{2,1,0:T(8,128)(2,1)S(1)}, u32[]{:S(2)}, u32[]{:S(2)}) collective-permute-start(bf16[4,128,128]{2,1,0:T(8,128)(2,1)S(1)} %get-tuple-element.85), channel_id=1, source_target_pairs={{0,12},{2,14},{4,8},{6,10},{8,4},{10,6},{12,0},{14,2},{1,13},{3,15... | collective-permute-start | bytes 393224 | tf_op jit(solution)/shard_map/ppermute | solution.py:25
  36.7 6.6 %collective-permute-start.8 = (bf16[4,128,128]{2,1,0:T(8,128)(2,1)S(1)}, bf16[4,128,128]{2,1,0:T(8,128)(2,1)S(1)}, u32[]{:S(2)}, u32[]{:S(2)}) collective-permute-start(bf16[4,128,128]{2,1,0:T(8,128)(2,1)S(1)} %get-tuple-element.89), channel_id=1, source_target_pairs={{0,1},{1,0},{2,3},{3,2},{4,5},{5,4},{6,7},{7,6},{8,9},{9,8},{10,11... | collective-permute-start | bytes 393224 | tf_op jit(solution)/shard_map/ppermute | solution.py:25
  44.2 6.5 %collective-permute-start.9 = (bf16[4,128,128]{2,1,0:T(8,128)(2,1)S(1)}, bf16[4,128,128]{2,1,0:T(8,128)(2,1)S(1)}, u32[]{:S(2)}, u32[]{:S(2)}) collective-permute-start(bf16[4,128,128]{2,1,0:T(8,128)(2,1)S(1)} %get-tuple-element.105), channel_id=1, source_target_pairs={{0,1},{1,0},{2,3},{3,2},{4,5},{5,4},{6,7},{7,6},{8,9},{9,8},{10,11... | collective-permute-start | bytes 393224 | tf_op jit(solution)/shard_map/ppermute | solution.py:25
  50.7 7.1 %collective-permute-start.13 = (bf16[656,128]{1,0:T(8,128)(2,1)S(1)}, bf16[656,128]{1,0:T(8,128)(2,1)S(1)}, u32[]{:S(2)}, u32[]{:S(2)}) collective-permute-start(bf16[656,128]{1,0:T(8,128)(2,1)S(1)} %message.1.refs_0_), channel_id=1, source_target_pairs={{0,8},{2,10},{4,12},{6,14},{8,0},{10,2},{12,4},{14,6},{1,9},{3,11}... | collective-permute-start | bytes 503816 | tf_op jit(solution)/shard_map/ppermute | solution.py:25
  50.8 8.5 %collective-permute-start.12 = (bf16[656,128]{1,0:T(8,128)(2,1)S(1)}, bf16[656,128]{1,0:T(8,128)(2,1)S(1)}, u32[]{:S(2)}, u32[]{:S(2)}) collective-permute-start(bf16[656,128]{1,0:T(8,128)(2,1)S(1)} %message.1.refs_0_), channel_id=1, source_target_pairs={{0,12},{2,14},{4,8},{6,10},{8,4},{10,6},{12,0},{14,2},{1,13},{3,15... | collective-permute-start | bytes 503816 | tf_op jit(solution)/shard_map/ppermute | solution.py:25
  52.5 6.8 %collective-permute-start.11 = (bf16[656,128]{1,0:T(8,128)(2,1)S(1)}, bf16[656,128]{1,0:T(8,128)(2,1)S(1)}, u32[]{:S(2)}, u32[]{:S(2)}) collective-permute-start(bf16[656,128]{1,0:T(8,128)(2,1)S(1)} %message.1.refs_0_), channel_id=1, source_target_pairs={{0,4},{2,6},{4,0},{6,2},{8,12},{10,14},{12,8},{14,10},{1,5},{3,7},... | collective-permute-start | bytes 503816 | tf_op jit(solution)/shard_map/ppermute | solution.py:25
  54.3 5.5 %collective-permute-start.10 = (bf16[656,128]{1,0:T(8,128)(2,1)S(1)}, bf16[656,128]{1,0:T(8,128)(2,1)S(1)}, u32[]{:S(2)}, u32[]{:S(2)}) collective-permute-start(bf16[656,128]{1,0:T(8,128)(2,1)S(1)} %message.1.refs_0_), channel_id=1, source_target_pairs={{0,2},{2,0},{4,6},{6,4},{8,10},{10,8},{12,14},{14,12},{1,3},{3,1},... | collective-permute-start | bytes 503816 | tf_op jit(solution)/shard_map/ppermute | solution.py:25
  59.3 1.4 %collective-permute-start.14 = (bf16[656,128]{1,0:T(8,128)(2,1)S(1)}, bf16[656,128]{1,0:T(8,128)(2,1)S(1)}, u32[]{:S(2)}, u32[]{:S(2)}) collective-permute-start(bf16[656,128]{1,0:T(8,128)(2,1)S(1)} %collective-permute-done.11.refs_2_), channel_id=1, source_target_pairs={{0,2},{2,0},{4,6},{6,4},{8,10},{10,8},{12,14},{14,12},{1,3},{3,1},... | collective-permute-start | bytes 503816 | tf_op jit(solution)/shard_map/ppermute | solution.py:25
  59.3 1.6 %collective-permute-start.15 = (bf16[656,128]{1,0:T(8,128)(2,1)S(1)}, bf16[656,128]{1,0:T(8,128)(2,1)S(1)}, u32[]{:S(2)}, u32[]{:S(2)}) collective-permute-start(bf16[656,128]{1,0:T(8,128)(2,1)S(1)} %collective-permute-done.13.refs_4_), channel_id=1, source_target_pairs={{0,2},{2,0},{4,6},{6,4},{8,10},{10,8},{12,14},{14,12},{1,3},{3,1},... | collective-permute-start | bytes 503816 | tf_op jit(solution)/shard_map/ppermute | solution.py:25
  59.8 1.4 %collective-permute-start.16 = (bf16[656,128]{1,0:T(8,128)(2,1)S(1)}, bf16[656,128]{1,0:T(8,128)(2,1)S(1)}, u32[]{:S(2)}, u32[]{:S(2)}) collective-permute-start(bf16[656,128]{1,0:T(8,128)(2,1)S(1)} %collective-permute-done.12.refs_6_), channel_id=1, source_target_pairs={{0,2},{2,0},{4,6},{6,4},{8,10},{10,8},{12,14},{14,12},{1,3},{3,1},... | collective-permute-start | bytes 503816 | tf_op jit(solution)/shard_map/ppermute | solution.py:25
  61.2 5.2 %collective-permute-start.17 = (f32[136,128]{1,0:T(8,128)S(1)}, f32[136,128]{1,0:T(8,128)S(1)}, u32[]{:S(2)}, u32[]{:S(2)}) collective-permute-start(f32[136,128]{1,0:T(8,128)S(1)} %grad_sum.1), channel_id=1, source_target_pairs={{0,16},{16,0},{32,48},{48,32},{64,80},{80,64},{96,112},{112,96},{1... | collective-permute-start | bytes 208904 | tf_op jit(solution)/shard_map/ppermute | solution.py:25
  66.4 13.6 %collective-permute-start.18 = (bf16[4,128,128]{2,1,0:T(8,128)(2,1)S(1)}, bf16[4,128,128]{2,1,0:T(8,128)(2,1)S(1)}, u32[]{:S(2)}, u32[]{:S(2)}) collective-permute-start(bf16[4,128,128]{2,1,0:T(8,128)(2,1)S(1)} %get-tuple-element.114), channel_id=1, source_target_pairs={{0,32},{16,48},{32,0},{48,16},{64,96},{80,112},{96,64},{112,80},{1... | collective-permute-start | bytes 393224 | tf_op jit(solution)/shard_map/ppermute | solution.py:25
  68.8 11.2 %collective-permute-start.19 = (bf16[4,128,128]{2,1,0:T(8,128)(2,1)S(1)}, bf16[4,128,128]{2,1,0:T(8,128)(2,1)S(1)}, u32[]{:S(2)}, u32[]{:S(2)}) collective-permute-start(bf16[4,128,128]{2,1,0:T(8,128)(2,1)S(1)} %get-tuple-element.115), channel_id=1, source_target_pairs={{0,64},{16,80},{32,96},{48,112},{64,0},{80,16},{96,32},{112,48},{1... | collective-permute-start | bytes 393224 | tf_op jit(solution)/shard_map/ppermute | solution.py:25
  75.6 6.2 %collective-permute-start.20 = (bf16[4,128,128]{2,1,0:T(8,128)(2,1)S(1)}, bf16[4,128,128]{2,1,0:T(8,128)(2,1)S(1)}, u32[]{:S(2)}, u32[]{:S(2)}) collective-permute-start(bf16[4,128,128]{2,1,0:T(8,128)(2,1)S(1)} %get-tuple-element.116), channel_id=1, source_target_pairs={{0,96},{16,112},{32,64},{48,80},{64,32},{80,48},{96,0},{112,16},{1... | collective-permute-start | bytes 393224 | tf_op jit(solution)/shard_map/ppermute | solution.py:25
  75.6 4.4 %collective-permute-start.21 = (f32[136,128]{1,0:T(8,128)S(1)}, f32[136,128]{1,0:T(8,128)S(1)}, u32[]{:S(2)}, u32[]{:S(2)}) collective-permute-start(f32[136,128]{1,0:T(8,128)S(1)} %add.10), channel_id=1, source_target_pairs={{0,32},{16,48},{32,0},{48,16},{64,96},{80,112},{96,64},{112,80},{1... | collective-permute-start | bytes 208904 | tf_op jit(solution)/shard_map/ppermute | solution.py:25
  81.8 11.2 %collective-permute-start.25 = (f32[136,128]{1,0:T(8,128)S(1)}, f32[136,128]{1,0:T(8,128)S(1)}, u32[]{:S(2)}, u32[]{:S(2)}) collective-permute-start(f32[136,128]{1,0:T(8,128)S(1)} %add.11.grads), channel_id=1, source_target_pairs={{0,64},{16,80},{32,96},{48,112},{64,0},{80,16},{96,32},{112,48},{1... | collective-permute-start | bytes 208904 | tf_op jit(solution)/shard_map/ppermute | solution.py:25
  83.4 5.9 %collective-permute-start.22 = (bf16[2,128,128]{2,1,0:T(8,128)(2,1)S(1)}, bf16[2,128,128]{2,1,0:T(8,128)(2,1)S(1)}, u32[]{:S(2)}, u32[]{:S(2)}) collective-permute-start(bf16[2,128,128]{2,1,0:T(8,128)(2,1)S(1)} %get-tuple-element.122), channel_id=1, source_target_pairs={{0,1},{1,0},{2,3},{3,2},{4,5},{5,4},{6,7},{7,6},{8,9},{9,8},{10,11... | collective-permute-start | bytes 196616 | tf_op jit(solution)/shard_map/ppermute | solution.py:25
  86.7 4.3 %collective-permute-start.24 = (bf16[2,128,128]{2,1,0:T(8,128)(2,1)S(1)}, bf16[2,128,128]{2,1,0:T(8,128)(2,1)S(1)}, u32[]{:S(2)}, u32[]{:S(2)}) collective-permute-start(bf16[2,128,128]{2,1,0:T(8,128)(2,1)S(1)} %get-tuple-element.123), channel_id=1, source_target_pairs={{0,16},{16,0},{32,48},{48,32},{64,80},{80,64},{96,112},{112,96},{1... | collective-permute-start | bytes 196616 | tf_op jit(solution)/shard_map/ppermute | solution.py:25
  87.5 5.5 %collective-permute-start.23 = (bf16[2,128,128]{2,1,0:T(8,128)(2,1)S(1)}, bf16[2,128,128]{2,1,0:T(8,128)(2,1)S(1)}, u32[]{:S(2)}, u32[]{:S(2)}) collective-permute-start(bf16[2,128,128]{2,1,0:T(8,128)(2,1)S(1)} %get-tuple-element.123), channel_id=1, source_target_pairs={{0,17},{1,16},{16,1},{17,0},{32,49},{33,48},{48,33},{49,32},{64,81... | collective-permute-start | bytes 196616 | tf_op jit(solution)/shard_map/ppermute | solution.py:25

commit v2 on v1

--- a/solution.py
+++ b/solution.py
@@ -13,6 +13,7 @@
 PER = 32
 FORWARD = 2
 BACKWARD = 4
+EARLY = 4
 VMEM = pl.BlockSpec(memory_space=pltpu.VMEM)
 SMEM = pl.BlockSpec(memory_space=pltpu.SMEM)
 ANY = pl.BlockSpec(memory_space=pl.ANY)
@@ -27,6 +28,10 @@
 
 def near(values):
     return pltpu.with_memory_space_constraint(values, pltpu.VMEM)
+
+
+def scalar(values):
+    return pltpu.with_memory_space_constraint(values, pltpu.SMEM)
 
 
 def far(values):
@@ -66,13 +71,19 @@
     return items, found[2:3], target, steps, slot
 
 
-def pick_kernel(n_out, count, ids, rows, columns, fetched, forward, slots, steps, row_copy, column_copy, arrived):
+def pick_kernel(
+    n_out, count, ids, rows, columns, tiles,
+    held, fetched, forward, steps, same_ids, slots,
+    row_copy, column_copy, fetched_copy, forward_copy, arrived, early,
+):
     copies = [
         pltpu.make_async_copy(rows.at[0], row_copy, arrived.at[0]),
         pltpu.make_async_copy(columns.at[0], column_copy, arrived.at[1]),
     ]
     for copy in copies:
         copy.start()
+    for k in range(3):
+        same_ids[k] = ids[k]
     for copy in copies:
         copy.wait()
     row, column = row_copy[...], column_copy[...]
@@ -80,41 +91,69 @@
     length = forward.shape[1]
     used = (index < count[0, 0]) & (((column >> 1) & 1) == ids[0])
     source = jnp.bitwise_xor(column >> 2, ids[2]) * 2 + (column & 1)
-    items, source, target, steps[0], slot = order(row, used, source, index, n_out, length, FORWARD)
-    fetched[...] = jnp.maximum(items, 0)
+    items, source, target, n_steps, slot = order(row, used, source, index, n_out, length, FORWARD)
+    fetched_copy[...] = jnp.maximum(items, 0)
+    first = pltpu.make_async_copy(fetched_copy, fetched, arrived.at[2])
+    first.start()
     here = jnp.where(items >= 0, iota(items.shape, 1), length)
-    forward[...] = here + source * 1024 + target * 65536
+    forward_copy[...] = here + source * 1024 + target * 65536
+    second = pltpu.make_async_copy(forward_copy, forward, arrived.at[3])
+    second.start()
     slots[...] = slot
-
-
-def pick(count, ids, rows, columns, n_out, n_back):
+    steps[0] = n_steps
+    first.wait()
+    n_early = jnp.minimum(n_steps, EARLY)
+    lax.fori_loop(0, n_early, functools.partial(start_fetch, tiles, fetched, held, early), 0)
+    held[held.shape[0] - 1] = jnp.zeros((TILE, TILE), BF16)
+    second.wait()
+    lax.fori_loop(0, n_early, functools.partial(end_fetch, tiles, held, early), 0)
+
+
+def start_fetch(tiles, fetched, held, arrived, g, carry):
+    for j in range(PER):
+        source = tiles.at[fetched[0, g * PER + j]]
+        pltpu.make_async_copy(source, held.at[g * PER + j], arrived.at[g]).start()
+    return carry
+
+
+def end_fetch(tiles, held, arrived, g, carry):
+    block = held.at[pl.ds(g * PER, PER)]
+    pltpu.make_async_copy(tiles.at[pl.ds(0, PER)], block, arrived.at[g]).wait()
+    return carry
+
+
+def pick(count, ids, rows, columns, tiles, n_out, n_back):
     length = rows.shape[-1] + max(n_out * (FORWARD - 1), n_back * (BACKWARD - 1)) + PER
     length = -(-length // TILE) * TILE
-    listed = jax.ShapeDtypeStruct((1, length), jnp.int32)
+    listed = (1, length)
     return pl.pallas_call(
         functools.partial(pick_kernel, n_out),
         out_shape=[
-            listed,
-            listed,
+            pltpu.VMEM((EARLY * PER + 1, TILE, TILE), BF16),
+            pltpu.SMEM(listed, jnp.int32),
+            pltpu.SMEM(listed, jnp.int32),
+            pltpu.SMEM((1,), jnp.int32),
+            pltpu.SMEM((3,), jnp.int32),
             pltpu.VMEM(rows.shape[1:], jnp.int32),
-            jax.ShapeDtypeStruct((1,), jnp.int32),
-        ],
-        in_specs=[SMEM, SMEM, ANY, ANY],
-        out_specs=[VMEM, VMEM, VMEM, SMEM],
+        ],
+        in_specs=[SMEM, SMEM, ANY, ANY, ANY],
+        out_specs=[VMEM, SMEM, SMEM, SMEM, SMEM, VMEM],
         scratch_shapes=[
             pltpu.VMEM(rows.shape[1:], jnp.int32),
             pltpu.VMEM(rows.shape[1:], jnp.int32),
-            pltpu.SemaphoreType.DMA((2,)),
+            pltpu.VMEM(listed, jnp.int32),
+            pltpu.VMEM(listed, jnp.int32),
+            pltpu.SemaphoreType.DMA((4,)),
+            pltpu.SemaphoreType.DMA((EARLY,)),
         ],
         compiler_params=PICK_PARAMS,
         name="pick_tiles",
-    )(count, ids, far(rows), far(columns))
-
-
-def prepare_kernel(
-    n_back, ids, rows, columns, slots, weight, bias, cotangent, *refs
-):
-    backward, steps, weight_copy, bias_copy, cotangent_copy, row_copy, column_copy, arrived = refs
+    )(count, ids, far(rows), far(columns), far(tiles))
+
+
+def prepare_kernel(n_back, ids, rows, columns, slots, weight, bias, cotangent, *refs):
+    backward, steps, weight_copy, bias_copy, cotangent_copy = refs[:5]
+    row_copy, column_copy, backward_copy, arrived = refs[5:]
     pairs = [
         (rows.at[0], row_copy),
         (columns.at[0], column_copy),
@@ -135,33 +174,38 @@
     place = (column >> 2) * 2 + (column & 1)
     source = jnp.bitwise_xor(row >> 2, ids[1]) * 4 + (row & 3)
     used = slot >= 0
-    items, source, target, steps[0], slot = order(
+    items, source, target, n_steps, slot = order(
         place, used, source, slot, n_back, length, BACKWARD
     )
     here = jnp.where(items >= 0, items, length)
-    backward[...] = here + source * 1024 + target * 65536
+    backward_copy[...] = here + source * 1024 + target * 65536
+    copy = pltpu.make_async_copy(backward_copy, backward, arrived.at[5])
+    copy.start()
+    steps[0] = n_steps
+    copy.wait()
 
 
 def prepare(ids, rows, columns, slots, length, n_back, weight, bias, cotangent):
     return pl.pallas_call(
         functools.partial(prepare_kernel, n_back),
         out_shape=[
-            jax.ShapeDtypeStruct((1, length), jnp.int32),
-            jax.ShapeDtypeStruct((1,), jnp.int32),
+            pltpu.SMEM((1, length), jnp.int32),
+            pltpu.SMEM((1,), jnp.int32),
             pltpu.VMEM(weight.shape, weight.dtype),
             pltpu.VMEM(bias.shape, bias.dtype),
             pltpu.VMEM(cotangent.shape, cotangent.dtype),
         ],
         in_specs=[SMEM, ANY, ANY, VMEM, ANY, ANY, ANY],
-        out_specs=[VMEM, SMEM, VMEM, VMEM, VMEM],
+        out_specs=[SMEM, SMEM, VMEM, VMEM, VMEM],
         scratch_shapes=[
             pltpu.VMEM(rows.shape[1:], jnp.int32),
             pltpu.VMEM(rows.shape[1:], jnp.int32),
-            pltpu.SemaphoreType.DMA((5,)),
+            pltpu.VMEM((1, length), jnp.int32),
+            pltpu.SemaphoreType.DMA((6,)),
         ],
         compiler_params=PICK_PARAMS,
         name="prepare",
-    )(ids, far(rows), far(columns), near(slots), far(weight), far(bias), far(cotangent))
+    )(scalar(ids), far(rows), far(columns), near(slots), far(weight), far(bias), far(cotangent))
 
 
 def join_kernel(a, b, out):
@@ -182,13 +226,14 @@
 
 
 def add_products(flipped, g, picked, held, source, total):
+    last = held.shape[0] - 1
     width = BACKWARD if flipped else FORWARD
     places = []
     products = []
     for at in range(0, PER, width):
         codes = [picked[0, g * PER + at + j] for j in range(width)]
         places.append(codes[0] >> 16)
-        mine = [held[code & 1023] for code in codes]
+        mine = [held[jnp.minimum(code & 1023, last)] for code in codes]
         other = [source[(code >> 10) & 63] for code in codes]
         left, right = (other, mine) if flipped else (mine, other)
         products.append(
@@ -200,36 +245,39 @@
         total[place] += product
 
 
-def forward_kernel(steps, ids, fetched, picked, tiles, *refs):
+def forward_kernel(steps, ids, fetched, picked, tiles, early, *refs):
     sources, (held, kept, sent, gathered, total, arrived) = refs[:-6], refs[-6:]
     count = steps[0]
-
-    def start(g, carry):
-        for j in range(PER):
-            source = tiles.at[fetched[0, g * PER + j]]
-            pltpu.make_async_copy(source, held.at[g * PER + j], arrived.at[g]).start()
-        return carry
-
-    lax.fori_loop(0, count, start, 0)
+    start = functools.partial(start_fetch, tiles, fetched, held, arrived)
+    lax.fori_loop(EARLY, jnp.maximum(count, EARLY), start, 0)
+    moved = pltpu.make_async_copy(
+        early.at[pl.ds(0, EARLY * PER)], held.at[pl.ds(0, EARLY * PER)], arrived.at[0]
+    )
+    moved.start()
     held[held.shape[0] - 1] = jnp.zeros((TILE, TILE), BF16)
     total[...] = jnp.zeros_like(total)
     for m, source in enumerate(sources):
         gathered[4 * m : 4 * m + 4] = source[...].reshape(4, TILE, TILE)
 
+    def early_step(g, carry):
+        add_products(False, g, picked, early, gathered, total)
+        return carry
+
     def step(g, carry):
-        block = held.at[pl.ds(g * PER, PER)]
-        pltpu.make_async_copy(tiles.at[pl.ds(0, PER)], block, arrived.at[g]).wait()
+        end_fetch(tiles, held, arrived, g, 0)
         add_products(False, g, picked, held, gathered, total)
         return carry
 
-    lax.fori_loop(0, count, step, 0)
+    lax.fori_loop(0, jnp.minimum(count, EARLY), early_step, 0)
+    lax.fori_loop(EARLY, jnp.maximum(count, EARLY), step, 0)
+    moved.wait()
     for k in range(kept.shape[0]):
         own = jnp.bitwise_xor(ids[1], 2 * k)
         kept[k] = total[pl.ds(own * 4, 4)]
         sent[k] = total[pl.ds(jnp.bitwise_xor(own, 1) * 4, 4)].astype(BF16)
 
 
-def tiles_forward(steps, ids, fetched, picked, tiles, sources, n_out):
+def tiles_forward(steps, ids, fetched, picked, tiles, early, sources, n_out):
     shape = (n_out // 8, 4, TILE, TILE)
     length = fetched.shape[1]
     return pl.pallas_call(
@@ -239,7 +287,7 @@
             pltpu.VMEM(shape, F32),
             pltpu.VMEM(shape, BF16),
         ],
-        in_specs=[SMEM, SMEM, SMEM, SMEM, ANY] + [VMEM] * len(sources),
+        in_specs=[SMEM, SMEM, SMEM, SMEM, ANY, VMEM] + [VMEM] * len(sources),
         out_specs=[VMEM] * 3,
         scratch_shapes=[
             pltpu.VMEM((4 * len(sources), TILE, TILE), BF16),
@@ -249,11 +297,12 @@
         compiler_params=PARAMS,
         name="tiles_forward",
     )(
-        steps,
-        ids,
-        fetched,
-        picked,
+        scalar(steps),
+        scalar(ids),
+        scalar(fetched),
+        scalar(picked),
         far(tiles),
+        near(early),
         *[near(values) for values in sources],
     )
 
@@ -269,10 +318,10 @@
         return carry
 
     lax.fori_loop(0, steps[0], step, 0)
-    across = ids[2] >> 1
-    kept[...] = total[pl.ds(across * 4, 4)]
-    for k, out in enumerate((first, second, third)):
-        out[...] = total[pl.ds(jnp.bitwise_xor(across, k + 1) * 4, 4)].astype(BF16)
+    for k, out in enumerate((kept, first, second, third)):
+        for z in range(2):
+            block = pl.ds(jnp.bitwise_xor(ids[2], 2 * k + z) * 2, 2)
+            out[2 * z : 2 * z + 2] = total[block].astype(out.dtype)
 
 
 def tiles_backward(steps, ids, picked, held, sources, n_back):
@@ -288,7 +337,7 @@
         ],
         compiler_params=PARAMS,
         name="tiles_backward",
-    )(steps, ids, picked, near(held), *[near(values) for values in sources])
+    )(scalar(steps), scalar(ids), scalar(picked), near(held), *[near(values) for values in sources])
 
 
 def pair_kernel(kept, got, first, *others):
@@ -368,81 +417,78 @@
     )(near(own), near(other), near(weight), near(bias), near(cotangent))
 
 
-def message_kernel(back, other, grads, message):
-    blocks = back.shape[0]
+def message_kernel(ids, back, other, grads, more, message):
+    rows = back.shape[0] * TILE
     value = back[...] + other[...].astype(F32)
-    message[0 : blocks * TILE] = value.astype(BF16).reshape(blocks * TILE, TILE)
-    message[blocks * TILE : (blocks + 1) * TILE] = grads[0:TILE].astype(BF16)
-    rest = jnp.concatenate([grads[TILE : TILE + 8]] * 2, 0)
+    message[0:rows] = value.astype(BF16).reshape(rows, TILE)
+    half = pl.ds((ids[1] & 1) * (TILE // 2), TILE // 2)
+    message[rows : rows + TILE // 2] = (grads[half] + more[half]).astype(BF16)
+    rest = grads[TILE : TILE + 8] + more[TILE : TILE + 8]
+    rest = jnp.concatenate([rest, rest], 0)
     line = iota(rest.shape, 0)
     terms = jnp.zeros(rest.shape, F32)
     for k in range(3):
         term = rest.astype(BF16).astype(F32)
         terms = jnp.where(line == k, term, terms)
         rest = rest - term
-    message[(blocks + 1) * TILE : (blocks + 1) * TILE + 16] = terms.astype(BF16)
-
-
-def message(back, other, grads):
-    rows = (back.shape[0] + 1) * TILE + 16
+    message[rows + TILE // 2 : rows + TILE // 2 + 16] = terms.astype(BF16)
+
+
+def message(ids, back, other, grads, more):
+    rows = back.shape[0] * TILE + TILE // 2 + 16
     return pl.pallas_call(
         message_kernel,
         out_shape=pltpu.VMEM((rows, TILE), BF16),
-        in_specs=[VMEM] * 3,
+        in_specs=[SMEM] + [VMEM] * 4,
         out_specs=VMEM,
         compiler_params=PARAMS,
         name="message",
-    )(near(back), near(other), near(grads))
-
-
-def grad_kernel(*refs):
+    )(scalar(ids), near(back), near(other), near(grads), near(more))
+
+
+def grad_kernel(ids, *refs):
     messages, grads = refs[:-1], refs[-1]
     last = messages[0].shape[0] - 16
-    weight = jnp.zeros((TILE, TILE), F32)
+    for k in range(2):
+        weight = jnp.zeros((TILE // 2, TILE), F32)
+        for one in messages[k::2]:
+            weight = weight + one[last - TILE // 2 : last].astype(F32)
+        grads[pl.ds(jnp.bitwise_xor(ids[1] & 1, k) * (TILE // 2), TILE // 2)] = weight
     bias = jnp.zeros((16, TILE), F32)
-    for one in messages:
-        weight = weight + one[last - TILE : last].astype(F32)
+    for one in messages[0::2]:
         bias = bias + one[last : last + 16].astype(F32)
-    grads[0:TILE] = weight
     grads[TILE : TILE + 8] = jnp.broadcast_to(jnp.sum(bias, axis=0, keepdims=True), (8, TILE))
 
 
-def grad_sum(messages):
+def grad_sum(ids, messages):
     return pl.pallas_call(
         grad_kernel,
         out_shape=pltpu.VMEM((TILE + 8, TILE), F32),
-        in_specs=[VMEM] * len(messages),
+        in_specs=[SMEM] + [VMEM] * len(messages),
         out_specs=VMEM,
         compiler_params=PARAMS,
         name="grad_sum",
-    )(*[near(one) for one in messages])
-
-
-def line_kernel(ids, kept, a, b, c, own, own_sent, other_sent):
+    )(scalar(ids), *[near(one) for one in messages])
+
+
+def line_kernel(kept, a, b, c, own, own_sent, other_sent):
     blocks = own.shape[0]
-    side = ids[2] & 1
-
-    def half(z):
-        block = pl.ds(z * blocks, blocks)
-        terms = [values[block].astype(F32) for values in (a, b, c)]
-        return kept[block] + terms[0] + terms[1] + terms[2]
-
-    mine = half(side)
-    own[...] = mine
-    own_sent[...] = mine.astype(BF16)
-    other_sent[...] = half(1 - side).astype(BF16)
-
-
-def line_sum(ids, kept, others):
+    value = kept[...] + a[...].astype(F32) + b[...].astype(F32) + c[...].astype(F32)
+    own[...] = value[:blocks]
+    own_sent[...] = value[:blocks].astype(BF16)
+    other_sent[...] = value[blocks:].astype(BF16)
+
+
+def line_sum(kept, others):
     shape = (kept.shape[0] // 2, TILE, TILE)
     return pl.pallas_call(
         line_kernel,
         out_shape=[pltpu.VMEM(shape, F32), pltpu.VMEM(shape, BF16), pltpu.VMEM(shape, BF16)],
-        in_specs=[SMEM] + [VMEM] * 4,
+        in_specs=[VMEM] * 4,
         out_specs=[VMEM] * 3,
         compiler_params=PARAMS,
         name="line_sum",
-    )(ids, near(kept), *[near(values) for values in others])
+    )(near(kept), *[near(values) for values in others])
 
 
 def finish_kernel(ids, own, beside, opposite, corner, grads, more, features, weight, bias):
@@ -468,7 +514,7 @@
         out_specs=[VMEM] * 3,
         compiler_params=PARAMS,
         name="finish",
-    )(ids, near(own), near(beside), near(opposite), near(corner), near(grads), near(more))
+    )(scalar(ids), near(own), near(beside), near(opposite), near(corner), near(grads), near(more))
 
 
 def local(
@@ -486,11 +532,11 @@
     beside, ids = lax.optimization_barrier((swap(mine, "row", 1), ids))
     pair = join(mine, beside)
     sources = [swap(pair, "row", mask) for mask in range(2, n_row, 2)]
-    lists = pick(tile_count, ids, tile_rows, tile_columns, n_out, n_back)
+    lists = pick(tile_count, ids, tile_rows, tile_columns, tiles, n_out, n_back)
     lists, sources = lax.optimization_barrier((lists, sources))
-    fetched, forward, slots, steps = lists
-
-    held, kept, sent = tiles_forward(steps, ids, fetched, forward, tiles, [pair, *sources], n_out)
+    early, fetched, forward, steps, ids, slots = lists
+
+    held, kept, sent = tiles_forward(steps, ids, fetched, forward, tiles, early, [pair, *sources], n_out)
     first, *others = pair_sum(kept, swap(sent, "col", 1))
     others = [swap(other, "col", 2 * k + 2) for k, other in enumerate(others)]
     own, sent = own_sum(first, others)
@@ -502,13 +548,14 @@
     backward, steps, weight, bias, cotangent = ready
     activations, back, back_sent, grads = middle(own, other, weight, bias, cotangent)
 
-    mine = message(back, swap(back_sent, "feat", 1), grads)
+    back_other, more = lax.optimization_barrier((swap(back_sent, "feat", 1), swap(grads, "col", 1)))
+    mine = message(ids, back, back_other, grads, more)
     across = [swap(mine, "col", mask) for mask in (2, 6, 4)]
     beside = swap(mine, "col", 1)
     across = lax.optimization_barrier(across)
     corners = [swap(values, "col", 1) for values in across]
     sources = [mine, beside, across[0], corners[0], across[2], corners[2], across[1], corners[1]]
-    grads = grad_sum(sources)
+    grads = grad_sum(ids, sources)
     more = swap(grads, "row", 1)
     kept, *others = tiles_backward(steps, ids, backward, held, sources, n_back)
     others, more = lax.optimization_barrier((others, more))
@@ -517,7 +564,8 @@
     others = [swap(other, "row", 2 * k + 2) for k, other in enumerate(others)]
     others, more = lax.optimization_barrier((others, swap(grads, "row", 2)))
     grads = grads + more
-    own, own_sent, other_sent = line_sum(ids, kept, others)
+    own, own_sent, other_sent = line_sum(kept, others)
+    own_sent, other_sent, grads = lax.optimization_barrier((own_sent, other_sent, grads))
     opposite = swap(own_sent, "feat", 1)
     corner = swap(other_sent, ("row", "feat"), 3)
     beside = swap(other_sent, "row", 1)

time: 94.1 us -> 105 us (1.12)
  local copies, waits for them, and re-layouts: 0.9 us -> 17.4 us
  waiting for transfers between devices: 38.3 us -> 32.7 us
  starting transfers between devices: 37.3 us -> 40.2 us
  Pallas kernels: 16.4 us -> 13.6 us
    unnamed x2 -> x6, local copies, waits for them, and re-layouts: 0.9 us -> 17.4 us
    ppermute x26 -> x27, waiting for transfers between devices: 38.3 us -> 32.7 us  [swap(): return lax.ppermute(values, axis, [(i, i ^ mask) for i in range(size)])]
    pallas_call x1, Pallas kernels: 5.39 us -> 2.16 us  [tiles_forward(): pl.pallas_call(forward_kernel, out_shape=[pltpu.VMEM((length + 1, TILE, T...]
    ppermute x26 -> x27, starting transfers between devices: 37.3 us -> 40.2 us  [swap(): return lax.ppermute(values, axis, [(i, i ^ mask) for i in range(size)])]
    pallas_call x2, Pallas kernels: 5.12 us -> 7.93 us  [the longest x1 5.34 us: pick(): pl.pallas_call(functools.partial(pick_kernel, n_out), out_shape=[pltpu.VM...]
    pallas_call x1, Pallas kernels: 2.71 us -> 1.51 us  [tiles_backward(): pl.pallas_call(backward_kernel, out_shape=[pltpu.VMEM(shape, F32)] + [plt...]
  transfers between devices with their start and end apart: 26 -> 27, of which waited for: 20 -> 18; matrix products, arithmetic and copies ran while one was open for 0% -> 0% of each run, Pallas kernels for 9% -> 9%
where the time goes in v2:
time: 105 us
  starting transfers between devices  40.2 us (38%)
  waiting for transfers between devices  32.7 us (31%)
  local copies, waits for them, and re-layouts  17.4 us (17%)
  Pallas kernels  13.6 us (13%)
  between operations  1.43 us (1%)
    ppermute x27, starting transfers between devices, swap(): return lax.ppermute(values, axis, [(i, i ^ mask) for i in range(size)])  40.2 us
    ppermute x27, waiting for transfers between devices, swap(): return lax.ppermute(values, axis, [(i, i ^ mask) for i in range(size)])  32.7 us
    unnamed x6, local copies, waits for them, and re-layouts  17.4 us
    pallas_call x1, Pallas kernels, pick(): pl.pallas_call(functools.partial(pick_kernel, n_out), out_shape=[pltpu.VM...  5.34 us
    pallas_call x1, Pallas kernels, prepare(): pl.pallas_call(functools.partial(prepare_kernel, n_back), out_shape=[pltp...  2.59 us
    pallas_call x1, Pallas kernels, tiles_forward(): pl.pallas_call(forward_kernel, out_shape=[pltpu.VMEM((length + 1, TILE, T...  2.16 us
  transfers between devices with their start and end apart: 27, of which 18 were waited for; matrix products, arithmetic and copies ran while one was open for 0% of the time, Pallas kernels for 9%

profile of v2, /device:TPU:0, one launch (start us, length us, event | category | flops | bytes accessed | tf_op | source)
XLA Modules:
  0.0 105.4 jit_solution(16111389876930274016)
XLA Ops:
  0.6 0.0 copy-start
  0.7 0.9 copy-done
  1.5 2.0 %collective-permute-start = (bf16[256,128]{1,0:T(8,128)(2,1)S(1)}, bf16[256,128]{1,0:T(8,128)(2,1)S(1)}, u32[]{:S(2)}, u32[]{:S(2)}) collective-permute-start(bf16[256,128]{1,0:T(8,128)(2,1)S(1)} %constant_dynamic-slice_fusion.a), channel_id=1, source_target_pairs={{0,16},{16,0},{32,48},{48,32},{64,80},{80,64},{96,112},{112,96},{1... | collective-permute-start | bytes 196616 | tf_op jit(solution)/shard_map/ppermute | solution.py:26
  3.5 0.1 pad_add_fusion.ids
  3.6 2.2 %collective-permute-done.b = bf16[256,128]{1,0:T(8,128)(2,1)S(1)} collective-permute-done((bf16[256,128]{1,0:T(8,128)(2,1)S(1)}, bf16[256,128]{1,0:T(8,128)(2,1)S(1)}, u32[]{:S(2)}, u32[]{:S(2)}) %collective-permute-start) | collective-permute-done | bytes 65568 | tf_op jit(solution)/shard_map/ppermute | solution.py:26
  5.8 3.2 %collective-permute-start.3 = (bf16[512,128]{1,0:T(8,128)(2,1)S(1)}, bf16[512,128]{1,0:T(8,128)(2,1)S(1)}, u32[]{:S(2)}, u32[]{:S(2)}) collective-permute-start(bf16[512,128]{1,0:T(8,128)(2,1)S(1)} %join.1.refs_0_), channel_id=1, source_target_pairs={{0,96},{16,112},{32,64},{48,80},{64,32},{80,48},{96,0},{112,16},{1... | collective-permute-start | bytes 393224 | tf_op jit(solution)/shard_map/ppermute | solution.py:26
  9.0 0.6 collective-permute-start.2
  9.6 0.4 collective-permute-start.1
  10.7 5.3 %pick_tiles.1 = (bf16[129,128,128]{2,1,0:T(8,128)(2,1)S(1)}, s32[1,768]{1,0:T(1,128)S(4)}, s32[1,768]{1,0:T(1,128)S(4)}, s32[1]{0:T(128)S(4)}, s32[3]{0:T(128)S(4)}, /*index=5*/s32[1,640]{1,0:T(1,128)S(1)}) custom-call(s32[1,1]{1,0:T(1,128)S(6)} %copy.12.count, s32[3]{0:T(128)S(1)} %pad_add_fusion.ids, s32[1,1,640]{2,1,0:T(1,128)} %rows.3, ...), custom_call_target="tpu_custom_call" | custom-call | tf_op jit(solution)/shard_map/pick_tiles/pallas_call | solution.py:129
  16.0 0.0 collective-permute-done.3.refs_3_
  16.0 0.0 collective-permute-done.2.refs_2_
  16.0 0.0 collective-permute-done.1.refs_1_
  16.0 2.2 %tiles_forward.1 = (bf16[769,128,128]{2,1,0:T(8,128)(2,1)S(1)}, f32[4,4,128,128]{3,2,1,0:T(8,128)S(1)}, bf16[4,4,128,128]{3,2,1,0:T(8,128)(2,1)S(1)}) custom-call(s32[1]{0:T(128)S(4)} %get-tuple-element.85.steps, s32[3]{0:T(128)S(4)} %get-tuple-element.86.ids, s32[1,768]{1,0:T(1,128)S(4)} %get-tuple-element.87.fetched, ...), custom_call_target="tpu_custom_call" | custom-call | tf_op jit(solution)/shard_map/tiles_forward/pallas_call | solution.py:283
  18.2 8.3 %copy-done.1 = bf16[769,128,128]{2,1,0:T(8,128)(2,1)} copy-done((bf16[769,128,128]{2,1,0:T(8,128)(2,1)}, bf16[769,128,128]{2,1,0:T(8,128)(2,1)S(1)}, u32[]{:S(2)}) %copy-start.1) | copy-done | bytes 25198616
  26.5 0.0 collective-permute-start.4
  26.5 1.9 %collective-permute-done.4.got = bf16[4,4,128,128]{3,2,1,0:T(8,128)(2,1)S(1)} collective-permute-done((bf16[4,4,128,128]{3,2,1,0:T(8,128)(2,1)S(1)}, bf16[4,4,128,128]{3,2,1,0:T(8,128)(2,1)S(1)}, u32[]{:S(2)}, u32[]{:S(2)}) %collective-permute-start.4) | collective-permute-done | bytes 524320 | tf_op jit(solution)/shard_map/ppermute | solution.py:26
  28.4 0.1 pair_sum.1
  28.5 1.5 %collective-permute-start.5 = (bf16[4,128,128]{2,1,0:T(8,128)(2,1)S(1)}, bf16[4,128,128]{2,1,0:T(8,128)(2,1)S(1)}, u32[]{:S(2)}, u32[]{:S(2)}) collective-permute-start(bf16[4,128,128]{2,1,0:T(8,128)(2,1)S(1)} %get-tuple-element.96), channel_id=1, source_target_pairs={{0,4},{2,6},{4,0},{6,2},{8,12},{10,14},{12,8},{14,10},{1,5},{3,7},... | collective-permute-start | bytes 393224 | tf_op jit(solution)/shard_map/ppermute | solution.py:26
  30.0 2.9 %collective-permute-start.6 = (bf16[4,128,128]{2,1,0:T(8,128)(2,1)S(1)}, bf16[4,128,128]{2,1,0:T(8,128)(2,1)S(1)}, u32[]{:S(2)}, u32[]{:S(2)}) collective-permute-start(bf16[4,128,128]{2,1,0:T(8,128)(2,1)S(1)} %get-tuple-element.97), channel_id=1, source_target_pairs={{0,8},{2,10},{4,12},{6,14},{8,0},{10,2},{12,4},{14,6},{1,9},{3,11}... | collective-permute-start | bytes 393224 | tf_op jit(solution)/shard_map/ppermute | solution.py:26
  32.9 0.4 collective-permute-start.7
  33.3 1.1 %collective-permute-done.5.a = bf16[4,128,128]{2,1,0:T(8,128)(2,1)S(1)} collective-permute-done((bf16[4,128,128]{2,1,0:T(8,128)(2,1)S(1)}, bf16[4,128,128]{2,1,0:T(8,128)(2,1)S(1)}, u32[]{:S(2)}, u32[]{:S(2)}) %collective-permute-start.5) | collective-permute-done | bytes 131104 | tf_op jit(solution)/shard_map/ppermute | solution.py:26
  34.4 4.9 %collective-permute-done.6.b = bf16[4,128,128]{2,1,0:T(8,128)(2,1)S(1)} collective-permute-done((bf16[4,128,128]{2,1,0:T(8,128)(2,1)S(1)}, bf16[4,128,128]{2,1,0:T(8,128)(2,1)S(1)}, u32[]{:S(2)}, u32[]{:S(2)}) %collective-permute-start.6) | collective-permute-done | bytes 131104 | tf_op jit(solution)/shard_map/ppermute | solution.py:26
  39.3 2.2 %collective-permute-done.7.c = bf16[4,128,128]{2,1,0:T(8,128)(2,1)S(1)} collective-permute-done((bf16[4,128,128]{2,1,0:T(8,128)(2,1)S(1)}, bf16[4,128,128]{2,1,0:T(8,128)(2,1)S(1)}, u32[]{:S(2)}, u32[]{:S(2)}) %collective-permute-start.7) | collective-permute-done | bytes 131104 | tf_op jit(solution)/shard_map/ppermute | solution.py:26
  41.5 0.1 own_sum.1
  41.6 4.1 %collective-permute-start.8 = (bf16[4,128,128]{2,1,0:T(8,128)(2,1)S(1)}, bf16[4,128,128]{2,1,0:T(8,128)(2,1)S(1)}, u32[]{:S(2)}, u32[]{:S(2)}) collective-permute-start(bf16[4,128,128]{2,1,0:T(8,128)(2,1)S(1)} %get-tuple-element.102), channel_id=1, source_target_pairs={{0,1},{1,0},{2,3},{3,2},{4,5},{5,4},{6,7},{7,6},{8,9},{9,8},{10,11... | collective-permute-start | bytes 393224 | tf_op jit(solution)/shard_map/ppermute | solution.py:26
  45.7 2.6 %prepare.1 = (s32[1,768]{1,0:T(1,128)S(4)}, s32[1]{0:T(128)S(4)}, bf16[128,128]{1,0:T(8,128)(2,1)S(1)}, f32[1,128]{1,0:T(1,128)S(1)}, bf16[512,128]{1,0:T(8,128)(2,1)S(1)}) custom-call(s32[3]{0:T(128)S(4)} %get-tuple-element.86.ids, s32[1,1,640]{2,1,0:T(1,128)} %rows.3, s32[1,1,640]{2,1,0:T(1,128)} %columns.3, s32[1,640]{1,0:T(1,128)S(1)} %get-tuple-element.103.slots, ...), custom_call_target="tpu_custom_call" | custom-call | tf_op jit(solution)/shard_map/prepare/pallas_call | solution.py:189
  48.3 0.6 collective-permute-done.8.other
  48.8 0.9 middle.1
  49.7 3.3 %collective-permute-start.9 = (bf16[4,128,128]{2,1,0:T(8,128)(2,1)S(1)}, bf16[4,128,128]{2,1,0:T(8,128)(2,1)S(1)}, u32[]{:S(2)}, u32[]{:S(2)}) collective-permute-start(bf16[4,128,128]{2,1,0:T(8,128)(2,1)S(1)} %get-tuple-element.118), channel_id=1, source_target_pairs={{0,1},{1,0},{2,3},{3,2},{4,5},{5,4},{6,7},{7,6},{8,9},{9,8},{10,11... | collective-permute-start | bytes 393224 | tf_op jit(solution)/shard_map/ppermute | solution.py:26
  53.1 0.0 collective-permute-start.10
  53.1 1.3 %collective-permute-done.10.more = f32[136,128]{1,0:T(8,128)S(1)} collective-permute-done((f32[136,128]{1,0:T(8,128)S(1)}, f32[136,128]{1,0:T(8,128)S(1)}, u32[]{:S(2)}, u32[]{:S(2)}) %collective-permute-start.10) | collective-permute-done | bytes 69664 | tf_op jit(solution)/shard_map/ppermute | solution.py:26
  54.3 1.9 %collective-permute-done.9.other = bf16[4,128,128]{2,1,0:T(8,128)(2,1)S(1)} collective-permute-done((bf16[4,128,128]{2,1,0:T(8,128)(2,1)S(1)}, bf16[4,128,128]{2,1,0:T(8,128)(2,1)S(1)}, u32[]{:S(2)}, u32[]{:S(2)}) %collective-permute-start.9) | collective-permute-done | bytes 131104 | tf_op jit(solution)/shard_map/ppermute | solution.py:26
  56.3 0.1 collective-permute-start.14
  56.4 1.6 %collective-permute-start.13 = (bf16[592,128]{1,0:T(8,128)(2,1)S(1)}, bf16[592,128]{1,0:T(8,128)(2,1)S(1)}, u32[]{:S(2)}, u32[]{:S(2)}) collective-permute-start(bf16[592,128]{1,0:T(8,128)(2,1)S(1)} %message.1.refs_0_), channel_id=1, source_target_pairs={{0,12},{2,14},{4,8},{6,10},{8,4},{10,6},{12,0},{14,2},{1,13},{3,15... | collective-permute-start | bytes 454664 | tf_op jit(solution)/shard_map/ppermute | solution.py:26
  57.9 1.9 %collective-permute-start.12 = (bf16[592,128]{1,0:T(8,128)(2,1)S(1)}, bf16[592,128]{1,0:T(8,128)(2,1)S(1)}, u32[]{:S(2)}, u32[]{:S(2)}) collective-permute-start(bf16[592,128]{1,0:T(8,128)(2,1)S(1)} %message.1.refs_0_), channel_id=1, source_target_pairs={{0,4},{2,6},{4,0},{6,2},{8,12},{10,14},{12,8},{14,10},{1,5},{3,7},... | collective-permute-start | bytes 454664 | tf_op jit(solution)/shard_map/ppermute | solution.py:26
  59.8 0.0 collective-permute-start.11
  59.8 3.8 %collective-permute-done.14.refs_4_ = bf16[592,128]{1,0:T(8,128)(2,1)S(1)} collective-permute-done((bf16[592,128]{1,0:T(8,128)(2,1)S(1)}, bf16[592,128]{1,0:T(8,128)(2,1)S(1)}, u32[]{:S(2)}, u32[]{:S(2)}) %collective-permute-start.14) | collective-permute-done | bytes 151584 | tf_op jit(solution)/shard_map/ppermute | solution.py:26
  63.7 1.3 %collective-permute-done.13.refs_6_ = bf16[592,128]{1,0:T(8,128)(2,1)S(1)} collective-permute-done((bf16[592,128]{1,0:T(8,128)(2,1)S(1)}, bf16[592,128]{1,0:T(8,128)(2,1)S(1)}, u32[]{:S(2)}, u32[]{:S(2)}) %collective-permute-start.13) | collective-permute-done | bytes 151584 | tf_op jit(solution)/shard_map/ppermute | solution.py:26
  65.0 0.5 collective-permute-start.16
  65.5 0.0 collective-permute-start.17
  65.5 0.0 collective-permute-done.11.refs_1_
  65.5 0.9 collective-permute-done.15.refs_3_
  66.4 0.2 collective-permute-done.16.refs_5_
  66.6 0.3 collective-permute-done.17.refs_7_
  66.9 2.9 %collective-permute-start.18 = (f32[136,128]{1,0:T(8,128)S(1)}, f32[136,128]{1,0:T(8,128)S(1)}, u32[]{:S(2)}, u32[]{:S(2)}) collective-permute-start(f32[136,128]{1,0:T(8,128)S(1)} %grad_sum.1), channel_id=1, source_target_pairs={{0,16},{16,0},{32,48},{48,32},{64,80},{80,64},{96,112},{112,96},{1... | collective-permute-start | bytes 208904 | tf_op jit(solution)/shard_map/ppermute | solution.py:26
  69.8 8.2 %copy-done.2 = bf16[769,128,128]{2,1,0:T(8,128)(2,1)S(1)} copy-done((bf16[769,128,128]{2,1,0:T(8,128)(2,1)S(1)}, bf16[769,128,128]{2,1,0:T(8,128)(2,1)}, u32[]{:S(2)}) %copy-start.2) | copy-done | bytes 25198616
  77.9 1.5 %tiles_backward.1 = (f32[4,128,128]{2,1,0:T(8,128)S(1)}, bf16[4,128,128]{2,1,0:T(8,128)(2,1)S(1)}, bf16[4,128,128]{2,1,0:T(8,128)(2,1)S(1)}, bf16[4,128,128]{2,1,0:T(8,128)(2,1)S(1)}) custom-call(s32[1]{0:T(128)S(4)} %get-tuple-element.114.steps, s32[3]{0:T(128)S(4)} %get-tuple-element.86.ids, s32[1,768]{1,0:T(1,128)S(4)} %get-tuple-element.115.picked, ...), custom_call_target="tpu_custom_call" | custom-call | tf_op jit(solution)/shard_map/tiles_backward/pallas_call | solution.py:329
  79.5 0.0 collective-permute-done.18
  79.5 0.5 collective-permute-start.19
  80.0 5.9 %collective-permute-start.20 = (bf16[4,128,128]{2,1,0:T(8,128)(2,1)S(1)}, bf16[4,128,128]{2,1,0:T(8,128)(2,1)S(1)}, u32[]{:S(2)}, u32[]{:S(2)}) collective-permute-start(bf16[4,128,128]{2,1,0:T(8,128)(2,1)S(1)} %get-tuple-element.130), channel_id=1, source_target_pairs={{0,64},{16,80},{32,96},{48,112},{64,0},{80,16},{96,32},{112,48},{1... | collective-permute-start | bytes 393224 | tf_op jit(solution)/shard_map/ppermute | solution.py:26
  85.8 0.1 collective-permute-start.21
  86.0 0.9 collective-permute-start.22
  86.9 4.4 %collective-permute-done.22 = f32[136,128]{1,0:T(8,128)S(1)} collective-permute-done((f32[136,128]{1,0:T(8,128)S(1)}, f32[136,128]{1,0:T(8,128)S(1)}, u32[]{:S(2)}, u32[]{:S(2)}) %collective-permute-start.22) | collective-permute-done | bytes 69664 | tf_op jit(solution)/shard_map/ppermute | solution.py:26
  91.3 1.6 %collective-permute-done.21.c = bf16[4,128,128]{2,1,0:T(8,128)(2,1)S(1)} collective-permute-done((bf16[4,128,128]{2,1,0:T(8,128)(2,1)S(1)}, bf16[4,128,128]{2,1,0:T(8,128)(2,1)S(1)}, u32[]{:S(2)}, u32[]{:S(2)}) %collective-permute-start.21) | collective-permute-done | bytes 131104 | tf_op jit(solution)/shard_map/ppermute | solution.py:26
  92.9 0.1 line_sum.1
  93.0 2.6 %collective-permute-start.26 = (f32[136,128]{1,0:T(8,128)S(1)}, f32[136,128]{1,0:T(8,128)S(1)}, u32[]{:S(2)}, u32[]{:S(2)}) collective-permute-start(f32[136,128]{1,0:T(8,128)S(1)} %add.11.grads), channel_id=1, source_target_pairs={{0,64},{16,80},{32,96},{48,112},{64,0},{80,16},{96,32},{112,48},{1... | collective-permute-start | bytes 208904 | tf_op jit(solution)/shard_map/ppermute | solution.py:26
  95.6 3.0 %collective-permute-start.23 = (bf16[2,128,128]{2,1,0:T(8,128)(2,1)S(1)}, bf16[2,128,128]{2,1,0:T(8,128)(2,1)S(1)}, u32[]{:S(2)}, u32[]{:S(2)}) collective-permute-start(bf16[2,128,128]{2,1,0:T(8,128)(2,1)S(1)} %get-tuple-element.140), channel_id=1, source_target_pairs={{0,1},{1,0},{2,3},{3,2},{4,5},{5,4},{6,7},{7,6},{8,9},{9,8},{10,11... | collective-permute-start | bytes 196616 | tf_op jit(solution)/shard_map/ppermute | solution.py:26
  98.5 0.5 collective-permute-start.25
  99.1 1.4 %collective-permute-start.24 = (bf16[2,128,128]{2,1,0:T(8,128)(2,1)S(1)}, bf16[2,128,128]{2,1,0:T(8,128)(2,1)S(1)}, u32[]{:S(2)}, u32[]{:S(2)}) collective-permute-start(bf16[2,128,128]{2,1,0:T(8,128)(2,1)S(1)} %get-tuple-element.141), channel_id=1, source_target_pairs={{0,17},{1,16},{16,1},{17,0},{32,49},{33,48},{48,33},{49,32},{64,81... | collective-permute-start | bytes 196616 | tf_op jit(solution)/shard_map/ppermute | solution.py:26
  100.4 1.6 %collective-permute-done.23.opposite = bf16[2,128,128]{2,1,0:T(8,128)(2,1)S(1)} collective-permute-done((bf16[2,128,128]{2,1,0:T(8,128)(2,1)S(1)}, bf16[2,128,128]{2,1,0:T(8,128)(2,1)S(1)}, u32[]{:S(2)}, u32[]{:S(2)}) %collective-permute-start.23) | collective-permute-done | bytes 65568 | tf_op jit(solution)/shard_map/ppermute | solution.py:26
  102.0 0.8 collective-permute-done.25.beside
  102.8 1.8 %collective-permute-done.24.corner = bf16[2,128,128]{2,1,0:T(8,128)(2,1)S(1)} collective-permute-done((bf16[2,128,128]{2,1,0:T(8,128)(2,1)S(1)}, bf16[2,128,128]{2,1,0:T(8,128)(2,1)S(1)}, u32[]{:S(2)}, u32[]{:S(2)}) %collective-permute-start.24) | collective-permute-done | bytes 65568 | tf_op jit(solution)/shard_map/ppermute | solution.py:26
  104.5 0.0 collective-permute-done.26.more
  104.6 0.8 finish.1
  (12 shorter events, 0.1 us)
Async XLA Ops:
  0.6 0.9 copy-start
  1.5 4.3 %collective-permute-start = (bf16[256,128]{1,0:T(8,128)(2,1)S(1)}, bf16[256,128]{1,0:T(8,128)(2,1)S(1)}, u32[]{:S(2)}, u32[]{:S(2)}) collective-permute-start(bf16[256,128]{1,0:T(8,128)(2,1)S(1)} %constant_dynamic-slice_fusion.a), channel_id=1, source_target_pairs={{0,16},{16,0},{32,48},{48,32},{64,80},{80,64},{96,112},{112,96},{1... | collective-permute-start | bytes 196616 | tf_op jit(solution)/shard_map/ppermute | solution.py:26
  5.8 10.2 %collective-permute-start.3 = (bf16[512,128]{1,0:T(8,128)(2,1)S(1)}, bf16[512,128]{1,0:T(8,128)(2,1)S(1)}, u32[]{:S(2)}, u32[]{:S(2)}) collective-permute-start(bf16[512,128]{1,0:T(8,128)(2,1)S(1)} %join.1.refs_0_), channel_id=1, source_target_pairs={{0,96},{16,112},{32,64},{48,80},{64,32},{80,48},{96,0},{112,16},{1... | collective-permute-start | bytes 393224 | tf_op jit(solution)/shard_map/ppermute | solution.py:26
  9.0 7.0 %collective-permute-start.2 = (bf16[512,128]{1,0:T(8,128)(2,1)S(1)}, bf16[512,128]{1,0:T(8,128)(2,1)S(1)}, u32[]{:S(2)}, u32[]{:S(2)}) collective-permute-start(bf16[512,128]{1,0:T(8,128)(2,1)S(1)} %join.1.refs_0_), channel_id=1, source_target_pairs={{0,64},{16,80},{32,96},{48,112},{64,0},{80,16},{96,32},{112,48},{1... | collective-permute-start | bytes 393224 | tf_op jit(solution)/shard_map/ppermute | solution.py:26
  9.6 6.4 %collective-permute-start.1 = (bf16[512,128]{1,0:T(8,128)(2,1)S(1)}, bf16[512,128]{1,0:T(8,128)(2,1)S(1)}, u32[]{:S(2)}, u32[]{:S(2)}) collective-permute-start(bf16[512,128]{1,0:T(8,128)(2,1)S(1)} %join.1.refs_0_), channel_id=1, source_target_pairs={{0,32},{16,48},{32,0},{48,16},{64,96},{80,112},{96,64},{112,80},{1... | collective-permute-start | bytes 393224 | tf_op jit(solution)/shard_map/ppermute | solution.py:26
  18.2 8.3 %copy-start.1 = (bf16[769,128,128]{2,1,0:T(8,128)(2,1)}, bf16[769,128,128]{2,1,0:T(8,128)(2,1)S(1)}, u32[]{:S(2)}) copy-start(bf16[769,128,128]{2,1,0:T(8,128)(2,1)S(1)} %get-tuple-element.116.held) | copy-start | bytes 75595776
  26.5 1.9 %collective-permute-start.4 = (bf16[4,4,128,128]{3,2,1,0:T(8,128)(2,1)S(1)}, bf16[4,4,128,128]{3,2,1,0:T(8,128)(2,1)S(1)}, u32[]{:S(2)}, u32[]{:S(2)}) collective-permute-start(bf16[4,4,128,128]{3,2,1,0:T(8,128)(2,1)S(1)} %get-tuple-element.94), channel_id=1, source_target_pairs={{0,2},{2,0},{4,6},{6,4},{8,10},{10,8},{12,14},{14,12},{1,3},{3,1},... | collective-permute-start | bytes 1572872 | tf_op jit(solution)/shard_map/ppermute | solution.py:26
  28.5 5.9 %collective-permute-start.5 = (bf16[4,128,128]{2,1,0:T(8,128)(2,1)S(1)}, bf16[4,128,128]{2,1,0:T(8,128)(2,1)S(1)}, u32[]{:S(2)}, u32[]{:S(2)}) collective-permute-start(bf16[4,128,128]{2,1,0:T(8,128)(2,1)S(1)} %get-tuple-element.96), channel_id=1, source_target_pairs={{0,4},{2,6},{4,0},{6,2},{8,12},{10,14},{12,8},{14,10},{1,5},{3,7},... | collective-permute-start | bytes 393224 | tf_op jit(solution)/shard_map/ppermute | solution.py:26
  30.0 9.3 %collective-permute-start.6 = (bf16[4,128,128]{2,1,0:T(8,128)(2,1)S(1)}, bf16[4,128,128]{2,1,0:T(8,128)(2,1)S(1)}, u32[]{:S(2)}, u32[]{:S(2)}) collective-permute-start(bf16[4,128,128]{2,1,0:T(8,128)(2,1)S(1)} %get-tuple-element.97), channel_id=1, source_target_pairs={{0,8},{2,10},{4,12},{6,14},{8,0},{10,2},{12,4},{14,6},{1,9},{3,11}... | collective-permute-start | bytes 393224 | tf_op jit(solution)/shard_map/ppermute | solution.py:26
  32.9 8.7 %collective-permute-start.7 = (bf16[4,128,128]{2,1,0:T(8,128)(2,1)S(1)}, bf16[4,128,128]{2,1,0:T(8,128)(2,1)S(1)}, u32[]{:S(2)}, u32[]{:S(2)}) collective-permute-start(bf16[4,128,128]{2,1,0:T(8,128)(2,1)S(1)} %get-tuple-element.98), channel_id=1, source_target_pairs={{0,12},{2,14},{4,8},{6,10},{8,4},{10,6},{12,0},{14,2},{1,13},{3,15... | collective-permute-start | bytes 393224 | tf_op jit(solution)/shard_map/ppermute | solution.py:26
  41.6 7.2 %collective-permute-start.8 = (bf16[4,128,128]{2,1,0:T(8,128)(2,1)S(1)}, bf16[4,128,128]{2,1,0:T(8,128)(2,1)S(1)}, u32[]{:S(2)}, u32[]{:S(2)}) collective-permute-start(bf16[4,128,128]{2,1,0:T(8,128)(2,1)S(1)} %get-tuple-element.102), channel_id=1, source_target_pairs={{0,1},{1,0},{2,3},{3,2},{4,5},{5,4},{6,7},{7,6},{8,9},{9,8},{10,11... | collective-permute-start | bytes 393224 | tf_op jit(solution)/shard_map/ppermute | solution.py:26
  49.7 6.5 %collective-permute-start.9 = (bf16[4,128,128]{2,1,0:T(8,128)(2,1)S(1)}, bf16[4,128,128]{2,1,0:T(8,128)(2,1)S(1)}, u32[]{:S(2)}, u32[]{:S(2)}) collective-permute-start(bf16[4,128,128]{2,1,0:T(8,128)(2,1)S(1)} %get-tuple-element.118), channel_id=1, source_target_pairs={{0,1},{1,0},{2,3},{3,2},{4,5},{5,4},{6,7},{7,6},{8,9},{9,8},{10,11... | collective-permute-start | bytes 393224 | tf_op jit(solution)/shard_map/ppermute | solution.py:26
  53.1 1.3 %collective-permute-start.10 = (f32[136,128]{1,0:T(8,128)S(1)}, f32[136,128]{1,0:T(8,128)S(1)}, u32[]{:S(2)}, u32[]{:S(2)}) collective-permute-start(f32[136,128]{1,0:T(8,128)S(1)} %get-tuple-element.119.grads), channel_id=1, source_target_pairs={{0,2},{2,0},{4,6},{6,4},{8,10},{10,8},{12,14},{14,12},{1,3},{3,1},... | collective-permute-start | bytes 208904 | tf_op jit(solution)/shard_map/ppermute | solution.py:26
  56.3 7.4 %collective-permute-start.14 = (bf16[592,128]{1,0:T(8,128)(2,1)S(1)}, bf16[592,128]{1,0:T(8,128)(2,1)S(1)}, u32[]{:S(2)}, u32[]{:S(2)}) collective-permute-start(bf16[592,128]{1,0:T(8,128)(2,1)S(1)} %message.1.refs_0_), channel_id=1, source_target_pairs={{0,8},{2,10},{4,12},{6,14},{8,0},{10,2},{12,4},{14,6},{1,9},{3,11}... | collective-permute-start | bytes 454664 | tf_op jit(solution)/shard_map/ppermute | solution.py:26
  56.4 8.6 %collective-permute-start.13 = (bf16[592,128]{1,0:T(8,128)(2,1)S(1)}, bf16[592,128]{1,0:T(8,128)(2,1)S(1)}, u32[]{:S(2)}, u32[]{:S(2)}) collective-permute-start(bf16[592,128]{1,0:T(8,128)(2,1)S(1)} %message.1.refs_0_), channel_id=1, source_target_pairs={{0,12},{2,14},{4,8},{6,10},{8,4},{10,6},{12,0},{14,2},{1,13},{3,15... | collective-permute-start | bytes 454664 | tf_op jit(solution)/shard_map/ppermute | solution.py:26
  57.9 7.1 %collective-permute-start.12 = (bf16[592,128]{1,0:T(8,128)(2,1)S(1)}, bf16[592,128]{1,0:T(8,128)(2,1)S(1)}, u32[]{:S(2)}, u32[]{:S(2)}) collective-permute-start(bf16[592,128]{1,0:T(8,128)(2,1)S(1)} %message.1.refs_0_), channel_id=1, source_target_pairs={{0,4},{2,6},{4,0},{6,2},{8,12},{10,14},{12,8},{14,10},{1,5},{3,7},... | collective-permute-start | bytes 454664 | tf_op jit(solution)/shard_map/ppermute | solution.py:26
  59.8 5.7 %collective-permute-start.11 = (bf16[592,128]{1,0:T(8,128)(2,1)S(1)}, bf16[592,128]{1,0:T(8,128)(2,1)S(1)}, u32[]{:S(2)}, u32[]{:S(2)}) collective-permute-start(bf16[592,128]{1,0:T(8,128)(2,1)S(1)} %message.1.refs_0_), channel_id=1, source_target_pairs={{0,2},{2,0},{4,6},{6,4},{8,10},{10,8},{12,14},{14,12},{1,3},{3,1},... | collective-permute-start | bytes 454664 | tf_op jit(solution)/shard_map/ppermute | solution.py:26
  65.0 1.4 %collective-permute-start.15 = (bf16[592,128]{1,0:T(8,128)(2,1)S(1)}, bf16[592,128]{1,0:T(8,128)(2,1)S(1)}, u32[]{:S(2)}, u32[]{:S(2)}) collective-permute-start(bf16[592,128]{1,0:T(8,128)(2,1)S(1)} %collective-permute-done.12.refs_2_), channel_id=1, source_target_pairs={{0,2},{2,0},{4,6},{6,4},{8,10},{10,8},{12,14},{14,12},{1,3},{3,1},... | collective-permute-start | bytes 454664 | tf_op jit(solution)/shard_map/ppermute | solution.py:26
  65.0 1.6 %collective-permute-start.16 = (bf16[592,128]{1,0:T(8,128)(2,1)S(1)}, bf16[592,128]{1,0:T(8,128)(2,1)S(1)}, u32[]{:S(2)}, u32[]{:S(2)}) collective-permute-start(bf16[592,128]{1,0:T(8,128)(2,1)S(1)} %collective-permute-done.14.refs_4_), channel_id=1, source_target_pairs={{0,2},{2,0},{4,6},{6,4},{8,10},{10,8},{12,14},{14,12},{1,3},{3,1},... | collective-permute-start | bytes 454664 | tf_op jit(solution)/shard_map/ppermute | solution.py:26
  65.5 1.4 %collective-permute-start.17 = (bf16[592,128]{1,0:T(8,128)(2,1)S(1)}, bf16[592,128]{1,0:T(8,128)(2,1)S(1)}, u32[]{:S(2)}, u32[]{:S(2)}) collective-permute-start(bf16[592,128]{1,0:T(8,128)(2,1)S(1)} %collective-permute-done.13.refs_6_), channel_id=1, source_target_pairs={{0,2},{2,0},{4,6},{6,4},{8,10},{10,8},{12,14},{14,12},{1,3},{3,1},... | collective-permute-start | bytes 454664 | tf_op jit(solution)/shard_map/ppermute | solution.py:26
  66.9 12.5 %collective-permute-start.18 = (f32[136,128]{1,0:T(8,128)S(1)}, f32[136,128]{1,0:T(8,128)S(1)}, u32[]{:S(2)}, u32[]{:S(2)}) collective-permute-start(f32[136,128]{1,0:T(8,128)S(1)} %grad_sum.1), channel_id=1, source_target_pairs={{0,16},{16,0},{32,48},{48,32},{64,80},{80,64},{96,112},{112,96},{1... | collective-permute-start | bytes 208904 | tf_op jit(solution)/shard_map/ppermute | solution.py:26
  69.8 8.2 %copy-start.2 = (bf16[769,128,128]{2,1,0:T(8,128)(2,1)S(1)}, bf16[769,128,128]{2,1,0:T(8,128)(2,1)}, u32[]{:S(2)}) copy-start(bf16[769,128,128]{2,1,0:T(8,128)(2,1)} %copy-done.1) | copy-start | bytes 75595776
  79.5 11.8 %collective-permute-start.19 = (bf16[4,128,128]{2,1,0:T(8,128)(2,1)S(1)}, bf16[4,128,128]{2,1,0:T(8,128)(2,1)S(1)}, u32[]{:S(2)}, u32[]{:S(2)}) collective-permute-start(bf16[4,128,128]{2,1,0:T(8,128)(2,1)S(1)} %get-tuple-element.129), channel_id=1, source_target_pairs={{0,32},{16,48},{32,0},{48,16},{64,96},{80,112},{96,64},{112,80},{1... | collective-permute-start | bytes 393224 | tf_op jit(solution)/shard_map/ppermute | solution.py:26
  80.0 11.3 %collective-permute-start.20 = (bf16[4,128,128]{2,1,0:T(8,128)(2,1)S(1)}, bf16[4,128,128]{2,1,0:T(8,128)(2,1)S(1)}, u32[]{:S(2)}, u32[]{:S(2)}) collective-permute-start(bf16[4,128,128]{2,1,0:T(8,128)(2,1)S(1)} %get-tuple-element.130), channel_id=1, source_target_pairs={{0,64},{16,80},{32,96},{48,112},{64,0},{80,16},{96,32},{112,48},{1... | collective-permute-start | bytes 393224 | tf_op jit(solution)/shard_map/ppermute | solution.py:26
  85.8 7.1 %collective-permute-start.21 = (bf16[4,128,128]{2,1,0:T(8,128)(2,1)S(1)}, bf16[4,128,128]{2,1,0:T(8,128)(2,1)S(1)}, u32[]{:S(2)}, u32[]{:S(2)}) collective-permute-start(bf16[4,128,128]{2,1,0:T(8,128)(2,1)S(1)} %get-tuple-element.131), channel_id=1, source_target_pairs={{0,96},{16,112},{32,64},{48,80},{64,32},{80,48},{96,0},{112,16},{1... | collective-permute-start | bytes 393224 | tf_op jit(solution)/shard_map/ppermute | solution.py:26
  86.0 5.3 %collective-permute-start.22 = (f32[136,128]{1,0:T(8,128)S(1)}, f32[136,128]{1,0:T(8,128)S(1)}, u32[]{:S(2)}, u32[]{:S(2)}) collective-permute-start(f32[136,128]{1,0:T(8,128)S(1)} %add.10), channel_id=1, source_target_pairs={{0,32},{16,48},{32,0},{48,16},{64,96},{80,112},{96,64},{112,80},{1... | collective-permute-start | bytes 208904 | tf_op jit(solution)/shard_map/ppermute | solution.py:26
  93.0 11.6 %collective-permute-start.26 = (f32[136,128]{1,0:T(8,128)S(1)}, f32[136,128]{1,0:T(8,128)S(1)}, u32[]{:S(2)}, u32[]{:S(2)}) collective-permute-start(f32[136,128]{1,0:T(8,128)S(1)} %add.11.grads), channel_id=1, source_target_pairs={{0,64},{16,80},{32,96},{48,112},{64,0},{80,16},{96,32},{112,48},{1... | collective-permute-start | bytes 208904 | tf_op jit(solution)/shard_map/ppermute | solution.py:26
  95.6 6.4 %collective-permute-start.23 = (bf16[2,128,128]{2,1,0:T(8,128)(2,1)S(1)}, bf16[2,128,128]{2,1,0:T(8,128)(2,1)S(1)}, u32[]{:S(2)}, u32[]{:S(2)}) collective-permute-start(bf16[2,128,128]{2,1,0:T(8,128)(2,1)S(1)} %get-tuple-element.140), channel_id=1, source_target_pairs={{0,1},{1,0},{2,3},{3,2},{4,5},{5,4},{6,7},{7,6},{8,9},{9,8},{10,11... | collective-permute-start | bytes 196616 | tf_op jit(solution)/shard_map/ppermute | solution.py:26
  98.5 4.3 %collective-permute-start.25 = (bf16[2,128,128]{2,1,0:T(8,128)(2,1)S(1)}, bf16[2,128,128]{2,1,0:T(8,128)(2,1)S(1)}, u32[]{:S(2)}, u32[]{:S(2)}) collective-permute-start(bf16[2,128,128]{2,1,0:T(8,128)(2,1)S(1)} %get-tuple-element.141), channel_id=1, source_target_pairs={{0,16},{16,0},{32,48},{48,32},{64,80},{80,64},{96,112},{112,96},{1... | collective-permute-start | bytes 196616 | tf_op jit(solution)/shard_map/ppermute | solution.py:26
  99.1 5.5 %collective-permute-start.24 = (bf16[2,128,128]{2,1,0:T(8,128)(2,1)S(1)}, bf16[2,128,128]{2,1,0:T(8,128)(2,1)S(1)}, u32[]{:S(2)}, u32[]{:S(2)}) collective-permute-start(bf16[2,128,128]{2,1,0:T(8,128)(2,1)S(1)} %get-tuple-element.141), channel_id=1, source_target_pairs={{0,17},{1,16},{16,1},{17,0},{32,49},{33,48},{48,33},{49,32},{64,81... | collective-permute-start | bytes 196616 | tf_op jit(solution)/shard_map/ppermute | solution.py:26

commit v3 on v2

--- a/solution.py
+++ b/solution.py
@@ -13,6 +13,7 @@
 PER = 32
 FORWARD = 2
 BACKWARD = 4
+SPARE = 1023
 EARLY = 4
 VMEM = pl.BlockSpec(memory_space=pltpu.VMEM)
 SMEM = pl.BlockSpec(memory_space=pltpu.SMEM)
@@ -71,11 +72,9 @@
     return items, found[2:3], target, steps, slot
 
 
-def pick_kernel(
-    n_out, count, ids, rows, columns, tiles,
-    held, fetched, forward, steps, same_ids, slots,
-    row_copy, column_copy, fetched_copy, forward_copy, arrived, early,
-):
+def pick_kernel(n_out, count, ids, rows, columns, *refs):
+    fetched, forward, steps, same_ids, slots = refs[:5]
+    row_copy, column_copy, fetched_copy, forward_copy, arrived = refs[5:]
     copies = [
         pltpu.make_async_copy(rows.at[0], row_copy, arrived.at[0]),
         pltpu.make_async_copy(columns.at[0], column_copy, arrived.at[1]),
@@ -93,20 +92,45 @@
     source = jnp.bitwise_xor(column >> 2, ids[2]) * 2 + (column & 1)
     items, source, target, n_steps, slot = order(row, used, source, index, n_out, length, FORWARD)
     fetched_copy[...] = jnp.maximum(items, 0)
-    first = pltpu.make_async_copy(fetched_copy, fetched, arrived.at[2])
-    first.start()
-    here = jnp.where(items >= 0, iota(items.shape, 1), length)
+    here = jnp.where(items >= 0, iota(items.shape, 1), SPARE)
     forward_copy[...] = here + source * 1024 + target * 65536
-    second = pltpu.make_async_copy(forward_copy, forward, arrived.at[3])
-    second.start()
+    copies = [
+        pltpu.make_async_copy(fetched_copy, fetched, arrived.at[0]),
+        pltpu.make_async_copy(forward_copy, forward, arrived.at[1]),
+    ]
+    for copy in copies:
+        copy.start()
     slots[...] = slot
     steps[0] = n_steps
-    first.wait()
-    n_early = jnp.minimum(n_steps, EARLY)
-    lax.fori_loop(0, n_early, functools.partial(start_fetch, tiles, fetched, held, early), 0)
-    held[held.shape[0] - 1] = jnp.zeros((TILE, TILE), BF16)
-    second.wait()
-    lax.fori_loop(0, n_early, functools.partial(end_fetch, tiles, held, early), 0)
+    for copy in copies:
+        copy.wait()
+
+
+def pick(count, ids, rows, columns, n_out, n_back):
+    length = rows.shape[-1] + max(n_out * (FORWARD - 1), n_back * (BACKWARD - 1)) + PER
+    length = -(-length // TILE) * TILE
+    listed = (1, length)
+    return pl.pallas_call(
+        functools.partial(pick_kernel, n_out),
+        out_shape=[
+            pltpu.SMEM(listed, jnp.int32),
+            pltpu.SMEM(listed, jnp.int32),
+            pltpu.SMEM((1,), jnp.int32),
+            pltpu.SMEM((3,), jnp.int32),
+            pltpu.VMEM(rows.shape[1:], jnp.int32),
+        ],
+        in_specs=[SMEM, SMEM, ANY, ANY],
+        out_specs=[SMEM, SMEM, SMEM, SMEM, VMEM],
+        scratch_shapes=[
+            pltpu.VMEM(rows.shape[1:], jnp.int32),
+            pltpu.VMEM(rows.shape[1:], jnp.int32),
+            pltpu.VMEM(listed, jnp.int32),
+            pltpu.VMEM(listed, jnp.int32),
+            pltpu.SemaphoreType.DMA((2,)),
+        ],
+        compiler_params=PICK_PARAMS,
+        name="pick_tiles",
+    )(count, ids, far(rows), far(columns))
 
 
 def start_fetch(tiles, fetched, held, arrived, g, carry):
@@ -122,33 +146,23 @@
     return carry
 
 
-def pick(count, ids, rows, columns, tiles, n_out, n_back):
-    length = rows.shape[-1] + max(n_out * (FORWARD - 1), n_back * (BACKWARD - 1)) + PER
-    length = -(-length // TILE) * TILE
-    listed = (1, length)
-    return pl.pallas_call(
-        functools.partial(pick_kernel, n_out),
-        out_shape=[
-            pltpu.VMEM((EARLY * PER + 1, TILE, TILE), BF16),
-            pltpu.SMEM(listed, jnp.int32),
-            pltpu.SMEM(listed, jnp.int32),
-            pltpu.SMEM((1,), jnp.int32),
-            pltpu.SMEM((3,), jnp.int32),
-            pltpu.VMEM(rows.shape[1:], jnp.int32),
-        ],
-        in_specs=[SMEM, SMEM, ANY, ANY, ANY],
-        out_specs=[VMEM, SMEM, SMEM, SMEM, SMEM, VMEM],
-        scratch_shapes=[
-            pltpu.VMEM(rows.shape[1:], jnp.int32),
-            pltpu.VMEM(rows.shape[1:], jnp.int32),
-            pltpu.VMEM(listed, jnp.int32),
-            pltpu.VMEM(listed, jnp.int32),
-            pltpu.SemaphoreType.DMA((4,)),
-            pltpu.SemaphoreType.DMA((EARLY,)),
-        ],
-        compiler_params=PICK_PARAMS,
-        name="pick_tiles",
-    )(count, ids, far(rows), far(columns), far(tiles))
+def early_kernel(steps, fetched, tiles, early, arrived):
+    count = jnp.minimum(steps[0], EARLY)
+    lax.fori_loop(0, count, functools.partial(start_fetch, tiles, fetched, early, arrived), 0)
+    early[early.shape[0] - 1] = jnp.zeros((TILE, TILE), BF16)
+    lax.fori_loop(0, count, functools.partial(end_fetch, tiles, early, arrived), 0)
+
+
+def early_tiles(steps, fetched, tiles):
+    return pl.pallas_call(
+        early_kernel,
+        out_shape=pltpu.VMEM((EARLY * PER + 1, TILE, TILE), BF16),
+        in_specs=[SMEM, SMEM, ANY],
+        out_specs=VMEM,
+        scratch_shapes=[pltpu.SemaphoreType.DMA((EARLY,))],
+        compiler_params=PARAMS,
+        name="early_tiles",
+    )(scalar(steps), scalar(fetched), far(tiles))
 
 
 def prepare_kernel(n_back, ids, rows, columns, slots, weight, bias, cotangent, *refs):
@@ -177,7 +191,7 @@
     items, source, target, n_steps, slot = order(
         place, used, source, slot, n_back, length, BACKWARD
     )
-    here = jnp.where(items >= 0, items, length)
+    here = jnp.where(items >= 0, items, SPARE)
     backward_copy[...] = here + source * 1024 + target * 65536
     copy = pltpu.make_async_copy(backward_copy, backward, arrived.at[5])
     copy.start()
@@ -279,7 +293,7 @@
 
 def tiles_forward(steps, ids, fetched, picked, tiles, early, sources, n_out):
     shape = (n_out // 8, 4, TILE, TILE)
-    length = fetched.shape[1]
+    length = -(-(tiles.shape[0] + n_out * (FORWARD - 1)) // PER) * PER
     return pl.pallas_call(
         forward_kernel,
         out_shape=[
@@ -529,12 +543,13 @@
     ids = jnp.stack([half, lax.axis_index("col"), lax.axis_index("row")]).astype(jnp.int32)
 
     mine = lax.dynamic_slice_in_dim(features, half * (own_rows // 2), own_rows // 2, 0)
-    beside, ids = lax.optimization_barrier((swap(mine, "row", 1), ids))
+    lists = pick(tile_count, ids, tile_rows, tile_columns, n_out, n_back)
+    beside, lists = lax.optimization_barrier((swap(mine, "row", 1), lists))
+    fetched, forward, steps, ids, slots = lists
     pair = join(mine, beside)
     sources = [swap(pair, "row", mask) for mask in range(2, n_row, 2)]
-    lists = pick(tile_count, ids, tile_rows, tile_columns, tiles, n_out, n_back)
-    lists, sources = lax.optimization_barrier((lists, sources))
-    early, fetched, forward, steps, ids, slots = lists
+    early = early_tiles(steps, fetched, tiles)
+    early, sources = lax.optimization_barrier((early, sources))
 
     held, kept, sent = tiles_forward(steps, ids, fetched, forward, tiles, early, [pair, *sources], n_out)
     first, *others = pair_sum(kept, swap(sent, "col", 1))
@@ -548,7 +563,8 @@
     backward, steps, weight, bias, cotangent = ready
     activations, back, back_sent, grads = middle(own, other, weight, bias, cotangent)
 
-    back_other, more = lax.optimization_barrier((swap(back_sent, "feat", 1), swap(grads, "col", 1)))
+    grads = grads + swap(grads, "col", 1)
+    back_other, more = lax.optimization_barrier((swap(back_sent, "feat", 1), swap(grads, "row", 1)))
     mine = message(ids, back, back_other, grads, more)
     across = [swap(mine, "col", mask) for mask in (2, 6, 4)]
     beside = swap(mine, "col", 1)
@@ -556,22 +572,17 @@
     corners = [swap(values, "col", 1) for values in across]
     sources = [mine, beside, across[0], corners[0], across[2], corners[2], across[1], corners[1]]
     grads = grad_sum(ids, sources)
-    more = swap(grads, "row", 1)
+    more = swap(grads, "row", 2)
     kept, *others = tiles_backward(steps, ids, backward, held, sources, n_back)
     others, more = lax.optimization_barrier((others, more))
     grads = grads + more
 
     others = [swap(other, "row", 2 * k + 2) for k, other in enumerate(others)]
-    others, more = lax.optimization_barrier((others, swap(grads, "row", 2)))
-    grads = grads + more
+    others, more = lax.optimization_barrier((others, swap(grads, "row", 4)))
     own, own_sent, other_sent = line_sum(kept, others)
-    own_sent, other_sent, grads = lax.optimization_barrier((own_sent, other_sent, grads))
     opposite = swap(own_sent, "feat", 1)
     corner = swap(other_sent, ("row", "feat"), 3)
     beside = swap(other_sent, "row", 1)
-    opposite, corner, beside, more = lax.optimization_barrier(
-        (opposite, corner, beside, swap(grads, "row", 4))
-    )
     grad_features, grad_weight, grad_bias = finish(ids, own, beside, opposite, corner, grads, more)
     return (activations, grad_features, grad_weight, grad_bias[0])
 

time: 105 us -> 95.2 us (0.907); the launches traced: 105 us -> 94.5 us
  local copies, waits for them, and re-layouts: 17.4 us -> 0.9 us
  waiting for transfers between devices: 32.7 us -> 35.9 us
  starting transfers between devices: 40.2 us -> 41.5 us
    unnamed x6 -> x2, local copies, waits for them, and re-layouts: 17.4 us -> 0.9 us
    ppermute x27, waiting for transfers between devices: 32.7 us -> 35.9 us  [swap(): return lax.ppermute(values, axis, [(i, i ^ mask) for i in range(size)])]
    ppermute x27, starting transfers between devices: 40.2 us -> 41.5 us  [swap(): return lax.ppermute(values, axis, [(i, i ^ mask) for i in range(size)])]
    pallas_call x1 -> x2, Pallas kernels: 5.34 us -> 6.4 us  [the longest x1 3.53 us: early_tiles(): pl.pallas_call(early_kernel, out_shape=pltpu.VMEM((EARLY * PER + 1, TILE,...]
  transfers between devices with their start and end apart: 27 -> 27, of which waited for: 18 -> 19; matrix products, arithmetic and copies ran while one was open for 0% -> 0% of each run, Pallas kernels for 9% -> 11%
where the time goes in v3:
time: 95.2 us; the launch traced here: 94.5 us
  starting transfers between devices  41.5 us (44%)
  waiting for transfers between devices  35.9 us (38%)
  Pallas kernels  14.6 us (15%)
  between operations  1.4 us (1%)
    ppermute x27, starting transfers between devices, swap(): return lax.ppermute(values, axis, [(i, i ^ mask) for i in range(size)])  41.5 us
    ppermute x27, waiting for transfers between devices, swap(): return lax.ppermute(values, axis, [(i, i ^ mask) for i in range(size)])  35.9 us
    pallas_call x1, Pallas kernels, early_tiles(): pl.pallas_call(early_kernel, out_shape=pltpu.VMEM((EARLY * PER + 1, TILE,...  3.53 us
    pallas_call x1, Pallas kernels, pick(): pl.pallas_call(functools.partial(pick_kernel, n_out), out_shape=[pltpu.SM...  2.87 us
    pallas_call x1, Pallas kernels, prepare(): pl.pallas_call(functools.partial(prepare_kernel, n_back), out_shape=[pltp...  2.59 us
    pallas_call x1, Pallas kernels, tiles_forward(): pl.pallas_call(forward_kernel, out_shape=[pltpu.VMEM((length + 1, TILE, T...  2.11 us
  transfers between devices with their start and end apart: 27, of which 19 were waited for; matrix products, arithmetic and copies ran while one was open for 0% of the time, Pallas kernels for 11%

profile of v3, /device:TPU:0, one launch (start us, length us, event | category | flops | bytes accessed | tf_op | source)
XLA Modules:
  0.0 94.5 jit_solution(5525796991606364236)
XLA Ops:
  0.6 0.0 copy-start
  0.7 0.9 copy-done
  1.5 2.0 %collective-permute-start = (bf16[256,128]{1,0:T(8,128)(2,1)S(1)}, bf16[256,128]{1,0:T(8,128)(2,1)S(1)}, u32[]{:S(2)}, u32[]{:S(2)}) collective-permute-start(bf16[256,128]{1,0:T(8,128)(2,1)S(1)} %constant_dynamic-slice_fusion.a), channel_id=1, source_target_pairs={{0,16},{16,0},{32,48},{48,32},{64,80},{80,64},{96,112},{112,96},{1... | collective-permute-start | bytes 196616 | tf_op jit(solution)/shard_map/ppermute | solution.py:27
  4.2 0.1 pad_add_fusion.ids
  4.3 2.9 %pick_tiles.1 = (s32[1,768]{1,0:T(1,128)S(4)}, s32[1,768]{1,0:T(1,128)S(4)}, s32[1]{0:T(128)S(4)}, s32[3]{0:T(128)S(4)}, s32[1,640]{1,0:T(1,128)S(1)}) custom-call(s32[1,1]{1,0:T(1,128)S(6)} %copy.12.count, s32[3]{0:T(128)S(1)} %pad_add_fusion.ids, s32[1,1,640]{2,1,0:T(1,128)} %rows.3, s32[1,1,640]{2,1,0:T(1,128)} %columns.3), custom_call_target="tpu_custom_call" | custom-call | tf_op jit(solution)/shard_map/pick_tiles/pallas_call | solution.py:113
  7.2 3.1 %collective-permute-start.3 = (bf16[512,128]{1,0:T(8,128)(2,1)S(1)}, bf16[512,128]{1,0:T(8,128)(2,1)S(1)}, u32[]{:S(2)}, u32[]{:S(2)}) collective-permute-start(bf16[512,128]{1,0:T(8,128)(2,1)S(1)} %join.1.refs_0_), channel_id=1, source_target_pairs={{0,96},{16,112},{32,64},{48,80},{64,32},{80,48},{96,0},{112,16},{1... | collective-permute-start | bytes 393224 | tf_op jit(solution)/shard_map/ppermute | solution.py:27
  10.3 0.6 collective-permute-start.2
  10.9 0.4 collective-permute-start.1
  11.4 3.5 %early_tiles.1.early = bf16[129,128,128]{2,1,0:T(8,128)(2,1)S(1)} custom-call(s32[1]{0:T(128)S(4)} %get-tuple-element.73.steps, s32[1,768]{1,0:T(1,128)S(4)} %get-tuple-element.75.fetched, bf16[640,128,128]{2,1,0:T(8,128)(2,1)} %bitcast.6), custom_call_target="tpu_custom_call" | custom-call | tf_op jit(solution)/shard_map/early_tiles/pallas_call | solution.py:157
  14.9 0.7 collective-permute-done.3.refs_3_
  15.6 2.3 %collective-permute-done.2.refs_2_ = bf16[512,128]{1,0:T(8,128)(2,1)S(1)} collective-permute-done((bf16[512,128]{1,0:T(8,128)(2,1)S(1)}, bf16[512,128]{1,0:T(8,128)(2,1)S(1)}, u32[]{:S(2)}, u32[]{:S(2)}) %collective-permute-start.2) | collective-permute-done | bytes 131104 | tf_op jit(solution)/shard_map/ppermute | solution.py:27
  17.9 0.0 collective-permute-done.1.refs_1_
  17.9 2.1 %tiles_forward.1 = (bf16[673,128,128]{2,1,0:T(8,128)(2,1)S(1)}, f32[4,4,128,128]{3,2,1,0:T(8,128)S(1)}, bf16[4,4,128,128]{3,2,1,0:T(8,128)(2,1)S(1)}) custom-call(s32[1]{0:T(128)S(4)} %get-tuple-element.73.steps, s32[3]{0:T(128)S(4)} %get-tuple-element.74.ids, s32[1,768]{1,0:T(1,128)S(4)} %get-tuple-element.75.fetched, ...), custom_call_target="tpu_custom_call" | custom-call | tf_op jit(solution)/shard_map/tiles_forward/pallas_call | solution.py:297
  20.0 1.3 %collective-permute-start.4 = (bf16[4,4,128,128]{3,2,1,0:T(8,128)(2,1)S(1)}, bf16[4,4,128,128]{3,2,1,0:T(8,128)(2,1)S(1)}, u32[]{:S(2)}, u32[]{:S(2)}) collective-permute-start(bf16[4,4,128,128]{3,2,1,0:T(8,128)(2,1)S(1)} %get-tuple-element.83), channel_id=1, source_target_pairs={{0,2},{2,0},{4,6},{6,4},{8,10},{10,8},{12,14},{14,12},{1,3},{3,1},... | collective-permute-start | bytes 1572872 | tf_op jit(solution)/shard_map/ppermute | solution.py:27
  21.3 1.5 %collective-permute-done.4.got = bf16[4,4,128,128]{3,2,1,0:T(8,128)(2,1)S(1)} collective-permute-done((bf16[4,4,128,128]{3,2,1,0:T(8,128)(2,1)S(1)}, bf16[4,4,128,128]{3,2,1,0:T(8,128)(2,1)S(1)}, u32[]{:S(2)}, u32[]{:S(2)}) %collective-permute-start.4) | collective-permute-done | bytes 524320 | tf_op jit(solution)/shard_map/ppermute | solution.py:27
  22.8 0.1 pair_sum.1
  22.9 0.7 collective-permute-start.5
  23.6 2.3 %collective-permute-start.6 = (bf16[4,128,128]{2,1,0:T(8,128)(2,1)S(1)}, bf16[4,128,128]{2,1,0:T(8,128)(2,1)S(1)}, u32[]{:S(2)}, u32[]{:S(2)}) collective-permute-start(bf16[4,128,128]{2,1,0:T(8,128)(2,1)S(1)} %get-tuple-element.86), channel_id=1, source_target_pairs={{0,8},{2,10},{4,12},{6,14},{8,0},{10,2},{12,4},{14,6},{1,9},{3,11}... | collective-permute-start | bytes 393224 | tf_op jit(solution)/shard_map/ppermute | solution.py:27
  25.9 1.8 %collective-permute-start.7 = (bf16[4,128,128]{2,1,0:T(8,128)(2,1)S(1)}, bf16[4,128,128]{2,1,0:T(8,128)(2,1)S(1)}, u32[]{:S(2)}, u32[]{:S(2)}) collective-permute-start(bf16[4,128,128]{2,1,0:T(8,128)(2,1)S(1)} %get-tuple-element.87), channel_id=1, source_target_pairs={{0,12},{2,14},{4,8},{6,10},{8,4},{10,6},{12,0},{14,2},{1,13},{3,15... | collective-permute-start | bytes 393224 | tf_op jit(solution)/shard_map/ppermute | solution.py:27
  27.7 1.6 %collective-permute-done.5.a = bf16[4,128,128]{2,1,0:T(8,128)(2,1)S(1)} collective-permute-done((bf16[4,128,128]{2,1,0:T(8,128)(2,1)S(1)}, bf16[4,128,128]{2,1,0:T(8,128)(2,1)S(1)}, u32[]{:S(2)}, u32[]{:S(2)}) %collective-permute-start.5) | collective-permute-done | bytes 131104 | tf_op jit(solution)/shard_map/ppermute | solution.py:27
  29.3 3.0 %collective-permute-done.6.b = bf16[4,128,128]{2,1,0:T(8,128)(2,1)S(1)} collective-permute-done((bf16[4,128,128]{2,1,0:T(8,128)(2,1)S(1)}, bf16[4,128,128]{2,1,0:T(8,128)(2,1)S(1)}, u32[]{:S(2)}, u32[]{:S(2)}) %collective-permute-start.6) | collective-permute-done | bytes 131104 | tf_op jit(solution)/shard_map/ppermute | solution.py:27
  32.4 2.2 %collective-permute-done.7.c = bf16[4,128,128]{2,1,0:T(8,128)(2,1)S(1)} collective-permute-done((bf16[4,128,128]{2,1,0:T(8,128)(2,1)S(1)}, bf16[4,128,128]{2,1,0:T(8,128)(2,1)S(1)}, u32[]{:S(2)}, u32[]{:S(2)}) %collective-permute-start.7) | collective-permute-done | bytes 131104 | tf_op jit(solution)/shard_map/ppermute | solution.py:27
  34.6 0.1 own_sum.1
  34.7 3.7 %collective-permute-start.8 = (bf16[4,128,128]{2,1,0:T(8,128)(2,1)S(1)}, bf16[4,128,128]{2,1,0:T(8,128)(2,1)S(1)}, u32[]{:S(2)}, u32[]{:S(2)}) collective-permute-start(bf16[4,128,128]{2,1,0:T(8,128)(2,1)S(1)} %get-tuple-element.91), channel_id=1, source_target_pairs={{0,1},{1,0},{2,3},{3,2},{4,5},{5,4},{6,7},{7,6},{8,9},{9,8},{10,11... | collective-permute-start | bytes 393224 | tf_op jit(solution)/shard_map/ppermute | solution.py:27
  38.4 2.6 %prepare.1 = (s32[1,768]{1,0:T(1,128)S(4)}, s32[1]{0:T(128)S(4)}, bf16[128,128]{1,0:T(8,128)(2,1)S(1)}, f32[1,128]{1,0:T(1,128)S(1)}, bf16[512,128]{1,0:T(8,128)(2,1)S(1)}) custom-call(s32[3]{0:T(128)S(4)} %get-tuple-element.74.ids, s32[1,1,640]{2,1,0:T(1,128)} %rows.3, s32[1,1,640]{2,1,0:T(1,128)} %columns.3, s32[1,640]{1,0:T(1,128)S(1)} %get-tuple-element.92.slots, ...), custom_call_target="tpu_custom_call" | custom-call | tf_op jit(solution)/shard_map/prepare/pallas_call | solution.py:203
  41.0 0.6 collective-permute-done.8.other
  41.6 0.9 middle.1
  42.5 3.2 %collective-permute-start.9 = (bf16[4,128,128]{2,1,0:T(8,128)(2,1)S(1)}, bf16[4,128,128]{2,1,0:T(8,128)(2,1)S(1)}, u32[]{:S(2)}, u32[]{:S(2)}) collective-permute-start(bf16[4,128,128]{2,1,0:T(8,128)(2,1)S(1)} %get-tuple-element.107), channel_id=1, source_target_pairs={{0,1},{1,0},{2,3},{3,2},{4,5},{5,4},{6,7},{7,6},{8,9},{9,8},{10,11... | collective-permute-start | bytes 393224 | tf_op jit(solution)/shard_map/ppermute | solution.py:27
  45.8 0.0 collective-permute-done.10
  45.8 2.4 %collective-permute-start.11 = (f32[136,128]{1,0:T(8,128)S(1)}, f32[136,128]{1,0:T(8,128)S(1)}, u32[]{:S(2)}, u32[]{:S(2)}) collective-permute-start(f32[136,128]{1,0:T(8,128)S(1)} %add.10.grads), channel_id=1, source_target_pairs={{0,16},{16,0},{32,48},{48,32},{64,80},{80,64},{96,112},{112,96},{1... | collective-permute-start | bytes 208904 | tf_op jit(solution)/shard_map/ppermute | solution.py:27
  48.2 1.8 %collective-permute-done.9.other = bf16[4,128,128]{2,1,0:T(8,128)(2,1)S(1)} collective-permute-done((bf16[4,128,128]{2,1,0:T(8,128)(2,1)S(1)}, bf16[4,128,128]{2,1,0:T(8,128)(2,1)S(1)}, u32[]{:S(2)}, u32[]{:S(2)}) %collective-permute-start.9) | collective-permute-done | bytes 131104 | tf_op jit(solution)/shard_map/ppermute | solution.py:27
  49.9 3.5 %collective-permute-done.11.more = f32[136,128]{1,0:T(8,128)S(1)} collective-permute-done((f32[136,128]{1,0:T(8,128)S(1)}, f32[136,128]{1,0:T(8,128)S(1)}, u32[]{:S(2)}, u32[]{:S(2)}) %collective-permute-start.11) | collective-permute-done | bytes 69664 | tf_op jit(solution)/shard_map/ppermute | solution.py:27
  53.5 2.0 %collective-permute-start.15 = (bf16[592,128]{1,0:T(8,128)(2,1)S(1)}, bf16[592,128]{1,0:T(8,128)(2,1)S(1)}, u32[]{:S(2)}, u32[]{:S(2)}) collective-permute-start(bf16[592,128]{1,0:T(8,128)(2,1)S(1)} %message.1.refs_0_), channel_id=1, source_target_pairs={{0,8},{2,10},{4,12},{6,14},{8,0},{10,2},{12,4},{14,6},{1,9},{3,11}... | collective-permute-start | bytes 454664 | tf_op jit(solution)/shard_map/ppermute | solution.py:27
  55.4 0.9 collective-permute-start.14
  56.3 0.7 collective-permute-start.13
  57.0 0.0 collective-permute-start.12
  57.0 4.3 %collective-permute-done.15.refs_4_ = bf16[592,128]{1,0:T(8,128)(2,1)S(1)} collective-permute-done((bf16[592,128]{1,0:T(8,128)(2,1)S(1)}, bf16[592,128]{1,0:T(8,128)(2,1)S(1)}, u32[]{:S(2)}, u32[]{:S(2)}) %collective-permute-start.15) | collective-permute-done | bytes 151584 | tf_op jit(solution)/shard_map/ppermute | solution.py:27
  61.3 2.5 %collective-permute-done.14.refs_6_ = bf16[592,128]{1,0:T(8,128)(2,1)S(1)} collective-permute-done((bf16[592,128]{1,0:T(8,128)(2,1)S(1)}, bf16[592,128]{1,0:T(8,128)(2,1)S(1)}, u32[]{:S(2)}, u32[]{:S(2)}) %collective-permute-start.14) | collective-permute-done | bytes 151584 | tf_op jit(solution)/shard_map/ppermute | solution.py:27
  63.9 0.0 collective-permute-done.13.refs_2_
  63.9 0.5 collective-permute-start.17
  64.4 0.0 collective-permute-start.18
  64.4 0.0 collective-permute-done.12.refs_1_
  64.4 0.9 collective-permute-done.16.refs_3_
  65.2 0.2 collective-permute-done.17.refs_5_
  65.5 0.3 collective-permute-done.18.refs_7_
  65.8 1.1 %collective-permute-start.19 = (f32[136,128]{1,0:T(8,128)S(1)}, f32[136,128]{1,0:T(8,128)S(1)}, u32[]{:S(2)}, u32[]{:S(2)}) collective-permute-start(f32[136,128]{1,0:T(8,128)S(1)} %grad_sum.1), channel_id=1, source_target_pairs={{0,32},{16,48},{32,0},{48,16},{64,96},{80,112},{96,64},{112,80},{1... | collective-permute-start | bytes 208904 | tf_op jit(solution)/shard_map/ppermute | solution.py:27
  66.9 1.5 %tiles_backward.1 = (f32[4,128,128]{2,1,0:T(8,128)S(1)}, bf16[4,128,128]{2,1,0:T(8,128)(2,1)S(1)}, bf16[4,128,128]{2,1,0:T(8,128)(2,1)S(1)}, bf16[4,128,128]{2,1,0:T(8,128)(2,1)S(1)}) custom-call(s32[1]{0:T(128)S(4)} %get-tuple-element.103.steps, s32[3]{0:T(128)S(4)} %get-tuple-element.74.ids, s32[1,768]{1,0:T(1,128)S(4)} %get-tuple-element.104.picked, ...), custom_call_target="tpu_custom_call" | custom-call | tf_op jit(solution)/shard_map/tiles_backward/pallas_call | solution.py:343
  68.4 1.8 %collective-permute-done.19 = f32[136,128]{1,0:T(8,128)S(1)} collective-permute-done((f32[136,128]{1,0:T(8,128)S(1)}, f32[136,128]{1,0:T(8,128)S(1)}, u32[]{:S(2)}, u32[]{:S(2)}) %collective-permute-start.19) | collective-permute-done | bytes 69664 | tf_op jit(solution)/shard_map/ppermute | solution.py:27
  70.2 3.3 %collective-permute-start.20 = (bf16[4,128,128]{2,1,0:T(8,128)(2,1)S(1)}, bf16[4,128,128]{2,1,0:T(8,128)(2,1)S(1)}, u32[]{:S(2)}, u32[]{:S(2)}) collective-permute-start(bf16[4,128,128]{2,1,0:T(8,128)(2,1)S(1)} %get-tuple-element.118), channel_id=1, source_target_pairs={{0,32},{16,48},{32,0},{48,16},{64,96},{80,112},{96,64},{112,80},{1... | collective-permute-start | bytes 393224 | tf_op jit(solution)/shard_map/ppermute | solution.py:27
  73.4 2.0 %collective-permute-start.21 = (bf16[4,128,128]{2,1,0:T(8,128)(2,1)S(1)}, bf16[4,128,128]{2,1,0:T(8,128)(2,1)S(1)}, u32[]{:S(2)}, u32[]{:S(2)}) collective-permute-start(bf16[4,128,128]{2,1,0:T(8,128)(2,1)S(1)} %get-tuple-element.119), channel_id=1, source_target_pairs={{0,64},{16,80},{32,96},{48,112},{64,0},{80,16},{96,32},{112,48},{1... | collective-permute-start | bytes 393224 | tf_op jit(solution)/shard_map/ppermute | solution.py:27
  75.5 0.7 collective-permute-start.22
  76.2 2.7 %collective-permute-start.23 = (f32[136,128]{1,0:T(8,128)S(1)}, f32[136,128]{1,0:T(8,128)S(1)}, u32[]{:S(2)}, u32[]{:S(2)}) collective-permute-start(f32[136,128]{1,0:T(8,128)S(1)} %add.11.grads), channel_id=1, source_target_pairs={{0,64},{16,80},{32,96},{48,112},{64,0},{80,16},{96,32},{112,48},{1... | collective-permute-start | bytes 208904 | tf_op jit(solution)/shard_map/ppermute | solution.py:27
  79.0 3.2 %collective-permute-done.23.more = f32[136,128]{1,0:T(8,128)S(1)} collective-permute-done((f32[136,128]{1,0:T(8,128)S(1)}, f32[136,128]{1,0:T(8,128)S(1)}, u32[]{:S(2)}, u32[]{:S(2)}) %collective-permute-start.23) | collective-permute-done | bytes 69664 | tf_op jit(solution)/shard_map/ppermute | solution.py:27
  82.2 0.0 collective-permute-done.20.a
  82.2 0.0 collective-permute-done.21.b
  82.2 1.2 %collective-permute-done.22.c = bf16[4,128,128]{2,1,0:T(8,128)(2,1)S(1)} collective-permute-done((bf16[4,128,128]{2,1,0:T(8,128)(2,1)S(1)}, bf16[4,128,128]{2,1,0:T(8,128)(2,1)S(1)}, u32[]{:S(2)}, u32[]{:S(2)}) %collective-permute-start.22) | collective-permute-done | bytes 131104 | tf_op jit(solution)/shard_map/ppermute | solution.py:27
  83.4 0.1 line_sum.1
  83.4 3.2 %collective-permute-start.25 = (bf16[2,128,128]{2,1,0:T(8,128)(2,1)S(1)}, bf16[2,128,128]{2,1,0:T(8,128)(2,1)S(1)}, u32[]{:S(2)}, u32[]{:S(2)}) collective-permute-start(bf16[2,128,128]{2,1,0:T(8,128)(2,1)S(1)} %get-tuple-element.127), channel_id=1, source_target_pairs={{0,1},{1,0},{2,3},{3,2},{4,5},{5,4},{6,7},{7,6},{8,9},{9,8},{10,11... | collective-permute-start | bytes 196616 | tf_op jit(solution)/shard_map/ppermute | solution.py:27
  86.6 2.7 %collective-permute-start.26 = (bf16[2,128,128]{2,1,0:T(8,128)(2,1)S(1)}, bf16[2,128,128]{2,1,0:T(8,128)(2,1)S(1)}, u32[]{:S(2)}, u32[]{:S(2)}) collective-permute-start(bf16[2,128,128]{2,1,0:T(8,128)(2,1)S(1)} %get-tuple-element.126), channel_id=1, source_target_pairs={{0,17},{1,16},{16,1},{17,0},{32,49},{33,48},{48,33},{49,32},{64,81... | collective-permute-start | bytes 196616 | tf_op jit(solution)/shard_map/ppermute | solution.py:27
  89.4 0.0 collective-permute-start.24
  89.4 0.0 collective-permute-done.25.opposite
  89.4 2.7 %collective-permute-done.26.corner = bf16[2,128,128]{2,1,0:T(8,128)(2,1)S(1)} collective-permute-done((bf16[2,128,128]{2,1,0:T(8,128)(2,1)S(1)}, bf16[2,128,128]{2,1,0:T(8,128)(2,1)S(1)}, u32[]{:S(2)}, u32[]{:S(2)}) %collective-permute-start.26) | collective-permute-done | bytes 65568 | tf_op jit(solution)/shard_map/ppermute | solution.py:27
  92.1 1.5 %collective-permute-done.24.beside = bf16[2,128,128]{2,1,0:T(8,128)(2,1)S(1)} collective-permute-done((bf16[2,128,128]{2,1,0:T(8,128)(2,1)S(1)}, bf16[2,128,128]{2,1,0:T(8,128)(2,1)S(1)}, u32[]{:S(2)}, u32[]{:S(2)}) %collective-permute-start.24) | collective-permute-done | bytes 65568 | tf_op jit(solution)/shard_map/ppermute | solution.py:27
  93.6 0.8 finish.1
  (9 shorter events, 0.1 us)
Async XLA Ops:
  0.6 0.9 copy-start
  1.5 5.6 %collective-permute-start = (bf16[256,128]{1,0:T(8,128)(2,1)S(1)}, bf16[256,128]{1,0:T(8,128)(2,1)S(1)}, u32[]{:S(2)}, u32[]{:S(2)}) collective-permute-start(bf16[256,128]{1,0:T(8,128)(2,1)S(1)} %constant_dynamic-slice_fusion.a), channel_id=1, source_target_pairs={{0,16},{16,0},{32,48},{48,32},{64,80},{80,64},{96,112},{112,96},{1... | collective-permute-start | bytes 196616 | tf_op jit(solution)/shard_map/ppermute | solution.py:27
  7.2 8.4 %collective-permute-start.3 = (bf16[512,128]{1,0:T(8,128)(2,1)S(1)}, bf16[512,128]{1,0:T(8,128)(2,1)S(1)}, u32[]{:S(2)}, u32[]{:S(2)}) collective-permute-start(bf16[512,128]{1,0:T(8,128)(2,1)S(1)} %join.1.refs_0_), channel_id=1, source_target_pairs={{0,96},{16,112},{32,64},{48,80},{64,32},{80,48},{96,0},{112,16},{1... | collective-permute-start | bytes 393224 | tf_op jit(solution)/shard_map/ppermute | solution.py:27
  10.3 7.6 %collective-permute-start.2 = (bf16[512,128]{1,0:T(8,128)(2,1)S(1)}, bf16[512,128]{1,0:T(8,128)(2,1)S(1)}, u32[]{:S(2)}, u32[]{:S(2)}) collective-permute-start(bf16[512,128]{1,0:T(8,128)(2,1)S(1)} %join.1.refs_0_), channel_id=1, source_target_pairs={{0,64},{16,80},{32,96},{48,112},{64,0},{80,16},{96,32},{112,48},{1... | collective-permute-start | bytes 393224 | tf_op jit(solution)/shard_map/ppermute | solution.py:27
  10.9 7.0 %collective-permute-start.1 = (bf16[512,128]{1,0:T(8,128)(2,1)S(1)}, bf16[512,128]{1,0:T(8,128)(2,1)S(1)}, u32[]{:S(2)}, u32[]{:S(2)}) collective-permute-start(bf16[512,128]{1,0:T(8,128)(2,1)S(1)} %join.1.refs_0_), channel_id=1, source_target_pairs={{0,32},{16,48},{32,0},{48,16},{64,96},{80,112},{96,64},{112,80},{1... | collective-permute-start | bytes 393224 | tf_op jit(solution)/shard_map/ppermute | solution.py:27
  20.0 2.8 %collective-permute-start.4 = (bf16[4,4,128,128]{3,2,1,0:T(8,128)(2,1)S(1)}, bf16[4,4,128,128]{3,2,1,0:T(8,128)(2,1)S(1)}, u32[]{:S(2)}, u32[]{:S(2)}) collective-permute-start(bf16[4,4,128,128]{3,2,1,0:T(8,128)(2,1)S(1)} %get-tuple-element.83), channel_id=1, source_target_pairs={{0,2},{2,0},{4,6},{6,4},{8,10},{10,8},{12,14},{14,12},{1,3},{3,1},... | collective-permute-start | bytes 1572872 | tf_op jit(solution)/shard_map/ppermute | solution.py:27
  22.9 6.4 %collective-permute-start.5 = (bf16[4,128,128]{2,1,0:T(8,128)(2,1)S(1)}, bf16[4,128,128]{2,1,0:T(8,128)(2,1)S(1)}, u32[]{:S(2)}, u32[]{:S(2)}) collective-permute-start(bf16[4,128,128]{2,1,0:T(8,128)(2,1)S(1)} %get-tuple-element.85), channel_id=1, source_target_pairs={{0,4},{2,6},{4,0},{6,2},{8,12},{10,14},{12,8},{14,10},{1,5},{3,7},... | collective-permute-start | bytes 393224 | tf_op jit(solution)/shard_map/ppermute | solution.py:27
  23.6 8.7 %collective-permute-start.6 = (bf16[4,128,128]{2,1,0:T(8,128)(2,1)S(1)}, bf16[4,128,128]{2,1,0:T(8,128)(2,1)S(1)}, u32[]{:S(2)}, u32[]{:S(2)}) collective-permute-start(bf16[4,128,128]{2,1,0:T(8,128)(2,1)S(1)} %get-tuple-element.86), channel_id=1, source_target_pairs={{0,8},{2,10},{4,12},{6,14},{8,0},{10,2},{12,4},{14,6},{1,9},{3,11}... | collective-permute-start | bytes 393224 | tf_op jit(solution)/shard_map/ppermute | solution.py:27
  25.9 8.7 %collective-permute-start.7 = (bf16[4,128,128]{2,1,0:T(8,128)(2,1)S(1)}, bf16[4,128,128]{2,1,0:T(8,128)(2,1)S(1)}, u32[]{:S(2)}, u32[]{:S(2)}) collective-permute-start(bf16[4,128,128]{2,1,0:T(8,128)(2,1)S(1)} %get-tuple-element.87), channel_id=1, source_target_pairs={{0,12},{2,14},{4,8},{6,10},{8,4},{10,6},{12,0},{14,2},{1,13},{3,15... | collective-permute-start | bytes 393224 | tf_op jit(solution)/shard_map/ppermute | solution.py:27
  34.7 6.9 %collective-permute-start.8 = (bf16[4,128,128]{2,1,0:T(8,128)(2,1)S(1)}, bf16[4,128,128]{2,1,0:T(8,128)(2,1)S(1)}, u32[]{:S(2)}, u32[]{:S(2)}) collective-permute-start(bf16[4,128,128]{2,1,0:T(8,128)(2,1)S(1)} %get-tuple-element.91), channel_id=1, source_target_pairs={{0,1},{1,0},{2,3},{3,2},{4,5},{5,4},{6,7},{7,6},{8,9},{9,8},{10,11... | collective-permute-start | bytes 393224 | tf_op jit(solution)/shard_map/ppermute | solution.py:27
  42.5 3.3 %collective-permute-start.10 = (f32[136,128]{1,0:T(8,128)S(1)}, f32[136,128]{1,0:T(8,128)S(1)}, u32[]{:S(2)}, u32[]{:S(2)}) collective-permute-start(f32[136,128]{1,0:T(8,128)S(1)} %get-tuple-element.108), channel_id=1, source_target_pairs={{0,2},{2,0},{4,6},{6,4},{8,10},{10,8},{12,14},{14,12},{1,3},{3,1},... | collective-permute-start | bytes 208904 | tf_op jit(solution)/shard_map/ppermute | solution.py:27
  42.5 7.4 %collective-permute-start.9 = (bf16[4,128,128]{2,1,0:T(8,128)(2,1)S(1)}, bf16[4,128,128]{2,1,0:T(8,128)(2,1)S(1)}, u32[]{:S(2)}, u32[]{:S(2)}) collective-permute-start(bf16[4,128,128]{2,1,0:T(8,128)(2,1)S(1)} %get-tuple-element.107), channel_id=1, source_target_pairs={{0,1},{1,0},{2,3},{3,2},{4,5},{5,4},{6,7},{7,6},{8,9},{9,8},{10,11... | collective-permute-start | bytes 393224 | tf_op jit(solution)/shard_map/ppermute | solution.py:27
  45.8 7.7 %collective-permute-start.11 = (f32[136,128]{1,0:T(8,128)S(1)}, f32[136,128]{1,0:T(8,128)S(1)}, u32[]{:S(2)}, u32[]{:S(2)}) collective-permute-start(f32[136,128]{1,0:T(8,128)S(1)} %add.10.grads), channel_id=1, source_target_pairs={{0,16},{16,0},{32,48},{48,32},{64,80},{80,64},{96,112},{112,96},{1... | collective-permute-start | bytes 208904 | tf_op jit(solution)/shard_map/ppermute | solution.py:27
  53.5 7.9 %collective-permute-start.15 = (bf16[592,128]{1,0:T(8,128)(2,1)S(1)}, bf16[592,128]{1,0:T(8,128)(2,1)S(1)}, u32[]{:S(2)}, u32[]{:S(2)}) collective-permute-start(bf16[592,128]{1,0:T(8,128)(2,1)S(1)} %message.1.refs_0_), channel_id=1, source_target_pairs={{0,8},{2,10},{4,12},{6,14},{8,0},{10,2},{12,4},{14,6},{1,9},{3,11}... | collective-permute-start | bytes 454664 | tf_op jit(solution)/shard_map/ppermute | solution.py:27
  55.4 8.4 %collective-permute-start.14 = (bf16[592,128]{1,0:T(8,128)(2,1)S(1)}, bf16[592,128]{1,0:T(8,128)(2,1)S(1)}, u32[]{:S(2)}, u32[]{:S(2)}) collective-permute-start(bf16[592,128]{1,0:T(8,128)(2,1)S(1)} %message.1.refs_0_), channel_id=1, source_target_pairs={{0,12},{2,14},{4,8},{6,10},{8,4},{10,6},{12,0},{14,2},{1,13},{3,15... | collective-permute-start | bytes 454664 | tf_op jit(solution)/shard_map/ppermute | solution.py:27
  56.3 7.5 %collective-permute-start.13 = (bf16[592,128]{1,0:T(8,128)(2,1)S(1)}, bf16[592,128]{1,0:T(8,128)(2,1)S(1)}, u32[]{:S(2)}, u32[]{:S(2)}) collective-permute-start(bf16[592,128]{1,0:T(8,128)(2,1)S(1)} %message.1.refs_0_), channel_id=1, source_target_pairs={{0,4},{2,6},{4,0},{6,2},{8,12},{10,14},{12,8},{14,10},{1,5},{3,7},... | collective-permute-start | bytes 454664 | tf_op jit(solution)/shard_map/ppermute | solution.py:27
  57.0 7.4 %collective-permute-start.12 = (bf16[592,128]{1,0:T(8,128)(2,1)S(1)}, bf16[592,128]{1,0:T(8,128)(2,1)S(1)}, u32[]{:S(2)}, u32[]{:S(2)}) collective-permute-start(bf16[592,128]{1,0:T(8,128)(2,1)S(1)} %message.1.refs_0_), channel_id=1, source_target_pairs={{0,2},{2,0},{4,6},{6,4},{8,10},{10,8},{12,14},{14,12},{1,3},{3,1},... | collective-permute-start | bytes 454664 | tf_op jit(solution)/shard_map/ppermute | solution.py:27
  63.9 1.4 %collective-permute-start.16 = (bf16[592,128]{1,0:T(8,128)(2,1)S(1)}, bf16[592,128]{1,0:T(8,128)(2,1)S(1)}, u32[]{:S(2)}, u32[]{:S(2)}) collective-permute-start(bf16[592,128]{1,0:T(8,128)(2,1)S(1)} %collective-permute-done.13.refs_2_), channel_id=1, source_target_pairs={{0,2},{2,0},{4,6},{6,4},{8,10},{10,8},{12,14},{14,12},{1,3},{3,1},... | collective-permute-start | bytes 454664 | tf_op jit(solution)/shard_map/ppermute | solution.py:27
  63.9 1.6 %collective-permute-start.17 = (bf16[592,128]{1,0:T(8,128)(2,1)S(1)}, bf16[592,128]{1,0:T(8,128)(2,1)S(1)}, u32[]{:S(2)}, u32[]{:S(2)}) collective-permute-start(bf16[592,128]{1,0:T(8,128)(2,1)S(1)} %collective-permute-done.15.refs_4_), channel_id=1, source_target_pairs={{0,2},{2,0},{4,6},{6,4},{8,10},{10,8},{12,14},{14,12},{1,3},{3,1},... | collective-permute-start | bytes 454664 | tf_op jit(solution)/shard_map/ppermute | solution.py:27
  64.4 1.4 %collective-permute-start.18 = (bf16[592,128]{1,0:T(8,128)(2,1)S(1)}, bf16[592,128]{1,0:T(8,128)(2,1)S(1)}, u32[]{:S(2)}, u32[]{:S(2)}) collective-permute-start(bf16[592,128]{1,0:T(8,128)(2,1)S(1)} %collective-permute-done.14.refs_6_), channel_id=1, source_target_pairs={{0,2},{2,0},{4,6},{6,4},{8,10},{10,8},{12,14},{14,12},{1,3},{3,1},... | collective-permute-start | bytes 454664 | tf_op jit(solution)/shard_map/ppermute | solution.py:27
  65.8 4.4 %collective-permute-start.19 = (f32[136,128]{1,0:T(8,128)S(1)}, f32[136,128]{1,0:T(8,128)S(1)}, u32[]{:S(2)}, u32[]{:S(2)}) collective-permute-start(f32[136,128]{1,0:T(8,128)S(1)} %grad_sum.1), channel_id=1, source_target_pairs={{0,32},{16,48},{32,0},{48,16},{64,96},{80,112},{96,64},{112,80},{1... | collective-permute-start | bytes 208904 | tf_op jit(solution)/shard_map/ppermute | solution.py:27
  70.2 12.0 %collective-permute-start.20 = (bf16[4,128,128]{2,1,0:T(8,128)(2,1)S(1)}, bf16[4,128,128]{2,1,0:T(8,128)(2,1)S(1)}, u32[]{:S(2)}, u32[]{:S(2)}) collective-permute-start(bf16[4,128,128]{2,1,0:T(8,128)(2,1)S(1)} %get-tuple-element.118), channel_id=1, source_target_pairs={{0,32},{16,48},{32,0},{48,16},{64,96},{80,112},{96,64},{112,80},{1... | collective-permute-start | bytes 393224 | tf_op jit(solution)/shard_map/ppermute | solution.py:27
  73.4 8.7 %collective-permute-start.21 = (bf16[4,128,128]{2,1,0:T(8,128)(2,1)S(1)}, bf16[4,128,128]{2,1,0:T(8,128)(2,1)S(1)}, u32[]{:S(2)}, u32[]{:S(2)}) collective-permute-start(bf16[4,128,128]{2,1,0:T(8,128)(2,1)S(1)} %get-tuple-element.119), channel_id=1, source_target_pairs={{0,64},{16,80},{32,96},{48,112},{64,0},{80,16},{96,32},{112,48},{1... | collective-permute-start | bytes 393224 | tf_op jit(solution)/shard_map/ppermute | solution.py:27
  75.5 7.9 %collective-permute-start.22 = (bf16[4,128,128]{2,1,0:T(8,128)(2,1)S(1)}, bf16[4,128,128]{2,1,0:T(8,128)(2,1)S(1)}, u32[]{:S(2)}, u32[]{:S(2)}) collective-permute-start(bf16[4,128,128]{2,1,0:T(8,128)(2,1)S(1)} %get-tuple-element.120), channel_id=1, source_target_pairs={{0,96},{16,112},{32,64},{48,80},{64,32},{80,48},{96,0},{112,16},{1... | collective-permute-start | bytes 393224 | tf_op jit(solution)/shard_map/ppermute | solution.py:27
  76.2 5.9 %collective-permute-start.23 = (f32[136,128]{1,0:T(8,128)S(1)}, f32[136,128]{1,0:T(8,128)S(1)}, u32[]{:S(2)}, u32[]{:S(2)}) collective-permute-start(f32[136,128]{1,0:T(8,128)S(1)} %add.11.grads), channel_id=1, source_target_pairs={{0,64},{16,80},{32,96},{48,112},{64,0},{80,16},{96,32},{112,48},{1... | collective-permute-start | bytes 208904 | tf_op jit(solution)/shard_map/ppermute | solution.py:27
  83.4 5.9 %collective-permute-start.25 = (bf16[2,128,128]{2,1,0:T(8,128)(2,1)S(1)}, bf16[2,128,128]{2,1,0:T(8,128)(2,1)S(1)}, u32[]{:S(2)}, u32[]{:S(2)}) collective-permute-start(bf16[2,128,128]{2,1,0:T(8,128)(2,1)S(1)} %get-tuple-element.127), channel_id=1, source_target_pairs={{0,1},{1,0},{2,3},{3,2},{4,5},{5,4},{6,7},{7,6},{8,9},{9,8},{10,11... | collective-permute-start | bytes 196616 | tf_op jit(solution)/shard_map/ppermute | solution.py:27
  86.6 5.5 %collective-permute-start.26 = (bf16[2,128,128]{2,1,0:T(8,128)(2,1)S(1)}, bf16[2,128,128]{2,1,0:T(8,128)(2,1)S(1)}, u32[]{:S(2)}, u32[]{:S(2)}) collective-permute-start(bf16[2,128,128]{2,1,0:T(8,128)(2,1)S(1)} %get-tuple-element.126), channel_id=1, source_target_pairs={{0,17},{1,16},{16,1},{17,0},{32,49},{33,48},{48,33},{49,32},{64,81... | collective-permute-start | bytes 196616 | tf_op jit(solution)/shard_map/ppermute | solution.py:27
  89.4 4.3 %collective-permute-start.24 = (bf16[2,128,128]{2,1,0:T(8,128)(2,1)S(1)}, bf16[2,128,128]{2,1,0:T(8,128)(2,1)S(1)}, u32[]{:S(2)}, u32[]{:S(2)}) collective-permute-start(bf16[2,128,128]{2,1,0:T(8,128)(2,1)S(1)} %get-tuple-element.126), channel_id=1, source_target_pairs={{0,16},{16,0},{32,48},{48,32},{64,80},{80,64},{96,112},{112,96},{1... | collective-permute-start | bytes 196616 | tf_op jit(solution)/shard_map/ppermute | solution.py:27

commit v4 on v3

--- a/solution.py
+++ b/solution.py
@@ -25,6 +25,11 @@
 def swap(values, axis, mask):
     size = lax.axis_size(axis)
     return lax.ppermute(values, axis, [(i, i ^ mask) for i in range(size)])
+
+
+def swap_line(values, axis):
+    second = swap(values[1], axis, 4)
+    return [swap(values[0], axis, 2), second, swap(values[2], axis, 6)]
 
 
 def near(values):
@@ -321,30 +326,62 @@
     )
 
 
+def write_terms(values, message, row):
+    rest = jnp.concatenate([values, values], 0)
+    line = iota(rest.shape, 0)
+    terms = jnp.zeros(rest.shape, F32)
+    for k in range(3):
+        term = rest.astype(BF16).astype(F32)
+        terms = jnp.where(line == k, term, terms)
+        rest = rest - term
+    message[row : row + 16] = terms.astype(BF16)
+
+
+def read_terms(messages, row):
+    terms = jnp.zeros((16, TILE), F32)
+    for one in messages:
+        terms = terms + one[row : row + 16].astype(F32)
+    return jnp.broadcast_to(jnp.sum(terms, axis=0, keepdims=True), (8, TILE))
+
+
 def backward_kernel(steps, ids, picked, held, *refs):
-    sources, (kept, first, second, third, gathered, total) = refs[:-6], refs[-6:]
+    messages, outs, (gathered, total) = refs[:-7], refs[-7:-2], refs[-2:]
+    kept, grads, outs = outs[0], outs[1], (outs[0], *outs[2:])
     total[...] = jnp.zeros_like(total)
-    for m, source in enumerate(sources):
-        gathered[4 * m : 4 * m + 4] = source[0 : 4 * TILE].reshape(4, TILE, TILE)
+    rows = 4 * TILE
+    for m, one in enumerate(messages):
+        gathered[4 * m : 4 * m + 4] = one[0:rows].reshape(4, TILE, TILE)
+
+    for k in range(2):
+        weight = jnp.zeros((TILE // 2, TILE), F32)
+        for one in messages[k::2]:
+            weight = weight + one[rows : rows + TILE // 2].astype(F32)
+        grads[pl.ds(jnp.bitwise_xor(ids[1] & 1, k) * (TILE // 2), TILE // 2)] = weight
+    bias = read_terms(messages[0::2], rows + TILE // 2)
+    grads[TILE : TILE + 8] = bias
+    for out in outs[1:]:
+        out[rows : rows + TILE] = grads[0:TILE].astype(BF16)
+        write_terms(bias, out, rows + TILE)
 
     def step(g, carry):
         add_products(True, g, picked, held, gathered, total)
         return carry
 
     lax.fori_loop(0, steps[0], step, 0)
-    for k, out in enumerate((kept, first, second, third)):
+    for k, out in enumerate(outs):
         for z in range(2):
-            block = pl.ds(jnp.bitwise_xor(ids[2], 2 * k + z) * 2, 2)
-            out[2 * z : 2 * z + 2] = total[block].astype(out.dtype)
+            block = total[pl.ds(jnp.bitwise_xor(ids[2], 2 * k + z) * 2, 2)]
+            out[2 * z * TILE : 2 * (z + 1) * TILE] = block.reshape(2 * TILE, TILE).astype(out.dtype)
 
 
 def tiles_backward(steps, ids, picked, held, sources, n_back):
-    shape = (n_back // 4, TILE, TILE)
+    rows = n_back // 4 * TILE
     return pl.pallas_call(
         backward_kernel,
-        out_shape=[pltpu.VMEM(shape, F32)] + [pltpu.VMEM(shape, BF16)] * 3,
+        out_shape=[pltpu.VMEM((rows, TILE), F32), pltpu.VMEM((TILE + 8, TILE), F32)]
+        + [pltpu.VMEM((rows + TILE + 16, TILE), BF16)] * 3,
         in_specs=[SMEM, SMEM, SMEM] + [VMEM] * (1 + len(sources)),
-        out_specs=[VMEM] * 4,
+        out_specs=[VMEM] * 5,
         scratch_shapes=[
             pltpu.VMEM((4 * len(sources), TILE, TILE), BF16),
             pltpu.VMEM((n_back + 1, TILE, TILE), F32),
@@ -437,15 +474,7 @@
     message[0:rows] = value.astype(BF16).reshape(rows, TILE)
     half = pl.ds((ids[1] & 1) * (TILE // 2), TILE // 2)
     message[rows : rows + TILE // 2] = (grads[half] + more[half]).astype(BF16)
-    rest = grads[TILE : TILE + 8] + more[TILE : TILE + 8]
-    rest = jnp.concatenate([rest, rest], 0)
-    line = iota(rest.shape, 0)
-    terms = jnp.zeros(rest.shape, F32)
-    for k in range(3):
-        term = rest.astype(BF16).astype(F32)
-        terms = jnp.where(line == k, term, terms)
-        rest = rest - term
-    message[rows + TILE // 2 : rows + TILE // 2 + 16] = terms.astype(BF16)
+    write_terms(grads[TILE : TILE + 8] + more[TILE : TILE + 8], message, rows + TILE // 2)
 
 
 def message(ids, back, other, grads, more):
@@ -460,75 +489,68 @@
     )(scalar(ids), near(back), near(other), near(grads), near(more))
 
 
-def grad_kernel(ids, *refs):
-    messages, grads = refs[:-1], refs[-1]
-    last = messages[0].shape[0] - 16
-    for k in range(2):
-        weight = jnp.zeros((TILE // 2, TILE), F32)
-        for one in messages[k::2]:
-            weight = weight + one[last - TILE // 2 : last].astype(F32)
-        grads[pl.ds(jnp.bitwise_xor(ids[1] & 1, k) * (TILE // 2), TILE // 2)] = weight
-    bias = jnp.zeros((16, TILE), F32)
-    for one in messages[0::2]:
-        bias = bias + one[last : last + 16].astype(F32)
-    grads[TILE : TILE + 8] = jnp.broadcast_to(jnp.sum(bias, axis=0, keepdims=True), (8, TILE))
-
-
-def grad_sum(ids, messages):
-    return pl.pallas_call(
-        grad_kernel,
-        out_shape=pltpu.VMEM((TILE + 8, TILE), F32),
-        in_specs=[SMEM] + [VMEM] * len(messages),
-        out_specs=VMEM,
-        compiler_params=PARAMS,
-        name="grad_sum",
-    )(scalar(ids), *[near(one) for one in messages])
-
-
-def line_kernel(kept, a, b, c, own, own_sent, other_sent):
-    blocks = own.shape[0]
-    value = kept[...] + a[...].astype(F32) + b[...].astype(F32) + c[...].astype(F32)
-    own[...] = value[:blocks]
-    own_sent[...] = value[:blocks].astype(BF16)
-    other_sent[...] = value[blocks:].astype(BF16)
-
-
-def line_sum(kept, others):
-    shape = (kept.shape[0] // 2, TILE, TILE)
+def line_kernel(kept, grads, a, b, c, own, own_grads, own_sent, other_sent, other_message):
+    rows = own.shape[0]
+    value = kept[...]
+    weight = grads[0:TILE]
+    for one in (a, b, c):
+        value = value + one[0 : 2 * rows].astype(F32)
+        weight = weight + one[2 * rows : 2 * rows + TILE].astype(F32)
+    bias = grads[TILE : TILE + 8] + read_terms((a, b, c), 2 * rows + TILE)
+    own[...] = value[:rows]
+    own_sent[...] = value[:rows].astype(BF16)
+    other = value[rows:].astype(BF16)
+    other_sent[...] = other
+    own_grads[0:TILE] = weight
+    own_grads[TILE : TILE + 8] = bias
+    other_message[0:rows] = other
+    other_message[rows : rows + TILE] = weight.astype(BF16)
+    write_terms(bias, other_message, rows + TILE)
+
+
+def line_sum(kept, grads, messages):
+    rows = kept.shape[0] // 2
     return pl.pallas_call(
         line_kernel,
-        out_shape=[pltpu.VMEM(shape, F32), pltpu.VMEM(shape, BF16), pltpu.VMEM(shape, BF16)],
-        in_specs=[VMEM] * 4,
-        out_specs=[VMEM] * 3,
+        out_shape=[
+            pltpu.VMEM((rows, TILE), F32),
+            pltpu.VMEM(grads.shape, F32),
+            pltpu.VMEM((rows, TILE), BF16),
+            pltpu.VMEM((rows, TILE), BF16),
+            pltpu.VMEM((rows + TILE + 16, TILE), BF16),
+        ],
+        in_specs=[VMEM] * 5,
+        out_specs=[VMEM] * 5,
         compiler_params=PARAMS,
         name="line_sum",
-    )(near(kept), *[near(values) for values in others])
-
-
-def finish_kernel(ids, own, beside, opposite, corner, grads, more, features, weight, bias):
-    blocks = own.shape[0]
-    for b in range(blocks):
-        mine = own[b] + beside[b].astype(F32)
-        other = opposite[b].astype(F32) + corner[b].astype(F32)
-        features[pl.ds((ids[0] * blocks + b) * TILE, TILE)] = mine.T
-        features[pl.ds(((1 - ids[0]) * blocks + b) * TILE, TILE)] = other.T
-    weight[...] = grads[0:TILE] + more[0:TILE]
-    bias[...] = grads[TILE : TILE + 1] + more[TILE : TILE + 1]
-
-
-def finish(ids, own, beside, opposite, corner, grads, more):
+    )(near(kept), near(grads), *[near(one) for one in messages])
+
+
+def finish_kernel(ids, own, grads, beside, opposite, corner, features, weight, bias):
+    rows = own.shape[0]
+    for b in range(rows // TILE):
+        block = pl.ds(b * TILE, TILE)
+        mine = own[block] + beside[block].astype(F32)
+        other = opposite[block].astype(F32) + corner[block].astype(F32)
+        features[pl.ds(ids[0] * rows + b * TILE, TILE)] = mine.T
+        features[pl.ds((1 - ids[0]) * rows + b * TILE, TILE)] = other.T
+    weight[...] = grads[0:TILE] + beside[rows : rows + TILE].astype(F32)
+    bias[...] = (grads[TILE : TILE + 8] + read_terms((beside,), rows + TILE))[0:1]
+
+
+def finish(ids, own, grads, beside, opposite, corner):
     return pl.pallas_call(
         finish_kernel,
         out_shape=[
-            jax.ShapeDtypeStruct((2 * own.shape[0] * TILE, TILE), F32),
+            jax.ShapeDtypeStruct((2 * own.shape[0], TILE), F32),
             jax.ShapeDtypeStruct((TILE, TILE), F32),
             jax.ShapeDtypeStruct((1, TILE), F32),
         ],
-        in_specs=[SMEM] + [VMEM] * 6,
+        in_specs=[SMEM] + [VMEM] * 5,
         out_specs=[VMEM] * 3,
         compiler_params=PARAMS,
         name="finish",
-    )(scalar(ids), near(own), near(beside), near(opposite), near(corner), near(grads), near(more))
+    )(scalar(ids), near(own), near(grads), near(beside), near(opposite), near(corner))
 
 
 def local(
@@ -553,7 +575,7 @@
 
     held, kept, sent = tiles_forward(steps, ids, fetched, forward, tiles, early, [pair, *sources], n_out)
     first, *others = pair_sum(kept, swap(sent, "col", 1))
-    others = [swap(other, "col", 2 * k + 2) for k, other in enumerate(others)]
+    others = swap_line(others, "col")
     own, sent = own_sum(first, others)
     sent, slots = lax.optimization_barrier((sent, slots))
     ready = prepare(
@@ -563,27 +585,21 @@
     backward, steps, weight, bias, cotangent = ready
     activations, back, back_sent, grads = middle(own, other, weight, bias, cotangent)
 
-    grads = grads + swap(grads, "col", 1)
-    back_other, more = lax.optimization_barrier((swap(back_sent, "feat", 1), swap(grads, "row", 1)))
+    back_other, more = lax.optimization_barrier((swap(back_sent, "feat", 1), swap(grads, "col", 1)))
     mine = message(ids, back, back_other, grads, more)
     across = [swap(mine, "col", mask) for mask in (2, 6, 4)]
     beside = swap(mine, "col", 1)
     across = lax.optimization_barrier(across)
     corners = [swap(values, "col", 1) for values in across]
     sources = [mine, beside, across[0], corners[0], across[2], corners[2], across[1], corners[1]]
-    grads = grad_sum(ids, sources)
-    more = swap(grads, "row", 2)
-    kept, *others = tiles_backward(steps, ids, backward, held, sources, n_back)
-    others, more = lax.optimization_barrier((others, more))
-    grads = grads + more
-
-    others = [swap(other, "row", 2 * k + 2) for k, other in enumerate(others)]
-    others, more = lax.optimization_barrier((others, swap(grads, "row", 4)))
-    own, own_sent, other_sent = line_sum(kept, others)
+    kept, grads, *others = tiles_backward(steps, ids, backward, held, sources, n_back)
+
+    others = swap_line(others, "row")
+    own, grads, own_sent, other_sent, other_message = line_sum(kept, grads, others)
     opposite = swap(own_sent, "feat", 1)
     corner = swap(other_sent, ("row", "feat"), 3)
-    beside = swap(other_sent, "row", 1)
-    grad_features, grad_weight, grad_bias = finish(ids, own, beside, opposite, corner, grads, more)
+    beside = swap(other_message, "row", 1)
+    grad_features, grad_weight, grad_bias = finish(ids, own, grads, beside, opposite, corner)
     return (activations, grad_features, grad_weight, grad_bias[0])
 
 

time: 95.2 us -> 90.2 us (0.947); the launches traced: 94.5 us -> 90.7 us
  starting transfers between devices: 41.5 us -> 36 us
  waiting for transfers between devices: 35.9 us -> 39.9 us
  Pallas kernels: 14.6 us -> 12.5 us
    ppermute x27 -> x24, starting transfers between devices: 41.5 us -> 36 us  [swap(): return lax.ppermute(values, axis, [(i, i ^ mask) for i in range(size)])]
    ppermute x27 -> x24, waiting for transfers between devices: 35.9 us -> 39.9 us  [swap(): return lax.ppermute(values, axis, [(i, i ^ mask) for i in range(size)])]
    pallas_call x1, Pallas kernels: 3.53 us -> 1.76 us  [early_tiles(): pl.pallas_call(early_kernel, out_shape=pltpu.VMEM((EARLY * PER + 1, TILE,...]
  transfers between devices with their start and end apart: 27 -> 24, of which waited for: 19 -> 18; matrix products, arithmetic and copies ran while one was open for 0% -> 0% of each run, Pallas kernels for 11% -> 8%
where the time goes in v4:
time: 90.2 us; the launch traced here: 90.7 us
  waiting for transfers between devices  39.9 us (44%)
  starting transfers between devices  36 us (40%)
  Pallas kernels  12.5 us (14%)
  between operations  1.41 us (2%)
    ppermute x24, waiting for transfers between devices, swap(): return lax.ppermute(values, axis, [(i, i ^ mask) for i in range(size)])  39.9 us
    ppermute x24, starting transfers between devices, swap(): return lax.ppermute(values, axis, [(i, i ^ mask) for i in range(size)])  36 us
    pallas_call x1, Pallas kernels, pick(): pl.pallas_call(functools.partial(pick_kernel, n_out), out_shape=[pltpu.SM...  2.87 us
    pallas_call x1, Pallas kernels, prepare(): pl.pallas_call(functools.partial(prepare_kernel, n_back), out_shape=[pltp...  2.59 us
  transfers between devices with their start and end apart: 24, of which 18 were waited for; matrix products, arithmetic and copies ran while one was open for 0% of the time, Pallas kernels for 8%

profile of v4, /device:TPU:0, one launch (start us, length us, event | category | flops | bytes accessed | tf_op | source)
XLA Modules:
  0.0 90.7 jit_solution(11478340732916951670)
XLA Ops:
  0.6 0.0 copy-start
  0.7 0.9 copy-done
  1.5 2.0 %collective-permute-start = (bf16[256,128]{1,0:T(8,128)(2,1)S(1)}, bf16[256,128]{1,0:T(8,128)(2,1)S(1)}, u32[]{:S(2)}, u32[]{:S(2)}) collective-permute-start(bf16[256,128]{1,0:T(8,128)(2,1)S(1)} %constant_dynamic-slice_fusion.a), channel_id=1, source_target_pairs={{0,16},{16,0},{32,48},{48,32},{64,80},{80,64},{96,112},{112,96},{1... | collective-permute-start | bytes 196616 | tf_op jit(solution)/shard_map/ppermute | solution.py:27
  4.2 0.1 pad_add_fusion.ids
  4.3 2.9 %pick_tiles.1 = (s32[1,768]{1,0:T(1,128)S(4)}, s32[1,768]{1,0:T(1,128)S(4)}, s32[1]{0:T(128)S(4)}, s32[3]{0:T(128)S(4)}, s32[1,640]{1,0:T(1,128)S(1)}) custom-call(s32[1,1]{1,0:T(1,128)S(6)} %copy.12.count, s32[3]{0:T(128)S(1)} %pad_add_fusion.ids, s32[1,1,640]{2,1,0:T(1,128)} %rows.3, s32[1,1,640]{2,1,0:T(1,128)} %columns.3), custom_call_target="tpu_custom_call" | custom-call | tf_op jit(solution)/shard_map/pick_tiles/pallas_call | solution.py:118
  7.2 0.0 collective-permute-done.b
  7.2 3.1 %collective-permute-start.3 = (bf16[512,128]{1,0:T(8,128)(2,1)S(1)}, bf16[512,128]{1,0:T(8,128)(2,1)S(1)}, u32[]{:S(2)}, u32[]{:S(2)}) collective-permute-start(bf16[512,128]{1,0:T(8,128)(2,1)S(1)} %join.1.refs_0_), channel_id=1, source_target_pairs={{0,96},{16,112},{32,64},{48,80},{64,32},{80,48},{96,0},{112,16},{1... | collective-permute-start | bytes 393224 | tf_op jit(solution)/shard_map/ppermute | solution.py:27
  10.3 0.6 collective-permute-start.2
  10.9 0.4 collective-permute-start.1
  11.4 1.8 %early_tiles.1.early = bf16[129,128,128]{2,1,0:T(8,128)(2,1)S(1)} custom-call(s32[1]{0:T(128)S(4)} %get-tuple-element.68.steps, s32[1,768]{1,0:T(1,128)S(4)} %get-tuple-element.70.fetched, bf16[640,128,128]{2,1,0:T(8,128)(2,1)} %bitcast.6), custom_call_target="tpu_custom_call" | custom-call | tf_op jit(solution)/shard_map/early_tiles/pallas_call | solution.py:162
  13.1 2.5 %collective-permute-done.3.refs_3_ = bf16[512,128]{1,0:T(8,128)(2,1)S(1)} collective-permute-done((bf16[512,128]{1,0:T(8,128)(2,1)S(1)}, bf16[512,128]{1,0:T(8,128)(2,1)S(1)}, u32[]{:S(2)}, u32[]{:S(2)}) %collective-permute-start.3) | collective-permute-done | bytes 131104 | tf_op jit(solution)/shard_map/ppermute | solution.py:27
  15.6 2.3 %collective-permute-done.2.refs_2_ = bf16[512,128]{1,0:T(8,128)(2,1)S(1)} collective-permute-done((bf16[512,128]{1,0:T(8,128)(2,1)S(1)}, bf16[512,128]{1,0:T(8,128)(2,1)S(1)}, u32[]{:S(2)}, u32[]{:S(2)}) %collective-permute-start.2) | collective-permute-done | bytes 131104 | tf_op jit(solution)/shard_map/ppermute | solution.py:27
  17.9 0.0 collective-permute-done.1.refs_1_
  17.9 1.7 %tiles_forward.1 = (bf16[673,128,128]{2,1,0:T(8,128)(2,1)S(1)}, f32[4,4,128,128]{3,2,1,0:T(8,128)S(1)}, bf16[4,4,128,128]{3,2,1,0:T(8,128)(2,1)S(1)}) custom-call(s32[1]{0:T(128)S(4)} %get-tuple-element.68.steps, s32[3]{0:T(128)S(4)} %get-tuple-element.69.ids, s32[1,768]{1,0:T(1,128)S(4)} %get-tuple-element.70.fetched, ...), custom_call_target="tpu_custom_call" | custom-call | tf_op jit(solution)/shard_map/tiles_forward/pallas_call | solution.py:302
  19.5 0.1 collective-permute-start.4
  19.6 1.9 %collective-permute-done.4.got = bf16[4,4,128,128]{3,2,1,0:T(8,128)(2,1)S(1)} collective-permute-done((bf16[4,4,128,128]{3,2,1,0:T(8,128)(2,1)S(1)}, bf16[4,4,128,128]{3,2,1,0:T(8,128)(2,1)S(1)}, u32[]{:S(2)}, u32[]{:S(2)}) %collective-permute-start.4) | collective-permute-done | bytes 524320 | tf_op jit(solution)/shard_map/ppermute | solution.py:27
  21.5 0.1 pair_sum.1
  21.6 2.0 %collective-permute-start.5 = (bf16[4,128,128]{2,1,0:T(8,128)(2,1)S(1)}, bf16[4,128,128]{2,1,0:T(8,128)(2,1)S(1)}, u32[]{:S(2)}, u32[]{:S(2)}) collective-permute-start(bf16[4,128,128]{2,1,0:T(8,128)(2,1)S(1)} %get-tuple-element.80), channel_id=1, source_target_pairs={{0,4},{2,6},{4,0},{6,2},{8,12},{10,14},{12,8},{14,10},{1,5},{3,7},... | collective-permute-start | bytes 393224 | tf_op jit(solution)/shard_map/ppermute | solution.py:27
  23.6 2.7 %collective-permute-start.6 = (bf16[4,128,128]{2,1,0:T(8,128)(2,1)S(1)}, bf16[4,128,128]{2,1,0:T(8,128)(2,1)S(1)}, u32[]{:S(2)}, u32[]{:S(2)}) collective-permute-start(bf16[4,128,128]{2,1,0:T(8,128)(2,1)S(1)} %get-tuple-element.81), channel_id=1, source_target_pairs={{0,8},{2,10},{4,12},{6,14},{8,0},{10,2},{12,4},{14,6},{1,9},{3,11}... | collective-permute-start | bytes 393224 | tf_op jit(solution)/shard_map/ppermute | solution.py:27
  26.4 0.0 collective-permute-start.7
  26.4 1.4 %collective-permute-done.5.a = bf16[4,128,128]{2,1,0:T(8,128)(2,1)S(1)} collective-permute-done((bf16[4,128,128]{2,1,0:T(8,128)(2,1)S(1)}, bf16[4,128,128]{2,1,0:T(8,128)(2,1)S(1)}, u32[]{:S(2)}, u32[]{:S(2)}) %collective-permute-start.5) | collective-permute-done | bytes 131104 | tf_op jit(solution)/shard_map/ppermute | solution.py:27
  27.8 5.0 %collective-permute-done.6.b = bf16[4,128,128]{2,1,0:T(8,128)(2,1)S(1)} collective-permute-done((bf16[4,128,128]{2,1,0:T(8,128)(2,1)S(1)}, bf16[4,128,128]{2,1,0:T(8,128)(2,1)S(1)}, u32[]{:S(2)}, u32[]{:S(2)}) %collective-permute-start.6) | collective-permute-done | bytes 131104 | tf_op jit(solution)/shard_map/ppermute | solution.py:27
  32.8 2.2 %collective-permute-done.7.c = bf16[4,128,128]{2,1,0:T(8,128)(2,1)S(1)} collective-permute-done((bf16[4,128,128]{2,1,0:T(8,128)(2,1)S(1)}, bf16[4,128,128]{2,1,0:T(8,128)(2,1)S(1)}, u32[]{:S(2)}, u32[]{:S(2)}) %collective-permute-start.7) | collective-permute-done | bytes 131104 | tf_op jit(solution)/shard_map/ppermute | solution.py:27
  35.0 0.1 own_sum.1
  35.1 3.7 %collective-permute-start.8 = (bf16[4,128,128]{2,1,0:T(8,128)(2,1)S(1)}, bf16[4,128,128]{2,1,0:T(8,128)(2,1)S(1)}, u32[]{:S(2)}, u32[]{:S(2)}) collective-permute-start(bf16[4,128,128]{2,1,0:T(8,128)(2,1)S(1)} %get-tuple-element.86), channel_id=1, source_target_pairs={{0,1},{1,0},{2,3},{3,2},{4,5},{5,4},{6,7},{7,6},{8,9},{9,8},{10,11... | collective-permute-start | bytes 393224 | tf_op jit(solution)/shard_map/ppermute | solution.py:27
  38.8 2.6 %prepare.1 = (s32[1,768]{1,0:T(1,128)S(4)}, s32[1]{0:T(128)S(4)}, bf16[128,128]{1,0:T(8,128)(2,1)S(1)}, f32[1,128]{1,0:T(1,128)S(1)}, bf16[512,128]{1,0:T(8,128)(2,1)S(1)}) custom-call(s32[3]{0:T(128)S(4)} %get-tuple-element.69.ids, s32[1,1,640]{2,1,0:T(1,128)} %rows.3, s32[1,1,640]{2,1,0:T(1,128)} %columns.3, s32[1,640]{1,0:T(1,128)S(1)} %get-tuple-element.87.slots, ...), custom_call_target="tpu_custom_call" | custom-call | tf_op jit(solution)/shard_map/prepare/pallas_call | solution.py:208
  41.4 0.6 collective-permute-done.8.other
  41.9 0.9 middle.1
  42.8 3.3 %collective-permute-start.9 = (bf16[4,128,128]{2,1,0:T(8,128)(2,1)S(1)}, bf16[4,128,128]{2,1,0:T(8,128)(2,1)S(1)}, u32[]{:S(2)}, u32[]{:S(2)}) collective-permute-start(bf16[4,128,128]{2,1,0:T(8,128)(2,1)S(1)} %get-tuple-element.102), channel_id=1, source_target_pairs={{0,1},{1,0},{2,3},{3,2},{4,5},{5,4},{6,7},{7,6},{8,9},{9,8},{10,11... | collective-permute-start | bytes 393224 | tf_op jit(solution)/shard_map/ppermute | solution.py:27
  46.1 0.0 collective-permute-start.10
  46.1 1.3 %collective-permute-done.10.more = f32[136,128]{1,0:T(8,128)S(1)} collective-permute-done((f32[136,128]{1,0:T(8,128)S(1)}, f32[136,128]{1,0:T(8,128)S(1)}, u32[]{:S(2)}, u32[]{:S(2)}) %collective-permute-start.10) | collective-permute-done | bytes 69664 | tf_op jit(solution)/shard_map/ppermute | solution.py:27
  47.4 1.9 %collective-permute-done.9.other = bf16[4,128,128]{2,1,0:T(8,128)(2,1)S(1)} collective-permute-done((bf16[4,128,128]{2,1,0:T(8,128)(2,1)S(1)}, bf16[4,128,128]{2,1,0:T(8,128)(2,1)S(1)}, u32[]{:S(2)}, u32[]{:S(2)}) %collective-permute-start.9) | collective-permute-done | bytes 131104 | tf_op jit(solution)/shard_map/ppermute | solution.py:27
  49.3 0.1 collective-permute-start.14
  49.4 1.8 %collective-permute-start.13 = (bf16[592,128]{1,0:T(8,128)(2,1)S(1)}, bf16[592,128]{1,0:T(8,128)(2,1)S(1)}, u32[]{:S(2)}, u32[]{:S(2)}) collective-permute-start(bf16[592,128]{1,0:T(8,128)(2,1)S(1)} %message.1.refs_0_), channel_id=1, source_target_pairs={{0,12},{2,14},{4,8},{6,10},{8,4},{10,6},{12,0},{14,2},{1,13},{3,15... | collective-permute-start | bytes 454664 | tf_op jit(solution)/shard_map/ppermute | solution.py:27
  51.2 1.7 %collective-permute-start.12 = (bf16[592,128]{1,0:T(8,128)(2,1)S(1)}, bf16[592,128]{1,0:T(8,128)(2,1)S(1)}, u32[]{:S(2)}, u32[]{:S(2)}) collective-permute-start(bf16[592,128]{1,0:T(8,128)(2,1)S(1)} %message.1.refs_0_), channel_id=1, source_target_pairs={{0,4},{2,6},{4,0},{6,2},{8,12},{10,14},{12,8},{14,10},{1,5},{3,7},... | collective-permute-start | bytes 454664 | tf_op jit(solution)/shard_map/ppermute | solution.py:27
  52.9 0.0 collective-permute-start.11
  52.9 3.8 %collective-permute-done.14.refs_4_ = bf16[592,128]{1,0:T(8,128)(2,1)S(1)} collective-permute-done((bf16[592,128]{1,0:T(8,128)(2,1)S(1)}, bf16[592,128]{1,0:T(8,128)(2,1)S(1)}, u32[]{:S(2)}, u32[]{:S(2)}) %collective-permute-start.14) | collective-permute-done | bytes 151584 | tf_op jit(solution)/shard_map/ppermute | solution.py:27
  56.8 1.3 %collective-permute-done.13.refs_6_ = bf16[592,128]{1,0:T(8,128)(2,1)S(1)} collective-permute-done((bf16[592,128]{1,0:T(8,128)(2,1)S(1)}, bf16[592,128]{1,0:T(8,128)(2,1)S(1)}, u32[]{:S(2)}, u32[]{:S(2)}) %collective-permute-start.13) | collective-permute-done | bytes 151584 | tf_op jit(solution)/shard_map/ppermute | solution.py:27
  58.1 0.0 collective-permute-done.12.refs_2_
  58.1 0.0 collective-permute-start.15
  58.1 0.5 collective-permute-start.16
  58.6 0.0 collective-permute-start.17
  58.6 0.0 collective-permute-done.11.refs_1_
  58.6 0.9 collective-permute-done.15.refs_3_
  59.5 0.2 collective-permute-done.16.refs_5_
  59.7 0.3 collective-permute-done.17.refs_7_
  60.0 1.5 %tiles_backward.1 = (f32[512,128]{1,0:T(8,128)S(1)}, f32[136,128]{1,0:T(8,128)S(1)}, bf16[656,128]{1,0:T(8,128)(2,1)S(1)}, bf16[656,128]{1,0:T(8,128)(2,1)S(1)}, bf16[656,128]{1,0:T(8,128)(2,1)S(1)}) custom-call(s32[1]{0:T(128)S(4)} %get-tuple-element.98.steps, s32[3]{0:T(128)S(4)} %get-tuple-element.69.ids, s32[1,768]{1,0:T(1,128)S(4)} %get-tuple-element.99.picked, ...), custom_call_target="tpu_custom_call" | custom-call | tf_op jit(solution)/shard_map/tiles_backward/pallas_call | solution.py:379
  61.5 0.2 collective-permute-start.18
  61.7 8.9 %collective-permute-start.19 = (bf16[656,128]{1,0:T(8,128)(2,1)S(1)}, bf16[656,128]{1,0:T(8,128)(2,1)S(1)}, u32[]{:S(2)}, u32[]{:S(2)}) collective-permute-start(bf16[656,128]{1,0:T(8,128)(2,1)S(1)} %get-tuple-element.112), channel_id=1, source_target_pairs={{0,64},{16,80},{32,96},{48,112},{64,0},{80,16},{96,32},{112,48},{1... | collective-permute-start | bytes 503816 | tf_op jit(solution)/shard_map/ppermute | solution.py:27
  70.6 0.0 collective-permute-start.20
  70.6 0.0 collective-permute-done.18.a
  70.6 8.5 %collective-permute-done.19.b = bf16[656,128]{1,0:T(8,128)(2,1)S(1)} collective-permute-done((bf16[656,128]{1,0:T(8,128)(2,1)S(1)}, bf16[656,128]{1,0:T(8,128)(2,1)S(1)}, u32[]{:S(2)}, u32[]{:S(2)}) %collective-permute-start.19) | collective-permute-done | bytes 167968 | tf_op jit(solution)/shard_map/ppermute | solution.py:27
  79.2 2.6 %collective-permute-done.20.c = bf16[656,128]{1,0:T(8,128)(2,1)S(1)} collective-permute-done((bf16[656,128]{1,0:T(8,128)(2,1)S(1)}, bf16[656,128]{1,0:T(8,128)(2,1)S(1)}, u32[]{:S(2)}, u32[]{:S(2)}) %collective-permute-start.20) | collective-permute-done | bytes 167968 | tf_op jit(solution)/shard_map/ppermute | solution.py:27
  81.8 0.1 line_sum.1
  81.9 0.1 collective-permute-start.21
  82.0 2.4 %collective-permute-start.22 = (bf16[256,128]{1,0:T(8,128)(2,1)S(1)}, bf16[256,128]{1,0:T(8,128)(2,1)S(1)}, u32[]{:S(2)}, u32[]{:S(2)}) collective-permute-start(bf16[256,128]{1,0:T(8,128)(2,1)S(1)} %get-tuple-element.117), channel_id=1, source_target_pairs={{0,1},{1,0},{2,3},{3,2},{4,5},{5,4},{6,7},{7,6},{8,9},{9,8},{10,11... | collective-permute-start | bytes 196616 | tf_op jit(solution)/shard_map/ppermute | solution.py:27
  84.4 2.3 %collective-permute-start.23 = (bf16[256,128]{1,0:T(8,128)(2,1)S(1)}, bf16[256,128]{1,0:T(8,128)(2,1)S(1)}, u32[]{:S(2)}, u32[]{:S(2)}) collective-permute-start(bf16[256,128]{1,0:T(8,128)(2,1)S(1)} %get-tuple-element.118), channel_id=1, source_target_pairs={{0,17},{1,16},{16,1},{17,0},{32,49},{33,48},{48,33},{49,32},{64,81... | collective-permute-start | bytes 196616 | tf_op jit(solution)/shard_map/ppermute | solution.py:27
  86.7 1.5 %collective-permute-done.22.opposite = bf16[256,128]{1,0:T(8,128)(2,1)S(1)} collective-permute-done((bf16[256,128]{1,0:T(8,128)(2,1)S(1)}, bf16[256,128]{1,0:T(8,128)(2,1)S(1)}, u32[]{:S(2)}, u32[]{:S(2)}) %collective-permute-start.22) | collective-permute-done | bytes 65568 | tf_op jit(solution)/shard_map/ppermute | solution.py:27
  88.2 1.7 %collective-permute-done.23.corner = bf16[256,128]{1,0:T(8,128)(2,1)S(1)} collective-permute-done((bf16[256,128]{1,0:T(8,128)(2,1)S(1)}, bf16[256,128]{1,0:T(8,128)(2,1)S(1)}, u32[]{:S(2)}, u32[]{:S(2)}) %collective-permute-start.23) | collective-permute-done | bytes 65568 | tf_op jit(solution)/shard_map/ppermute | solution.py:27
  89.8 0.0 collective-permute-done.21.beside
  89.8 0.9 finish.1
  (3 shorter events, 0.1 us)
Async XLA Ops:
  0.6 0.9 %copy-start = (bf16[512,128]{1,0:T(8,128)(2,1)S(1)}, bf16[512,128]{1,0:T(8,128)(2,1)}, u32[]{:S(2)}) copy-start(bf16[512,128]{1,0:T(8,128)(2,1)} %param.8) | copy-start | bytes 393220
  1.5 5.6 %collective-permute-start = (bf16[256,128]{1,0:T(8,128)(2,1)S(1)}, bf16[256,128]{1,0:T(8,128)(2,1)S(1)}, u32[]{:S(2)}, u32[]{:S(2)}) collective-permute-start(bf16[256,128]{1,0:T(8,128)(2,1)S(1)} %constant_dynamic-slice_fusion.a), channel_id=1, source_target_pairs={{0,16},{16,0},{32,48},{48,32},{64,80},{80,64},{96,112},{112,96},{1... | collective-permute-start | bytes 196616 | tf_op jit(solution)/shard_map/ppermute | solution.py:27
  7.2 8.4 %collective-permute-start.3 = (bf16[512,128]{1,0:T(8,128)(2,1)S(1)}, bf16[512,128]{1,0:T(8,128)(2,1)S(1)}, u32[]{:S(2)}, u32[]{:S(2)}) collective-permute-start(bf16[512,128]{1,0:T(8,128)(2,1)S(1)} %join.1.refs_0_), channel_id=1, source_target_pairs={{0,96},{16,112},{32,64},{48,80},{64,32},{80,48},{96,0},{112,16},{1... | collective-permute-start | bytes 393224 | tf_op jit(solution)/shard_map/ppermute | solution.py:27
  10.3 7.6 %collective-permute-start.2 = (bf16[512,128]{1,0:T(8,128)(2,1)S(1)}, bf16[512,128]{1,0:T(8,128)(2,1)S(1)}, u32[]{:S(2)}, u32[]{:S(2)}) collective-permute-start(bf16[512,128]{1,0:T(8,128)(2,1)S(1)} %join.1.refs_0_), channel_id=1, source_target_pairs={{0,64},{16,80},{32,96},{48,112},{64,0},{80,16},{96,32},{112,48},{1... | collective-permute-start | bytes 393224 | tf_op jit(solution)/shard_map/ppermute | solution.py:27
  10.9 7.0 %collective-permute-start.1 = (bf16[512,128]{1,0:T(8,128)(2,1)S(1)}, bf16[512,128]{1,0:T(8,128)(2,1)S(1)}, u32[]{:S(2)}, u32[]{:S(2)}) collective-permute-start(bf16[512,128]{1,0:T(8,128)(2,1)S(1)} %join.1.refs_0_), channel_id=1, source_target_pairs={{0,32},{16,48},{32,0},{48,16},{64,96},{80,112},{96,64},{112,80},{1... | collective-permute-start | bytes 393224 | tf_op jit(solution)/shard_map/ppermute | solution.py:27
  19.5 2.0 %collective-permute-start.4 = (bf16[4,4,128,128]{3,2,1,0:T(8,128)(2,1)S(1)}, bf16[4,4,128,128]{3,2,1,0:T(8,128)(2,1)S(1)}, u32[]{:S(2)}, u32[]{:S(2)}) collective-permute-start(bf16[4,4,128,128]{3,2,1,0:T(8,128)(2,1)S(1)} %get-tuple-element.78), channel_id=1, source_target_pairs={{0,2},{2,0},{4,6},{6,4},{8,10},{10,8},{12,14},{14,12},{1,3},{3,1},... | collective-permute-start | bytes 1572872 | tf_op jit(solution)/shard_map/ppermute | solution.py:27
  21.6 6.2 %collective-permute-start.5 = (bf16[4,128,128]{2,1,0:T(8,128)(2,1)S(1)}, bf16[4,128,128]{2,1,0:T(8,128)(2,1)S(1)}, u32[]{:S(2)}, u32[]{:S(2)}) collective-permute-start(bf16[4,128,128]{2,1,0:T(8,128)(2,1)S(1)} %get-tuple-element.80), channel_id=1, source_target_pairs={{0,4},{2,6},{4,0},{6,2},{8,12},{10,14},{12,8},{14,10},{1,5},{3,7},... | collective-permute-start | bytes 393224 | tf_op jit(solution)/shard_map/ppermute | solution.py:27
  23.6 9.2 %collective-permute-start.6 = (bf16[4,128,128]{2,1,0:T(8,128)(2,1)S(1)}, bf16[4,128,128]{2,1,0:T(8,128)(2,1)S(1)}, u32[]{:S(2)}, u32[]{:S(2)}) collective-permute-start(bf16[4,128,128]{2,1,0:T(8,128)(2,1)S(1)} %get-tuple-element.81), channel_id=1, source_target_pairs={{0,8},{2,10},{4,12},{6,14},{8,0},{10,2},{12,4},{14,6},{1,9},{3,11}... | collective-permute-start | bytes 393224 | tf_op jit(solution)/shard_map/ppermute | solution.py:27
  26.4 8.7 %collective-permute-start.7 = (bf16[4,128,128]{2,1,0:T(8,128)(2,1)S(1)}, bf16[4,128,128]{2,1,0:T(8,128)(2,1)S(1)}, u32[]{:S(2)}, u32[]{:S(2)}) collective-permute-start(bf16[4,128,128]{2,1,0:T(8,128)(2,1)S(1)} %get-tuple-element.82), channel_id=1, source_target_pairs={{0,12},{2,14},{4,8},{6,10},{8,4},{10,6},{12,0},{14,2},{1,13},{3,15... | collective-permute-start | bytes 393224 | tf_op jit(solution)/shard_map/ppermute | solution.py:27
  35.1 6.8 %collective-permute-start.8 = (bf16[4,128,128]{2,1,0:T(8,128)(2,1)S(1)}, bf16[4,128,128]{2,1,0:T(8,128)(2,1)S(1)}, u32[]{:S(2)}, u32[]{:S(2)}) collective-permute-start(bf16[4,128,128]{2,1,0:T(8,128)(2,1)S(1)} %get-tuple-element.86), channel_id=1, source_target_pairs={{0,1},{1,0},{2,3},{3,2},{4,5},{5,4},{6,7},{7,6},{8,9},{9,8},{10,11... | collective-permute-start | bytes 393224 | tf_op jit(solution)/shard_map/ppermute | solution.py:27
  42.8 6.5 %collective-permute-start.9 = (bf16[4,128,128]{2,1,0:T(8,128)(2,1)S(1)}, bf16[4,128,128]{2,1,0:T(8,128)(2,1)S(1)}, u32[]{:S(2)}, u32[]{:S(2)}) collective-permute-start(bf16[4,128,128]{2,1,0:T(8,128)(2,1)S(1)} %get-tuple-element.102), channel_id=1, source_target_pairs={{0,1},{1,0},{2,3},{3,2},{4,5},{5,4},{6,7},{7,6},{8,9},{9,8},{10,11... | collective-permute-start | bytes 393224 | tf_op jit(solution)/shard_map/ppermute | solution.py:27
  46.1 1.3 %collective-permute-start.10 = (f32[136,128]{1,0:T(8,128)S(1)}, f32[136,128]{1,0:T(8,128)S(1)}, u32[]{:S(2)}, u32[]{:S(2)}) collective-permute-start(f32[136,128]{1,0:T(8,128)S(1)} %get-tuple-element.103.grads), channel_id=1, source_target_pairs={{0,2},{2,0},{4,6},{6,4},{8,10},{10,8},{12,14},{14,12},{1,3},{3,1},... | collective-permute-start | bytes 208904 | tf_op jit(solution)/shard_map/ppermute | solution.py:27
  49.3 7.4 %collective-permute-start.14 = (bf16[592,128]{1,0:T(8,128)(2,1)S(1)}, bf16[592,128]{1,0:T(8,128)(2,1)S(1)}, u32[]{:S(2)}, u32[]{:S(2)}) collective-permute-start(bf16[592,128]{1,0:T(8,128)(2,1)S(1)} %message.1.refs_0_), channel_id=1, source_target_pairs={{0,8},{2,10},{4,12},{6,14},{8,0},{10,2},{12,4},{14,6},{1,9},{3,11}... | collective-permute-start | bytes 454664 | tf_op jit(solution)/shard_map/ppermute | solution.py:27
  49.4 8.6 %collective-permute-start.13 = (bf16[592,128]{1,0:T(8,128)(2,1)S(1)}, bf16[592,128]{1,0:T(8,128)(2,1)S(1)}, u32[]{:S(2)}, u32[]{:S(2)}) collective-permute-start(bf16[592,128]{1,0:T(8,128)(2,1)S(1)} %message.1.refs_0_), channel_id=1, source_target_pairs={{0,12},{2,14},{4,8},{6,10},{8,4},{10,6},{12,0},{14,2},{1,13},{3,15... | collective-permute-start | bytes 454664 | tf_op jit(solution)/shard_map/ppermute | solution.py:27
  51.2 6.9 %collective-permute-start.12 = (bf16[592,128]{1,0:T(8,128)(2,1)S(1)}, bf16[592,128]{1,0:T(8,128)(2,1)S(1)}, u32[]{:S(2)}, u32[]{:S(2)}) collective-permute-start(bf16[592,128]{1,0:T(8,128)(2,1)S(1)} %message.1.refs_0_), channel_id=1, source_target_pairs={{0,4},{2,6},{4,0},{6,2},{8,12},{10,14},{12,8},{14,10},{1,5},{3,7},... | collective-permute-start | bytes 454664 | tf_op jit(solution)/shard_map/ppermute | solution.py:27
  52.9 5.7 %collective-permute-start.11 = (bf16[592,128]{1,0:T(8,128)(2,1)S(1)}, bf16[592,128]{1,0:T(8,128)(2,1)S(1)}, u32[]{:S(2)}, u32[]{:S(2)}) collective-permute-start(bf16[592,128]{1,0:T(8,128)(2,1)S(1)} %message.1.refs_0_), channel_id=1, source_target_pairs={{0,2},{2,0},{4,6},{6,4},{8,10},{10,8},{12,14},{14,12},{1,3},{3,1},... | collective-permute-start | bytes 454664 | tf_op jit(solution)/shard_map/ppermute | solution.py:27
  58.1 1.4 %collective-permute-start.15 = (bf16[592,128]{1,0:T(8,128)(2,1)S(1)}, bf16[592,128]{1,0:T(8,128)(2,1)S(1)}, u32[]{:S(2)}, u32[]{:S(2)}) collective-permute-start(bf16[592,128]{1,0:T(8,128)(2,1)S(1)} %collective-permute-done.12.refs_2_), channel_id=1, source_target_pairs={{0,2},{2,0},{4,6},{6,4},{8,10},{10,8},{12,14},{14,12},{1,3},{3,1},... | collective-permute-start | bytes 454664 | tf_op jit(solution)/shard_map/ppermute | solution.py:27
  58.1 1.6 %collective-permute-start.16 = (bf16[592,128]{1,0:T(8,128)(2,1)S(1)}, bf16[592,128]{1,0:T(8,128)(2,1)S(1)}, u32[]{:S(2)}, u32[]{:S(2)}) collective-permute-start(bf16[592,128]{1,0:T(8,128)(2,1)S(1)} %collective-permute-done.14.refs_4_), channel_id=1, source_target_pairs={{0,2},{2,0},{4,6},{6,4},{8,10},{10,8},{12,14},{14,12},{1,3},{3,1},... | collective-permute-start | bytes 454664 | tf_op jit(solution)/shard_map/ppermute | solution.py:27
  58.6 1.4 %collective-permute-start.17 = (bf16[592,128]{1,0:T(8,128)(2,1)S(1)}, bf16[592,128]{1,0:T(8,128)(2,1)S(1)}, u32[]{:S(2)}, u32[]{:S(2)}) collective-permute-start(bf16[592,128]{1,0:T(8,128)(2,1)S(1)} %collective-permute-done.13.refs_6_), channel_id=1, source_target_pairs={{0,2},{2,0},{4,6},{6,4},{8,10},{10,8},{12,14},{14,12},{1,3},{3,1},... | collective-permute-start | bytes 454664 | tf_op jit(solution)/shard_map/ppermute | solution.py:27
  61.5 9.1 %collective-permute-start.18 = (bf16[656,128]{1,0:T(8,128)(2,1)S(1)}, bf16[656,128]{1,0:T(8,128)(2,1)S(1)}, u32[]{:S(2)}, u32[]{:S(2)}) collective-permute-start(bf16[656,128]{1,0:T(8,128)(2,1)S(1)} %get-tuple-element.111), channel_id=1, source_target_pairs={{0,32},{16,48},{32,0},{48,16},{64,96},{80,112},{96,64},{112,80},{1... | collective-permute-start | bytes 503816 | tf_op jit(solution)/shard_map/ppermute | solution.py:27
  61.7 17.5 %collective-permute-start.19 = (bf16[656,128]{1,0:T(8,128)(2,1)S(1)}, bf16[656,128]{1,0:T(8,128)(2,1)S(1)}, u32[]{:S(2)}, u32[]{:S(2)}) collective-permute-start(bf16[656,128]{1,0:T(8,128)(2,1)S(1)} %get-tuple-element.112), channel_id=1, source_target_pairs={{0,64},{16,80},{32,96},{48,112},{64,0},{80,16},{96,32},{112,48},{1... | collective-permute-start | bytes 503816 | tf_op jit(solution)/shard_map/ppermute | solution.py:27
  70.6 11.2 %collective-permute-start.20 = (bf16[656,128]{1,0:T(8,128)(2,1)S(1)}, bf16[656,128]{1,0:T(8,128)(2,1)S(1)}, u32[]{:S(2)}, u32[]{:S(2)}) collective-permute-start(bf16[656,128]{1,0:T(8,128)(2,1)S(1)} %get-tuple-element.113), channel_id=1, source_target_pairs={{0,96},{16,112},{32,64},{48,80},{64,32},{80,48},{96,0},{112,16},{1... | collective-permute-start | bytes 503816 | tf_op jit(solution)/shard_map/ppermute | solution.py:27
  81.9 8.0 %collective-permute-start.21 = (bf16[400,128]{1,0:T(8,128)(2,1)S(1)}, bf16[400,128]{1,0:T(8,128)(2,1)S(1)}, u32[]{:S(2)}, u32[]{:S(2)}) collective-permute-start(bf16[400,128]{1,0:T(8,128)(2,1)S(1)} %get-tuple-element.116), channel_id=1, source_target_pairs={{0,16},{16,0},{32,48},{48,32},{64,80},{80,64},{96,112},{112,96},{1... | collective-permute-start | bytes 307208 | tf_op jit(solution)/shard_map/ppermute | solution.py:27
  82.0 6.2 %collective-permute-start.22 = (bf16[256,128]{1,0:T(8,128)(2,1)S(1)}, bf16[256,128]{1,0:T(8,128)(2,1)S(1)}, u32[]{:S(2)}, u32[]{:S(2)}) collective-permute-start(bf16[256,128]{1,0:T(8,128)(2,1)S(1)} %get-tuple-element.117), channel_id=1, source_target_pairs={{0,1},{1,0},{2,3},{3,2},{4,5},{5,4},{6,7},{7,6},{8,9},{9,8},{10,11... | collective-permute-start | bytes 196616 | tf_op jit(solution)/shard_map/ppermute | solution.py:27
  84.4 5.5 %collective-permute-start.23 = (bf16[256,128]{1,0:T(8,128)(2,1)S(1)}, bf16[256,128]{1,0:T(8,128)(2,1)S(1)}, u32[]{:S(2)}, u32[]{:S(2)}) collective-permute-start(bf16[256,128]{1,0:T(8,128)(2,1)S(1)} %get-tuple-element.118), channel_id=1, source_target_pairs={{0,17},{1,16},{16,1},{17,0},{32,49},{33,48},{48,33},{49,32},{64,81... | collective-permute-start | bytes 196616 | tf_op jit(solution)/shard_map/ppermute | solution.py:27

commit v5 on v4

--- a/solution.py
+++ b/solution.py
@@ -11,10 +11,11 @@
 BF16 = jnp.bfloat16
 TILE = 128
 PER = 32
+MERGED = 5
 FORWARD = 2
 BACKWARD = 4
 SPARE = 1023
-EARLY = 4
+EARLY = 5
 VMEM = pl.BlockSpec(memory_space=pltpu.VMEM)
 SMEM = pl.BlockSpec(memory_space=pltpu.SMEM)
 ANY = pl.BlockSpec(memory_space=pl.ANY)
@@ -244,13 +245,13 @@
     )(near(a), near(b))
 
 
-def add_products(flipped, g, picked, held, source, total):
+def add_products(flipped, first, picked, held, source, total):
     last = held.shape[0] - 1
     width = BACKWARD if flipped else FORWARD
     places = []
     products = []
     for at in range(0, PER, width):
-        codes = [picked[0, g * PER + at + j] for j in range(width)]
+        codes = [picked[0, first + at + j] for j in range(width)]
         places.append(codes[0] >> 16)
         mine = [held[jnp.minimum(code & 1023, last)] for code in codes]
         other = [source[(code >> 10) & 63] for code in codes]
@@ -262,6 +263,22 @@
         )
     for place, product in zip(places, products):
         total[place] += product
+
+
+def run_steps(first, last, step):
+    passes = (last - first) // MERGED
+
+    def merged(k, carry):
+        for j in range(MERGED):
+            step(first + k * MERGED + j)
+        return carry
+
+    def single(g, carry):
+        step(g)
+        return carry
+
+    lax.fori_loop(0, passes, merged, 0)
+    lax.fori_loop(first + passes * MERGED, last, single, 0)
 
 
 def forward_kernel(steps, ids, fetched, picked, tiles, early, *refs):
@@ -278,17 +295,15 @@
     for m, source in enumerate(sources):
         gathered[4 * m : 4 * m + 4] = source[...].reshape(4, TILE, TILE)
 
-    def early_step(g, carry):
-        add_products(False, g, picked, early, gathered, total)
-        return carry
-
-    def step(g, carry):
+    def early_step(g):
+        add_products(False, g * PER, picked, early, gathered, total)
+
+    def step(g):
         end_fetch(tiles, held, arrived, g, 0)
-        add_products(False, g, picked, held, gathered, total)
-        return carry
-
-    lax.fori_loop(0, jnp.minimum(count, EARLY), early_step, 0)
-    lax.fori_loop(EARLY, jnp.maximum(count, EARLY), step, 0)
+        add_products(False, g * PER, picked, held, gathered, total)
+
+    run_steps(0, jnp.minimum(count, EARLY), early_step)
+    run_steps(EARLY, jnp.maximum(count, EARLY), step)
     moved.wait()
     for k in range(kept.shape[0]):
         own = jnp.bitwise_xor(ids[1], 2 * k)
@@ -363,11 +378,7 @@
         out[rows : rows + TILE] = grads[0:TILE].astype(BF16)
         write_terms(bias, out, rows + TILE)
 
-    def step(g, carry):
-        add_products(True, g, picked, held, gathered, total)
-        return carry
-
-    lax.fori_loop(0, steps[0], step, 0)
+    run_steps(0, steps[0], lambda g: add_products(True, g * PER, picked, held, gathered, total))
     for k, out in enumerate(outs):
         for z in range(2):
             block = total[pl.ds(jnp.bitwise_xor(ids[2], 2 * k + z) * 2, 2)]

time: 90.2 us -> 88.4 us (0.980)
  Pallas kernels: 12.5 us -> 15.3 us
  starting transfers between devices: 36 us -> 33.2 us
  waiting for transfers between devices: 39.9 us -> 37.3 us
    ppermute x24, starting transfers between devices: 36 us -> 33.2 us  [swap(): return lax.ppermute(values, axis, [(i, i ^ mask) for i in range(size)])]
    ppermute x24, waiting for transfers between devices: 39.9 us -> 37.3 us  [swap(): return lax.ppermute(values, axis, [(i, i ^ mask) for i in range(size)])]
    pallas_call x1, Pallas kernels: 1.76 us -> 3.86 us  [early_tiles(): pl.pallas_call(early_kernel, out_shape=pltpu.VMEM((EARLY * PER + 1, TILE,...]
  transfers between devices with their start and end apart: 24 -> 24, of which waited for: 18 -> 19; matrix products, arithmetic and copies ran while one was open for 0% -> 0% of each run, Pallas kernels for 8% -> 11%
where the time goes in v5:
time: 88.4 us; the launch traced here: 88.2 us
  waiting for transfers between devices  37.3 us (42%)
  starting transfers between devices  33.2 us (38%)
  Pallas kernels  15.3 us (17%)
  between operations  1.41 us (2%)
  local copies, waits for them, and re-layouts  0.9 us (1%)
    ppermute x24, waiting for transfers between devices, swap(): return lax.ppermute(values, axis, [(i, i ^ mask) for i in range(size)])  37.3 us
    ppermute x24, starting transfers between devices, swap(): return lax.ppermute(values, axis, [(i, i ^ mask) for i in range(size)])  33.2 us
    pallas_call x1, Pallas kernels, early_tiles(): pl.pallas_call(early_kernel, out_shape=pltpu.VMEM((EARLY * PER + 1, TILE,...  3.86 us
    pallas_call x1, Pallas kernels, pick(): pl.pallas_call(functools.partial(pick_kernel, n_out), out_shape=[pltpu.SM...  2.87 us
    pallas_call x1, Pallas kernels, prepare(): pl.pallas_call(functools.partial(prepare_kernel, n_back), out_shape=[pltp...  2.59 us
    pallas_call x1, Pallas kernels, tiles_forward(): pl.pallas_call(forward_kernel, out_shape=[pltpu.VMEM((length + 1, TILE, T...  2.21 us
  transfers between devices with their start and end apart: 24, of which 19 were waited for; matrix products, arithmetic and copies ran while one was open for 0% of the time, Pallas kernels for 11%

profile of v5, /device:TPU:0, one launch (start us, length us, event | category | flops | bytes accessed | tf_op | source)
XLA Modules:
  0.0 88.2 jit_solution(4461659843734481876)
XLA Ops:
  0.6 0.0 copy-start
  0.7 0.9 %copy-done = bf16[512,128]{1,0:T(8,128)(2,1)S(1)} copy-done((bf16[512,128]{1,0:T(8,128)(2,1)S(1)}, bf16[512,128]{1,0:T(8,128)(2,1)}, u32[]{:S(2)}) %copy-start) | copy-done | bytes 131096
  1.5 2.0 %collective-permute-start = (bf16[256,128]{1,0:T(8,128)(2,1)S(1)}, bf16[256,128]{1,0:T(8,128)(2,1)S(1)}, u32[]{:S(2)}, u32[]{:S(2)}) collective-permute-start(bf16[256,128]{1,0:T(8,128)(2,1)S(1)} %constant_dynamic-slice_fusion.a), channel_id=1, source_target_pairs={{0,16},{16,0},{32,48},{48,32},{64,80},{80,64},{96,112},{112,96},{1... | collective-permute-start | bytes 196616 | tf_op jit(solution)/shard_map/ppermute | solution.py:28
  4.2 0.1 pad_add_fusion.ids
  4.3 2.9 %pick_tiles.1 = (s32[1,768]{1,0:T(1,128)S(4)}, s32[1,768]{1,0:T(1,128)S(4)}, s32[1]{0:T(128)S(4)}, s32[3]{0:T(128)S(4)}, s32[1,640]{1,0:T(1,128)S(1)}) custom-call(s32[1,1]{1,0:T(1,128)S(6)} %copy.12.count, s32[3]{0:T(128)S(1)} %pad_add_fusion.ids, s32[1,1,640]{2,1,0:T(1,128)} %rows.3, s32[1,1,640]{2,1,0:T(1,128)} %columns.3), custom_call_target="tpu_custom_call" | custom-call | tf_op jit(solution)/shard_map/pick_tiles/pallas_call | solution.py:119
  7.2 0.0 collective-permute-done.b
  7.2 3.1 %collective-permute-start.3 = (bf16[512,128]{1,0:T(8,128)(2,1)S(1)}, bf16[512,128]{1,0:T(8,128)(2,1)S(1)}, u32[]{:S(2)}, u32[]{:S(2)}) collective-permute-start(bf16[512,128]{1,0:T(8,128)(2,1)S(1)} %join.1.refs_0_), channel_id=1, source_target_pairs={{0,96},{16,112},{32,64},{48,80},{64,32},{80,48},{96,0},{112,16},{1... | collective-permute-start | bytes 393224 | tf_op jit(solution)/shard_map/ppermute | solution.py:28
  10.3 0.6 collective-permute-start.2
  10.9 0.5 collective-permute-start.1
  11.4 3.9 %early_tiles.1.early = bf16[161,128,128]{2,1,0:T(8,128)(2,1)S(1)} custom-call(s32[1]{0:T(128)S(4)} %get-tuple-element.68.steps, s32[1,768]{1,0:T(1,128)S(4)} %get-tuple-element.70.fetched, bf16[640,128,128]{2,1,0:T(8,128)(2,1)} %bitcast.6), custom_call_target="tpu_custom_call" | custom-call | tf_op jit(solution)/shard_map/early_tiles/pallas_call | solution.py:163
  15.2 0.4 collective-permute-done.3.refs_3_
  15.6 2.3 %collective-permute-done.2.refs_2_ = bf16[512,128]{1,0:T(8,128)(2,1)S(1)} collective-permute-done((bf16[512,128]{1,0:T(8,128)(2,1)S(1)}, bf16[512,128]{1,0:T(8,128)(2,1)S(1)}, u32[]{:S(2)}, u32[]{:S(2)}) %collective-permute-start.2) | collective-permute-done | bytes 131104 | tf_op jit(solution)/shard_map/ppermute | solution.py:28
  17.9 0.0 collective-permute-done.1.refs_1_
  17.9 2.2 %tiles_forward.1 = (bf16[673,128,128]{2,1,0:T(8,128)(2,1)S(1)}, f32[4,4,128,128]{3,2,1,0:T(8,128)S(1)}, bf16[4,4,128,128]{3,2,1,0:T(8,128)(2,1)S(1)}) custom-call(s32[1]{0:T(128)S(4)} %get-tuple-element.68.steps, s32[3]{0:T(128)S(4)} %get-tuple-element.69.ids, s32[1,768]{1,0:T(1,128)S(4)} %get-tuple-element.70.fetched, ...), custom_call_target="tpu_custom_call" | custom-call | tf_op jit(solution)/shard_map/tiles_forward/pallas_call | solution.py:317
  20.1 0.1 collective-permute-start.4
  20.2 1.9 %collective-permute-done.4.got = bf16[4,4,128,128]{3,2,1,0:T(8,128)(2,1)S(1)} collective-permute-done((bf16[4,4,128,128]{3,2,1,0:T(8,128)(2,1)S(1)}, bf16[4,4,128,128]{3,2,1,0:T(8,128)(2,1)S(1)}, u32[]{:S(2)}, u32[]{:S(2)}) %collective-permute-start.4) | collective-permute-done | bytes 524320 | tf_op jit(solution)/shard_map/ppermute | solution.py:28
  22.1 0.1 pair_sum.1
  22.2 1.6 %collective-permute-start.5 = (bf16[4,128,128]{2,1,0:T(8,128)(2,1)S(1)}, bf16[4,128,128]{2,1,0:T(8,128)(2,1)S(1)}, u32[]{:S(2)}, u32[]{:S(2)}) collective-permute-start(bf16[4,128,128]{2,1,0:T(8,128)(2,1)S(1)} %get-tuple-element.80), channel_id=1, source_target_pairs={{0,4},{2,6},{4,0},{6,2},{8,12},{10,14},{12,8},{14,10},{1,5},{3,7},... | collective-permute-start | bytes 393224 | tf_op jit(solution)/shard_map/ppermute | solution.py:28
  23.7 2.7 %collective-permute-start.6 = (bf16[4,128,128]{2,1,0:T(8,128)(2,1)S(1)}, bf16[4,128,128]{2,1,0:T(8,128)(2,1)S(1)}, u32[]{:S(2)}, u32[]{:S(2)}) collective-permute-start(bf16[4,128,128]{2,1,0:T(8,128)(2,1)S(1)} %get-tuple-element.81), channel_id=1, source_target_pairs={{0,8},{2,10},{4,12},{6,14},{8,0},{10,2},{12,4},{14,6},{1,9},{3,11}... | collective-permute-start | bytes 393224 | tf_op jit(solution)/shard_map/ppermute | solution.py:28
  26.5 0.5 collective-permute-start.7
  26.9 1.6 %collective-permute-done.5.a = bf16[4,128,128]{2,1,0:T(8,128)(2,1)S(1)} collective-permute-done((bf16[4,128,128]{2,1,0:T(8,128)(2,1)S(1)}, bf16[4,128,128]{2,1,0:T(8,128)(2,1)S(1)}, u32[]{:S(2)}, u32[]{:S(2)}) %collective-permute-start.5) | collective-permute-done | bytes 131104 | tf_op jit(solution)/shard_map/ppermute | solution.py:28
  28.6 4.3 %collective-permute-done.6.b = bf16[4,128,128]{2,1,0:T(8,128)(2,1)S(1)} collective-permute-done((bf16[4,128,128]{2,1,0:T(8,128)(2,1)S(1)}, bf16[4,128,128]{2,1,0:T(8,128)(2,1)S(1)}, u32[]{:S(2)}, u32[]{:S(2)}) %collective-permute-start.6) | collective-permute-done | bytes 131104 | tf_op jit(solution)/shard_map/ppermute | solution.py:28
  32.9 2.2 %collective-permute-done.7.c = bf16[4,128,128]{2,1,0:T(8,128)(2,1)S(1)} collective-permute-done((bf16[4,128,128]{2,1,0:T(8,128)(2,1)S(1)}, bf16[4,128,128]{2,1,0:T(8,128)(2,1)S(1)}, u32[]{:S(2)}, u32[]{:S(2)}) %collective-permute-start.7) | collective-permute-done | bytes 131104 | tf_op jit(solution)/shard_map/ppermute | solution.py:28
  35.1 0.1 own_sum.1
  35.2 3.7 %collective-permute-start.8 = (bf16[4,128,128]{2,1,0:T(8,128)(2,1)S(1)}, bf16[4,128,128]{2,1,0:T(8,128)(2,1)S(1)}, u32[]{:S(2)}, u32[]{:S(2)}) collective-permute-start(bf16[4,128,128]{2,1,0:T(8,128)(2,1)S(1)} %get-tuple-element.86), channel_id=1, source_target_pairs={{0,1},{1,0},{2,3},{3,2},{4,5},{5,4},{6,7},{7,6},{8,9},{9,8},{10,11... | collective-permute-start | bytes 393224 | tf_op jit(solution)/shard_map/ppermute | solution.py:28
  38.9 2.6 %prepare.1 = (s32[1,768]{1,0:T(1,128)S(4)}, s32[1]{0:T(128)S(4)}, bf16[128,128]{1,0:T(8,128)(2,1)S(1)}, f32[1,128]{1,0:T(1,128)S(1)}, bf16[512,128]{1,0:T(8,128)(2,1)S(1)}) custom-call(s32[3]{0:T(128)S(4)} %get-tuple-element.69.ids, s32[1,1,640]{2,1,0:T(1,128)} %rows.3, s32[1,1,640]{2,1,0:T(1,128)} %columns.3, s32[1,640]{1,0:T(1,128)S(1)} %get-tuple-element.87.slots, ...), custom_call_target="tpu_custom_call" | custom-call | tf_op jit(solution)/shard_map/prepare/pallas_call | solution.py:209
  41.5 0.6 collective-permute-done.8.other
  42.0 0.9 %middle.1 = (bf16[512,128]{1,0:T(8,128)(2,1)}, f32[4,128,128]{2,1,0:T(8,128)S(1)}, bf16[4,128,128]{2,1,0:T(8,128)(2,1)S(1)}, f32[136,128]{1,0:T(8,128)S(1)}) custom-call(f32[4,128,128]{2,1,0:T(8,128)S(1)} %get-tuple-element.83.own, bf16[4,128,128]{2,1,0:T(8,128)(2,1)S(1)} %collective-permute-done.8.other, bf16[128,128]{1,0:T(8,128)(2,1)S(1)} %get-tuple-element.94.weight, ...), custom_call_target="tpu_custom_call" | custom-call | tf_op jit(solution)/shard_map/middle/pallas_call | solution.py:467
  42.9 3.3 %collective-permute-start.9 = (bf16[4,128,128]{2,1,0:T(8,128)(2,1)S(1)}, bf16[4,128,128]{2,1,0:T(8,128)(2,1)S(1)}, u32[]{:S(2)}, u32[]{:S(2)}) collective-permute-start(bf16[4,128,128]{2,1,0:T(8,128)(2,1)S(1)} %get-tuple-element.102), channel_id=1, source_target_pairs={{0,1},{1,0},{2,3},{3,2},{4,5},{5,4},{6,7},{7,6},{8,9},{9,8},{10,11... | collective-permute-start | bytes 393224 | tf_op jit(solution)/shard_map/ppermute | solution.py:28
  46.2 0.0 collective-permute-start.10
  46.2 1.3 %collective-permute-done.10.more = f32[136,128]{1,0:T(8,128)S(1)} collective-permute-done((f32[136,128]{1,0:T(8,128)S(1)}, f32[136,128]{1,0:T(8,128)S(1)}, u32[]{:S(2)}, u32[]{:S(2)}) %collective-permute-start.10) | collective-permute-done | bytes 69664 | tf_op jit(solution)/shard_map/ppermute | solution.py:28
  47.5 1.9 %collective-permute-done.9.other = bf16[4,128,128]{2,1,0:T(8,128)(2,1)S(1)} collective-permute-done((bf16[4,128,128]{2,1,0:T(8,128)(2,1)S(1)}, bf16[4,128,128]{2,1,0:T(8,128)(2,1)S(1)}, u32[]{:S(2)}, u32[]{:S(2)}) %collective-permute-start.9) | collective-permute-done | bytes 131104 | tf_op jit(solution)/shard_map/ppermute | solution.py:28
  49.4 0.1 collective-permute-start.14
  49.5 1.3 %collective-permute-start.13 = (bf16[592,128]{1,0:T(8,128)(2,1)S(1)}, bf16[592,128]{1,0:T(8,128)(2,1)S(1)}, u32[]{:S(2)}, u32[]{:S(2)}) collective-permute-start(bf16[592,128]{1,0:T(8,128)(2,1)S(1)} %message.1.refs_0_), channel_id=1, source_target_pairs={{0,12},{2,14},{4,8},{6,10},{8,4},{10,6},{12,0},{14,2},{1,13},{3,15... | collective-permute-start | bytes 454664 | tf_op jit(solution)/shard_map/ppermute | solution.py:28
  50.9 2.1 %collective-permute-start.12 = (bf16[592,128]{1,0:T(8,128)(2,1)S(1)}, bf16[592,128]{1,0:T(8,128)(2,1)S(1)}, u32[]{:S(2)}, u32[]{:S(2)}) collective-permute-start(bf16[592,128]{1,0:T(8,128)(2,1)S(1)} %message.1.refs_0_), channel_id=1, source_target_pairs={{0,4},{2,6},{4,0},{6,2},{8,12},{10,14},{12,8},{14,10},{1,5},{3,7},... | collective-permute-start | bytes 454664 | tf_op jit(solution)/shard_map/ppermute | solution.py:28
  53.0 0.0 collective-permute-start.11
  53.0 3.8 %collective-permute-done.14.refs_4_ = bf16[592,128]{1,0:T(8,128)(2,1)S(1)} collective-permute-done((bf16[592,128]{1,0:T(8,128)(2,1)S(1)}, bf16[592,128]{1,0:T(8,128)(2,1)S(1)}, u32[]{:S(2)}, u32[]{:S(2)}) %collective-permute-start.14) | collective-permute-done | bytes 151584 | tf_op jit(solution)/shard_map/ppermute | solution.py:28
  56.9 1.3 %collective-permute-done.13.refs_6_ = bf16[592,128]{1,0:T(8,128)(2,1)S(1)} collective-permute-done((bf16[592,128]{1,0:T(8,128)(2,1)S(1)}, bf16[592,128]{1,0:T(8,128)(2,1)S(1)}, u32[]{:S(2)}, u32[]{:S(2)}) %collective-permute-start.13) | collective-permute-done | bytes 151584 | tf_op jit(solution)/shard_map/ppermute | solution.py:28
  58.2 0.0 collective-permute-done.12.refs_2_
  58.2 0.0 collective-permute-start.15
  58.2 0.5 collective-permute-start.16
  58.7 0.0 collective-permute-start.17
  58.7 0.0 collective-permute-done.11.refs_1_
  58.7 0.9 collective-permute-done.15.refs_3_
  59.6 0.2 collective-permute-done.16.refs_5_
  59.8 0.3 collective-permute-done.17.refs_7_
  60.1 1.7 %tiles_backward.1 = (f32[512,128]{1,0:T(8,128)S(1)}, f32[136,128]{1,0:T(8,128)S(1)}, bf16[656,128]{1,0:T(8,128)(2,1)S(1)}, bf16[656,128]{1,0:T(8,128)(2,1)S(1)}, bf16[656,128]{1,0:T(8,128)(2,1)S(1)}) custom-call(s32[1]{0:T(128)S(4)} %get-tuple-element.98.steps, s32[3]{0:T(128)S(4)} %get-tuple-element.69.ids, s32[1,768]{1,0:T(1,128)S(4)} %get-tuple-element.99.picked, ...), custom_call_target="tpu_custom_call" | custom-call | tf_op jit(solution)/shard_map/tiles_backward/pallas_call | solution.py:390
  61.8 3.5 %collective-permute-start.18 = (bf16[656,128]{1,0:T(8,128)(2,1)S(1)}, bf16[656,128]{1,0:T(8,128)(2,1)S(1)}, u32[]{:S(2)}, u32[]{:S(2)}) collective-permute-start(bf16[656,128]{1,0:T(8,128)(2,1)S(1)} %get-tuple-element.111), channel_id=1, source_target_pairs={{0,32},{16,48},{32,0},{48,16},{64,96},{80,112},{96,64},{112,80},{1... | collective-permute-start | bytes 503816 | tf_op jit(solution)/shard_map/ppermute | solution.py:28
  65.3 1.9 %collective-permute-start.19 = (bf16[656,128]{1,0:T(8,128)(2,1)S(1)}, bf16[656,128]{1,0:T(8,128)(2,1)S(1)}, u32[]{:S(2)}, u32[]{:S(2)}) collective-permute-start(bf16[656,128]{1,0:T(8,128)(2,1)S(1)} %get-tuple-element.112), channel_id=1, source_target_pairs={{0,64},{16,80},{32,96},{48,112},{64,0},{80,16},{96,32},{112,48},{1... | collective-permute-start | bytes 503816 | tf_op jit(solution)/shard_map/ppermute | solution.py:28
  67.2 0.8 collective-permute-start.20
  68.1 2.1 %collective-permute-done.18.a = bf16[656,128]{1,0:T(8,128)(2,1)S(1)} collective-permute-done((bf16[656,128]{1,0:T(8,128)(2,1)S(1)}, bf16[656,128]{1,0:T(8,128)(2,1)S(1)}, u32[]{:S(2)}, u32[]{:S(2)}) %collective-permute-start.18) | collective-permute-done | bytes 167968 | tf_op jit(solution)/shard_map/ppermute | solution.py:28
  70.2 4.4 %collective-permute-done.19.b = bf16[656,128]{1,0:T(8,128)(2,1)S(1)} collective-permute-done((bf16[656,128]{1,0:T(8,128)(2,1)S(1)}, bf16[656,128]{1,0:T(8,128)(2,1)S(1)}, u32[]{:S(2)}, u32[]{:S(2)}) %collective-permute-start.19) | collective-permute-done | bytes 167968 | tf_op jit(solution)/shard_map/ppermute | solution.py:28
  74.6 3.6 %collective-permute-done.20.c = bf16[656,128]{1,0:T(8,128)(2,1)S(1)} collective-permute-done((bf16[656,128]{1,0:T(8,128)(2,1)S(1)}, bf16[656,128]{1,0:T(8,128)(2,1)S(1)}, u32[]{:S(2)}, u32[]{:S(2)}) %collective-permute-start.20) | collective-permute-done | bytes 167968 | tf_op jit(solution)/shard_map/ppermute | solution.py:28
  78.2 0.1 line_sum.1
  78.3 0.1 collective-permute-start.21
  78.4 3.4 %collective-permute-start.22 = (bf16[256,128]{1,0:T(8,128)(2,1)S(1)}, bf16[256,128]{1,0:T(8,128)(2,1)S(1)}, u32[]{:S(2)}, u32[]{:S(2)}) collective-permute-start(bf16[256,128]{1,0:T(8,128)(2,1)S(1)} %get-tuple-element.117), channel_id=1, source_target_pairs={{0,1},{1,0},{2,3},{3,2},{4,5},{5,4},{6,7},{7,6},{8,9},{9,8},{10,11... | collective-permute-start | bytes 196616 | tf_op jit(solution)/shard_map/ppermute | solution.py:28
  81.8 1.3 %collective-permute-start.23 = (bf16[256,128]{1,0:T(8,128)(2,1)S(1)}, bf16[256,128]{1,0:T(8,128)(2,1)S(1)}, u32[]{:S(2)}, u32[]{:S(2)}) collective-permute-start(bf16[256,128]{1,0:T(8,128)(2,1)S(1)} %get-tuple-element.118), channel_id=1, source_target_pairs={{0,17},{1,16},{16,1},{17,0},{32,49},{33,48},{48,33},{49,32},{64,81... | collective-permute-start | bytes 196616 | tf_op jit(solution)/shard_map/ppermute | solution.py:28
  83.1 3.1 %collective-permute-done.22.opposite = bf16[256,128]{1,0:T(8,128)(2,1)S(1)} collective-permute-done((bf16[256,128]{1,0:T(8,128)(2,1)S(1)}, bf16[256,128]{1,0:T(8,128)(2,1)S(1)}, u32[]{:S(2)}, u32[]{:S(2)}) %collective-permute-start.22) | collective-permute-done | bytes 65568 | tf_op jit(solution)/shard_map/ppermute | solution.py:28
  86.2 1.2 %collective-permute-done.23.corner = bf16[256,128]{1,0:T(8,128)(2,1)S(1)} collective-permute-done((bf16[256,128]{1,0:T(8,128)(2,1)S(1)}, bf16[256,128]{1,0:T(8,128)(2,1)S(1)}, u32[]{:S(2)}, u32[]{:S(2)}) %collective-permute-start.23) | collective-permute-done | bytes 65568 | tf_op jit(solution)/shard_map/ppermute | solution.py:28
  87.3 0.0 collective-permute-done.21.beside
  87.3 0.9 finish.1
  (3 shorter events, 0.1 us)
Async XLA Ops:
  0.6 0.9 %copy-start = (bf16[512,128]{1,0:T(8,128)(2,1)S(1)}, bf16[512,128]{1,0:T(8,128)(2,1)}, u32[]{:S(2)}) copy-start(bf16[512,128]{1,0:T(8,128)(2,1)} %param.8) | copy-start | bytes 393220
  1.5 5.6 %collective-permute-start = (bf16[256,128]{1,0:T(8,128)(2,1)S(1)}, bf16[256,128]{1,0:T(8,128)(2,1)S(1)}, u32[]{:S(2)}, u32[]{:S(2)}) collective-permute-start(bf16[256,128]{1,0:T(8,128)(2,1)S(1)} %constant_dynamic-slice_fusion.a), channel_id=1, source_target_pairs={{0,16},{16,0},{32,48},{48,32},{64,80},{80,64},{96,112},{112,96},{1... | collective-permute-start | bytes 196616 | tf_op jit(solution)/shard_map/ppermute | solution.py:28
  7.2 8.4 %collective-permute-start.3 = (bf16[512,128]{1,0:T(8,128)(2,1)S(1)}, bf16[512,128]{1,0:T(8,128)(2,1)S(1)}, u32[]{:S(2)}, u32[]{:S(2)}) collective-permute-start(bf16[512,128]{1,0:T(8,128)(2,1)S(1)} %join.1.refs_0_), channel_id=1, source_target_pairs={{0,96},{16,112},{32,64},{48,80},{64,32},{80,48},{96,0},{112,16},{1... | collective-permute-start | bytes 393224 | tf_op jit(solution)/shard_map/ppermute | solution.py:28
  10.3 7.6 %collective-permute-start.2 = (bf16[512,128]{1,0:T(8,128)(2,1)S(1)}, bf16[512,128]{1,0:T(8,128)(2,1)S(1)}, u32[]{:S(2)}, u32[]{:S(2)}) collective-permute-start(bf16[512,128]{1,0:T(8,128)(2,1)S(1)} %join.1.refs_0_), channel_id=1, source_target_pairs={{0,64},{16,80},{32,96},{48,112},{64,0},{80,16},{96,32},{112,48},{1... | collective-permute-start | bytes 393224 | tf_op jit(solution)/shard_map/ppermute | solution.py:28
  10.9 7.0 %collective-permute-start.1 = (bf16[512,128]{1,0:T(8,128)(2,1)S(1)}, bf16[512,128]{1,0:T(8,128)(2,1)S(1)}, u32[]{:S(2)}, u32[]{:S(2)}) collective-permute-start(bf16[512,128]{1,0:T(8,128)(2,1)S(1)} %join.1.refs_0_), channel_id=1, source_target_pairs={{0,32},{16,48},{32,0},{48,16},{64,96},{80,112},{96,64},{112,80},{1... | collective-permute-start | bytes 393224 | tf_op jit(solution)/shard_map/ppermute | solution.py:28
  20.1 2.0 %collective-permute-start.4 = (bf16[4,4,128,128]{3,2,1,0:T(8,128)(2,1)S(1)}, bf16[4,4,128,128]{3,2,1,0:T(8,128)(2,1)S(1)}, u32[]{:S(2)}, u32[]{:S(2)}) collective-permute-start(bf16[4,4,128,128]{3,2,1,0:T(8,128)(2,1)S(1)} %get-tuple-element.78), channel_id=1, source_target_pairs={{0,2},{2,0},{4,6},{6,4},{8,10},{10,8},{12,14},{14,12},{1,3},{3,1},... | collective-permute-start | bytes 1572872 | tf_op jit(solution)/shard_map/ppermute | solution.py:28
  22.2 6.4 %collective-permute-start.5 = (bf16[4,128,128]{2,1,0:T(8,128)(2,1)S(1)}, bf16[4,128,128]{2,1,0:T(8,128)(2,1)S(1)}, u32[]{:S(2)}, u32[]{:S(2)}) collective-permute-start(bf16[4,128,128]{2,1,0:T(8,128)(2,1)S(1)} %get-tuple-element.80), channel_id=1, source_target_pairs={{0,4},{2,6},{4,0},{6,2},{8,12},{10,14},{12,8},{14,10},{1,5},{3,7},... | collective-permute-start | bytes 393224 | tf_op jit(solution)/shard_map/ppermute | solution.py:28
  23.7 9.2 %collective-permute-start.6 = (bf16[4,128,128]{2,1,0:T(8,128)(2,1)S(1)}, bf16[4,128,128]{2,1,0:T(8,128)(2,1)S(1)}, u32[]{:S(2)}, u32[]{:S(2)}) collective-permute-start(bf16[4,128,128]{2,1,0:T(8,128)(2,1)S(1)} %get-tuple-element.81), channel_id=1, source_target_pairs={{0,8},{2,10},{4,12},{6,14},{8,0},{10,2},{12,4},{14,6},{1,9},{3,11}... | collective-permute-start | bytes 393224 | tf_op jit(solution)/shard_map/ppermute | solution.py:28
  26.5 8.7 %collective-permute-start.7 = (bf16[4,128,128]{2,1,0:T(8,128)(2,1)S(1)}, bf16[4,128,128]{2,1,0:T(8,128)(2,1)S(1)}, u32[]{:S(2)}, u32[]{:S(2)}) collective-permute-start(bf16[4,128,128]{2,1,0:T(8,128)(2,1)S(1)} %get-tuple-element.82), channel_id=1, source_target_pairs={{0,12},{2,14},{4,8},{6,10},{8,4},{10,6},{12,0},{14,2},{1,13},{3,15... | collective-permute-start | bytes 393224 | tf_op jit(solution)/shard_map/ppermute | solution.py:28
  35.2 6.8 %collective-permute-start.8 = (bf16[4,128,128]{2,1,0:T(8,128)(2,1)S(1)}, bf16[4,128,128]{2,1,0:T(8,128)(2,1)S(1)}, u32[]{:S(2)}, u32[]{:S(2)}) collective-permute-start(bf16[4,128,128]{2,1,0:T(8,128)(2,1)S(1)} %get-tuple-element.86), channel_id=1, source_target_pairs={{0,1},{1,0},{2,3},{3,2},{4,5},{5,4},{6,7},{7,6},{8,9},{9,8},{10,11... | collective-permute-start | bytes 393224 | tf_op jit(solution)/shard_map/ppermute | solution.py:28
  42.9 6.5 %collective-permute-start.9 = (bf16[4,128,128]{2,1,0:T(8,128)(2,1)S(1)}, bf16[4,128,128]{2,1,0:T(8,128)(2,1)S(1)}, u32[]{:S(2)}, u32[]{:S(2)}) collective-permute-start(bf16[4,128,128]{2,1,0:T(8,128)(2,1)S(1)} %get-tuple-element.102), channel_id=1, source_target_pairs={{0,1},{1,0},{2,3},{3,2},{4,5},{5,4},{6,7},{7,6},{8,9},{9,8},{10,11... | collective-permute-start | bytes 393224 | tf_op jit(solution)/shard_map/ppermute | solution.py:28
  46.2 1.3 %collective-permute-start.10 = (f32[136,128]{1,0:T(8,128)S(1)}, f32[136,128]{1,0:T(8,128)S(1)}, u32[]{:S(2)}, u32[]{:S(2)}) collective-permute-start(f32[136,128]{1,0:T(8,128)S(1)} %get-tuple-element.103.grads), channel_id=1, source_target_pairs={{0,2},{2,0},{4,6},{6,4},{8,10},{10,8},{12,14},{14,12},{1,3},{3,1},... | collective-permute-start | bytes 208904 | tf_op jit(solution)/shard_map/ppermute | solution.py:28
  49.4 7.4 %collective-permute-start.14 = (bf16[592,128]{1,0:T(8,128)(2,1)S(1)}, bf16[592,128]{1,0:T(8,128)(2,1)S(1)}, u32[]{:S(2)}, u32[]{:S(2)}) collective-permute-start(bf16[592,128]{1,0:T(8,128)(2,1)S(1)} %message.1.refs_0_), channel_id=1, source_target_pairs={{0,8},{2,10},{4,12},{6,14},{8,0},{10,2},{12,4},{14,6},{1,9},{3,11}... | collective-permute-start | bytes 454664 | tf_op jit(solution)/shard_map/ppermute | solution.py:28
  49.5 8.6 %collective-permute-start.13 = (bf16[592,128]{1,0:T(8,128)(2,1)S(1)}, bf16[592,128]{1,0:T(8,128)(2,1)S(1)}, u32[]{:S(2)}, u32[]{:S(2)}) collective-permute-start(bf16[592,128]{1,0:T(8,128)(2,1)S(1)} %message.1.refs_0_), channel_id=1, source_target_pairs={{0,12},{2,14},{4,8},{6,10},{8,4},{10,6},{12,0},{14,2},{1,13},{3,15... | collective-permute-start | bytes 454664 | tf_op jit(solution)/shard_map/ppermute | solution.py:28
  50.9 7.3 %collective-permute-start.12 = (bf16[592,128]{1,0:T(8,128)(2,1)S(1)}, bf16[592,128]{1,0:T(8,128)(2,1)S(1)}, u32[]{:S(2)}, u32[]{:S(2)}) collective-permute-start(bf16[592,128]{1,0:T(8,128)(2,1)S(1)} %message.1.refs_0_), channel_id=1, source_target_pairs={{0,4},{2,6},{4,0},{6,2},{8,12},{10,14},{12,8},{14,10},{1,5},{3,7},... | collective-permute-start | bytes 454664 | tf_op jit(solution)/shard_map/ppermute | solution.py:28
  53.0 5.7 %collective-permute-start.11 = (bf16[592,128]{1,0:T(8,128)(2,1)S(1)}, bf16[592,128]{1,0:T(8,128)(2,1)S(1)}, u32[]{:S(2)}, u32[]{:S(2)}) collective-permute-start(bf16[592,128]{1,0:T(8,128)(2,1)S(1)} %message.1.refs_0_), channel_id=1, source_target_pairs={{0,2},{2,0},{4,6},{6,4},{8,10},{10,8},{12,14},{14,12},{1,3},{3,1},... | collective-permute-start | bytes 454664 | tf_op jit(solution)/shard_map/ppermute | solution.py:28
  58.2 1.4 %collective-permute-start.15 = (bf16[592,128]{1,0:T(8,128)(2,1)S(1)}, bf16[592,128]{1,0:T(8,128)(2,1)S(1)}, u32[]{:S(2)}, u32[]{:S(2)}) collective-permute-start(bf16[592,128]{1,0:T(8,128)(2,1)S(1)} %collective-permute-done.12.refs_2_), channel_id=1, source_target_pairs={{0,2},{2,0},{4,6},{6,4},{8,10},{10,8},{12,14},{14,12},{1,3},{3,1},... | collective-permute-start | bytes 454664 | tf_op jit(solution)/shard_map/ppermute | solution.py:28
  58.2 1.6 %collective-permute-start.16 = (bf16[592,128]{1,0:T(8,128)(2,1)S(1)}, bf16[592,128]{1,0:T(8,128)(2,1)S(1)}, u32[]{:S(2)}, u32[]{:S(2)}) collective-permute-start(bf16[592,128]{1,0:T(8,128)(2,1)S(1)} %collective-permute-done.14.refs_4_), channel_id=1, source_target_pairs={{0,2},{2,0},{4,6},{6,4},{8,10},{10,8},{12,14},{14,12},{1,3},{3,1},... | collective-permute-start | bytes 454664 | tf_op jit(solution)/shard_map/ppermute | solution.py:28
  58.7 1.4 %collective-permute-start.17 = (bf16[592,128]{1,0:T(8,128)(2,1)S(1)}, bf16[592,128]{1,0:T(8,128)(2,1)S(1)}, u32[]{:S(2)}, u32[]{:S(2)}) collective-permute-start(bf16[592,128]{1,0:T(8,128)(2,1)S(1)} %collective-permute-done.13.refs_6_), channel_id=1, source_target_pairs={{0,2},{2,0},{4,6},{6,4},{8,10},{10,8},{12,14},{14,12},{1,3},{3,1},... | collective-permute-start | bytes 454664 | tf_op jit(solution)/shard_map/ppermute | solution.py:28
  61.8 8.4 %collective-permute-start.18 = (bf16[656,128]{1,0:T(8,128)(2,1)S(1)}, bf16[656,128]{1,0:T(8,128)(2,1)S(1)}, u32[]{:S(2)}, u32[]{:S(2)}) collective-permute-start(bf16[656,128]{1,0:T(8,128)(2,1)S(1)} %get-tuple-element.111), channel_id=1, source_target_pairs={{0,32},{16,48},{32,0},{48,16},{64,96},{80,112},{96,64},{112,80},{1... | collective-permute-start | bytes 503816 | tf_op jit(solution)/shard_map/ppermute | solution.py:28
  65.3 9.3 %collective-permute-start.19 = (bf16[656,128]{1,0:T(8,128)(2,1)S(1)}, bf16[656,128]{1,0:T(8,128)(2,1)S(1)}, u32[]{:S(2)}, u32[]{:S(2)}) collective-permute-start(bf16[656,128]{1,0:T(8,128)(2,1)S(1)} %get-tuple-element.112), channel_id=1, source_target_pairs={{0,64},{16,80},{32,96},{48,112},{64,0},{80,16},{96,32},{112,48},{1... | collective-permute-start | bytes 503816 | tf_op jit(solution)/shard_map/ppermute | solution.py:28
  67.2 11.0 %collective-permute-start.20 = (bf16[656,128]{1,0:T(8,128)(2,1)S(1)}, bf16[656,128]{1,0:T(8,128)(2,1)S(1)}, u32[]{:S(2)}, u32[]{:S(2)}) collective-permute-start(bf16[656,128]{1,0:T(8,128)(2,1)S(1)} %get-tuple-element.113), channel_id=1, source_target_pairs={{0,96},{16,112},{32,64},{48,80},{64,32},{80,48},{96,0},{112,16},{1... | collective-permute-start | bytes 503816 | tf_op jit(solution)/shard_map/ppermute | solution.py:28
  78.3 9.0 %collective-permute-start.21 = (bf16[400,128]{1,0:T(8,128)(2,1)S(1)}, bf16[400,128]{1,0:T(8,128)(2,1)S(1)}, u32[]{:S(2)}, u32[]{:S(2)}) collective-permute-start(bf16[400,128]{1,0:T(8,128)(2,1)S(1)} %get-tuple-element.116), channel_id=1, source_target_pairs={{0,16},{16,0},{32,48},{48,32},{64,80},{80,64},{96,112},{112,96},{1... | collective-permute-start | bytes 307208 | tf_op jit(solution)/shard_map/ppermute | solution.py:28
  78.4 7.7 %collective-permute-start.22 = (bf16[256,128]{1,0:T(8,128)(2,1)S(1)}, bf16[256,128]{1,0:T(8,128)(2,1)S(1)}, u32[]{:S(2)}, u32[]{:S(2)}) collective-permute-start(bf16[256,128]{1,0:T(8,128)(2,1)S(1)} %get-tuple-element.117), channel_id=1, source_target_pairs={{0,1},{1,0},{2,3},{3,2},{4,5},{5,4},{6,7},{7,6},{8,9},{9,8},{10,11... | collective-permute-start | bytes 196616 | tf_op jit(solution)/shard_map/ppermute | solution.py:28
  81.8 5.5 %collective-permute-start.23 = (bf16[256,128]{1,0:T(8,128)(2,1)S(1)}, bf16[256,128]{1,0:T(8,128)(2,1)S(1)}, u32[]{:S(2)}, u32[]{:S(2)}) collective-permute-start(bf16[256,128]{1,0:T(8,128)(2,1)S(1)} %get-tuple-element.118), channel_id=1, source_target_pairs={{0,17},{1,16},{16,1},{17,0},{32,49},{33,48},{48,33},{49,32},{64,81... | collective-permute-start | bytes 196616 | tf_op jit(solution)/shard_map/ppermute | solution.py:28

commit v6 on v5

--- a/solution.py
+++ b/solution.py
@@ -29,8 +29,7 @@
 
 
 def swap_line(values, axis):
-    second = swap(values[1], axis, 4)
-    return [swap(values[0], axis, 2), second, swap(values[2], axis, 6)]
+    return [swap(one, axis, mask) for one, mask in zip(values, (4, 2, 6))]
 
 
 def near(values):
@@ -78,7 +77,7 @@
     return items, found[2:3], target, steps, slot
 
 
-def pick_kernel(n_out, count, ids, rows, columns, *refs):
+def pick_kernel(n_out, ids, rows, columns, *refs):
     fetched, forward, steps, same_ids, slots = refs[:5]
     row_copy, column_copy, fetched_copy, forward_copy, arrived = refs[5:]
     copies = [
@@ -94,7 +93,7 @@
     row, column = row_copy[...], column_copy[...]
     index = iota(row.shape, 1)
     length = forward.shape[1]
-    used = (index < count[0, 0]) & (((column >> 1) & 1) == ids[0])
+    used = (index < ids[3]) & (((column >> 1) & 1) == ids[0])
     source = jnp.bitwise_xor(column >> 2, ids[2]) * 2 + (column & 1)
     items, source, target, n_steps, slot = order(row, used, source, index, n_out, length, FORWARD)
     fetched_copy[...] = jnp.maximum(items, 0)
@@ -112,7 +111,7 @@
         copy.wait()
 
 
-def pick(count, ids, rows, columns, n_out, n_back):
+def pick(ids, rows, columns, n_out, n_back):
     length = rows.shape[-1] + max(n_out * (FORWARD - 1), n_back * (BACKWARD - 1)) + PER
     length = -(-length // TILE) * TILE
     listed = (1, length)
@@ -125,7 +124,7 @@
             pltpu.SMEM((3,), jnp.int32),
             pltpu.VMEM(rows.shape[1:], jnp.int32),
         ],
-        in_specs=[SMEM, SMEM, ANY, ANY],
+        in_specs=[SMEM, ANY, ANY],
         out_specs=[SMEM, SMEM, SMEM, SMEM, VMEM],
         scratch_shapes=[
             pltpu.VMEM(rows.shape[1:], jnp.int32),
@@ -136,7 +135,7 @@
         ],
         compiler_params=PICK_PARAMS,
         name="pick_tiles",
-    )(count, ids, far(rows), far(columns))
+    )(ids, far(rows), far(columns))
 
 
 def start_fetch(tiles, fetched, held, arrived, g, carry):
@@ -379,7 +378,7 @@
         write_terms(bias, out, rows + TILE)
 
     run_steps(0, steps[0], lambda g: add_products(True, g * PER, picked, held, gathered, total))
-    for k, out in enumerate(outs):
+    for k, out in zip((0, 2, 1, 3), outs):
         for z in range(2):
             block = total[pl.ds(jnp.bitwise_xor(ids[2], 2 * k + z) * 2, 2)]
             out[2 * z * TILE : 2 * (z + 1) * TILE] = block.reshape(2 * TILE, TILE).astype(out.dtype)
@@ -404,8 +403,8 @@
 
 def pair_kernel(kept, got, first, *others):
     first[...] = kept[0] + got[0].astype(F32)
-    for k, other in enumerate(others):
-        other[...] = (kept[k + 1] + got[k + 1].astype(F32)).astype(BF16)
+    for k, other in zip((2, 1, 3), others):
+        other[...] = (kept[k] + got[k].astype(F32)).astype(BF16)
 
 
 def pair_sum(kept, got):
@@ -500,7 +499,7 @@
     )(scalar(ids), near(back), near(other), near(grads), near(more))
 
 
-def line_kernel(kept, grads, a, b, c, own, own_grads, own_sent, other_sent, other_message):
+def line_kernel(kept, grads, a, b, c, own_sent, other_sent, other_message, own, own_grads):
     rows = own.shape[0]
     value = kept[...]
     weight = grads[0:TILE]
@@ -524,11 +523,11 @@
     return pl.pallas_call(
         line_kernel,
         out_shape=[
-            pltpu.VMEM((rows, TILE), F32),
-            pltpu.VMEM(grads.shape, F32),
             pltpu.VMEM((rows, TILE), BF16),
             pltpu.VMEM((rows, TILE), BF16),
             pltpu.VMEM((rows + TILE + 16, TILE), BF16),
+            pltpu.VMEM((rows, TILE), F32),
+            pltpu.VMEM(grads.shape, F32),
         ],
         in_specs=[VMEM] * 5,
         out_specs=[VMEM] * 5,
@@ -537,7 +536,7 @@
     )(near(kept), near(grads), *[near(one) for one in messages])
 
 
-def finish_kernel(ids, own, grads, beside, opposite, corner, features, weight, bias):
+def finish_kernel(ids, own, grads, opposite, corner, beside, features, weight, bias):
     rows = own.shape[0]
     for b in range(rows // TILE):
         block = pl.ds(b * TILE, TILE)
@@ -549,7 +548,7 @@
     bias[...] = (grads[TILE : TILE + 8] + read_terms((beside,), rows + TILE))[0:1]
 
 
-def finish(ids, own, grads, beside, opposite, corner):
+def finish(ids, own, grads, opposite, corner, beside):
     return pl.pallas_call(
         finish_kernel,
         out_shape=[
@@ -561,7 +560,7 @@
         out_specs=[VMEM] * 3,
         compiler_params=PARAMS,
         name="finish",
-    )(scalar(ids), near(own), near(grads), near(beside), near(opposite), near(corner))
+    )(scalar(ids), near(own), near(grads), near(opposite), near(corner), near(beside))
 
 
 def local(
@@ -573,18 +572,20 @@
     blocks = own_rows // TILE
     n_out, n_back = blocks * n_col, blocks // 2 * n_row
     half = lax.axis_index("feat")
-    ids = jnp.stack([half, lax.axis_index("col"), lax.axis_index("row")]).astype(jnp.int32)
+    places = [half, lax.axis_index("col"), lax.axis_index("row"), tile_count[0, 0]]
+    ids = jnp.stack(places).astype(jnp.int32)
 
     mine = lax.dynamic_slice_in_dim(features, half * (own_rows // 2), own_rows // 2, 0)
-    lists = pick(tile_count, ids, tile_rows, tile_columns, n_out, n_back)
+    mine, ids = lax.optimization_barrier((mine, ids))
+    lists = pick(ids, tile_rows, tile_columns, n_out, n_back)
     beside, lists = lax.optimization_barrier((swap(mine, "row", 1), lists))
     fetched, forward, steps, ids, slots = lists
     pair = join(mine, beside)
-    sources = [swap(pair, "row", mask) for mask in range(2, n_row, 2)]
+    second, first, third = swap_line([pair] * 3, "row")
     early = early_tiles(steps, fetched, tiles)
-    early, sources = lax.optimization_barrier((early, sources))
-
-    held, kept, sent = tiles_forward(steps, ids, fetched, forward, tiles, early, [pair, *sources], n_out)
+    early, first, third, second = lax.optimization_barrier((early, first, third, second))
+
+    held, kept, sent = tiles_forward(steps, ids, fetched, forward, tiles, early, [pair, first, second, third], n_out)
     first, *others = pair_sum(kept, swap(sent, "col", 1))
     others = swap_line(others, "col")
     own, sent = own_sum(first, others)
@@ -606,11 +607,11 @@
     kept, grads, *others = tiles_backward(steps, ids, backward, held, sources, n_back)
 
     others = swap_line(others, "row")
-    own, grads, own_sent, other_sent, other_message = line_sum(kept, grads, others)
+    own_sent, other_sent, other_message, own, grads = line_sum(kept, grads, others)
     opposite = swap(own_sent, "feat", 1)
     corner = swap(other_sent, ("row", "feat"), 3)
     beside = swap(other_message, "row", 1)
-    grad_features, grad_weight, grad_bias = finish(ids, own, grads, beside, opposite, corner)
+    grad_features, grad_weight, grad_bias = finish(ids, own, grads, opposite, corner, beside)
     return (activations, grad_features, grad_weight, grad_bias[0])
 
 

time: 88.4 us -> 84.2 us (0.952)
  waiting for transfers between devices: 37.3 us -> 30.8 us
  starting transfers between devices: 33.2 us -> 36.7 us
    ppermute x24, waiting for transfers between devices: 37.3 us -> 30.8 us  [swap(): return lax.ppermute(values, axis, [(i, i ^ mask) for i in range(size)])]
    ppermute x24, starting transfers between devices: 33.2 us -> 36.7 us  [swap(): return lax.ppermute(values, axis, [(i, i ^ mask) for i in range(size)])]
  transfers between devices with their start and end apart: 24 -> 24, of which waited for: 19 -> 17; matrix products, arithmetic and copies ran while one was open for 0% -> 0% of each run, Pallas kernels for 11% -> 11%
where the time goes in v6:
time: 84.2 us; the launch traced here: 84.3 us
  starting transfers between devices  36.7 us (44%)
  waiting for transfers between devices  30.8 us (37%)
  Pallas kernels  15.1 us (18%)
  between operations  1.44 us (2%)
    ppermute x24, starting transfers between devices, swap(): return lax.ppermute(values, axis, [(i, i ^ mask) for i in range(size)])  36.7 us
    ppermute x24, waiting for transfers between devices, swap(): return lax.ppermute(values, axis, [(i, i ^ mask) for i in range(size)])  30.8 us
    pallas_call x1, Pallas kernels, early_tiles(): pl.pallas_call(early_kernel, out_shape=pltpu.VMEM((EARLY * PER + 1, TILE,...  3.62 us
    pallas_call x1, Pallas kernels, pick(): pl.pallas_call(functools.partial(pick_kernel, n_out), out_shape=[pltpu.SM...  2.87 us
    pallas_call x1, Pallas kernels, prepare(): pl.pallas_call(functools.partial(prepare_kernel, n_back), out_shape=[pltp...  2.59 us
    pallas_call x1, Pallas kernels, tiles_forward(): pl.pallas_call(forward_kernel, out_shape=[pltpu.VMEM((length + 1, TILE, T...  2.21 us
    pallas_call x1, Pallas kernels, tiles_backward(): pl.pallas_call(backward_kernel, out_shape=[pltpu.VMEM((rows, TILE), F32),...  1.72 us
  transfers between devices with their start and end apart: 24, of which 17 were waited for; matrix products, arithmetic and copies ran while one was open for 0% of the time, Pallas kernels for 11%

profile of v6, /device:TPU:0, one launch (start us, length us, event | category | flops | bytes accessed | tf_op | source)
XLA Modules:
  0.0 84.3 jit_solution(10770568056947441426)
XLA Ops:
  0.6 0.0 copy-start
  1.3 0.2 copy-done
  1.6 0.1 pad_add_fusion.ids
  1.6 2.0 %collective-permute-start = (bf16[256,128]{1,0:T(8,128)(2,1)S(1)}, bf16[256,128]{1,0:T(8,128)(2,1)S(1)}, u32[]{:S(2)}, u32[]{:S(2)}) collective-permute-start(bf16[256,128]{1,0:T(8,128)(2,1)S(1)} %constant_dynamic-slice_fusion.a), channel_id=1, source_target_pairs={{0,16},{16,0},{32,48},{48,32},{64,80},{80,64},{96,112},{112,96},{1... | collective-permute-start | bytes 196616 | tf_op jit(solution)/shard_map/ppermute | solution.py:28
  3.7 2.9 %pick_tiles.1 = (s32[1,768]{1,0:T(1,128)S(4)}, s32[1,768]{1,0:T(1,128)S(4)}, s32[1]{0:T(128)S(4)}, s32[3]{0:T(128)S(4)}, s32[1,640]{1,0:T(1,128)S(1)}) custom-call(s32[4]{0:T(128)S(1)} %pad_add_fusion.ids, s32[1,1,640]{2,1,0:T(1,128)} %rows.3, s32[1,1,640]{2,1,0:T(1,128)} %columns.3), custom_call_target="tpu_custom_call" | custom-call | tf_op jit(solution)/shard_map/pick_tiles/pallas_call | solution.py:118
  6.5 0.0 collective-permute-done.b
  6.6 3.3 %collective-permute-start.3 = (bf16[512,128]{1,0:T(8,128)(2,1)S(1)}, bf16[512,128]{1,0:T(8,128)(2,1)S(1)}, u32[]{:S(2)}, u32[]{:S(2)}) collective-permute-start(bf16[512,128]{1,0:T(8,128)(2,1)S(1)} %join.1.refs_0_), channel_id=1, source_target_pairs={{0,64},{16,80},{32,96},{48,112},{64,0},{80,16},{96,32},{112,48},{1... | collective-permute-start | bytes 393224 | tf_op jit(solution)/shard_map/ppermute | solution.py:28
  9.8 1.1 %collective-permute-start.2 = (bf16[512,128]{1,0:T(8,128)(2,1)S(1)}, bf16[512,128]{1,0:T(8,128)(2,1)S(1)}, u32[]{:S(2)}, u32[]{:S(2)}) collective-permute-start(bf16[512,128]{1,0:T(8,128)(2,1)S(1)} %join.1.refs_0_), channel_id=1, source_target_pairs={{0,96},{16,112},{32,64},{48,80},{64,32},{80,48},{96,0},{112,16},{1... | collective-permute-start | bytes 393224 | tf_op jit(solution)/shard_map/ppermute | solution.py:28
  10.9 0.0 collective-permute-start.1
  10.9 3.6 %early_tiles.1.early = bf16[161,128,128]{2,1,0:T(8,128)(2,1)S(1)} custom-call(s32[1]{0:T(128)S(4)} %get-tuple-element.72.steps, s32[1,768]{1,0:T(1,128)S(4)} %get-tuple-element.74.fetched, bf16[640,128,128]{2,1,0:T(8,128)(2,1)} %bitcast.8), custom_call_target="tpu_custom_call" | custom-call | tf_op jit(solution)/shard_map/early_tiles/pallas_call | solution.py:162
  14.5 0.0 collective-permute-done.3.refs_2_
  14.5 1.5 %collective-permute-done.2.refs_3_ = bf16[512,128]{1,0:T(8,128)(2,1)S(1)} collective-permute-done((bf16[512,128]{1,0:T(8,128)(2,1)S(1)}, bf16[512,128]{1,0:T(8,128)(2,1)S(1)}, u32[]{:S(2)}, u32[]{:S(2)}) %collective-permute-start.2) | collective-permute-done | bytes 131104 | tf_op jit(solution)/shard_map/ppermute | solution.py:28
  16.0 0.2 collective-permute-done.1.refs_1_
  16.3 2.2 %tiles_forward.1 = (bf16[673,128,128]{2,1,0:T(8,128)(2,1)S(1)}, f32[4,4,128,128]{3,2,1,0:T(8,128)S(1)}, bf16[4,4,128,128]{3,2,1,0:T(8,128)(2,1)S(1)}) custom-call(s32[1]{0:T(128)S(4)} %get-tuple-element.72.steps, s32[3]{0:T(128)S(4)} %get-tuple-element.73.ids, s32[1,768]{1,0:T(1,128)S(4)} %get-tuple-element.74.fetched, ...), custom_call_target="tpu_custom_call" | custom-call | tf_op jit(solution)/shard_map/tiles_forward/pallas_call | solution.py:316
  18.5 0.1 collective-permute-start.4
  18.6 1.9 %collective-permute-done.4.got = bf16[4,4,128,128]{3,2,1,0:T(8,128)(2,1)S(1)} collective-permute-done((bf16[4,4,128,128]{3,2,1,0:T(8,128)(2,1)S(1)}, bf16[4,4,128,128]{3,2,1,0:T(8,128)(2,1)S(1)}, u32[]{:S(2)}, u32[]{:S(2)}) %collective-permute-start.4) | collective-permute-done | bytes 524320 | tf_op jit(solution)/shard_map/ppermute | solution.py:28
  20.5 0.1 pair_sum.1
  20.6 3.1 %collective-permute-start.5 = (bf16[4,128,128]{2,1,0:T(8,128)(2,1)S(1)}, bf16[4,128,128]{2,1,0:T(8,128)(2,1)S(1)}, u32[]{:S(2)}, u32[]{:S(2)}) collective-permute-start(bf16[4,128,128]{2,1,0:T(8,128)(2,1)S(1)} %get-tuple-element.84), channel_id=1, source_target_pairs={{0,8},{2,10},{4,12},{6,14},{8,0},{10,2},{12,4},{14,6},{1,9},{3,11}... | collective-permute-start | bytes 393224 | tf_op jit(solution)/shard_map/ppermute | solution.py:28
  23.7 4.0 %collective-permute-start.6 = (bf16[4,128,128]{2,1,0:T(8,128)(2,1)S(1)}, bf16[4,128,128]{2,1,0:T(8,128)(2,1)S(1)}, u32[]{:S(2)}, u32[]{:S(2)}) collective-permute-start(bf16[4,128,128]{2,1,0:T(8,128)(2,1)S(1)} %get-tuple-element.85), channel_id=1, source_target_pairs={{0,4},{2,6},{4,0},{6,2},{8,12},{10,14},{12,8},{14,10},{1,5},{3,7},... | collective-permute-start | bytes 393224 | tf_op jit(solution)/shard_map/ppermute | solution.py:28
  27.7 0.0 collective-permute-start.7
  27.7 0.0 collective-permute-done.5.a
  27.7 6.3 %collective-permute-done.6.b = bf16[4,128,128]{2,1,0:T(8,128)(2,1)S(1)} collective-permute-done((bf16[4,128,128]{2,1,0:T(8,128)(2,1)S(1)}, bf16[4,128,128]{2,1,0:T(8,128)(2,1)S(1)}, u32[]{:S(2)}, u32[]{:S(2)}) %collective-permute-start.6) | collective-permute-done | bytes 131104 | tf_op jit(solution)/shard_map/ppermute | solution.py:28
  34.0 0.0 collective-permute-done.7.c
  34.0 0.1 own_sum.1
  34.1 3.7 %collective-permute-start.8 = (bf16[4,128,128]{2,1,0:T(8,128)(2,1)S(1)}, bf16[4,128,128]{2,1,0:T(8,128)(2,1)S(1)}, u32[]{:S(2)}, u32[]{:S(2)}) collective-permute-start(bf16[4,128,128]{2,1,0:T(8,128)(2,1)S(1)} %get-tuple-element.90), channel_id=1, source_target_pairs={{0,1},{1,0},{2,3},{3,2},{4,5},{5,4},{6,7},{7,6},{8,9},{9,8},{10,11... | collective-permute-start | bytes 393224 | tf_op jit(solution)/shard_map/ppermute | solution.py:28
  37.8 2.6 %prepare.1 = (s32[1,768]{1,0:T(1,128)S(4)}, s32[1]{0:T(128)S(4)}, bf16[128,128]{1,0:T(8,128)(2,1)S(1)}, f32[1,128]{1,0:T(1,128)S(1)}, bf16[512,128]{1,0:T(8,128)(2,1)S(1)}) custom-call(s32[3]{0:T(128)S(4)} %get-tuple-element.73.ids, s32[1,1,640]{2,1,0:T(1,128)} %rows.3, s32[1,1,640]{2,1,0:T(1,128)} %columns.3, s32[1,640]{1,0:T(1,128)S(1)} %get-tuple-element.91.slots, ...), custom_call_target="tpu_custom_call" | custom-call | tf_op jit(solution)/shard_map/prepare/pallas_call | solution.py:208
  40.4 0.4 collective-permute-done.8.other
  40.7 0.9 %middle.1 = (bf16[512,128]{1,0:T(8,128)(2,1)}, f32[4,128,128]{2,1,0:T(8,128)S(1)}, bf16[4,128,128]{2,1,0:T(8,128)(2,1)S(1)}, f32[136,128]{1,0:T(8,128)S(1)}) custom-call(f32[4,128,128]{2,1,0:T(8,128)S(1)} %get-tuple-element.87.own, bf16[4,128,128]{2,1,0:T(8,128)(2,1)S(1)} %collective-permute-done.8.other, bf16[128,128]{1,0:T(8,128)(2,1)S(1)} %get-tuple-element.98.weight, ...), custom_call_target="tpu_custom_call" | custom-call | tf_op jit(solution)/shard_map/middle/pallas_call | solution.py:466
  41.6 3.5 %collective-permute-start.9 = (bf16[4,128,128]{2,1,0:T(8,128)(2,1)S(1)}, bf16[4,128,128]{2,1,0:T(8,128)(2,1)S(1)}, u32[]{:S(2)}, u32[]{:S(2)}) collective-permute-start(bf16[4,128,128]{2,1,0:T(8,128)(2,1)S(1)} %get-tuple-element.106), channel_id=1, source_target_pairs={{0,1},{1,0},{2,3},{3,2},{4,5},{5,4},{6,7},{7,6},{8,9},{9,8},{10,11... | collective-permute-start | bytes 393224 | tf_op jit(solution)/shard_map/ppermute | solution.py:28
  45.1 0.0 collective-permute-start.10
  45.1 1.3 %collective-permute-done.10.more = f32[136,128]{1,0:T(8,128)S(1)} collective-permute-done((f32[136,128]{1,0:T(8,128)S(1)}, f32[136,128]{1,0:T(8,128)S(1)}, u32[]{:S(2)}, u32[]{:S(2)}) %collective-permute-start.10) | collective-permute-done | bytes 69664 | tf_op jit(solution)/shard_map/ppermute | solution.py:28
  46.4 1.7 %collective-permute-done.9.other = bf16[4,128,128]{2,1,0:T(8,128)(2,1)S(1)} collective-permute-done((bf16[4,128,128]{2,1,0:T(8,128)(2,1)S(1)}, bf16[4,128,128]{2,1,0:T(8,128)(2,1)S(1)}, u32[]{:S(2)}, u32[]{:S(2)}) %collective-permute-start.9) | collective-permute-done | bytes 131104 | tf_op jit(solution)/shard_map/ppermute | solution.py:28
  48.1 1.3 %collective-permute-start.14 = (bf16[592,128]{1,0:T(8,128)(2,1)S(1)}, bf16[592,128]{1,0:T(8,128)(2,1)S(1)}, u32[]{:S(2)}, u32[]{:S(2)}) collective-permute-start(bf16[592,128]{1,0:T(8,128)(2,1)S(1)} %message.1.refs_0_), channel_id=1, source_target_pairs={{0,8},{2,10},{4,12},{6,14},{8,0},{10,2},{12,4},{14,6},{1,9},{3,11}... | collective-permute-start | bytes 454664 | tf_op jit(solution)/shard_map/ppermute | solution.py:28
  49.4 2.4 %collective-permute-start.13 = (bf16[592,128]{1,0:T(8,128)(2,1)S(1)}, bf16[592,128]{1,0:T(8,128)(2,1)S(1)}, u32[]{:S(2)}, u32[]{:S(2)}) collective-permute-start(bf16[592,128]{1,0:T(8,128)(2,1)S(1)} %message.1.refs_0_), channel_id=1, source_target_pairs={{0,12},{2,14},{4,8},{6,10},{8,4},{10,6},{12,0},{14,2},{1,13},{3,15... | collective-permute-start | bytes 454664 | tf_op jit(solution)/shard_map/ppermute | solution.py:28
  51.8 0.6 collective-permute-start.12
  52.4 0.0 collective-permute-start.11
  52.4 4.0 %collective-permute-done.14.refs_4_ = bf16[592,128]{1,0:T(8,128)(2,1)S(1)} collective-permute-done((bf16[592,128]{1,0:T(8,128)(2,1)S(1)}, bf16[592,128]{1,0:T(8,128)(2,1)S(1)}, u32[]{:S(2)}, u32[]{:S(2)}) %collective-permute-start.14) | collective-permute-done | bytes 151584 | tf_op jit(solution)/shard_map/ppermute | solution.py:28
  56.4 0.9 %collective-permute-done.13.refs_6_ = bf16[592,128]{1,0:T(8,128)(2,1)S(1)} collective-permute-done((bf16[592,128]{1,0:T(8,128)(2,1)S(1)}, bf16[592,128]{1,0:T(8,128)(2,1)S(1)}, u32[]{:S(2)}, u32[]{:S(2)}) %collective-permute-start.13) | collective-permute-done | bytes 151584 | tf_op jit(solution)/shard_map/ppermute | solution.py:28
  57.3 0.6 collective-permute-done.12.refs_2_
  57.9 0.0 collective-permute-start.15
  57.9 0.5 collective-permute-start.16
  58.4 0.0 collective-permute-start.17
  58.4 0.0 collective-permute-done.11.refs_1_
  58.4 0.9 %collective-permute-done.15.refs_3_ = bf16[592,128]{1,0:T(8,128)(2,1)S(1)} collective-permute-done((bf16[592,128]{1,0:T(8,128)(2,1)S(1)}, bf16[592,128]{1,0:T(8,128)(2,1)S(1)}, u32[]{:S(2)}, u32[]{:S(2)}) %collective-permute-start.15) | collective-permute-done | bytes 151584 | tf_op jit(solution)/shard_map/ppermute | solution.py:28
  59.3 0.2 collective-permute-done.16.refs_5_
  59.5 0.3 collective-permute-done.17.refs_7_
  59.8 1.7 %tiles_backward.1 = (f32[512,128]{1,0:T(8,128)S(1)}, f32[136,128]{1,0:T(8,128)S(1)}, bf16[656,128]{1,0:T(8,128)(2,1)S(1)}, bf16[656,128]{1,0:T(8,128)(2,1)S(1)}, bf16[656,128]{1,0:T(8,128)(2,1)S(1)}) custom-call(s32[1]{0:T(128)S(4)} %get-tuple-element.102.steps, s32[3]{0:T(128)S(4)} %get-tuple-element.73.ids, s32[1,768]{1,0:T(1,128)S(4)} %get-tuple-element.103.picked, ...), custom_call_target="tpu_custom_call" | custom-call | tf_op jit(solution)/shard_map/tiles_backward/pallas_call | solution.py:389
  61.5 3.0 %collective-permute-start.18 = (bf16[656,128]{1,0:T(8,128)(2,1)S(1)}, bf16[656,128]{1,0:T(8,128)(2,1)S(1)}, u32[]{:S(2)}, u32[]{:S(2)}) collective-permute-start(bf16[656,128]{1,0:T(8,128)(2,1)S(1)} %get-tuple-element.115), channel_id=1, source_target_pairs={{0,64},{16,80},{32,96},{48,112},{64,0},{80,16},{96,32},{112,48},{1... | collective-permute-start | bytes 503816 | tf_op jit(solution)/shard_map/ppermute | solution.py:28
  64.5 1.1 %collective-permute-start.19 = (bf16[656,128]{1,0:T(8,128)(2,1)S(1)}, bf16[656,128]{1,0:T(8,128)(2,1)S(1)}, u32[]{:S(2)}, u32[]{:S(2)}) collective-permute-start(bf16[656,128]{1,0:T(8,128)(2,1)S(1)} %get-tuple-element.116), channel_id=1, source_target_pairs={{0,32},{16,48},{32,0},{48,16},{64,96},{80,112},{96,64},{112,80},{1... | collective-permute-start | bytes 503816 | tf_op jit(solution)/shard_map/ppermute | solution.py:28
  65.6 2.4 %collective-permute-start.20 = (bf16[656,128]{1,0:T(8,128)(2,1)S(1)}, bf16[656,128]{1,0:T(8,128)(2,1)S(1)}, u32[]{:S(2)}, u32[]{:S(2)}) collective-permute-start(bf16[656,128]{1,0:T(8,128)(2,1)S(1)} %get-tuple-element.117), channel_id=1, source_target_pairs={{0,96},{16,112},{32,64},{48,80},{64,32},{80,48},{96,0},{112,16},{1... | collective-permute-start | bytes 503816 | tf_op jit(solution)/shard_map/ppermute | solution.py:28
  67.9 2.3 %collective-permute-done.18.a = bf16[656,128]{1,0:T(8,128)(2,1)S(1)} collective-permute-done((bf16[656,128]{1,0:T(8,128)(2,1)S(1)}, bf16[656,128]{1,0:T(8,128)(2,1)S(1)}, u32[]{:S(2)}, u32[]{:S(2)}) %collective-permute-start.18) | collective-permute-done | bytes 167968 | tf_op jit(solution)/shard_map/ppermute | solution.py:28
  70.2 2.9 %collective-permute-done.19.b = bf16[656,128]{1,0:T(8,128)(2,1)S(1)} collective-permute-done((bf16[656,128]{1,0:T(8,128)(2,1)S(1)}, bf16[656,128]{1,0:T(8,128)(2,1)S(1)}, u32[]{:S(2)}, u32[]{:S(2)}) %collective-permute-start.19) | collective-permute-done | bytes 167968 | tf_op jit(solution)/shard_map/ppermute | solution.py:28
  73.1 0.0 collective-permute-done.20.c
  73.1 0.1 line_sum.1
  73.2 0.9 %collective-permute-start.23 = (bf16[400,128]{1,0:T(8,128)(2,1)S(1)}, bf16[400,128]{1,0:T(8,128)(2,1)S(1)}, u32[]{:S(2)}, u32[]{:S(2)}) collective-permute-start(bf16[400,128]{1,0:T(8,128)(2,1)S(1)} %get-tuple-element.122), channel_id=1, source_target_pairs={{0,16},{16,0},{32,48},{48,32},{64,80},{80,64},{96,112},{112,96},{1... | collective-permute-start | bytes 307208 | tf_op jit(solution)/shard_map/ppermute | solution.py:28
  74.1 3.9 %collective-permute-start.21 = (bf16[256,128]{1,0:T(8,128)(2,1)S(1)}, bf16[256,128]{1,0:T(8,128)(2,1)S(1)}, u32[]{:S(2)}, u32[]{:S(2)}) collective-permute-start(bf16[256,128]{1,0:T(8,128)(2,1)S(1)} %get-tuple-element.120), channel_id=1, source_target_pairs={{0,1},{1,0},{2,3},{3,2},{4,5},{5,4},{6,7},{7,6},{8,9},{9,8},{10,11... | collective-permute-start | bytes 196616 | tf_op jit(solution)/shard_map/ppermute | solution.py:28
  78.0 0.1 collective-permute-start.22
  78.0 3.6 %collective-permute-done.21.opposite = bf16[256,128]{1,0:T(8,128)(2,1)S(1)} collective-permute-done((bf16[256,128]{1,0:T(8,128)(2,1)S(1)}, bf16[256,128]{1,0:T(8,128)(2,1)S(1)}, u32[]{:S(2)}, u32[]{:S(2)}) %collective-permute-start.21) | collective-permute-done | bytes 65568 | tf_op jit(solution)/shard_map/ppermute | solution.py:28
  81.6 1.8 %collective-permute-done.22.corner = bf16[256,128]{1,0:T(8,128)(2,1)S(1)} collective-permute-done((bf16[256,128]{1,0:T(8,128)(2,1)S(1)}, bf16[256,128]{1,0:T(8,128)(2,1)S(1)}, u32[]{:S(2)}, u32[]{:S(2)}) %collective-permute-start.22) | collective-permute-done | bytes 65568 | tf_op jit(solution)/shard_map/ppermute | solution.py:28
  83.4 0.0 collective-permute-done.23.beside
  83.4 0.8 %finish.1 = (f32[512,128]{1,0:T(8,128)}, f32[128,128]{1,0:T(8,128)}, f32[1,128]{1,0:T(1,128)}) custom-call(s32[3]{0:T(128)S(4)} %get-tuple-element.73.ids, f32[256,128]{1,0:T(8,128)S(1)} %get-tuple-element.118.own, f32[136,128]{1,0:T(8,128)S(1)} %get-tuple-element.119.grads, bf16[256,128]{1,0:T(8,128)(2,1)S(1)} %collective-permute-done.21.opposite, ...), custom_call_target="tpu_custom_call" | custom-call | tf_op jit(solution)/shard_map/finish/pallas_call | solution.py:552
  (3 shorter events, 0.1 us)
Async XLA Ops:
  0.6 0.9 %copy-start = (bf16[512,128]{1,0:T(8,128)(2,1)S(1)}, bf16[512,128]{1,0:T(8,128)(2,1)}, u32[]{:S(2)}) copy-start(bf16[512,128]{1,0:T(8,128)(2,1)} %param.8) | copy-start | bytes 393220
  1.6 4.9 %collective-permute-start = (bf16[256,128]{1,0:T(8,128)(2,1)S(1)}, bf16[256,128]{1,0:T(8,128)(2,1)S(1)}, u32[]{:S(2)}, u32[]{:S(2)}) collective-permute-start(bf16[256,128]{1,0:T(8,128)(2,1)S(1)} %constant_dynamic-slice_fusion.a), channel_id=1, source_target_pairs={{0,16},{16,0},{32,48},{48,32},{64,80},{80,64},{96,112},{112,96},{1... | collective-permute-start | bytes 196616 | tf_op jit(solution)/shard_map/ppermute | solution.py:28
  6.6 8.0 %collective-permute-start.3 = (bf16[512,128]{1,0:T(8,128)(2,1)S(1)}, bf16[512,128]{1,0:T(8,128)(2,1)S(1)}, u32[]{:S(2)}, u32[]{:S(2)}) collective-permute-start(bf16[512,128]{1,0:T(8,128)(2,1)S(1)} %join.1.refs_0_), channel_id=1, source_target_pairs={{0,64},{16,80},{32,96},{48,112},{64,0},{80,16},{96,32},{112,48},{1... | collective-permute-start | bytes 393224 | tf_op jit(solution)/shard_map/ppermute | solution.py:28
  9.8 6.2 %collective-permute-start.2 = (bf16[512,128]{1,0:T(8,128)(2,1)S(1)}, bf16[512,128]{1,0:T(8,128)(2,1)S(1)}, u32[]{:S(2)}, u32[]{:S(2)}) collective-permute-start(bf16[512,128]{1,0:T(8,128)(2,1)S(1)} %join.1.refs_0_), channel_id=1, source_target_pairs={{0,96},{16,112},{32,64},{48,80},{64,32},{80,48},{96,0},{112,16},{1... | collective-permute-start | bytes 393224 | tf_op jit(solution)/shard_map/ppermute | solution.py:28
  10.9 5.4 %collective-permute-start.1 = (bf16[512,128]{1,0:T(8,128)(2,1)S(1)}, bf16[512,128]{1,0:T(8,128)(2,1)S(1)}, u32[]{:S(2)}, u32[]{:S(2)}) collective-permute-start(bf16[512,128]{1,0:T(8,128)(2,1)S(1)} %join.1.refs_0_), channel_id=1, source_target_pairs={{0,32},{16,48},{32,0},{48,16},{64,96},{80,112},{96,64},{112,80},{1... | collective-permute-start | bytes 393224 | tf_op jit(solution)/shard_map/ppermute | solution.py:28
  18.5 2.0 %collective-permute-start.4 = (bf16[4,4,128,128]{3,2,1,0:T(8,128)(2,1)S(1)}, bf16[4,4,128,128]{3,2,1,0:T(8,128)(2,1)S(1)}, u32[]{:S(2)}, u32[]{:S(2)}) collective-permute-start(bf16[4,4,128,128]{3,2,1,0:T(8,128)(2,1)S(1)} %get-tuple-element.82), channel_id=1, source_target_pairs={{0,2},{2,0},{4,6},{6,4},{8,10},{10,8},{12,14},{14,12},{1,3},{3,1},... | collective-permute-start | bytes 1572872 | tf_op jit(solution)/shard_map/ppermute | solution.py:28
  20.6 7.1 %collective-permute-start.5 = (bf16[4,128,128]{2,1,0:T(8,128)(2,1)S(1)}, bf16[4,128,128]{2,1,0:T(8,128)(2,1)S(1)}, u32[]{:S(2)}, u32[]{:S(2)}) collective-permute-start(bf16[4,128,128]{2,1,0:T(8,128)(2,1)S(1)} %get-tuple-element.84), channel_id=1, source_target_pairs={{0,8},{2,10},{4,12},{6,14},{8,0},{10,2},{12,4},{14,6},{1,9},{3,11}... | collective-permute-start | bytes 393224 | tf_op jit(solution)/shard_map/ppermute | solution.py:28
  23.7 10.4 %collective-permute-start.6 = (bf16[4,128,128]{2,1,0:T(8,128)(2,1)S(1)}, bf16[4,128,128]{2,1,0:T(8,128)(2,1)S(1)}, u32[]{:S(2)}, u32[]{:S(2)}) collective-permute-start(bf16[4,128,128]{2,1,0:T(8,128)(2,1)S(1)} %get-tuple-element.85), channel_id=1, source_target_pairs={{0,4},{2,6},{4,0},{6,2},{8,12},{10,14},{12,8},{14,10},{1,5},{3,7},... | collective-permute-start | bytes 393224 | tf_op jit(solution)/shard_map/ppermute | solution.py:28
  27.7 6.4 %collective-permute-start.7 = (bf16[4,128,128]{2,1,0:T(8,128)(2,1)S(1)}, bf16[4,128,128]{2,1,0:T(8,128)(2,1)S(1)}, u32[]{:S(2)}, u32[]{:S(2)}) collective-permute-start(bf16[4,128,128]{2,1,0:T(8,128)(2,1)S(1)} %get-tuple-element.86), channel_id=1, source_target_pairs={{0,12},{2,14},{4,8},{6,10},{8,4},{10,6},{12,0},{14,2},{1,13},{3,15... | collective-permute-start | bytes 393224 | tf_op jit(solution)/shard_map/ppermute | solution.py:28
  34.1 6.6 %collective-permute-start.8 = (bf16[4,128,128]{2,1,0:T(8,128)(2,1)S(1)}, bf16[4,128,128]{2,1,0:T(8,128)(2,1)S(1)}, u32[]{:S(2)}, u32[]{:S(2)}) collective-permute-start(bf16[4,128,128]{2,1,0:T(8,128)(2,1)S(1)} %get-tuple-element.90), channel_id=1, source_target_pairs={{0,1},{1,0},{2,3},{3,2},{4,5},{5,4},{6,7},{7,6},{8,9},{9,8},{10,11... | collective-permute-start | bytes 393224 | tf_op jit(solution)/shard_map/ppermute | solution.py:28
  41.6 6.5 %collective-permute-start.9 = (bf16[4,128,128]{2,1,0:T(8,128)(2,1)S(1)}, bf16[4,128,128]{2,1,0:T(8,128)(2,1)S(1)}, u32[]{:S(2)}, u32[]{:S(2)}) collective-permute-start(bf16[4,128,128]{2,1,0:T(8,128)(2,1)S(1)} %get-tuple-element.106), channel_id=1, source_target_pairs={{0,1},{1,0},{2,3},{3,2},{4,5},{5,4},{6,7},{7,6},{8,9},{9,8},{10,11... | collective-permute-start | bytes 393224 | tf_op jit(solution)/shard_map/ppermute | solution.py:28
  45.1 1.3 %collective-permute-start.10 = (f32[136,128]{1,0:T(8,128)S(1)}, f32[136,128]{1,0:T(8,128)S(1)}, u32[]{:S(2)}, u32[]{:S(2)}) collective-permute-start(f32[136,128]{1,0:T(8,128)S(1)} %get-tuple-element.107.grads), channel_id=1, source_target_pairs={{0,2},{2,0},{4,6},{6,4},{8,10},{10,8},{12,14},{14,12},{1,3},{3,1},... | collective-permute-start | bytes 208904 | tf_op jit(solution)/shard_map/ppermute | solution.py:28
  48.1 8.3 %collective-permute-start.14 = (bf16[592,128]{1,0:T(8,128)(2,1)S(1)}, bf16[592,128]{1,0:T(8,128)(2,1)S(1)}, u32[]{:S(2)}, u32[]{:S(2)}) collective-permute-start(bf16[592,128]{1,0:T(8,128)(2,1)S(1)} %message.1.refs_0_), channel_id=1, source_target_pairs={{0,8},{2,10},{4,12},{6,14},{8,0},{10,2},{12,4},{14,6},{1,9},{3,11}... | collective-permute-start | bytes 454664 | tf_op jit(solution)/shard_map/ppermute | solution.py:28
  49.4 7.9 %collective-permute-start.13 = (bf16[592,128]{1,0:T(8,128)(2,1)S(1)}, bf16[592,128]{1,0:T(8,128)(2,1)S(1)}, u32[]{:S(2)}, u32[]{:S(2)}) collective-permute-start(bf16[592,128]{1,0:T(8,128)(2,1)S(1)} %message.1.refs_0_), channel_id=1, source_target_pairs={{0,12},{2,14},{4,8},{6,10},{8,4},{10,6},{12,0},{14,2},{1,13},{3,15... | collective-permute-start | bytes 454664 | tf_op jit(solution)/shard_map/ppermute | solution.py:28
  51.8 6.0 %collective-permute-start.12 = (bf16[592,128]{1,0:T(8,128)(2,1)S(1)}, bf16[592,128]{1,0:T(8,128)(2,1)S(1)}, u32[]{:S(2)}, u32[]{:S(2)}) collective-permute-start(bf16[592,128]{1,0:T(8,128)(2,1)S(1)} %message.1.refs_0_), channel_id=1, source_target_pairs={{0,4},{2,6},{4,0},{6,2},{8,12},{10,14},{12,8},{14,10},{1,5},{3,7},... | collective-permute-start | bytes 454664 | tf_op jit(solution)/shard_map/ppermute | solution.py:28
  52.4 6.0 %collective-permute-start.11 = (bf16[592,128]{1,0:T(8,128)(2,1)S(1)}, bf16[592,128]{1,0:T(8,128)(2,1)S(1)}, u32[]{:S(2)}, u32[]{:S(2)}) collective-permute-start(bf16[592,128]{1,0:T(8,128)(2,1)S(1)} %message.1.refs_0_), channel_id=1, source_target_pairs={{0,2},{2,0},{4,6},{6,4},{8,10},{10,8},{12,14},{14,12},{1,3},{3,1},... | collective-permute-start | bytes 454664 | tf_op jit(solution)/shard_map/ppermute | solution.py:28
  57.9 1.4 %collective-permute-start.15 = (bf16[592,128]{1,0:T(8,128)(2,1)S(1)}, bf16[592,128]{1,0:T(8,128)(2,1)S(1)}, u32[]{:S(2)}, u32[]{:S(2)}) collective-permute-start(bf16[592,128]{1,0:T(8,128)(2,1)S(1)} %collective-permute-done.12.refs_2_), channel_id=1, source_target_pairs={{0,2},{2,0},{4,6},{6,4},{8,10},{10,8},{12,14},{14,12},{1,3},{3,1},... | collective-permute-start | bytes 454664 | tf_op jit(solution)/shard_map/ppermute | solution.py:28
  57.9 1.6 %collective-permute-start.16 = (bf16[592,128]{1,0:T(8,128)(2,1)S(1)}, bf16[592,128]{1,0:T(8,128)(2,1)S(1)}, u32[]{:S(2)}, u32[]{:S(2)}) collective-permute-start(bf16[592,128]{1,0:T(8,128)(2,1)S(1)} %collective-permute-done.14.refs_4_), channel_id=1, source_target_pairs={{0,2},{2,0},{4,6},{6,4},{8,10},{10,8},{12,14},{14,12},{1,3},{3,1},... | collective-permute-start | bytes 454664 | tf_op jit(solution)/shard_map/ppermute | solution.py:28
  58.4 1.4 %collective-permute-start.17 = (bf16[592,128]{1,0:T(8,128)(2,1)S(1)}, bf16[592,128]{1,0:T(8,128)(2,1)S(1)}, u32[]{:S(2)}, u32[]{:S(2)}) collective-permute-start(bf16[592,128]{1,0:T(8,128)(2,1)S(1)} %collective-permute-done.13.refs_6_), channel_id=1, source_target_pairs={{0,2},{2,0},{4,6},{6,4},{8,10},{10,8},{12,14},{14,12},{1,3},{3,1},... | collective-permute-start | bytes 454664 | tf_op jit(solution)/shard_map/ppermute | solution.py:28
  61.5 8.7 %collective-permute-start.18 = (bf16[656,128]{1,0:T(8,128)(2,1)S(1)}, bf16[656,128]{1,0:T(8,128)(2,1)S(1)}, u32[]{:S(2)}, u32[]{:S(2)}) collective-permute-start(bf16[656,128]{1,0:T(8,128)(2,1)S(1)} %get-tuple-element.115), channel_id=1, source_target_pairs={{0,64},{16,80},{32,96},{48,112},{64,0},{80,16},{96,32},{112,48},{1... | collective-permute-start | bytes 503816 | tf_op jit(solution)/shard_map/ppermute | solution.py:28
  64.5 8.7 %collective-permute-start.19 = (bf16[656,128]{1,0:T(8,128)(2,1)S(1)}, bf16[656,128]{1,0:T(8,128)(2,1)S(1)}, u32[]{:S(2)}, u32[]{:S(2)}) collective-permute-start(bf16[656,128]{1,0:T(8,128)(2,1)S(1)} %get-tuple-element.116), channel_id=1, source_target_pairs={{0,32},{16,48},{32,0},{48,16},{64,96},{80,112},{96,64},{112,80},{1... | collective-permute-start | bytes 503816 | tf_op jit(solution)/shard_map/ppermute | solution.py:28
  65.6 7.6 %collective-permute-start.20 = (bf16[656,128]{1,0:T(8,128)(2,1)S(1)}, bf16[656,128]{1,0:T(8,128)(2,1)S(1)}, u32[]{:S(2)}, u32[]{:S(2)}) collective-permute-start(bf16[656,128]{1,0:T(8,128)(2,1)S(1)} %get-tuple-element.117), channel_id=1, source_target_pairs={{0,96},{16,112},{32,64},{48,80},{64,32},{80,48},{96,0},{112,16},{1... | collective-permute-start | bytes 503816 | tf_op jit(solution)/shard_map/ppermute | solution.py:28
  73.2 10.2 %collective-permute-start.23 = (bf16[400,128]{1,0:T(8,128)(2,1)S(1)}, bf16[400,128]{1,0:T(8,128)(2,1)S(1)}, u32[]{:S(2)}, u32[]{:S(2)}) collective-permute-start(bf16[400,128]{1,0:T(8,128)(2,1)S(1)} %get-tuple-element.122), channel_id=1, source_target_pairs={{0,16},{16,0},{32,48},{48,32},{64,80},{80,64},{96,112},{112,96},{1... | collective-permute-start | bytes 307208 | tf_op jit(solution)/shard_map/ppermute | solution.py:28
  74.1 7.5 %collective-permute-start.21 = (bf16[256,128]{1,0:T(8,128)(2,1)S(1)}, bf16[256,128]{1,0:T(8,128)(2,1)S(1)}, u32[]{:S(2)}, u32[]{:S(2)}) collective-permute-start(bf16[256,128]{1,0:T(8,128)(2,1)S(1)} %get-tuple-element.120), channel_id=1, source_target_pairs={{0,1},{1,0},{2,3},{3,2},{4,5},{5,4},{6,7},{7,6},{8,9},{9,8},{10,11... | collective-permute-start | bytes 196616 | tf_op jit(solution)/shard_map/ppermute | solution.py:28
  78.0 5.5 %collective-permute-start.22 = (bf16[256,128]{1,0:T(8,128)(2,1)S(1)}, bf16[256,128]{1,0:T(8,128)(2,1)S(1)}, u32[]{:S(2)}, u32[]{:S(2)}) collective-permute-start(bf16[256,128]{1,0:T(8,128)(2,1)S(1)} %get-tuple-element.121), channel_id=1, source_target_pairs={{0,17},{1,16},{16,1},{17,0},{32,49},{33,48},{48,33},{49,32},{64,81... | collective-permute-start | bytes 196616 | tf_op jit(solution)/shard_map/ppermute | solution.py:28

commit v7 on v6

--- a/solution.py
+++ b/solution.py
@@ -48,18 +48,27 @@
     return lax.broadcasted_iota(jnp.int32, shape, dim)
 
 
-def order(key, used, source, item, n_keys, length, width):
+def order(key, used, source, item, n_keys, length, width, split=0):
     n = key.shape[1]
     hit = ((iota((n_keys, n), 0) == key) & used).astype(F32)
     upto = (iota((n, n), 0) <= iota((n, n), 1)).astype(BF16)
     rank = jnp.dot(hit.astype(BF16), upto, preferred_element_type=F32)
     groups = jnp.floor((rank[:, n - 1 :] + (width - 1)) * (1.0 / width))
     below = (iota((n_keys, n_keys), 0) >= iota((n_keys, n_keys), 1)).astype(BF16)
+    groups = jnp.broadcast_to(groups, (n_keys, TILE))
     high = jnp.floor(groups * (1.0 / 128))
-    lane = iota((n_keys, TILE), 1)
-    parts = jnp.where(lane == 0, groups - high * 128, jnp.where(lane == 1, high, 0.0))
-    ends = jnp.dot(below, parts.astype(BF16), preferred_element_type=F32)
-    end = ends[:, 0:1] + ends[:, 1:2] * 128
+    low = groups - high * 128
+    end = jnp.dot(below, low.astype(BF16), preferred_element_type=F32)
+    end = end + jnp.dot(below, high.astype(BF16), preferred_element_type=F32) * 128
+    n_first = 0
+    if split:
+        part = iota((n_keys, TILE), 0) < split
+        before = jnp.where(part, end, 0.0)
+        n_first = (jnp.max(before).astype(jnp.int32) * width + PER - 1) // PER
+        before = jnp.max(before, axis=0, keepdims=True)
+        steps = jnp.floor((before * width + (PER - 1)) * (1.0 / PER))
+        end = end + jnp.where(part, 0.0, steps * (PER // width) - before)
+    groups, end = groups[:, :1], end[:, :1]
     first = (end - groups) * width
     slot = jnp.sum(hit * (first + rank - 1.0), axis=0, keepdims=True)
     slot = jnp.where(used, slot.astype(jnp.int32), -1)
@@ -74,28 +83,21 @@
     target = jnp.sum(passed.astype(F32), axis=0, keepdims=True).astype(jnp.int32)
     items = jnp.where(found[3:4] > 0, found[0:1] + found[1:2] * 256, -1)
     steps = (jnp.max(end).astype(jnp.int32) * width + PER - 1) // PER
-    return items, found[2:3], target, steps, slot
+    return items, found[2:3], target, steps, slot, n_first
 
 
 def pick_kernel(n_out, ids, rows, columns, *refs):
-    fetched, forward, steps, same_ids, slots = refs[:5]
-    row_copy, column_copy, fetched_copy, forward_copy, arrived = refs[5:]
-    copies = [
-        pltpu.make_async_copy(rows.at[0], row_copy, arrived.at[0]),
-        pltpu.make_async_copy(columns.at[0], column_copy, arrived.at[1]),
-    ]
-    for copy in copies:
-        copy.start()
+    fetched, forward, steps, same_ids, slots, fetched_copy, forward_copy, arrived = refs
     for k in range(3):
         same_ids[k] = ids[k]
-    for copy in copies:
-        copy.wait()
-    row, column = row_copy[...], column_copy[...]
+    row, column = rows[0], columns[0]
     index = iota(row.shape, 1)
     length = forward.shape[1]
     used = (index < ids[3]) & (((column >> 1) & 1) == ids[0])
     source = jnp.bitwise_xor(column >> 2, ids[2]) * 2 + (column & 1)
-    items, source, target, n_steps, slot = order(row, used, source, index, n_out, length, FORWARD)
+    items, source, target, n_steps, slot, _ = order(
+        row, used, source, index, n_out, length, FORWARD
+    )
     fetched_copy[...] = jnp.maximum(items, 0)
     here = jnp.where(items >= 0, iota(items.shape, 1), SPARE)
     forward_copy[...] = here + source * 1024 + target * 65536
@@ -112,7 +114,7 @@
 
 
 def pick(ids, rows, columns, n_out, n_back):
-    length = rows.shape[-1] + max(n_out * (FORWARD - 1), n_back * (BACKWARD - 1)) + PER
+    length = rows.shape[-1] + max(n_out * (FORWARD - 1), n_back * (BACKWARD - 1)) + 2 * PER
     length = -(-length // TILE) * TILE
     listed = (1, length)
     return pl.pallas_call(
@@ -124,11 +126,9 @@
             pltpu.SMEM((3,), jnp.int32),
             pltpu.VMEM(rows.shape[1:], jnp.int32),
         ],
-        in_specs=[SMEM, ANY, ANY],
+        in_specs=[SMEM, VMEM, VMEM],
         out_specs=[SMEM, SMEM, SMEM, SMEM, VMEM],
         scratch_shapes=[
-            pltpu.VMEM(rows.shape[1:], jnp.int32),
-            pltpu.VMEM(rows.shape[1:], jnp.int32),
             pltpu.VMEM(listed, jnp.int32),
             pltpu.VMEM(listed, jnp.int32),
             pltpu.SemaphoreType.DMA((2,)),
@@ -190,17 +190,21 @@
         copy.wait()
     row, column, slot = row_copy[...], column_copy[...], slots[...]
     length = backward.shape[1]
-    place = (column >> 2) * 2 + (column & 1)
+    owner = jnp.bitwise_xor(column >> 2, ids[2])
+    chip = owner >> 1
+    chip = jnp.where(chip == 2, 0, jnp.where(chip == 1, 1, jnp.where(chip == 3, 2, 3)))
+    place = chip * 4 + (owner & 1) * 2 + (column & 1)
     source = jnp.bitwise_xor(row >> 2, ids[1]) * 4 + (row & 3)
     used = slot >= 0
-    items, source, target, n_steps, slot = order(
-        place, used, source, slot, n_back, length, BACKWARD
+    items, source, target, n_steps, slot, n_first = order(
+        place, used, source, slot, n_back, length, BACKWARD, 4
     )
     here = jnp.where(items >= 0, items, SPARE)
     backward_copy[...] = here + source * 1024 + target * 65536
     copy = pltpu.make_async_copy(backward_copy, backward, arrived.at[5])
     copy.start()
-    steps[0] = n_steps
+    steps[0] = n_first
+    steps[1] = n_steps
     copy.wait()
 
 
@@ -209,7 +213,7 @@
         functools.partial(prepare_kernel, n_back),
         out_shape=[
             pltpu.SMEM((1, length), jnp.int32),
-            pltpu.SMEM((1,), jnp.int32),
+            pltpu.SMEM((2,), jnp.int32),
             pltpu.VMEM(weight.shape, weight.dtype),
             pltpu.VMEM(bias.shape, bias.dtype),
             pltpu.VMEM(cotangent.shape, cotangent.dtype),
@@ -358,9 +362,8 @@
     return jnp.broadcast_to(jnp.sum(terms, axis=0, keepdims=True), (8, TILE))
 
 
-def backward_kernel(steps, ids, picked, held, *refs):
-    messages, outs, (gathered, total) = refs[:-7], refs[-7:-2], refs[-2:]
-    kept, grads, outs = outs[0], outs[1], (outs[0], *outs[2:])
+def first_kernel(steps, ids, picked, held, *refs):
+    messages, (gathered, grads, out, total) = refs[:-4], refs[-4:]
     total[...] = jnp.zeros_like(total)
     rows = 4 * TILE
     for m, one in enumerate(messages):
@@ -373,32 +376,57 @@
         grads[pl.ds(jnp.bitwise_xor(ids[1] & 1, k) * (TILE // 2), TILE // 2)] = weight
     bias = read_terms(messages[0::2], rows + TILE // 2)
     grads[TILE : TILE + 8] = bias
-    for out in outs[1:]:
+    out[rows : rows + TILE] = grads[0:TILE].astype(BF16)
+    write_terms(bias, out, rows + TILE)
+    run_steps(0, steps[0], lambda g: add_products(True, g * PER, picked, held, gathered, total))
+    out[0:rows] = total[0:4].reshape(rows, TILE).astype(BF16)
+
+
+def tiles_first(steps, ids, picked, held, sources):
+    rows = 4 * TILE
+    return pl.pallas_call(
+        first_kernel,
+        out_shape=[
+            pltpu.VMEM((4 * len(sources), TILE, TILE), BF16),
+            pltpu.VMEM((TILE + 8, TILE), F32),
+            pltpu.VMEM((rows + TILE + 16, TILE), BF16),
+        ],
+        in_specs=[SMEM, SMEM, SMEM] + [VMEM] * (1 + len(sources)),
+        out_specs=[VMEM] * 3,
+        scratch_shapes=[pltpu.VMEM((5, TILE, TILE), F32)],
+        compiler_params=PARAMS,
+        name="tiles_first",
+    )(scalar(steps), scalar(ids), scalar(picked), near(held), *[near(values) for values in sources])
+
+
+def second_kernel(steps, picked, held, gathered, grads, kept, second, third, total):
+    total[...] = jnp.zeros_like(total)
+    rows = 4 * TILE
+    for out in (second, third):
         out[rows : rows + TILE] = grads[0:TILE].astype(BF16)
-        write_terms(bias, out, rows + TILE)
-
-    run_steps(0, steps[0], lambda g: add_products(True, g * PER, picked, held, gathered, total))
-    for k, out in zip((0, 2, 1, 3), outs):
-        for z in range(2):
-            block = total[pl.ds(jnp.bitwise_xor(ids[2], 2 * k + z) * 2, 2)]
-            out[2 * z * TILE : 2 * (z + 1) * TILE] = block.reshape(2 * TILE, TILE).astype(out.dtype)
-
-
-def tiles_backward(steps, ids, picked, held, sources, n_back):
-    rows = n_back // 4 * TILE
-    return pl.pallas_call(
-        backward_kernel,
-        out_shape=[pltpu.VMEM((rows, TILE), F32), pltpu.VMEM((TILE + 8, TILE), F32)]
-        + [pltpu.VMEM((rows + TILE + 16, TILE), BF16)] * 3,
-        in_specs=[SMEM, SMEM, SMEM] + [VMEM] * (1 + len(sources)),
-        out_specs=[VMEM] * 5,
-        scratch_shapes=[
-            pltpu.VMEM((4 * len(sources), TILE, TILE), BF16),
-            pltpu.VMEM((n_back + 1, TILE, TILE), F32),
-        ],
-        compiler_params=PARAMS,
-        name="tiles_backward",
-    )(scalar(steps), scalar(ids), scalar(picked), near(held), *[near(values) for values in sources])
+        write_terms(grads[TILE : TILE + 8], out, rows + TILE)
+    run_steps(steps[0], steps[1], lambda g: add_products(True, g * PER, picked, held, gathered, total))
+    for k, out in enumerate((second, third, kept)):
+        out[0:rows] = total[4 * k + 4 : 4 * k + 8].reshape(rows, TILE).astype(out.dtype)
+
+
+def tiles_second(steps, picked, held, gathered, grads, n_back):
+    rows = 4 * TILE
+    return pl.pallas_call(
+        second_kernel,
+        out_shape=[pltpu.VMEM((rows, TILE), F32)]
+        + [pltpu.VMEM((rows + TILE + 16, TILE), BF16)] * 2,
+        in_specs=[SMEM, SMEM] + [VMEM] * 3,
+        out_specs=[VMEM] * 3,
+        scratch_shapes=[pltpu.VMEM((n_back + 1, TILE, TILE), F32)],
+        compiler_params=PARAMS,
+        cost_estimate=pl.CostEstimate(
+            flops=held.shape[0] * 2 * TILE**3,
+            bytes_accessed=held.shape[0] * 2 * TILE**2,
+            transcendentals=0,
+        ),
+        name="tiles_second",
+    )(scalar(steps), scalar(picked), near(held), near(gathered), near(grads))
 
 
 def pair_kernel(kept, got, first, *others):
@@ -499,14 +527,32 @@
     )(scalar(ids), near(back), near(other), near(grads), near(more))
 
 
-def line_kernel(kept, grads, a, b, c, own_sent, other_sent, other_message, own, own_grads):
+def near_kernel(kept, grads, a, value, sums):
+    rows = kept.shape[0]
+    value[...] = kept[...] + a[0:rows].astype(F32)
+    sums[0:TILE] = grads[0:TILE] + a[rows : rows + TILE].astype(F32)
+    sums[TILE : TILE + 8] = grads[TILE : TILE + 8] + read_terms((a,), rows + TILE)
+
+
+def first_sum(kept, grads, message):
+    return pl.pallas_call(
+        near_kernel,
+        out_shape=[pltpu.VMEM(kept.shape, F32), pltpu.VMEM(grads.shape, F32)],
+        in_specs=[VMEM] * 3,
+        out_specs=[VMEM] * 2,
+        compiler_params=PARAMS,
+        name="first_sum",
+    )(near(kept), near(grads), near(message))
+
+
+def line_kernel(kept, grads, a, b, own_sent, other_sent, other_message, own, own_grads):
     rows = own.shape[0]
     value = kept[...]
     weight = grads[0:TILE]
-    for one in (a, b, c):
+    for one in (a, b):
         value = value + one[0 : 2 * rows].astype(F32)
         weight = weight + one[2 * rows : 2 * rows + TILE].astype(F32)
-    bias = grads[TILE : TILE + 8] + read_terms((a, b, c), 2 * rows + TILE)
+    bias = grads[TILE : TILE + 8] + read_terms((a, b), 2 * rows + TILE)
     own[...] = value[:rows]
     own_sent[...] = value[:rows].astype(BF16)
     other = value[rows:].astype(BF16)
@@ -529,7 +575,7 @@
             pltpu.VMEM((rows, TILE), F32),
             pltpu.VMEM(grads.shape, F32),
         ],
-        in_specs=[VMEM] * 5,
+        in_specs=[VMEM] * 4,
         out_specs=[VMEM] * 5,
         compiler_params=PARAMS,
         name="line_sum",
@@ -604,9 +650,12 @@
     across = lax.optimization_barrier(across)
     corners = [swap(values, "col", 1) for values in across]
     sources = [mine, beside, across[0], corners[0], across[2], corners[2], across[1], corners[1]]
-    kept, grads, *others = tiles_backward(steps, ids, backward, held, sources, n_back)
-
-    others = swap_line(others, "row")
+    gathered, grads, first = tiles_first(steps, ids, backward, held, sources)
+
+    first = swap(first, "row", 4)
+    kept, second, third = tiles_second(steps, backward, held, gathered, grads, n_back)
+    others = [swap(second, "row", 2), swap(third, "row", 6)]
+    kept, grads = first_sum(kept, grads, first)
     own_sent, other_sent, other_message, own, grads = line_sum(kept, grads, others)
     opposite = swap(own_sent, "feat", 1)
     corner = swap(other_sent, ("row", "feat"), 3)

time: 84.2 us -> 83.3 us (0.989)
  waiting for transfers between devices: 30.8 us -> 34.1 us
  Pallas kernels: 15.1 us -> 12.6 us
  starting transfers between devices: 36.7 us -> 34.2 us
    ppermute x24, waiting for transfers between devices: 30.8 us -> 34.1 us  [swap(): return lax.ppermute(values, axis, [(i, i ^ mask) for i in range(size)])]
    ppermute x24, starting transfers between devices: 36.7 us -> 34.2 us  [swap(): return lax.ppermute(values, axis, [(i, i ^ mask) for i in range(size)])]
    pallas_call x1, Pallas kernels: 3.62 us -> 2.15 us  [early_tiles(): pl.pallas_call(early_kernel, out_shape=pltpu.VMEM((EARLY * PER + 1, TILE,...]
    pallas_call x1 -> x3, Pallas kernels: 1.72 us -> 1.8 us  [the longest x1 1 us: tiles_second(): pl.pallas_call(second_kernel, out_shape=[pltpu.VMEM((rows, TILE), F32)] +...]
  transfers between devices with their start and end apart: 24 -> 24, of which waited for: 17 -> 19; matrix products, arithmetic and copies ran while one was open for 0% -> 0% of each run, Pallas kernels for 11% -> 10%
where the time goes in v7:
time: 83.3 us; the launch traced here: 82.7 us
  starting transfers between devices  34.2 us (41%)
  waiting for transfers between devices  34.1 us (41%)
  Pallas kernels  12.6 us (15%)
  between operations  1.43 us (2%)
    ppermute x24, starting transfers between devices, swap(): return lax.ppermute(values, axis, [(i, i ^ mask) for i in range(size)])  34.2 us
    ppermute x24, waiting for transfers between devices, swap(): return lax.ppermute(values, axis, [(i, i ^ mask) for i in range(size)])  34.1 us
    pallas_call x1, Pallas kernels, prepare(): pl.pallas_call(functools.partial(prepare_kernel, n_back), out_shape=[pltp...  2.55 us
    pallas_call x1, Pallas kernels, pick(): pl.pallas_call(functools.partial(pick_kernel, n_out), out_shape=[pltpu.SM...  2.28 us
    pallas_call x1, Pallas kernels, early_tiles(): pl.pallas_call(early_kernel, out_shape=pltpu.VMEM((EARLY * PER + 1, TILE,...  2.15 us
    pallas_call x1, Pallas kernels, tiles_forward(): pl.pallas_call(forward_kernel, out_shape=[pltpu.VMEM((length + 1, TILE, T...  1.77 us
  transfers between devices with their start and end apart: 24, of which 19 were waited for; matrix products, arithmetic and copies ran while one was open for 0% of the time, Pallas kernels for 10%

profile of v7, /device:TPU:0, one launch (start us, length us, event | category | flops | bytes accessed | tf_op | source)
XLA Modules:
  0.0 82.7 jit_solution(5805377610000721984)
XLA Ops:
  0.6 0.0 copy-start
  1.3 0.2 copy-done
  1.6 0.1 pad_add_fusion.ids
  1.6 2.0 %collective-permute-start = (bf16[256,128]{1,0:T(8,128)(2,1)S(1)}, bf16[256,128]{1,0:T(8,128)(2,1)S(1)}, u32[]{:S(2)}, u32[]{:S(2)}) collective-permute-start(bf16[256,128]{1,0:T(8,128)(2,1)S(1)} %constant_dynamic-slice_fusion.a), channel_id=1, source_target_pairs={{0,16},{16,0},{32,48},{48,32},{64,80},{80,64},{96,112},{112,96},{1... | collective-permute-start | bytes 196616 | tf_op jit(solution)/shard_map/ppermute | solution.py:28
  3.7 2.3 %pick_tiles.1 = (s32[1,768]{1,0:T(1,128)S(4)}, s32[1,768]{1,0:T(1,128)S(4)}, s32[1]{0:T(128)S(4)}, s32[3]{0:T(128)S(4)}, s32[1,640]{1,0:T(1,128)S(1)}) custom-call(s32[4]{0:T(128)S(1)} %pad_add_fusion.ids, s32[1,1,640]{2,1,0:T(1,128)} %rows.3, s32[1,1,640]{2,1,0:T(1,128)} %columns.3), custom_call_target="tpu_custom_call" | custom-call | tf_op jit(solution)/shard_map/pick_tiles/pallas_call | solution.py:120
  5.9 0.0 collective-permute-done.b
  6.0 3.3 %collective-permute-start.3 = (bf16[512,128]{1,0:T(8,128)(2,1)S(1)}, bf16[512,128]{1,0:T(8,128)(2,1)S(1)}, u32[]{:S(2)}, u32[]{:S(2)}) collective-permute-start(bf16[512,128]{1,0:T(8,128)(2,1)S(1)} %join.1.refs_0_), channel_id=1, source_target_pairs={{0,64},{16,80},{32,96},{48,112},{64,0},{80,16},{96,32},{112,48},{1... | collective-permute-start | bytes 393224 | tf_op jit(solution)/shard_map/ppermute | solution.py:28
  9.3 1.1 %collective-permute-start.2 = (bf16[512,128]{1,0:T(8,128)(2,1)S(1)}, bf16[512,128]{1,0:T(8,128)(2,1)S(1)}, u32[]{:S(2)}, u32[]{:S(2)}) collective-permute-start(bf16[512,128]{1,0:T(8,128)(2,1)S(1)} %join.1.refs_0_), channel_id=1, source_target_pairs={{0,96},{16,112},{32,64},{48,80},{64,32},{80,48},{96,0},{112,16},{1... | collective-permute-start | bytes 393224 | tf_op jit(solution)/shard_map/ppermute | solution.py:28
  10.3 0.0 collective-permute-start.1
  10.4 2.2 %early_tiles.1.early = bf16[161,128,128]{2,1,0:T(8,128)(2,1)S(1)} custom-call(s32[1]{0:T(128)S(4)} %get-tuple-element.75.steps, s32[1,768]{1,0:T(1,128)S(4)} %get-tuple-element.77.fetched, bf16[640,128,128]{2,1,0:T(8,128)(2,1)} %bitcast.8), custom_call_target="tpu_custom_call" | custom-call | tf_op jit(solution)/shard_map/early_tiles/pallas_call | solution.py:162
  12.5 0.7 collective-permute-done.3.refs_2_
  13.2 2.3 %collective-permute-done.2.refs_3_ = bf16[512,128]{1,0:T(8,128)(2,1)S(1)} collective-permute-done((bf16[512,128]{1,0:T(8,128)(2,1)S(1)}, bf16[512,128]{1,0:T(8,128)(2,1)S(1)}, u32[]{:S(2)}, u32[]{:S(2)}) %collective-permute-start.2) | collective-permute-done | bytes 131104 | tf_op jit(solution)/shard_map/ppermute | solution.py:28
  15.5 0.2 collective-permute-done.1.refs_1_
  15.7 1.8 %tiles_forward.1 = (bf16[673,128,128]{2,1,0:T(8,128)(2,1)S(1)}, f32[4,4,128,128]{3,2,1,0:T(8,128)S(1)}, bf16[4,4,128,128]{3,2,1,0:T(8,128)(2,1)S(1)}) custom-call(s32[1]{0:T(128)S(4)} %get-tuple-element.75.steps, s32[3]{0:T(128)S(4)} %get-tuple-element.76.ids, s32[1,768]{1,0:T(1,128)S(4)} %get-tuple-element.77.fetched, ...), custom_call_target="tpu_custom_call" | custom-call | tf_op jit(solution)/shard_map/tiles_forward/pallas_call | solution.py:320
  17.5 2.9 %collective-permute-start.4 = (bf16[4,4,128,128]{3,2,1,0:T(8,128)(2,1)S(1)}, bf16[4,4,128,128]{3,2,1,0:T(8,128)(2,1)S(1)}, u32[]{:S(2)}, u32[]{:S(2)}) collective-permute-start(bf16[4,4,128,128]{3,2,1,0:T(8,128)(2,1)S(1)} %get-tuple-element.85), channel_id=1, source_target_pairs={{0,2},{2,0},{4,6},{6,4},{8,10},{10,8},{12,14},{14,12},{1,3},{3,1},... | collective-permute-start | bytes 1572872 | tf_op jit(solution)/shard_map/ppermute | solution.py:28
  20.4 1.5 %collective-permute-done.4.got = bf16[4,4,128,128]{3,2,1,0:T(8,128)(2,1)S(1)} collective-permute-done((bf16[4,4,128,128]{3,2,1,0:T(8,128)(2,1)S(1)}, bf16[4,4,128,128]{3,2,1,0:T(8,128)(2,1)S(1)}, u32[]{:S(2)}, u32[]{:S(2)}) %collective-permute-start.4) | collective-permute-done | bytes 524320 | tf_op jit(solution)/shard_map/ppermute | solution.py:28
  22.0 0.1 pair_sum.1
  22.1 1.0 %collective-permute-start.5 = (bf16[4,128,128]{2,1,0:T(8,128)(2,1)S(1)}, bf16[4,128,128]{2,1,0:T(8,128)(2,1)S(1)}, u32[]{:S(2)}, u32[]{:S(2)}) collective-permute-start(bf16[4,128,128]{2,1,0:T(8,128)(2,1)S(1)} %get-tuple-element.87), channel_id=1, source_target_pairs={{0,8},{2,10},{4,12},{6,14},{8,0},{10,2},{12,4},{14,6},{1,9},{3,11}... | collective-permute-start | bytes 393224 | tf_op jit(solution)/shard_map/ppermute | solution.py:28
  23.1 0.2 collective-permute-start.6
  23.3 3.0 %collective-permute-start.7 = (bf16[4,128,128]{2,1,0:T(8,128)(2,1)S(1)}, bf16[4,128,128]{2,1,0:T(8,128)(2,1)S(1)}, u32[]{:S(2)}, u32[]{:S(2)}) collective-permute-start(bf16[4,128,128]{2,1,0:T(8,128)(2,1)S(1)} %get-tuple-element.89), channel_id=1, source_target_pairs={{0,12},{2,14},{4,8},{6,10},{8,4},{10,6},{12,0},{14,2},{1,13},{3,15... | collective-permute-start | bytes 393224 | tf_op jit(solution)/shard_map/ppermute | solution.py:28
  26.3 3.8 %collective-permute-done.5.a = bf16[4,128,128]{2,1,0:T(8,128)(2,1)S(1)} collective-permute-done((bf16[4,128,128]{2,1,0:T(8,128)(2,1)S(1)}, bf16[4,128,128]{2,1,0:T(8,128)(2,1)S(1)}, u32[]{:S(2)}, u32[]{:S(2)}) %collective-permute-start.5) | collective-permute-done | bytes 131104 | tf_op jit(solution)/shard_map/ppermute | solution.py:28
  30.0 0.0 collective-permute-done.6.b
  30.0 2.2 %collective-permute-done.7.c = bf16[4,128,128]{2,1,0:T(8,128)(2,1)S(1)} collective-permute-done((bf16[4,128,128]{2,1,0:T(8,128)(2,1)S(1)}, bf16[4,128,128]{2,1,0:T(8,128)(2,1)S(1)}, u32[]{:S(2)}, u32[]{:S(2)}) %collective-permute-start.7) | collective-permute-done | bytes 131104 | tf_op jit(solution)/shard_map/ppermute | solution.py:28
  32.2 0.1 own_sum.1
  32.3 3.7 %collective-permute-start.8 = (bf16[4,128,128]{2,1,0:T(8,128)(2,1)S(1)}, bf16[4,128,128]{2,1,0:T(8,128)(2,1)S(1)}, u32[]{:S(2)}, u32[]{:S(2)}) collective-permute-start(bf16[4,128,128]{2,1,0:T(8,128)(2,1)S(1)} %get-tuple-element.93), channel_id=1, source_target_pairs={{0,1},{1,0},{2,3},{3,2},{4,5},{5,4},{6,7},{7,6},{8,9},{9,8},{10,11... | collective-permute-start | bytes 393224 | tf_op jit(solution)/shard_map/ppermute | solution.py:28
  36.1 2.5 %prepare.1 = (s32[1,768]{1,0:T(1,128)S(4)}, s32[2]{0:T(128)S(4)}, bf16[128,128]{1,0:T(8,128)(2,1)S(1)}, f32[1,128]{1,0:T(1,128)S(1)}, bf16[512,128]{1,0:T(8,128)(2,1)S(1)}) custom-call(s32[3]{0:T(128)S(4)} %get-tuple-element.76.ids, s32[1,1,640]{2,1,0:T(1,128)} %rows.3, s32[1,1,640]{2,1,0:T(1,128)} %columns.3, s32[1,640]{1,0:T(1,128)S(1)} %get-tuple-element.94.slots, ...), custom_call_target="tpu_custom_call" | custom-call | tf_op jit(solution)/shard_map/prepare/pallas_call | solution.py:212
  38.6 1.1 %collective-permute-done.8.other = bf16[4,128,128]{2,1,0:T(8,128)(2,1)S(1)} collective-permute-done((bf16[4,128,128]{2,1,0:T(8,128)(2,1)S(1)}, bf16[4,128,128]{2,1,0:T(8,128)(2,1)S(1)}, u32[]{:S(2)}, u32[]{:S(2)}) %collective-permute-start.8) | collective-permute-done | bytes 131104 | tf_op jit(solution)/shard_map/ppermute | solution.py:28
  39.7 0.9 %middle.1 = (bf16[512,128]{1,0:T(8,128)(2,1)}, f32[4,128,128]{2,1,0:T(8,128)S(1)}, bf16[4,128,128]{2,1,0:T(8,128)(2,1)S(1)}, f32[136,128]{1,0:T(8,128)S(1)}) custom-call(f32[4,128,128]{2,1,0:T(8,128)S(1)} %get-tuple-element.90.own, bf16[4,128,128]{2,1,0:T(8,128)(2,1)S(1)} %collective-permute-done.8.other, bf16[128,128]{1,0:T(8,128)(2,1)S(1)} %get-tuple-element.101.weight, ...), custom_call_target="tpu_custom_call" | custom-call | tf_op jit(solution)/shard_map/middle/pallas_call | solution.py:494
  40.6 3.2 %collective-permute-start.9 = (bf16[4,128,128]{2,1,0:T(8,128)(2,1)S(1)}, bf16[4,128,128]{2,1,0:T(8,128)(2,1)S(1)}, u32[]{:S(2)}, u32[]{:S(2)}) collective-permute-start(bf16[4,128,128]{2,1,0:T(8,128)(2,1)S(1)} %get-tuple-element.109), channel_id=1, source_target_pairs={{0,1},{1,0},{2,3},{3,2},{4,5},{5,4},{6,7},{7,6},{8,9},{9,8},{10,11... | collective-permute-start | bytes 393224 | tf_op jit(solution)/shard_map/ppermute | solution.py:28
  43.9 0.0 collective-permute-start.10
  43.9 1.3 %collective-permute-done.10.more = f32[136,128]{1,0:T(8,128)S(1)} collective-permute-done((f32[136,128]{1,0:T(8,128)S(1)}, f32[136,128]{1,0:T(8,128)S(1)}, u32[]{:S(2)}, u32[]{:S(2)}) %collective-permute-start.10) | collective-permute-done | bytes 69664 | tf_op jit(solution)/shard_map/ppermute | solution.py:28
  45.1 2.0 %collective-permute-done.9.other = bf16[4,128,128]{2,1,0:T(8,128)(2,1)S(1)} collective-permute-done((bf16[4,128,128]{2,1,0:T(8,128)(2,1)S(1)}, bf16[4,128,128]{2,1,0:T(8,128)(2,1)S(1)}, u32[]{:S(2)}, u32[]{:S(2)}) %collective-permute-start.9) | collective-permute-done | bytes 131104 | tf_op jit(solution)/shard_map/ppermute | solution.py:28
  47.1 1.0 %collective-permute-start.14 = (bf16[592,128]{1,0:T(8,128)(2,1)S(1)}, bf16[592,128]{1,0:T(8,128)(2,1)S(1)}, u32[]{:S(2)}, u32[]{:S(2)}) collective-permute-start(bf16[592,128]{1,0:T(8,128)(2,1)S(1)} %message.1.refs_0_), channel_id=1, source_target_pairs={{0,8},{2,10},{4,12},{6,14},{8,0},{10,2},{12,4},{14,6},{1,9},{3,11}... | collective-permute-start | bytes 454664 | tf_op jit(solution)/shard_map/ppermute | solution.py:28
  48.2 0.7 collective-permute-start.13
  48.9 1.8 %collective-permute-start.12 = (bf16[592,128]{1,0:T(8,128)(2,1)S(1)}, bf16[592,128]{1,0:T(8,128)(2,1)S(1)}, u32[]{:S(2)}, u32[]{:S(2)}) collective-permute-start(bf16[592,128]{1,0:T(8,128)(2,1)S(1)} %message.1.refs_0_), channel_id=1, source_target_pairs={{0,4},{2,6},{4,0},{6,2},{8,12},{10,14},{12,8},{14,10},{1,5},{3,7},... | collective-permute-start | bytes 454664 | tf_op jit(solution)/shard_map/ppermute | solution.py:28
  50.7 0.0 collective-permute-start.11
  50.7 3.9 %collective-permute-done.14.refs_4_ = bf16[592,128]{1,0:T(8,128)(2,1)S(1)} collective-permute-done((bf16[592,128]{1,0:T(8,128)(2,1)S(1)}, bf16[592,128]{1,0:T(8,128)(2,1)S(1)}, u32[]{:S(2)}, u32[]{:S(2)}) %collective-permute-start.14) | collective-permute-done | bytes 151584 | tf_op jit(solution)/shard_map/ppermute | solution.py:28
  54.6 1.6 %collective-permute-done.13.refs_6_ = bf16[592,128]{1,0:T(8,128)(2,1)S(1)} collective-permute-done((bf16[592,128]{1,0:T(8,128)(2,1)S(1)}, bf16[592,128]{1,0:T(8,128)(2,1)S(1)}, u32[]{:S(2)}, u32[]{:S(2)}) %collective-permute-start.13) | collective-permute-done | bytes 151584 | tf_op jit(solution)/shard_map/ppermute | solution.py:28
  56.2 0.0 collective-permute-done.12.refs_2_
  56.2 0.0 collective-permute-start.15
  56.2 0.5 collective-permute-start.16
  56.7 0.0 collective-permute-start.17
  56.7 0.0 collective-permute-done.11.refs_1_
  56.7 0.9 %collective-permute-done.15.refs_3_ = bf16[592,128]{1,0:T(8,128)(2,1)S(1)} collective-permute-done((bf16[592,128]{1,0:T(8,128)(2,1)S(1)}, bf16[592,128]{1,0:T(8,128)(2,1)S(1)}, u32[]{:S(2)}, u32[]{:S(2)}) %collective-permute-start.15) | collective-permute-done | bytes 151584 | tf_op jit(solution)/shard_map/ppermute | solution.py:28
  57.5 0.2 collective-permute-done.16.refs_5_
  57.8 0.3 collective-permute-done.17.refs_7_
  58.1 0.7 tiles_first.1
  58.8 2.1 %collective-permute-start.18 = (bf16[656,128]{1,0:T(8,128)(2,1)S(1)}, bf16[656,128]{1,0:T(8,128)(2,1)S(1)}, u32[]{:S(2)}, u32[]{:S(2)}) collective-permute-start(bf16[656,128]{1,0:T(8,128)(2,1)S(1)} %get-tuple-element.119), channel_id=1, source_target_pairs={{0,64},{16,80},{32,96},{48,112},{64,0},{80,16},{96,32},{112,48},{1... | collective-permute-start | bytes 503816 | tf_op jit(solution)/shard_map/ppermute | solution.py:28
  60.9 1.0 %tiles_second.1 = (f32[512,128]{1,0:T(8,128)S(1)}, bf16[656,128]{1,0:T(8,128)(2,1)S(1)}, bf16[656,128]{1,0:T(8,128)(2,1)S(1)}) custom-call(s32[2]{0:T(128)S(4)} %get-tuple-element.105.steps, s32[1,768]{1,0:T(1,128)S(4)} %get-tuple-element.106.picked, bf16[673,128,128]{2,1,0:T(8,128)(2,1)S(1)} %get-tuple-element.107.held, ...), custom_call_target="tpu_custom_call" | custom-call | flops 2822766592 | bytes 22052864 | tf_op jit(solution)/shard_map/tiles_second/pallas_call | solution.py:415
  61.9 2.7 %collective-permute-start.19 = (bf16[656,128]{1,0:T(8,128)(2,1)S(1)}, bf16[656,128]{1,0:T(8,128)(2,1)S(1)}, u32[]{:S(2)}, u32[]{:S(2)}) collective-permute-start(bf16[656,128]{1,0:T(8,128)(2,1)S(1)} %get-tuple-element.122), channel_id=1, source_target_pairs={{0,32},{16,48},{32,0},{48,16},{64,96},{80,112},{96,64},{112,80},{1... | collective-permute-start | bytes 503816 | tf_op jit(solution)/shard_map/ppermute | solution.py:28
  64.6 0.0 collective-permute-start.20
  64.6 2.8 %collective-permute-done.18.a = bf16[656,128]{1,0:T(8,128)(2,1)S(1)} collective-permute-done((bf16[656,128]{1,0:T(8,128)(2,1)S(1)}, bf16[656,128]{1,0:T(8,128)(2,1)S(1)}, u32[]{:S(2)}, u32[]{:S(2)}) %collective-permute-start.18) | collective-permute-done | bytes 167968 | tf_op jit(solution)/shard_map/ppermute | solution.py:28
  67.4 0.1 first_sum.1
  67.5 4.0 %collective-permute-done.19.a = bf16[656,128]{1,0:T(8,128)(2,1)S(1)} collective-permute-done((bf16[656,128]{1,0:T(8,128)(2,1)S(1)}, bf16[656,128]{1,0:T(8,128)(2,1)S(1)}, u32[]{:S(2)}, u32[]{:S(2)}) %collective-permute-start.19) | collective-permute-done | bytes 167968 | tf_op jit(solution)/shard_map/ppermute | solution.py:28
  71.5 0.3 collective-permute-done.20.b
  71.9 0.1 line_sum.1
  71.9 0.4 collective-permute-start.23
  72.3 3.0 %collective-permute-start.21 = (bf16[256,128]{1,0:T(8,128)(2,1)S(1)}, bf16[256,128]{1,0:T(8,128)(2,1)S(1)}, u32[]{:S(2)}, u32[]{:S(2)}) collective-permute-start(bf16[256,128]{1,0:T(8,128)(2,1)S(1)} %get-tuple-element.126), channel_id=1, source_target_pairs={{0,1},{1,0},{2,3},{3,2},{4,5},{5,4},{6,7},{7,6},{8,9},{9,8},{10,11... | collective-permute-start | bytes 196616 | tf_op jit(solution)/shard_map/ppermute | solution.py:28
  75.3 1.4 %collective-permute-start.22 = (bf16[256,128]{1,0:T(8,128)(2,1)S(1)}, bf16[256,128]{1,0:T(8,128)(2,1)S(1)}, u32[]{:S(2)}, u32[]{:S(2)}) collective-permute-start(bf16[256,128]{1,0:T(8,128)(2,1)S(1)} %get-tuple-element.127), channel_id=1, source_target_pairs={{0,17},{1,16},{16,1},{17,0},{32,49},{33,48},{48,33},{49,32},{64,81... | collective-permute-start | bytes 196616 | tf_op jit(solution)/shard_map/ppermute | solution.py:28
  76.7 3.8 %collective-permute-done.21.opposite = bf16[256,128]{1,0:T(8,128)(2,1)S(1)} collective-permute-done((bf16[256,128]{1,0:T(8,128)(2,1)S(1)}, bf16[256,128]{1,0:T(8,128)(2,1)S(1)}, u32[]{:S(2)}, u32[]{:S(2)}) %collective-permute-start.21) | collective-permute-done | bytes 65568 | tf_op jit(solution)/shard_map/ppermute | solution.py:28
  80.5 1.3 %collective-permute-done.22.corner = bf16[256,128]{1,0:T(8,128)(2,1)S(1)} collective-permute-done((bf16[256,128]{1,0:T(8,128)(2,1)S(1)}, bf16[256,128]{1,0:T(8,128)(2,1)S(1)}, u32[]{:S(2)}, u32[]{:S(2)}) %collective-permute-start.22) | collective-permute-done | bytes 65568 | tf_op jit(solution)/shard_map/ppermute | solution.py:28
  81.8 0.0 collective-permute-done.23.beside
  81.8 0.9 %finish.1 = (f32[512,128]{1,0:T(8,128)}, f32[128,128]{1,0:T(8,128)}, f32[1,128]{1,0:T(1,128)}) custom-call(s32[3]{0:T(128)S(4)} %get-tuple-element.76.ids, f32[256,128]{1,0:T(8,128)S(1)} %get-tuple-element.124.own, f32[136,128]{1,0:T(8,128)S(1)} %get-tuple-element.125.grads, bf16[256,128]{1,0:T(8,128)(2,1)S(1)} %collective-permute-done.21.opposite, ...), custom_call_target="tpu_custom_call" | custom-call | tf_op jit(solution)/shard_map/finish/pallas_call | solution.py:598
  (3 shorter events, 0.1 us)
Async XLA Ops:
  0.6 0.9 %copy-start = (bf16[512,128]{1,0:T(8,128)(2,1)S(1)}, bf16[512,128]{1,0:T(8,128)(2,1)}, u32[]{:S(2)}) copy-start(bf16[512,128]{1,0:T(8,128)(2,1)} %param.8) | copy-start | bytes 393220
  1.6 4.3 %collective-permute-start = (bf16[256,128]{1,0:T(8,128)(2,1)S(1)}, bf16[256,128]{1,0:T(8,128)(2,1)S(1)}, u32[]{:S(2)}, u32[]{:S(2)}) collective-permute-start(bf16[256,128]{1,0:T(8,128)(2,1)S(1)} %constant_dynamic-slice_fusion.a), channel_id=1, source_target_pairs={{0,16},{16,0},{32,48},{48,32},{64,80},{80,64},{96,112},{112,96},{1... | collective-permute-start | bytes 196616 | tf_op jit(solution)/shard_map/ppermute | solution.py:28
  6.0 7.2 %collective-permute-start.3 = (bf16[512,128]{1,0:T(8,128)(2,1)S(1)}, bf16[512,128]{1,0:T(8,128)(2,1)S(1)}, u32[]{:S(2)}, u32[]{:S(2)}) collective-permute-start(bf16[512,128]{1,0:T(8,128)(2,1)S(1)} %join.1.refs_0_), channel_id=1, source_target_pairs={{0,64},{16,80},{32,96},{48,112},{64,0},{80,16},{96,32},{112,48},{1... | collective-permute-start | bytes 393224 | tf_op jit(solution)/shard_map/ppermute | solution.py:28
  9.3 6.2 %collective-permute-start.2 = (bf16[512,128]{1,0:T(8,128)(2,1)S(1)}, bf16[512,128]{1,0:T(8,128)(2,1)S(1)}, u32[]{:S(2)}, u32[]{:S(2)}) collective-permute-start(bf16[512,128]{1,0:T(8,128)(2,1)S(1)} %join.1.refs_0_), channel_id=1, source_target_pairs={{0,96},{16,112},{32,64},{48,80},{64,32},{80,48},{96,0},{112,16},{1... | collective-permute-start | bytes 393224 | tf_op jit(solution)/shard_map/ppermute | solution.py:28
  10.3 5.4 %collective-permute-start.1 = (bf16[512,128]{1,0:T(8,128)(2,1)S(1)}, bf16[512,128]{1,0:T(8,128)(2,1)S(1)}, u32[]{:S(2)}, u32[]{:S(2)}) collective-permute-start(bf16[512,128]{1,0:T(8,128)(2,1)S(1)} %join.1.refs_0_), channel_id=1, source_target_pairs={{0,32},{16,48},{32,0},{48,16},{64,96},{80,112},{96,64},{112,80},{1... | collective-permute-start | bytes 393224 | tf_op jit(solution)/shard_map/ppermute | solution.py:28
  17.5 4.5 %collective-permute-start.4 = (bf16[4,4,128,128]{3,2,1,0:T(8,128)(2,1)S(1)}, bf16[4,4,128,128]{3,2,1,0:T(8,128)(2,1)S(1)}, u32[]{:S(2)}, u32[]{:S(2)}) collective-permute-start(bf16[4,4,128,128]{3,2,1,0:T(8,128)(2,1)S(1)} %get-tuple-element.85), channel_id=1, source_target_pairs={{0,2},{2,0},{4,6},{6,4},{8,10},{10,8},{12,14},{14,12},{1,3},{3,1},... | collective-permute-start | bytes 1572872 | tf_op jit(solution)/shard_map/ppermute | solution.py:28
  22.1 8.0 %collective-permute-start.5 = (bf16[4,128,128]{2,1,0:T(8,128)(2,1)S(1)}, bf16[4,128,128]{2,1,0:T(8,128)(2,1)S(1)}, u32[]{:S(2)}, u32[]{:S(2)}) collective-permute-start(bf16[4,128,128]{2,1,0:T(8,128)(2,1)S(1)} %get-tuple-element.87), channel_id=1, source_target_pairs={{0,8},{2,10},{4,12},{6,14},{8,0},{10,2},{12,4},{14,6},{1,9},{3,11}... | collective-permute-start | bytes 393224 | tf_op jit(solution)/shard_map/ppermute | solution.py:28
  23.1 6.9 %collective-permute-start.6 = (bf16[4,128,128]{2,1,0:T(8,128)(2,1)S(1)}, bf16[4,128,128]{2,1,0:T(8,128)(2,1)S(1)}, u32[]{:S(2)}, u32[]{:S(2)}) collective-permute-start(bf16[4,128,128]{2,1,0:T(8,128)(2,1)S(1)} %get-tuple-element.88), channel_id=1, source_target_pairs={{0,4},{2,6},{4,0},{6,2},{8,12},{10,14},{12,8},{14,10},{1,5},{3,7},... | collective-permute-start | bytes 393224 | tf_op jit(solution)/shard_map/ppermute | solution.py:28
  23.3 9.0 %collective-permute-start.7 = (bf16[4,128,128]{2,1,0:T(8,128)(2,1)S(1)}, bf16[4,128,128]{2,1,0:T(8,128)(2,1)S(1)}, u32[]{:S(2)}, u32[]{:S(2)}) collective-permute-start(bf16[4,128,128]{2,1,0:T(8,128)(2,1)S(1)} %get-tuple-element.89), channel_id=1, source_target_pairs={{0,12},{2,14},{4,8},{6,10},{8,4},{10,6},{12,0},{14,2},{1,13},{3,15... | collective-permute-start | bytes 393224 | tf_op jit(solution)/shard_map/ppermute | solution.py:28
  32.3 7.4 %collective-permute-start.8 = (bf16[4,128,128]{2,1,0:T(8,128)(2,1)S(1)}, bf16[4,128,128]{2,1,0:T(8,128)(2,1)S(1)}, u32[]{:S(2)}, u32[]{:S(2)}) collective-permute-start(bf16[4,128,128]{2,1,0:T(8,128)(2,1)S(1)} %get-tuple-element.93), channel_id=1, source_target_pairs={{0,1},{1,0},{2,3},{3,2},{4,5},{5,4},{6,7},{7,6},{8,9},{9,8},{10,11... | collective-permute-start | bytes 393224 | tf_op jit(solution)/shard_map/ppermute | solution.py:28
  40.6 6.5 %collective-permute-start.9 = (bf16[4,128,128]{2,1,0:T(8,128)(2,1)S(1)}, bf16[4,128,128]{2,1,0:T(8,128)(2,1)S(1)}, u32[]{:S(2)}, u32[]{:S(2)}) collective-permute-start(bf16[4,128,128]{2,1,0:T(8,128)(2,1)S(1)} %get-tuple-element.109), channel_id=1, source_target_pairs={{0,1},{1,0},{2,3},{3,2},{4,5},{5,4},{6,7},{7,6},{8,9},{9,8},{10,11... | collective-permute-start | bytes 393224 | tf_op jit(solution)/shard_map/ppermute | solution.py:28
  43.9 1.3 %collective-permute-start.10 = (f32[136,128]{1,0:T(8,128)S(1)}, f32[136,128]{1,0:T(8,128)S(1)}, u32[]{:S(2)}, u32[]{:S(2)}) collective-permute-start(f32[136,128]{1,0:T(8,128)S(1)} %get-tuple-element.110.grads), channel_id=1, source_target_pairs={{0,2},{2,0},{4,6},{6,4},{8,10},{10,8},{12,14},{14,12},{1,3},{3,1},... | collective-permute-start | bytes 208904 | tf_op jit(solution)/shard_map/ppermute | solution.py:28
  47.1 7.4 %collective-permute-start.14 = (bf16[592,128]{1,0:T(8,128)(2,1)S(1)}, bf16[592,128]{1,0:T(8,128)(2,1)S(1)}, u32[]{:S(2)}, u32[]{:S(2)}) collective-permute-start(bf16[592,128]{1,0:T(8,128)(2,1)S(1)} %message.1.refs_0_), channel_id=1, source_target_pairs={{0,8},{2,10},{4,12},{6,14},{8,0},{10,2},{12,4},{14,6},{1,9},{3,11}... | collective-permute-start | bytes 454664 | tf_op jit(solution)/shard_map/ppermute | solution.py:28
  48.2 8.0 %collective-permute-start.13 = (bf16[592,128]{1,0:T(8,128)(2,1)S(1)}, bf16[592,128]{1,0:T(8,128)(2,1)S(1)}, u32[]{:S(2)}, u32[]{:S(2)}) collective-permute-start(bf16[592,128]{1,0:T(8,128)(2,1)S(1)} %message.1.refs_0_), channel_id=1, source_target_pairs={{0,12},{2,14},{4,8},{6,10},{8,4},{10,6},{12,0},{14,2},{1,13},{3,15... | collective-permute-start | bytes 454664 | tf_op jit(solution)/shard_map/ppermute | solution.py:28
  48.9 7.3 %collective-permute-start.12 = (bf16[592,128]{1,0:T(8,128)(2,1)S(1)}, bf16[592,128]{1,0:T(8,128)(2,1)S(1)}, u32[]{:S(2)}, u32[]{:S(2)}) collective-permute-start(bf16[592,128]{1,0:T(8,128)(2,1)S(1)} %message.1.refs_0_), channel_id=1, source_target_pairs={{0,4},{2,6},{4,0},{6,2},{8,12},{10,14},{12,8},{14,10},{1,5},{3,7},... | collective-permute-start | bytes 454664 | tf_op jit(solution)/shard_map/ppermute | solution.py:28
  50.7 6.0 %collective-permute-start.11 = (bf16[592,128]{1,0:T(8,128)(2,1)S(1)}, bf16[592,128]{1,0:T(8,128)(2,1)S(1)}, u32[]{:S(2)}, u32[]{:S(2)}) collective-permute-start(bf16[592,128]{1,0:T(8,128)(2,1)S(1)} %message.1.refs_0_), channel_id=1, source_target_pairs={{0,2},{2,0},{4,6},{6,4},{8,10},{10,8},{12,14},{14,12},{1,3},{3,1},... | collective-permute-start | bytes 454664 | tf_op jit(solution)/shard_map/ppermute | solution.py:28
  56.2 1.4 %collective-permute-start.15 = (bf16[592,128]{1,0:T(8,128)(2,1)S(1)}, bf16[592,128]{1,0:T(8,128)(2,1)S(1)}, u32[]{:S(2)}, u32[]{:S(2)}) collective-permute-start(bf16[592,128]{1,0:T(8,128)(2,1)S(1)} %collective-permute-done.12.refs_2_), channel_id=1, source_target_pairs={{0,2},{2,0},{4,6},{6,4},{8,10},{10,8},{12,14},{14,12},{1,3},{3,1},... | collective-permute-start | bytes 454664 | tf_op jit(solution)/shard_map/ppermute | solution.py:28
  56.2 1.6 %collective-permute-start.16 = (bf16[592,128]{1,0:T(8,128)(2,1)S(1)}, bf16[592,128]{1,0:T(8,128)(2,1)S(1)}, u32[]{:S(2)}, u32[]{:S(2)}) collective-permute-start(bf16[592,128]{1,0:T(8,128)(2,1)S(1)} %collective-permute-done.14.refs_4_), channel_id=1, source_target_pairs={{0,2},{2,0},{4,6},{6,4},{8,10},{10,8},{12,14},{14,12},{1,3},{3,1},... | collective-permute-start | bytes 454664 | tf_op jit(solution)/shard_map/ppermute | solution.py:28
  56.7 1.4 %collective-permute-start.17 = (bf16[592,128]{1,0:T(8,128)(2,1)S(1)}, bf16[592,128]{1,0:T(8,128)(2,1)S(1)}, u32[]{:S(2)}, u32[]{:S(2)}) collective-permute-start(bf16[592,128]{1,0:T(8,128)(2,1)S(1)} %collective-permute-done.13.refs_6_), channel_id=1, source_target_pairs={{0,2},{2,0},{4,6},{6,4},{8,10},{10,8},{12,14},{14,12},{1,3},{3,1},... | collective-permute-start | bytes 454664 | tf_op jit(solution)/shard_map/ppermute | solution.py:28
  58.8 8.6 %collective-permute-start.18 = (bf16[656,128]{1,0:T(8,128)(2,1)S(1)}, bf16[656,128]{1,0:T(8,128)(2,1)S(1)}, u32[]{:S(2)}, u32[]{:S(2)}) collective-permute-start(bf16[656,128]{1,0:T(8,128)(2,1)S(1)} %get-tuple-element.119), channel_id=1, source_target_pairs={{0,64},{16,80},{32,96},{48,112},{64,0},{80,16},{96,32},{112,48},{1... | collective-permute-start | bytes 503816 | tf_op jit(solution)/shard_map/ppermute | solution.py:28
  61.9 9.6 %collective-permute-start.19 = (bf16[656,128]{1,0:T(8,128)(2,1)S(1)}, bf16[656,128]{1,0:T(8,128)(2,1)S(1)}, u32[]{:S(2)}, u32[]{:S(2)}) collective-permute-start(bf16[656,128]{1,0:T(8,128)(2,1)S(1)} %get-tuple-element.122), channel_id=1, source_target_pairs={{0,32},{16,48},{32,0},{48,16},{64,96},{80,112},{96,64},{112,80},{1... | collective-permute-start | bytes 503816 | tf_op jit(solution)/shard_map/ppermute | solution.py:28
  64.6 7.2 %collective-permute-start.20 = (bf16[656,128]{1,0:T(8,128)(2,1)S(1)}, bf16[656,128]{1,0:T(8,128)(2,1)S(1)}, u32[]{:S(2)}, u32[]{:S(2)}) collective-permute-start(bf16[656,128]{1,0:T(8,128)(2,1)S(1)} %get-tuple-element.123), channel_id=1, source_target_pairs={{0,96},{16,112},{32,64},{48,80},{64,32},{80,48},{96,0},{112,16},{1... | collective-permute-start | bytes 503816 | tf_op jit(solution)/shard_map/ppermute | solution.py:28
  71.9 9.9 %collective-permute-start.23 = (bf16[400,128]{1,0:T(8,128)(2,1)S(1)}, bf16[400,128]{1,0:T(8,128)(2,1)S(1)}, u32[]{:S(2)}, u32[]{:S(2)}) collective-permute-start(bf16[400,128]{1,0:T(8,128)(2,1)S(1)} %get-tuple-element.128), channel_id=1, source_target_pairs={{0,16},{16,0},{32,48},{48,32},{64,80},{80,64},{96,112},{112,96},{1... | collective-permute-start | bytes 307208 | tf_op jit(solution)/shard_map/ppermute | solution.py:28
  72.3 8.2 %collective-permute-start.21 = (bf16[256,128]{1,0:T(8,128)(2,1)S(1)}, bf16[256,128]{1,0:T(8,128)(2,1)S(1)}, u32[]{:S(2)}, u32[]{:S(2)}) collective-permute-start(bf16[256,128]{1,0:T(8,128)(2,1)S(1)} %get-tuple-element.126), channel_id=1, source_target_pairs={{0,1},{1,0},{2,3},{3,2},{4,5},{5,4},{6,7},{7,6},{8,9},{9,8},{10,11... | collective-permute-start | bytes 196616 | tf_op jit(solution)/shard_map/ppermute | solution.py:28
  75.3 6.5 %collective-permute-start.22 = (bf16[256,128]{1,0:T(8,128)(2,1)S(1)}, bf16[256,128]{1,0:T(8,128)(2,1)S(1)}, u32[]{:S(2)}, u32[]{:S(2)}) collective-permute-start(bf16[256,128]{1,0:T(8,128)(2,1)S(1)} %get-tuple-element.127), channel_id=1, source_target_pairs={{0,17},{1,16},{16,1},{17,0},{32,49},{33,48},{48,33},{49,32},{64,81... | collective-permute-start | bytes 196616 | tf_op jit(solution)/shard_map/ppermute | solution.py:28

commit v8 on v7

--- a/solution.py
+++ b/solution.py
@@ -285,7 +285,7 @@
 
 
 def forward_kernel(steps, ids, fetched, picked, tiles, early, *refs):
-    sources, (held, kept, sent, gathered, total, arrived) = refs[:-6], refs[-6:]
+    sources, (held, kept, distant, sent, gathered, total, arrived) = refs[:-7], refs[-7:]
     count = steps[0]
     start = functools.partial(start_fetch, tiles, fetched, held, arrived)
     lax.fori_loop(EARLY, jnp.maximum(count, EARLY), start, 0)
@@ -311,7 +311,11 @@
     for k in range(kept.shape[0]):
         own = jnp.bitwise_xor(ids[1], 2 * k)
         kept[k] = total[pl.ds(own * 4, 4)]
-        sent[k] = total[pl.ds(jnp.bitwise_xor(own, 1) * 4, 4)].astype(BF16)
+        value = total[pl.ds(jnp.bitwise_xor(own, 1) * 4, 4)].astype(BF16)
+        if k == 2:
+            distant[...] = value
+        else:
+            sent[min(k, 2)] = value
 
 
 def tiles_forward(steps, ids, fetched, picked, tiles, early, sources, n_out):
@@ -322,10 +326,11 @@
         out_shape=[
             pltpu.VMEM((length + 1, TILE, TILE), BF16),
             pltpu.VMEM(shape, F32),
-            pltpu.VMEM(shape, BF16),
+            pltpu.VMEM(shape[1:], BF16),
+            pltpu.VMEM((shape[0] - 1, *shape[1:]), BF16),
         ],
         in_specs=[SMEM, SMEM, SMEM, SMEM, ANY, VMEM] + [VMEM] * len(sources),
-        out_specs=[VMEM] * 3,
+        out_specs=[VMEM] * 4,
         scratch_shapes=[
             pltpu.VMEM((4 * len(sources), TILE, TILE), BF16),
             pltpu.VMEM((n_out + 1, TILE, TILE), F32),
@@ -429,20 +434,34 @@
     )(scalar(steps), scalar(picked), near(held), near(gathered), near(grads))
 
 
-def pair_kernel(kept, got, first, *others):
+def distant_kernel(kept, got, out):
+    out[...] = (kept[2] + got[...].astype(F32)).astype(BF16)
+
+
+def distant_sum(kept, got):
+    return pl.pallas_call(
+        distant_kernel,
+        out_shape=pltpu.VMEM(got.shape, BF16),
+        in_specs=[VMEM] * 2,
+        out_specs=VMEM,
+        compiler_params=PARAMS,
+        name="distant_sum",
+    )(near(kept), near(got))
+
+
+def pair_kernel(kept, got, first, second, third):
     first[...] = kept[0] + got[0].astype(F32)
-    for k, other in zip((2, 1, 3), others):
-        other[...] = (kept[k] + got[k].astype(F32)).astype(BF16)
+    second[...] = (kept[1] + got[1].astype(F32)).astype(BF16)
+    third[...] = (kept[3] + got[2].astype(F32)).astype(BF16)
 
 
 def pair_sum(kept, got):
     shape = kept.shape[1:]
-    n = kept.shape[0] - 1
     return pl.pallas_call(
         pair_kernel,
-        out_shape=[pltpu.VMEM(shape, F32)] + [pltpu.VMEM(shape, BF16)] * n,
+        out_shape=[pltpu.VMEM(shape, F32)] + [pltpu.VMEM(shape, BF16)] * 2,
         in_specs=[VMEM] * 2,
-        out_specs=[VMEM] * (n + 1),
+        out_specs=[VMEM] * 3,
         compiler_params=PARAMS,
         name="pair_sum",
     )(near(kept), near(got))
@@ -631,9 +650,10 @@
     early = early_tiles(steps, fetched, tiles)
     early, first, third, second = lax.optimization_barrier((early, first, third, second))
 
-    held, kept, sent = tiles_forward(steps, ids, fetched, forward, tiles, early, [pair, first, second, third], n_out)
-    first, *others = pair_sum(kept, swap(sent, "col", 1))
-    others = swap_line(others, "col")
+    held, kept, distant, sent = tiles_forward(steps, ids, fetched, forward, tiles, early, [pair, first, second, third], n_out)
+    distant = distant_sum(kept, swap(distant, "col", 1))
+    first, second, third = pair_sum(kept, swap(sent, "col", 1))
+    others = swap_line([distant, second, third], "col")
     own, sent = own_sum(first, others)
     sent, slots = lax.optimization_barrier((sent, slots))
     ready = prepare(

time: 83.3 us -> 83.5 us (level)
  Pallas kernels: 12.6 us -> 19.9 us
  waiting for transfers between devices: 34.1 us -> 30.9 us
  starting transfers between devices: 34.2 us -> 31.1 us
    pallas_call x1, Pallas kernels: 1.77 us -> 5.63 us  [tiles_forward(): pl.pallas_call(forward_kernel, out_shape=[pltpu.VMEM((length + 1, TILE, T...]
    ppermute x24 -> x25, waiting for transfers between devices: 34.1 us -> 30.9 us  [swap(): return lax.ppermute(values, axis, [(i, i ^ mask) for i in range(size)])]
    ppermute x24 -> x25, starting transfers between devices: 34.2 us -> 31.1 us  [swap(): return lax.ppermute(values, axis, [(i, i ^ mask) for i in range(size)])]
    pallas_call x1, Pallas kernels: 1 us -> 3.42 us  [tiles_second(): pl.pallas_call(second_kernel, out_shape=[pltpu.VMEM((rows, TILE), F32)] +...]
  transfers between devices with their start and end apart: 24 -> 25, of which waited for: 19 -> 19; matrix products, arithmetic and copies ran while one was open for 0% -> 0% of each run, Pallas kernels for 10% -> 13%
where the time goes in v8:
time: 83.5 us; the launch traced here: 83.7 us
  starting transfers between devices  31.1 us (37%)
  waiting for transfers between devices  30.9 us (37%)
  Pallas kernels  19.9 us (24%)
  between operations  1.47 us (2%)
    ppermute x25, starting transfers between devices, swap(): return lax.ppermute(values, axis, [(i, i ^ mask) for i in range(size)])  31.1 us
    ppermute x25, waiting for transfers between devices, swap(): return lax.ppermute(values, axis, [(i, i ^ mask) for i in range(size)])  30.9 us
    pallas_call x1, Pallas kernels, tiles_forward(): pl.pallas_call(forward_kernel, out_shape=[pltpu.VMEM((length + 1, TILE, T...  5.63 us
    pallas_call x1, Pallas kernels, tiles_second(): pl.pallas_call(second_kernel, out_shape=[pltpu.VMEM((rows, TILE), F32)] +...  3.42 us
    pallas_call x1, Pallas kernels, prepare(): pl.pallas_call(functools.partial(prepare_kernel, n_back), out_shape=[pltp...  2.55 us
    pallas_call x1, Pallas kernels, early_tiles(): pl.pallas_call(early_kernel, out_shape=pltpu.VMEM((EARLY * PER + 1, TILE,...  2.5 us
    pallas_call x1, Pallas kernels, pick(): pl.pallas_call(functools.partial(pick_kernel, n_out), out_shape=[pltpu.SM...  2.28 us
  transfers between devices with their start and end apart: 25, of which 19 were waited for; matrix products, arithmetic and copies ran while one was open for 0% of the time, Pallas kernels for 13%

profile of v8, /device:TPU:0, one launch (start us, length us, event | category | flops | bytes accessed | tf_op | source)
XLA Modules:
  0.0 83.7 jit_solution(4298040615129888265)
XLA Ops:
  0.6 0.0 copy-start
  1.3 0.2 copy-done
  1.6 0.1 pad_add_fusion.ids
  1.6 2.0 %collective-permute-start = (bf16[256,128]{1,0:T(8,128)(2,1)S(1)}, bf16[256,128]{1,0:T(8,128)(2,1)S(1)}, u32[]{:S(2)}, u32[]{:S(2)}) collective-permute-start(bf16[256,128]{1,0:T(8,128)(2,1)S(1)} %constant_dynamic-slice_fusion.a), channel_id=1, source_target_pairs={{0,16},{16,0},{32,48},{48,32},{64,80},{80,64},{96,112},{112,96},{1... | collective-permute-start | bytes 196616 | tf_op jit(solution)/shard_map/ppermute | solution.py:28
  3.7 2.3 %pick_tiles.1 = (s32[1,768]{1,0:T(1,128)S(4)}, s32[1,768]{1,0:T(1,128)S(4)}, s32[1]{0:T(128)S(4)}, s32[3]{0:T(128)S(4)}, s32[1,640]{1,0:T(1,128)S(1)}) custom-call(s32[4]{0:T(128)S(1)} %pad_add_fusion.ids, s32[1,1,640]{2,1,0:T(1,128)} %rows.3, s32[1,1,640]{2,1,0:T(1,128)} %columns.3), custom_call_target="tpu_custom_call" | custom-call | tf_op jit(solution)/shard_map/pick_tiles/pallas_call | solution.py:120
  5.9 0.0 collective-permute-done.b
  6.0 3.3 %collective-permute-start.3 = (bf16[512,128]{1,0:T(8,128)(2,1)S(1)}, bf16[512,128]{1,0:T(8,128)(2,1)S(1)}, u32[]{:S(2)}, u32[]{:S(2)}) collective-permute-start(bf16[512,128]{1,0:T(8,128)(2,1)S(1)} %join.1.refs_0_), channel_id=1, source_target_pairs={{0,64},{16,80},{32,96},{48,112},{64,0},{80,16},{96,32},{112,48},{1... | collective-permute-start | bytes 393224 | tf_op jit(solution)/shard_map/ppermute | solution.py:28
  9.3 1.1 %collective-permute-start.2 = (bf16[512,128]{1,0:T(8,128)(2,1)S(1)}, bf16[512,128]{1,0:T(8,128)(2,1)S(1)}, u32[]{:S(2)}, u32[]{:S(2)}) collective-permute-start(bf16[512,128]{1,0:T(8,128)(2,1)S(1)} %join.1.refs_0_), channel_id=1, source_target_pairs={{0,96},{16,112},{32,64},{48,80},{64,32},{80,48},{96,0},{112,16},{1... | collective-permute-start | bytes 393224 | tf_op jit(solution)/shard_map/ppermute | solution.py:28
  10.3 0.0 collective-permute-start.1
  10.4 2.5 %early_tiles.1.early = bf16[161,128,128]{2,1,0:T(8,128)(2,1)S(1)} custom-call(s32[1]{0:T(128)S(4)} %get-tuple-element.75.steps, s32[1,768]{1,0:T(1,128)S(4)} %get-tuple-element.77.fetched, bf16[640,128,128]{2,1,0:T(8,128)(2,1)} %bitcast.8), custom_call_target="tpu_custom_call" | custom-call | tf_op jit(solution)/shard_map/early_tiles/pallas_call | solution.py:162
  12.9 0.3 collective-permute-done.3.refs_2_
  13.2 2.3 %collective-permute-done.2.refs_3_ = bf16[512,128]{1,0:T(8,128)(2,1)S(1)} collective-permute-done((bf16[512,128]{1,0:T(8,128)(2,1)S(1)}, bf16[512,128]{1,0:T(8,128)(2,1)S(1)}, u32[]{:S(2)}, u32[]{:S(2)}) %collective-permute-start.2) | collective-permute-done | bytes 131104 | tf_op jit(solution)/shard_map/ppermute | solution.py:28
  15.5 0.2 collective-permute-done.1.refs_1_
  15.7 5.6 %tiles_forward.1 = (bf16[673,128,128]{2,1,0:T(8,128)(2,1)S(1)}, f32[4,4,128,128]{3,2,1,0:T(8,128)S(1)}, bf16[4,128,128]{2,1,0:T(8,128)(2,1)S(1)}, bf16[3,4,128,128]{3,2,1,0:T(8,128)(2,1)S(1)}) custom-call(s32[1]{0:T(128)S(4)} %get-tuple-element.75.steps, s32[3]{0:T(128)S(4)} %get-tuple-element.76.ids, s32[1,768]{1,0:T(1,128)S(4)} %get-tuple-element.77.fetched, ...), custom_call_target="tpu_custom_call" | custom-call | tf_op jit(solution)/shard_map/tiles_forward/pallas_call | solution.py:324
  21.4 0.1 collective-permute-start.4
  21.5 0.5 collective-permute-start.5
  22.0 1.4 %collective-permute-done.5.got = bf16[4,128,128]{2,1,0:T(8,128)(2,1)S(1)} collective-permute-done((bf16[4,128,128]{2,1,0:T(8,128)(2,1)S(1)}, bf16[4,128,128]{2,1,0:T(8,128)(2,1)S(1)}, u32[]{:S(2)}, u32[]{:S(2)}) %collective-permute-start.5) | collective-permute-done | bytes 131104 | tf_op jit(solution)/shard_map/ppermute | solution.py:28
  23.4 0.1 collective-permute-start.6
  23.5 0.0 collective-permute-done.4.got
  23.5 0.1 pair_sum.1
  23.6 0.7 collective-permute-start.7
  24.3 3.5 %collective-permute-start.8 = (bf16[4,128,128]{2,1,0:T(8,128)(2,1)S(1)}, bf16[4,128,128]{2,1,0:T(8,128)(2,1)S(1)}, u32[]{:S(2)}, u32[]{:S(2)}) collective-permute-start(bf16[4,128,128]{2,1,0:T(8,128)(2,1)S(1)} %get-tuple-element.89), channel_id=1, source_target_pairs={{0,12},{2,14},{4,8},{6,10},{8,4},{10,6},{12,0},{14,2},{1,13},{3,15... | collective-permute-start | bytes 393224 | tf_op jit(solution)/shard_map/ppermute | solution.py:28
  27.7 3.6 %collective-permute-done.6.a = bf16[4,128,128]{2,1,0:T(8,128)(2,1)S(1)} collective-permute-done((bf16[4,128,128]{2,1,0:T(8,128)(2,1)S(1)}, bf16[4,128,128]{2,1,0:T(8,128)(2,1)S(1)}, u32[]{:S(2)}, u32[]{:S(2)}) %collective-permute-start.6) | collective-permute-done | bytes 131104 | tf_op jit(solution)/shard_map/ppermute | solution.py:28
  31.3 0.0 collective-permute-done.7.b
  31.3 2.0 %collective-permute-done.8.c = bf16[4,128,128]{2,1,0:T(8,128)(2,1)S(1)} collective-permute-done((bf16[4,128,128]{2,1,0:T(8,128)(2,1)S(1)}, bf16[4,128,128]{2,1,0:T(8,128)(2,1)S(1)}, u32[]{:S(2)}, u32[]{:S(2)}) %collective-permute-start.8) | collective-permute-done | bytes 131104 | tf_op jit(solution)/shard_map/ppermute | solution.py:28
  33.3 0.1 own_sum.1
  33.4 4.0 %collective-permute-start.9 = (bf16[4,128,128]{2,1,0:T(8,128)(2,1)S(1)}, bf16[4,128,128]{2,1,0:T(8,128)(2,1)S(1)}, u32[]{:S(2)}, u32[]{:S(2)}) collective-permute-start(bf16[4,128,128]{2,1,0:T(8,128)(2,1)S(1)} %get-tuple-element.93), channel_id=1, source_target_pairs={{0,1},{1,0},{2,3},{3,2},{4,5},{5,4},{6,7},{7,6},{8,9},{9,8},{10,11... | collective-permute-start | bytes 393224 | tf_op jit(solution)/shard_map/ppermute | solution.py:28
  37.3 2.5 %prepare.1 = (s32[1,768]{1,0:T(1,128)S(4)}, s32[2]{0:T(128)S(4)}, bf16[128,128]{1,0:T(8,128)(2,1)S(1)}, f32[1,128]{1,0:T(1,128)S(1)}, bf16[512,128]{1,0:T(8,128)(2,1)S(1)}) custom-call(s32[3]{0:T(128)S(4)} %get-tuple-element.76.ids, s32[1,1,640]{2,1,0:T(1,128)} %rows.3, s32[1,1,640]{2,1,0:T(1,128)} %columns.3, s32[1,640]{1,0:T(1,128)S(1)} %get-tuple-element.94.slots, ...), custom_call_target="tpu_custom_call" | custom-call | tf_op jit(solution)/shard_map/prepare/pallas_call | solution.py:212
  39.9 1.1 %collective-permute-done.9.other = bf16[4,128,128]{2,1,0:T(8,128)(2,1)S(1)} collective-permute-done((bf16[4,128,128]{2,1,0:T(8,128)(2,1)S(1)}, bf16[4,128,128]{2,1,0:T(8,128)(2,1)S(1)}, u32[]{:S(2)}, u32[]{:S(2)}) %collective-permute-start.9) | collective-permute-done | bytes 131104 | tf_op jit(solution)/shard_map/ppermute | solution.py:28
  41.0 0.9 %middle.1 = (bf16[512,128]{1,0:T(8,128)(2,1)}, f32[4,128,128]{2,1,0:T(8,128)S(1)}, bf16[4,128,128]{2,1,0:T(8,128)(2,1)S(1)}, f32[136,128]{1,0:T(8,128)S(1)}) custom-call(f32[4,128,128]{2,1,0:T(8,128)S(1)} %get-tuple-element.90.own, bf16[4,128,128]{2,1,0:T(8,128)(2,1)S(1)} %collective-permute-done.9.other, bf16[128,128]{1,0:T(8,128)(2,1)S(1)} %get-tuple-element.101.weight, ...), custom_call_target="tpu_custom_call" | custom-call | tf_op jit(solution)/shard_map/middle/pallas_call | solution.py:513
  41.9 3.2 %collective-permute-start.10 = (bf16[4,128,128]{2,1,0:T(8,128)(2,1)S(1)}, bf16[4,128,128]{2,1,0:T(8,128)(2,1)S(1)}, u32[]{:S(2)}, u32[]{:S(2)}) collective-permute-start(bf16[4,128,128]{2,1,0:T(8,128)(2,1)S(1)} %get-tuple-element.109), channel_id=1, source_target_pairs={{0,1},{1,0},{2,3},{3,2},{4,5},{5,4},{6,7},{7,6},{8,9},{9,8},{10,11... | collective-permute-start | bytes 393224 | tf_op jit(solution)/shard_map/ppermute | solution.py:28
  45.2 0.0 collective-permute-start.11
  45.2 1.3 %collective-permute-done.11.more = f32[136,128]{1,0:T(8,128)S(1)} collective-permute-done((f32[136,128]{1,0:T(8,128)S(1)}, f32[136,128]{1,0:T(8,128)S(1)}, u32[]{:S(2)}, u32[]{:S(2)}) %collective-permute-start.11) | collective-permute-done | bytes 69664 | tf_op jit(solution)/shard_map/ppermute | solution.py:28
  46.4 2.0 %collective-permute-done.10.other = bf16[4,128,128]{2,1,0:T(8,128)(2,1)S(1)} collective-permute-done((bf16[4,128,128]{2,1,0:T(8,128)(2,1)S(1)}, bf16[4,128,128]{2,1,0:T(8,128)(2,1)S(1)}, u32[]{:S(2)}, u32[]{:S(2)}) %collective-permute-start.10) | collective-permute-done | bytes 131104 | tf_op jit(solution)/shard_map/ppermute | solution.py:28
  48.4 0.2 collective-permute-start.15
  48.6 0.9 %collective-permute-start.14 = (bf16[592,128]{1,0:T(8,128)(2,1)S(1)}, bf16[592,128]{1,0:T(8,128)(2,1)S(1)}, u32[]{:S(2)}, u32[]{:S(2)}) collective-permute-start(bf16[592,128]{1,0:T(8,128)(2,1)S(1)} %message.1.refs_0_), channel_id=1, source_target_pairs={{0,12},{2,14},{4,8},{6,10},{8,4},{10,6},{12,0},{14,2},{1,13},{3,15... | collective-permute-start | bytes 454664 | tf_op jit(solution)/shard_map/ppermute | solution.py:28
  49.6 2.4 %collective-permute-start.13 = (bf16[592,128]{1,0:T(8,128)(2,1)S(1)}, bf16[592,128]{1,0:T(8,128)(2,1)S(1)}, u32[]{:S(2)}, u32[]{:S(2)}) collective-permute-start(bf16[592,128]{1,0:T(8,128)(2,1)S(1)} %message.1.refs_0_), channel_id=1, source_target_pairs={{0,4},{2,6},{4,0},{6,2},{8,12},{10,14},{12,8},{14,10},{1,5},{3,7},... | collective-permute-start | bytes 454664 | tf_op jit(solution)/shard_map/ppermute | solution.py:28
  52.0 0.0 collective-permute-start.12
  52.0 3.9 %collective-permute-done.15.refs_4_ = bf16[592,128]{1,0:T(8,128)(2,1)S(1)} collective-permute-done((bf16[592,128]{1,0:T(8,128)(2,1)S(1)}, bf16[592,128]{1,0:T(8,128)(2,1)S(1)}, u32[]{:S(2)}, u32[]{:S(2)}) %collective-permute-start.15) | collective-permute-done | bytes 151584 | tf_op jit(solution)/shard_map/ppermute | solution.py:28
  55.9 1.3 %collective-permute-done.14.refs_6_ = bf16[592,128]{1,0:T(8,128)(2,1)S(1)} collective-permute-done((bf16[592,128]{1,0:T(8,128)(2,1)S(1)}, bf16[592,128]{1,0:T(8,128)(2,1)S(1)}, u32[]{:S(2)}, u32[]{:S(2)}) %collective-permute-start.14) | collective-permute-done | bytes 151584 | tf_op jit(solution)/shard_map/ppermute | solution.py:28
  57.2 0.0 collective-permute-done.13.refs_2_
  57.2 0.0 collective-permute-start.16
  57.2 0.5 collective-permute-start.17
  57.8 0.0 collective-permute-start.18
  57.8 0.0 collective-permute-done.12.refs_1_
  57.8 0.9 %collective-permute-done.16.refs_3_ = bf16[592,128]{1,0:T(8,128)(2,1)S(1)} collective-permute-done((bf16[592,128]{1,0:T(8,128)(2,1)S(1)}, bf16[592,128]{1,0:T(8,128)(2,1)S(1)}, u32[]{:S(2)}, u32[]{:S(2)}) %collective-permute-start.16) | collective-permute-done | bytes 151584 | tf_op jit(solution)/shard_map/ppermute | solution.py:28
  58.6 0.2 collective-permute-done.17.refs_5_
  58.8 0.3 collective-permute-done.18.refs_7_
  59.1 1.4 %tiles_first.1 = (bf16[32,128,128]{2,1,0:T(8,128)(2,1)S(1)}, f32[136,128]{1,0:T(8,128)S(1)}, bf16[656,128]{1,0:T(8,128)(2,1)S(1)}) custom-call(s32[2]{0:T(128)S(4)} %get-tuple-element.105.steps, s32[3]{0:T(128)S(4)} %get-tuple-element.76.ids, s32[1,768]{1,0:T(1,128)S(4)} %get-tuple-element.106.picked, bf16[673,128,128]{2,1,0:T(8,128)(2,1)S(1)} %get-tuple-element.107.held, ...), custom_call_target="tpu_custom_call" | custom-call | tf_op jit(solution)/shard_map/tiles_first/pallas_call | solution.py:392
  60.6 2.5 %collective-permute-start.19 = (bf16[656,128]{1,0:T(8,128)(2,1)S(1)}, bf16[656,128]{1,0:T(8,128)(2,1)S(1)}, u32[]{:S(2)}, u32[]{:S(2)}) collective-permute-start(bf16[656,128]{1,0:T(8,128)(2,1)S(1)} %get-tuple-element.119), channel_id=1, source_target_pairs={{0,64},{16,80},{32,96},{48,112},{64,0},{80,16},{96,32},{112,48},{1... | collective-permute-start | bytes 503816 | tf_op jit(solution)/shard_map/ppermute | solution.py:28
  63.1 3.4 %tiles_second.1 = (f32[512,128]{1,0:T(8,128)S(1)}, bf16[656,128]{1,0:T(8,128)(2,1)S(1)}, bf16[656,128]{1,0:T(8,128)(2,1)S(1)}) custom-call(s32[2]{0:T(128)S(4)} %get-tuple-element.105.steps, s32[1,768]{1,0:T(1,128)S(4)} %get-tuple-element.106.picked, bf16[673,128,128]{2,1,0:T(8,128)(2,1)S(1)} %get-tuple-element.107.held, ...), custom_call_target="tpu_custom_call" | custom-call | flops 2822766592 | bytes 22052864 | tf_op jit(solution)/shard_map/tiles_second/pallas_call | solution.py:420
  66.5 0.1 collective-permute-start.20
  66.6 1.2 %collective-permute-start.21 = (bf16[656,128]{1,0:T(8,128)(2,1)S(1)}, bf16[656,128]{1,0:T(8,128)(2,1)S(1)}, u32[]{:S(2)}, u32[]{:S(2)}) collective-permute-start(bf16[656,128]{1,0:T(8,128)(2,1)S(1)} %get-tuple-element.123), channel_id=1, source_target_pairs={{0,96},{16,112},{32,64},{48,80},{64,32},{80,48},{96,0},{112,16},{1... | collective-permute-start | bytes 503816 | tf_op jit(solution)/shard_map/ppermute | solution.py:28
  67.8 1.3 %collective-permute-done.19.a = bf16[656,128]{1,0:T(8,128)(2,1)S(1)} collective-permute-done((bf16[656,128]{1,0:T(8,128)(2,1)S(1)}, bf16[656,128]{1,0:T(8,128)(2,1)S(1)}, u32[]{:S(2)}, u32[]{:S(2)}) %collective-permute-start.19) | collective-permute-done | bytes 167968 | tf_op jit(solution)/shard_map/ppermute | solution.py:28
  69.1 0.1 first_sum.1
  69.2 2.8 %collective-permute-done.20.a = bf16[656,128]{1,0:T(8,128)(2,1)S(1)} collective-permute-done((bf16[656,128]{1,0:T(8,128)(2,1)S(1)}, bf16[656,128]{1,0:T(8,128)(2,1)S(1)}, u32[]{:S(2)}, u32[]{:S(2)}) %collective-permute-start.20) | collective-permute-done | bytes 167968 | tf_op jit(solution)/shard_map/ppermute | solution.py:28
  72.0 1.3 %collective-permute-done.21.b = bf16[656,128]{1,0:T(8,128)(2,1)S(1)} collective-permute-done((bf16[656,128]{1,0:T(8,128)(2,1)S(1)}, bf16[656,128]{1,0:T(8,128)(2,1)S(1)}, u32[]{:S(2)}, u32[]{:S(2)}) %collective-permute-start.21) | collective-permute-done | bytes 167968 | tf_op jit(solution)/shard_map/ppermute | solution.py:28
  73.3 0.1 line_sum.1
  73.4 1.3 %collective-permute-start.24 = (bf16[400,128]{1,0:T(8,128)(2,1)S(1)}, bf16[400,128]{1,0:T(8,128)(2,1)S(1)}, u32[]{:S(2)}, u32[]{:S(2)}) collective-permute-start(bf16[400,128]{1,0:T(8,128)(2,1)S(1)} %get-tuple-element.128), channel_id=1, source_target_pairs={{0,16},{16,0},{32,48},{48,32},{64,80},{80,64},{96,112},{112,96},{1... | collective-permute-start | bytes 307208 | tf_op jit(solution)/shard_map/ppermute | solution.py:28
  74.6 2.7 %collective-permute-start.22 = (bf16[256,128]{1,0:T(8,128)(2,1)S(1)}, bf16[256,128]{1,0:T(8,128)(2,1)S(1)}, u32[]{:S(2)}, u32[]{:S(2)}) collective-permute-start(bf16[256,128]{1,0:T(8,128)(2,1)S(1)} %get-tuple-element.126), channel_id=1, source_target_pairs={{0,1},{1,0},{2,3},{3,2},{4,5},{5,4},{6,7},{7,6},{8,9},{9,8},{10,11... | collective-permute-start | bytes 196616 | tf_op jit(solution)/shard_map/ppermute | solution.py:28
  77.3 0.8 collective-permute-start.23
  78.1 2.5 %collective-permute-done.22.opposite = bf16[256,128]{1,0:T(8,128)(2,1)S(1)} collective-permute-done((bf16[256,128]{1,0:T(8,128)(2,1)S(1)}, bf16[256,128]{1,0:T(8,128)(2,1)S(1)}, u32[]{:S(2)}, u32[]{:S(2)}) %collective-permute-start.22) | collective-permute-done | bytes 65568 | tf_op jit(solution)/shard_map/ppermute | solution.py:28
  80.7 2.1 %collective-permute-done.23.corner = bf16[256,128]{1,0:T(8,128)(2,1)S(1)} collective-permute-done((bf16[256,128]{1,0:T(8,128)(2,1)S(1)}, bf16[256,128]{1,0:T(8,128)(2,1)S(1)}, u32[]{:S(2)}, u32[]{:S(2)}) %collective-permute-start.23) | collective-permute-done | bytes 65568 | tf_op jit(solution)/shard_map/ppermute | solution.py:28
  82.8 0.9 %finish.1 = (f32[512,128]{1,0:T(8,128)}, f32[128,128]{1,0:T(8,128)}, f32[1,128]{1,0:T(1,128)}) custom-call(s32[3]{0:T(128)S(4)} %get-tuple-element.76.ids, f32[256,128]{1,0:T(8,128)S(1)} %get-tuple-element.124.own, f32[136,128]{1,0:T(8,128)S(1)} %get-tuple-element.125.grads, bf16[256,128]{1,0:T(8,128)(2,1)S(1)} %collective-permute-done.22.opposite, ...), custom_call_target="tpu_custom_call" | custom-call | tf_op jit(solution)/shard_map/finish/pallas_call | solution.py:617
  (5 shorter events, 0.1 us)
Async XLA Ops:
  0.6 0.9 %copy-start = (bf16[512,128]{1,0:T(8,128)(2,1)S(1)}, bf16[512,128]{1,0:T(8,128)(2,1)}, u32[]{:S(2)}) copy-start(bf16[512,128]{1,0:T(8,128)(2,1)} %param.8) | copy-start | bytes 393220
  1.6 4.3 %collective-permute-start = (bf16[256,128]{1,0:T(8,128)(2,1)S(1)}, bf16[256,128]{1,0:T(8,128)(2,1)S(1)}, u32[]{:S(2)}, u32[]{:S(2)}) collective-permute-start(bf16[256,128]{1,0:T(8,128)(2,1)S(1)} %constant_dynamic-slice_fusion.a), channel_id=1, source_target_pairs={{0,16},{16,0},{32,48},{48,32},{64,80},{80,64},{96,112},{112,96},{1... | collective-permute-start | bytes 196616 | tf_op jit(solution)/shard_map/ppermute | solution.py:28
  6.0 7.2 %collective-permute-start.3 = (bf16[512,128]{1,0:T(8,128)(2,1)S(1)}, bf16[512,128]{1,0:T(8,128)(2,1)S(1)}, u32[]{:S(2)}, u32[]{:S(2)}) collective-permute-start(bf16[512,128]{1,0:T(8,128)(2,1)S(1)} %join.1.refs_0_), channel_id=1, source_target_pairs={{0,64},{16,80},{32,96},{48,112},{64,0},{80,16},{96,32},{112,48},{1... | collective-permute-start | bytes 393224 | tf_op jit(solution)/shard_map/ppermute | solution.py:28
  9.3 6.2 %collective-permute-start.2 = (bf16[512,128]{1,0:T(8,128)(2,1)S(1)}, bf16[512,128]{1,0:T(8,128)(2,1)S(1)}, u32[]{:S(2)}, u32[]{:S(2)}) collective-permute-start(bf16[512,128]{1,0:T(8,128)(2,1)S(1)} %join.1.refs_0_), channel_id=1, source_target_pairs={{0,96},{16,112},{32,64},{48,80},{64,32},{80,48},{96,0},{112,16},{1... | collective-permute-start | bytes 393224 | tf_op jit(solution)/shard_map/ppermute | solution.py:28
  10.3 5.4 %collective-permute-start.1 = (bf16[512,128]{1,0:T(8,128)(2,1)S(1)}, bf16[512,128]{1,0:T(8,128)(2,1)S(1)}, u32[]{:S(2)}, u32[]{:S(2)}) collective-permute-start(bf16[512,128]{1,0:T(8,128)(2,1)S(1)} %join.1.refs_0_), channel_id=1, source_target_pairs={{0,32},{16,48},{32,0},{48,16},{64,96},{80,112},{96,64},{112,80},{1... | collective-permute-start | bytes 393224 | tf_op jit(solution)/shard_map/ppermute | solution.py:28
  21.4 2.1 %collective-permute-start.4 = (bf16[3,4,128,128]{3,2,1,0:T(8,128)(2,1)S(1)}, bf16[3,4,128,128]{3,2,1,0:T(8,128)(2,1)S(1)}, u32[]{:S(2)}, u32[]{:S(2)}) collective-permute-start(bf16[3,4,128,128]{3,2,1,0:T(8,128)(2,1)S(1)} %get-tuple-element.85), channel_id=1, source_target_pairs={{0,2},{2,0},{4,6},{6,4},{8,10},{10,8},{12,14},{14,12},{1,3},{3,1},... | collective-permute-start | bytes 1179656 | tf_op jit(solution)/shard_map/ppermute | solution.py:28
  21.5 1.9 %collective-permute-start.5 = (bf16[4,128,128]{2,1,0:T(8,128)(2,1)S(1)}, bf16[4,128,128]{2,1,0:T(8,128)(2,1)S(1)}, u32[]{:S(2)}, u32[]{:S(2)}) collective-permute-start(bf16[4,128,128]{2,1,0:T(8,128)(2,1)S(1)} %get-tuple-element.87), channel_id=1, source_target_pairs={{0,2},{2,0},{4,6},{6,4},{8,10},{10,8},{12,14},{14,12},{1,3},{3,1},... | collective-permute-start | bytes 393224 | tf_op jit(solution)/shard_map/ppermute | solution.py:28
  23.4 7.9 %collective-permute-start.6 = (bf16[4,128,128]{2,1,0:T(8,128)(2,1)S(1)}, bf16[4,128,128]{2,1,0:T(8,128)(2,1)S(1)}, u32[]{:S(2)}, u32[]{:S(2)}) collective-permute-start(bf16[4,128,128]{2,1,0:T(8,128)(2,1)S(1)} %distant_sum.1), channel_id=1, source_target_pairs={{0,8},{2,10},{4,12},{6,14},{8,0},{10,2},{12,4},{14,6},{1,9},{3,11}... | collective-permute-start | bytes 393224 | tf_op jit(solution)/shard_map/ppermute | solution.py:28
  23.6 7.8 %collective-permute-start.7 = (bf16[4,128,128]{2,1,0:T(8,128)(2,1)S(1)}, bf16[4,128,128]{2,1,0:T(8,128)(2,1)S(1)}, u32[]{:S(2)}, u32[]{:S(2)}) collective-permute-start(bf16[4,128,128]{2,1,0:T(8,128)(2,1)S(1)} %get-tuple-element.88), channel_id=1, source_target_pairs={{0,4},{2,6},{4,0},{6,2},{8,12},{10,14},{12,8},{14,10},{1,5},{3,7},... | collective-permute-start | bytes 393224 | tf_op jit(solution)/shard_map/ppermute | solution.py:28
  24.3 9.1 %collective-permute-start.8 = (bf16[4,128,128]{2,1,0:T(8,128)(2,1)S(1)}, bf16[4,128,128]{2,1,0:T(8,128)(2,1)S(1)}, u32[]{:S(2)}, u32[]{:S(2)}) collective-permute-start(bf16[4,128,128]{2,1,0:T(8,128)(2,1)S(1)} %get-tuple-element.89), channel_id=1, source_target_pairs={{0,12},{2,14},{4,8},{6,10},{8,4},{10,6},{12,0},{14,2},{1,13},{3,15... | collective-permute-start | bytes 393224 | tf_op jit(solution)/shard_map/ppermute | solution.py:28
  33.4 7.6 %collective-permute-start.9 = (bf16[4,128,128]{2,1,0:T(8,128)(2,1)S(1)}, bf16[4,128,128]{2,1,0:T(8,128)(2,1)S(1)}, u32[]{:S(2)}, u32[]{:S(2)}) collective-permute-start(bf16[4,128,128]{2,1,0:T(8,128)(2,1)S(1)} %get-tuple-element.93), channel_id=1, source_target_pairs={{0,1},{1,0},{2,3},{3,2},{4,5},{5,4},{6,7},{7,6},{8,9},{9,8},{10,11... | collective-permute-start | bytes 393224 | tf_op jit(solution)/shard_map/ppermute | solution.py:28
  41.9 6.5 %collective-permute-start.10 = (bf16[4,128,128]{2,1,0:T(8,128)(2,1)S(1)}, bf16[4,128,128]{2,1,0:T(8,128)(2,1)S(1)}, u32[]{:S(2)}, u32[]{:S(2)}) collective-permute-start(bf16[4,128,128]{2,1,0:T(8,128)(2,1)S(1)} %get-tuple-element.109), channel_id=1, source_target_pairs={{0,1},{1,0},{2,3},{3,2},{4,5},{5,4},{6,7},{7,6},{8,9},{9,8},{10,11... | collective-permute-start | bytes 393224 | tf_op jit(solution)/shard_map/ppermute | solution.py:28
  45.2 1.3 %collective-permute-start.11 = (f32[136,128]{1,0:T(8,128)S(1)}, f32[136,128]{1,0:T(8,128)S(1)}, u32[]{:S(2)}, u32[]{:S(2)}) collective-permute-start(f32[136,128]{1,0:T(8,128)S(1)} %get-tuple-element.110.grads), channel_id=1, source_target_pairs={{0,2},{2,0},{4,6},{6,4},{8,10},{10,8},{12,14},{14,12},{1,3},{3,1},... | collective-permute-start | bytes 208904 | tf_op jit(solution)/shard_map/ppermute | solution.py:28
  48.4 7.5 %collective-permute-start.15 = (bf16[592,128]{1,0:T(8,128)(2,1)S(1)}, bf16[592,128]{1,0:T(8,128)(2,1)S(1)}, u32[]{:S(2)}, u32[]{:S(2)}) collective-permute-start(bf16[592,128]{1,0:T(8,128)(2,1)S(1)} %message.1.refs_0_), channel_id=1, source_target_pairs={{0,8},{2,10},{4,12},{6,14},{8,0},{10,2},{12,4},{14,6},{1,9},{3,11}... | collective-permute-start | bytes 454664 | tf_op jit(solution)/shard_map/ppermute | solution.py:28
  48.6 8.6 %collective-permute-start.14 = (bf16[592,128]{1,0:T(8,128)(2,1)S(1)}, bf16[592,128]{1,0:T(8,128)(2,1)S(1)}, u32[]{:S(2)}, u32[]{:S(2)}) collective-permute-start(bf16[592,128]{1,0:T(8,128)(2,1)S(1)} %message.1.refs_0_), channel_id=1, source_target_pairs={{0,12},{2,14},{4,8},{6,10},{8,4},{10,6},{12,0},{14,2},{1,13},{3,15... | collective-permute-start | bytes 454664 | tf_op jit(solution)/shard_map/ppermute | solution.py:28
  49.6 7.7 %collective-permute-start.13 = (bf16[592,128]{1,0:T(8,128)(2,1)S(1)}, bf16[592,128]{1,0:T(8,128)(2,1)S(1)}, u32[]{:S(2)}, u32[]{:S(2)}) collective-permute-start(bf16[592,128]{1,0:T(8,128)(2,1)S(1)} %message.1.refs_0_), channel_id=1, source_target_pairs={{0,4},{2,6},{4,0},{6,2},{8,12},{10,14},{12,8},{14,10},{1,5},{3,7},... | collective-permute-start | bytes 454664 | tf_op jit(solution)/shard_map/ppermute | solution.py:28
  52.0 5.8 %collective-permute-start.12 = (bf16[592,128]{1,0:T(8,128)(2,1)S(1)}, bf16[592,128]{1,0:T(8,128)(2,1)S(1)}, u32[]{:S(2)}, u32[]{:S(2)}) collective-permute-start(bf16[592,128]{1,0:T(8,128)(2,1)S(1)} %message.1.refs_0_), channel_id=1, source_target_pairs={{0,2},{2,0},{4,6},{6,4},{8,10},{10,8},{12,14},{14,12},{1,3},{3,1},... | collective-permute-start | bytes 454664 | tf_op jit(solution)/shard_map/ppermute | solution.py:28
  57.2 1.4 %collective-permute-start.16 = (bf16[592,128]{1,0:T(8,128)(2,1)S(1)}, bf16[592,128]{1,0:T(8,128)(2,1)S(1)}, u32[]{:S(2)}, u32[]{:S(2)}) collective-permute-start(bf16[592,128]{1,0:T(8,128)(2,1)S(1)} %collective-permute-done.13.refs_2_), channel_id=1, source_target_pairs={{0,2},{2,0},{4,6},{6,4},{8,10},{10,8},{12,14},{14,12},{1,3},{3,1},... | collective-permute-start | bytes 454664 | tf_op jit(solution)/shard_map/ppermute | solution.py:28
  57.2 1.6 %collective-permute-start.17 = (bf16[592,128]{1,0:T(8,128)(2,1)S(1)}, bf16[592,128]{1,0:T(8,128)(2,1)S(1)}, u32[]{:S(2)}, u32[]{:S(2)}) collective-permute-start(bf16[592,128]{1,0:T(8,128)(2,1)S(1)} %collective-permute-done.15.refs_4_), channel_id=1, source_target_pairs={{0,2},{2,0},{4,6},{6,4},{8,10},{10,8},{12,14},{14,12},{1,3},{3,1},... | collective-permute-start | bytes 454664 | tf_op jit(solution)/shard_map/ppermute | solution.py:28
  57.8 1.4 %collective-permute-start.18 = (bf16[592,128]{1,0:T(8,128)(2,1)S(1)}, bf16[592,128]{1,0:T(8,128)(2,1)S(1)}, u32[]{:S(2)}, u32[]{:S(2)}) collective-permute-start(bf16[592,128]{1,0:T(8,128)(2,1)S(1)} %collective-permute-done.14.refs_6_), channel_id=1, source_target_pairs={{0,2},{2,0},{4,6},{6,4},{8,10},{10,8},{12,14},{14,12},{1,3},{3,1},... | collective-permute-start | bytes 454664 | tf_op jit(solution)/shard_map/ppermute | solution.py:28
  60.6 8.5 %collective-permute-start.19 = (bf16[656,128]{1,0:T(8,128)(2,1)S(1)}, bf16[656,128]{1,0:T(8,128)(2,1)S(1)}, u32[]{:S(2)}, u32[]{:S(2)}) collective-permute-start(bf16[656,128]{1,0:T(8,128)(2,1)S(1)} %get-tuple-element.119), channel_id=1, source_target_pairs={{0,64},{16,80},{32,96},{48,112},{64,0},{80,16},{96,32},{112,48},{1... | collective-permute-start | bytes 503816 | tf_op jit(solution)/shard_map/ppermute | solution.py:28
  66.5 5.4 %collective-permute-start.20 = (bf16[656,128]{1,0:T(8,128)(2,1)S(1)}, bf16[656,128]{1,0:T(8,128)(2,1)S(1)}, u32[]{:S(2)}, u32[]{:S(2)}) collective-permute-start(bf16[656,128]{1,0:T(8,128)(2,1)S(1)} %get-tuple-element.122), channel_id=1, source_target_pairs={{0,32},{16,48},{32,0},{48,16},{64,96},{80,112},{96,64},{112,80},{1... | collective-permute-start | bytes 503816 | tf_op jit(solution)/shard_map/ppermute | solution.py:28
  66.6 6.7 %collective-permute-start.21 = (bf16[656,128]{1,0:T(8,128)(2,1)S(1)}, bf16[656,128]{1,0:T(8,128)(2,1)S(1)}, u32[]{:S(2)}, u32[]{:S(2)}) collective-permute-start(bf16[656,128]{1,0:T(8,128)(2,1)S(1)} %get-tuple-element.123), channel_id=1, source_target_pairs={{0,96},{16,112},{32,64},{48,80},{64,32},{80,48},{96,0},{112,16},{1... | collective-permute-start | bytes 503816 | tf_op jit(solution)/shard_map/ppermute | solution.py:28
  73.4 9.4 %collective-permute-start.24 = (bf16[400,128]{1,0:T(8,128)(2,1)S(1)}, bf16[400,128]{1,0:T(8,128)(2,1)S(1)}, u32[]{:S(2)}, u32[]{:S(2)}) collective-permute-start(bf16[400,128]{1,0:T(8,128)(2,1)S(1)} %get-tuple-element.128), channel_id=1, source_target_pairs={{0,16},{16,0},{32,48},{48,32},{64,80},{80,64},{96,112},{112,96},{1... | collective-permute-start | bytes 307208 | tf_op jit(solution)/shard_map/ppermute | solution.py:28
  74.6 6.0 %collective-permute-start.22 = (bf16[256,128]{1,0:T(8,128)(2,1)S(1)}, bf16[256,128]{1,0:T(8,128)(2,1)S(1)}, u32[]{:S(2)}, u32[]{:S(2)}) collective-permute-start(bf16[256,128]{1,0:T(8,128)(2,1)S(1)} %get-tuple-element.126), channel_id=1, source_target_pairs={{0,1},{1,0},{2,3},{3,2},{4,5},{5,4},{6,7},{7,6},{8,9},{9,8},{10,11... | collective-permute-start | bytes 196616 | tf_op jit(solution)/shard_map/ppermute | solution.py:28
  77.3 5.5 %collective-permute-start.23 = (bf16[256,128]{1,0:T(8,128)(2,1)S(1)}, bf16[256,128]{1,0:T(8,128)(2,1)S(1)}, u32[]{:S(2)}, u32[]{:S(2)}) collective-permute-start(bf16[256,128]{1,0:T(8,128)(2,1)S(1)} %get-tuple-element.127), channel_id=1, source_target_pairs={{0,17},{1,16},{16,1},{17,0},{32,49},{33,48},{48,33},{49,32},{64,81... | collective-permute-start | bytes 196616 | tf_op jit(solution)/shard_map/ppermute | solution.py:28
